TPU v7x, 256 devices: a whole 4x4x8 slice. The times are simulated.
256 devices in a mesh: src: 8 (over y, core), obs: 32 (over x, z).
Axes of the slice: x: 4, y: 4, z: 8, core: 2. Of those that a mesh axis runs over, the one named last changes fastest.
Arguments:
- krylov_basis: float32 [16, 2, 8, 1048576], P(None, None, None, ('src', 'obs')), as said below
- near_field: bfloat16 [2, 8192, 128, 128], P(None, ('src', 'obs')), as said below
- leaf_in: bfloat16 [2, 8192, 128, 128], P(None, ('src', 'obs')), may hold values from -0.375 to 0.375
- leaf_out: bfloat16 [2, 8192, 128, 128], P(None, ('src', 'obs')), may hold values from -0.375 to 0.375
- level_mixers: float32 [5, 2, 2, 128, 32768], P(None, None, None, None, ('src', 'obs')), may hold values from -0.25 to 0.25
- block_ranks: int32 [5, 8192], P(None, ('src', 'obs')), may hold values from 64 to 128
- partner_tables: int32 [5, 256, 32], P(None, ('src', 'obs')), may hold values from 0 to 31, each once within a row
Outputs:
- gram_coeffs: float32 [16, 2, 8, 8], replicated
- new_block: float32 [2, 8, 1048576], P(None, None, ('src', 'obs'))
- block_gram: float32 [2, 8, 8], replicated
Inputs may be any that keep to these rules, and one draw needn't show every extreme that they name: `krylov_basis`: real and imaginary parts of basis entries; the blocks are not mutually orthogonal. `near_field`: real and imaginary parts of each leaf's self-interaction block. `partner_tables`: each row of 32 entries is a permutation of 0 to 31.
All inputs are finite; a program needn't handle non-finite values.
Results may differ from a plain program's by a relative error of at most 0.0034.
Values sent between devices are 32-bit elements; how exact they have to be, the bound alone decides.
No kernel may reach another device: no remote copies, remote signals or barrier semaphores. Data moves between devices by JAX's collectives and lax.ppermute only.
A program may use at most 128 MiB of HBM per device.

v0:
```python
import jax
import jax.numpy as jnp
from jax import lax
from jax.experimental import pallas as pl
from jax.experimental.pallas import tpu as pltpu
from jax.sharding import PartitionSpec as P

NT = (((1,), (1,)), ((), ()))
NN = (((1,), (0,)), ((), ()))
KERNEL_VMEM = 24 * 1024 * 1024


def dot_nt(left, right):
    return lax.dot_general(left, right, NT, preferred_element_type=jnp.float32)


def dot_nn(left, right):
    return lax.dot_general(left, right, NN, preferred_element_type=jnp.float32)


def split3(value):
    high = value.astype(jnp.bfloat16)
    rest = value - high.astype(jnp.float32)
    middle = rest.astype(jnp.bfloat16)
    low = (rest - middle.astype(jnp.float32)).astype(jnp.bfloat16)
    return high, middle, low


def complex_rows(rows):
    real, imag = rows[:8], rows[8:]
    return jnp.concatenate(
        [jnp.concatenate([real, -imag], axis=1), jnp.concatenate([imag, real], axis=1)], axis=0
    )


def leaf_product(rows, real, imag):
    return dot_nt(
        complex_rows(rows).astype(jnp.bfloat16), jnp.concatenate([real, imag], axis=1)
    )


def leaves_kernel(basis_ref, leaf_ref, out_ref):
    count = leaf_ref.shape[1]
    for leaf in range(count):
        rows = basis_ref[0, :, :, leaf * 128 : (leaf + 1) * 128].reshape(16, 128)
        rows = rows.astype(jnp.bfloat16).astype(jnp.float32)
        out_ref[leaf] = leaf_product(rows, leaf_ref[0, leaf], leaf_ref[1, leaf])


def apply_leaves(krylov_basis, leaves, steps):
    last = krylov_basis.shape[0] - 1
    count = leaves.shape[1]
    part = count // steps
    return pl.pallas_call(
        leaves_kernel,
        grid=(steps,),
        in_specs=[
            pl.BlockSpec((1, 2, 8, part * 128), lambda i: (last, 0, 0, i)),
            pl.BlockSpec((2, part, 128, 128), lambda i: (0, i, 0, 0)),
        ],
        out_specs=pl.BlockSpec((part, 16, 128), lambda i: (i, 0, 0)),
        out_shape=jax.ShapeDtypeStruct((count, 16, 128), jnp.float32),
        compiler_params=pltpu.CompilerParams(vmem_limit_bytes=KERNEL_VMEM),
        cost_estimate=pl.CostEstimate(
            flops=count * 16 * 256 * 128 * 2, bytes_accessed=count * 73728, transcendentals=0
        ),
    )(krylov_basis, leaves)


def stacked(basis):
    width = basis.shape[3]
    return jnp.concatenate(
        [basis[:, 0].reshape(128, width), basis[:, 1].reshape(128, width)], axis=0
    )


def basis_gram_kernel(basis_ref, out_ref, even_ref, odd_ref):
    step = pl.program_id(0)

    @pl.when(step == 0)
    def _():
        even_ref[...] = jnp.zeros_like(even_ref)
        odd_ref[...] = jnp.zeros_like(odd_ref)

    high, middle, low = split3(stacked(basis_ref[...]))
    even_ref[...] += dot_nt(high, high) + dot_nt(middle, middle)
    odd_ref[...] += dot_nt(high, middle) + dot_nt(high, low)

    @pl.when(step == pl.num_programs(0) - 1)
    def _():
        gram = even_ref[...] + odd_ref[...] + odd_ref[...].T
        real = gram[:128, :128] + gram[128:, 128:]
        imag = gram[:128, 128:] - gram[128:, :128]
        row = lax.broadcasted_iota(jnp.int32, (128, 128), 0)
        column = lax.broadcasted_iota(jnp.int32, (128, 128), 1)
        out_ref[...] = jnp.where(row <= column, real, imag)


def basis_gram(krylov_basis, steps):
    width = krylov_basis.shape[3] // steps
    return pl.pallas_call(
        basis_gram_kernel,
        grid=(steps,),
        in_specs=[pl.BlockSpec((16, 2, 8, width), lambda i: (0, 0, 0, i))],
        out_specs=pl.BlockSpec((128, 128), lambda i: (0, 0)),
        out_shape=jax.ShapeDtypeStruct((128, 128), jnp.float32),
        scratch_shapes=[pltpu.VMEM((256, 256), jnp.float32)] * 2,
        compiler_params=pltpu.CompilerParams(vmem_limit_bytes=KERNEL_VMEM),
        cost_estimate=pl.CostEstimate(
            flops=4 * 2 * 256 * 256 * 4096, bytes_accessed=4 << 20, transcendentals=0
        ),
    )(krylov_basis)


def mix(level, own_ref, partner_ref, mixer_ref, rank_ref, table_ref, picked_ref, write):
    for leaf in range(32):
        picked_ref[leaf] = partner_ref[table_ref[level, 0, leaf]]
    both = jnp.concatenate(
        [own_ref[...].reshape(512, 128), picked_ref[...].reshape(512, 128)], axis=1
    )
    mixer = mixer_ref[0]
    weights = jnp.concatenate(
        [
            jnp.concatenate([mixer[0, 0], mixer[0, 1]], axis=1),
            jnp.concatenate([mixer[1, 0], mixer[1, 1]], axis=1),
        ],
        axis=0,
    )
    product = jnp.dot(
        both, weights, precision=lax.Precision.HIGHEST, preferred_element_type=jnp.float32
    )
    column = lax.broadcasted_iota(jnp.int32, (16, 128), 1)
    for leaf in range(32):
        by_real = product[leaf * 16 : (leaf + 1) * 16, :128]
        by_imag = product[leaf * 16 : (leaf + 1) * 16, 128:]
        mixed = jnp.concatenate([by_real[:8] - by_imag[8:], by_real[8:] + by_imag[:8]], axis=0)
        write(leaf, jnp.where(column < rank_ref[level, leaf], mixed, 0.0))


def level_kernel(level, own_ref, partner_ref, mixer_ref, rank_ref, table_ref, out_ref, picked_ref):
    def write(leaf, value):
        out_ref[leaf] = value

    mix(level, own_ref, partner_ref, mixer_ref, rank_ref, table_ref, picked_ref, write)


def whole(shape):
    return pl.BlockSpec(shape, lambda i: (0,) * len(shape))


def level_specs(level):
    return [
        whole((32, 16, 128)),
        whole((32, 16, 128)),
        pl.BlockSpec((1, 2, 2, 128, 128), lambda i: (level, 0, 0, 0, 0)),
        pl.BlockSpec(memory_space=pltpu.SMEM),
        pl.BlockSpec(memory_space=pltpu.SMEM),
    ]


def next_level(level, own, partner, level_mixers, block_ranks, partner_tables):
    return pl.pallas_call(
        lambda *refs: level_kernel(level, *refs),
        grid=(1,),
        in_specs=level_specs(level),
        out_specs=whole((32, 16, 128)),
        out_shape=jax.ShapeDtypeStruct((32, 16, 128), jnp.float32),
        scratch_shapes=[pltpu.VMEM((32, 16, 128), jnp.float32)],
        compiler_params=pltpu.CompilerParams(vmem_limit_bytes=KERNEL_VMEM),
        cost_estimate=pl.CostEstimate(
            flops=6 * 512 * 256 * 256 * 2, bytes_accessed=1 << 20, transcendentals=0
        ),
    )(own, partner, level_mixers, block_ranks, partner_tables)


def project_kernel(
    level, own_ref, partner_ref, mixer_ref, rank_ref, table_ref, leaf_ref, close_ref, basis_ref,
    image_ref, sums_ref, picked_ref,
):
    def write(leaf, value):
        rounded = value.astype(jnp.bfloat16).astype(jnp.float32)
        far = leaf_product(rounded, leaf_ref[0, leaf], leaf_ref[1, leaf])
        image_ref[:, leaf * 128 : (leaf + 1) * 128] = far + close_ref[leaf]

    mix(level, own_ref, partner_ref, mixer_ref, rank_ref, table_ref, picked_ref, write)
    image = image_ref[...]
    high, middle, low = split3(image)
    three = jnp.concatenate([high, middle, low], axis=0)
    two = three[:32]
    inner = jnp.zeros((16, 256), jnp.float32)
    width = 1024
    for start in range(0, 4096, width):
        here = slice(start, start + width)
        b_high, b_middle, b_low = split3(stacked(basis_ref[:, :, :, here]))
        one = dot_nt(three[:, here], b_high)
        inner += one[:16] + one[16:32] + one[32:]
        one = dot_nt(two[:, here], b_middle)
        inner += one[:16] + one[16:]
        inner += dot_nt(high[:, here], b_low)
    sums_ref[0:8] = inner[:8, :128] + inner[8:, 128:]
    sums_ref[8:16] = inner[8:, :128] - inner[:8, 128:]
    one = dot_nt(three, high)
    square = one[:16] + one[16:32] + one[32:]
    one = dot_nt(two, middle)
    square += one[:16] + one[16:]
    square += dot_nt(high, low)
    real = square[:8, :8] + square[8:, 8:]
    imag = square[:8, 8:] - square[8:, :8]
    sums_ref[16:24] = jnp.concatenate([real, imag, jnp.zeros((8, 112), jnp.float32)], axis=1)


def project(level, own, partner, level_mixers, block_ranks, partner_tables, leaf_out, close, krylov_basis):
    return pl.pallas_call(
        lambda *refs: project_kernel(level, *refs),
        grid=(1,),
        in_specs=level_specs(level)
        + [whole(leaf_out.shape), whole(close.shape), whole(krylov_basis.shape)],
        out_specs=[whole((16, 4096)), whole((24, 128))],
        out_shape=[
            jax.ShapeDtypeStruct((16, 4096), jnp.float32),
            jax.ShapeDtypeStruct((24, 128), jnp.float32),
        ],
        scratch_shapes=[pltpu.VMEM((32, 16, 128), jnp.float32)],
        compiler_params=pltpu.CompilerParams(vmem_limit_bytes=KERNEL_VMEM),
        cost_estimate=pl.CostEstimate(
            flops=6 * 512 * 256 * 256 * 2, bytes_accessed=8 << 20, transcendentals=0
        ),
    )(own, partner, level_mixers, block_ranks, partner_tables, leaf_out, close, krylov_basis)


def dot_high(left, right, numbers):
    return lax.dot_general(
        left, right, numbers, precision=lax.Precision.HIGHEST, preferred_element_type=jnp.float32
    )


def finish_kernel(scale, sums_ref, gram_ref, image_ref, basis_ref, total_ref, new_ref, block_ref):
    sums = jnp.sum(sums_ref[...], axis=0) * scale
    first = sums[:16]
    packed = gram_ref[...] * scale
    row = lax.broadcasted_iota(jnp.int32, (128, 128), 0)
    column = lax.broadcasted_iota(jnp.int32, (128, 128), 1)
    flipped = packed.T
    gram_real = jnp.where(row <= column, packed, flipped)
    gram_imag = jnp.where(row > column, packed, jnp.where(row < column, -flipped, 0.0))
    gram = jnp.concatenate([gram_real, gram_imag], axis=1)

    def by_gram(rows):
        one = dot_high(rows, gram, NN)
        real = one[:8, :128] + one[8:, 128:]
        imag = one[8:, :128] - one[:8, 128:]
        return jnp.concatenate([real, imag], axis=0)

    total = first + (first - by_gram(first))
    rest = first - by_gram(total)

    def inner(left, right):
        one = dot_high(left, right, NT)
        return one[:8, :8] + one[8:, 8:], one[:8, 8:] - one[8:, :8]

    one_real, one_imag = inner(first, total)
    two_real, two_imag = inner(total, rest)
    block_ref[0] = sums[16:24, 0:8] - one_real - two_real
    block_ref[1] = sums[16:24, 8:16] - one_imag - two_imag
    turned = total.T
    total_ref[:, 0] = turned[:, :8].reshape(16, 8, 8)
    total_ref[:, 1] = turned[:, 8:].reshape(16, 8, 8)
    high, middle, low = split3(complex_rows(total))
    three = jnp.concatenate([high, middle, low], axis=0)
    two = three[:32]
    width = 1024
    for start in range(0, 4096, width):
        here = slice(start, start + width)
        b_high, b_middle, b_low = split3(stacked(basis_ref[:, :, :, here]))
        one = dot_nn(three, b_high)
        taken = one[:16] + one[16:32] + one[32:]
        one = dot_nn(two, b_middle)
        taken += one[:16] + one[16:]
        taken += dot_nn(high, b_low)
        new_ref[:, :, here] = (image_ref[:, here] - taken).reshape(2, 8, width)


def finish(scale, sums, gram, image, krylov_basis):
    return pl.pallas_call(
        lambda *refs: finish_kernel(scale, *refs),
        grid=(1,),
        in_specs=[
            whole(sums.shape),
            whole(gram.shape),
            whole(image.shape),
            whole(krylov_basis.shape),
        ],
        out_specs=[whole((16, 2, 8, 8)), whole((2, 8, 4096)), whole((2, 8, 8))],
        out_shape=[
            jax.ShapeDtypeStruct((16, 2, 8, 8), jnp.float32),
            jax.ShapeDtypeStruct((2, 8, 4096), jnp.float32),
            jax.ShapeDtypeStruct((2, 8, 8), jnp.float32),
        ],
        compiler_params=pltpu.CompilerParams(vmem_limit_bytes=KERNEL_VMEM),
        cost_estimate=pl.CostEstimate(
            flops=6 * 16 * 256 * 4096 * 2, bytes_accessed=6 << 20, transcendentals=0
        ),
    )(sums, gram, image, krylov_basis)


def exchange(value, axis, bit_number):
    pairs = [(source, source ^ (1 << bit_number)) for source in range(lax.axis_size(axis))]
    return lax.ppermute(value, axis, pairs)


def from_all(value, axis):
    copies = jnp.broadcast_to(value[None], (lax.axis_size(axis),) + value.shape)
    return lax.all_to_all(copies, axis, 0, 0)


def per_device(
    krylov_basis, near_field, leaf_in, leaf_out, level_mixers, block_ranks, partner_tables
):
    src_bits = lax.axis_size("src").bit_length() - 1
    obs_bits = lax.axis_size("obs").bit_length() - 1
    plan = [
        ("src", src_bits - 1),
        ("src", src_bits - 2),
        ("obs", obs_bits - 1),
        ("obs", obs_bits - 2),
        ("obs", obs_bits - 3),
    ]
    coeffs = apply_leaves(krylov_basis, leaf_in, 4)
    close = apply_leaves(krylov_basis, near_field, 4)
    gram = basis_gram(krylov_basis, 4)
    for axis, bits in (("src", src_bits), ("obs", obs_bits)):
        for bit in range(bits):
            gram = gram + exchange(gram, axis, bit)
    for level, (axis, bit) in enumerate(plan):
        partner = exchange(coeffs, axis, bit)
        if level < len(plan) - 1:
            coeffs = next_level(level, coeffs, partner, level_mixers, block_ranks, partner_tables)
        else:
            image, sums = project(
                level, coeffs, partner, level_mixers, block_ranks, partner_tables,
                leaf_out, close, krylov_basis,
            )
    sums = jnp.sum(from_all(sums, "src"), axis=0)
    sums = from_all(sums, "obs")
    devices = lax.axis_size("src") * lax.axis_size("obs")
    scale = 1.0 / (krylov_basis.shape[3] * devices)
    return tuple(finish(scale, sums, gram, image, krylov_basis))


def solution(mesh):
    in_specs = (
        P(None, None, None, ("src", "obs")),
        P(None, ("src", "obs"), None, None),
        P(None, ("src", "obs"), None, None),
        P(None, ("src", "obs"), None, None),
        P(None, None, None, None, ("src", "obs")),
        P(None, ("src", "obs")),
        P(None, ("src", "obs"), None),
    )
    out_specs = (P(), P(None, None, ("src", "obs")), P())
    return jax.shard_map(
        per_device, mesh=mesh, in_specs=in_specs, out_specs=out_specs, check_vma=False
    )
```

profile of v0, /device:TPU:2, one launch (start us, length us, event | category | flops | bytes accessed | tf_op | source)
XLA Modules:
  0.0 133.4 jit_solution(16727668474534613010)
XLA Ops:
  0.6 0.0 copy-start
  0.6 2.2 %copy-done = f32[16,2,8,4096]{3,2,1,0:T(8,128)S(1)} copy-done((f32[16,2,8,4096]{3,2,1,0:T(8,128)S(1)}, f32[16,2,8,4096]{3,2,1,0:T(8,128)}, u32[]{:S(2)}) %copy-start) | copy-done | bytes 4194328
  2.8 1.6 %copy-done.5 = bf16[2,32,128,128]{3,2,1,0:T(8,128)(2,1)S(1)} copy-done((bf16[2,32,128,128]{3,2,1,0:T(8,128)(2,1)S(1)}, bf16[2,32,128,128]{3,2,1,0:T(8,128)(2,1)}, u32[]{:S(2)}) %copy-start.5) | copy-done | bytes 2097176
  4.4 1.2 shard_map.94.refs_0_
  5.6 3.2 %collective-permute-start = (f32[32,16,128]{2,1,0:T(8,128)S(1)}, f32[32,16,128]{2,1,0:T(8,128)S(1)}, u32[]{:S(2)}, u32[]{:S(2)}) collective-permute-start(f32[32,16,128]{2,1,0:T(8,128)S(1)} %shard_map.94.refs_0_), channel_id=1, source_target_pairs={{0,128},{32,160},{64,192},{96,224},{128,0},{160,32},{192,64},{224,... | collective-permute-start | bytes 786440 | tf_op jit(solution)/shard_map/ppermute | solution.py:308
  8.8 6.4 %collective-permute-done.refs_1_ = f32[32,16,128]{2,1,0:T(8,128)S(1)} collective-permute-done((f32[32,16,128]{2,1,0:T(8,128)S(1)}, f32[32,16,128]{2,1,0:T(8,128)S(1)}, u32[]{:S(2)}, u32[]{:S(2)}) %collective-permute-start) | collective-permute-done | bytes 262176 | tf_op jit(solution)/shard_map/ppermute | solution.py:308
  15.2 1.2 shard_map.95.refs_0_
  16.4 1.7 %collective-permute-start.1 = (f32[32,16,128]{2,1,0:T(8,128)S(1)}, f32[32,16,128]{2,1,0:T(8,128)S(1)}, u32[]{:S(2)}, u32[]{:S(2)}) collective-permute-start(f32[32,16,128]{2,1,0:T(8,128)S(1)} %shard_map.95.refs_0_), channel_id=1, source_target_pairs={{0,64},{32,96},{64,0},{96,32},{128,192},{160,224},{192,128},{224,1... | collective-permute-start | bytes 786440 | tf_op jit(solution)/shard_map/ppermute | solution.py:308
  18.1 5.6 %collective-permute-done.1.refs_1_ = f32[32,16,128]{2,1,0:T(8,128)S(1)} collective-permute-done((f32[32,16,128]{2,1,0:T(8,128)S(1)}, f32[32,16,128]{2,1,0:T(8,128)S(1)}, u32[]{:S(2)}, u32[]{:S(2)}) %collective-permute-start.1) | collective-permute-done | bytes 262176 | tf_op jit(solution)/shard_map/ppermute | solution.py:308
  23.7 1.2 shard_map.96.refs_0_
  24.9 0.0 copy-start.1
  24.9 2.2 %collective-permute-start.2 = (f32[32,16,128]{2,1,0:T(8,128)S(1)}, f32[32,16,128]{2,1,0:T(8,128)S(1)}, u32[]{:S(2)}, u32[]{:S(2)}) collective-permute-start(f32[32,16,128]{2,1,0:T(8,128)S(1)} %shard_map.96.refs_0_), channel_id=1, source_target_pairs={{0,16},{1,17},{2,18},{3,19},{4,20},{5,21},{6,22},{7,23},{8,24},{9,... | collective-permute-start | bytes 786440 | tf_op jit(solution)/shard_map/ppermute | solution.py:308
  27.1 5.7 %collective-permute-done.2.refs_1_ = f32[32,16,128]{2,1,0:T(8,128)S(1)} collective-permute-done((f32[32,16,128]{2,1,0:T(8,128)S(1)}, f32[32,16,128]{2,1,0:T(8,128)S(1)}, u32[]{:S(2)}, u32[]{:S(2)}) %collective-permute-start.2) | collective-permute-done | bytes 262176 | tf_op jit(solution)/shard_map/ppermute | solution.py:308
  32.9 1.2 shard_map.97.refs_0_
  34.1 0.5 collective-permute-start.3
  34.6 6.0 %collective-permute-done.3.refs_1_ = f32[32,16,128]{2,1,0:T(8,128)S(1)} collective-permute-done((f32[32,16,128]{2,1,0:T(8,128)S(1)}, f32[32,16,128]{2,1,0:T(8,128)S(1)}, u32[]{:S(2)}, u32[]{:S(2)}) %collective-permute-start.3) | collective-permute-done | bytes 262176 | tf_op jit(solution)/shard_map/ppermute | solution.py:308
  40.6 1.2 shard_map.98.refs_0_
  41.8 0.0 copy-start.7
  41.8 7.3 %collective-permute-start.4 = (f32[32,16,128]{2,1,0:T(8,128)S(1)}, f32[32,16,128]{2,1,0:T(8,128)S(1)}, u32[]{:S(2)}, u32[]{:S(2)}) collective-permute-start(f32[32,16,128]{2,1,0:T(8,128)S(1)} %shard_map.98.refs_0_), channel_id=1, source_target_pairs={{0,4},{1,5},{2,6},{3,7},{4,0},{5,1},{6,2},{7,3},{8,12},{9,13},{10,... | collective-permute-start | bytes 786440 | tf_op jit(solution)/shard_map/ppermute | solution.py:308
  49.1 1.2 shard_map.99.refs_6_
  50.2 3.6 %collective-permute-done.4.refs_1_ = f32[32,16,128]{2,1,0:T(8,128)S(1)} collective-permute-done((f32[32,16,128]{2,1,0:T(8,128)S(1)}, f32[32,16,128]{2,1,0:T(8,128)S(1)}, u32[]{:S(2)}, u32[]{:S(2)}) %collective-permute-start.4) | collective-permute-done | bytes 262176 | tf_op jit(solution)/shard_map/ppermute | solution.py:308
  53.8 4.5 %shard_map.100 = (f32[16,4096]{1,0:T(8,128)S(1)}, f32[24,128]{1,0:T(8,128)S(1)}) custom-call(f32[32,16,128]{2,1,0:T(8,128)S(1)} %shard_map.98.refs_0_, f32[32,16,128]{2,1,0:T(8,128)S(1)} %collective-permute-done.4.refs_1_, f32[5,2,2,128,128]{4,3,2,1,0:T(8,128)S(1)} %copy-done.4, s32[5,32]{1,0:T(8,128)S(1)} %copy-done.8, s32[5,1,32]{2,1,0:T(1,128)S(1)} %copy-done.9, ...), custom_call_target="tpu_custom_call" | custom-call | flops 402653184 | bytes 8388608 | tf_op jit(solution)/shard_map/pallas_call | solution.py:213
  58.3 10.1 %all_to_all.10 = f32[8,24,128]{2,1,0:T(8,128)S(1)} all-to-all(f32[8,24,128]{2,1,0:T(8,128)S(1)} %broadcast_in_dim.4), channel_id=1, replica_groups=mesh['src'=8,'obs'=32] {'src'}, dimensions={0} | all-to-all | bytes 196608 | tf_op jit(solution)/shard_map/all_to_all | solution.py:313
  68.4 0.8 broadcast_in_dim.5
  69.2 12.7 %all-to-all-start.1 = ((f32[32,24,128]{2,1,0:T(8,128)}), f32[32,24,128]{2,1,0:T(8,128)S(1)}, u32[]{:S(2)}, u32[]{:S(2)}) async-start(f32[32,24,128]{2,1,0:T(8,128)} %broadcast_in_dim.5), calls=%async_computation.1 | async-start | bytes 786432 | tf_op jit(solution)/shard_map/all_to_all | solution.py:313
  82.0 0.0 copy-start.2
  82.0 2.2 %copy-done.2 = f32[16,2,8,4096]{3,2,1,0:T(8,128)S(1)} copy-done((f32[16,2,8,4096]{3,2,1,0:T(8,128)S(1)}, f32[16,2,8,4096]{3,2,1,0:T(8,128)}, u32[]{:S(2)}) %copy-start.2) | copy-done | bytes 4194328
  84.1 3.5 %shard_map.101 = f32[128,128]{1,0:T(8,128)S(1)} custom-call(f32[16,2,8,4096]{3,2,1,0:T(8,128)S(1)} %copy-done.2), custom_call_target="tpu_custom_call" | custom-call | flops 2147483648 | bytes 4194304 | tf_op jit(solution)/shard_map/pallas_call | solution.py:101
  87.7 0.1 collective-permute-start.5
  87.8 1.2 collective-permute-done.5
  89.0 0.6 collective-permute-start.6
  89.7 3.7 %collective-permute-done.6 = f32[128,128]{1,0:T(8,128)S(1)} collective-permute-done((f32[128,128]{1,0:T(8,128)S(1)}, f32[128,128]{1,0:T(8,128)S(1)}, u32[]{:S(2)}, u32[]{:S(2)}) %collective-permute-start.6) | collective-permute-done | bytes 65568 | tf_op jit(solution)/shard_map/ppermute | solution.py:308
  93.4 1.0 collective-permute-start.7
  94.4 4.9 %collective-permute-done.7 = f32[128,128]{1,0:T(8,128)S(1)} collective-permute-done((f32[128,128]{1,0:T(8,128)S(1)}, f32[128,128]{1,0:T(8,128)S(1)}, u32[]{:S(2)}, u32[]{:S(2)}) %collective-permute-start.7) | collective-permute-done | bytes 65568 | tf_op jit(solution)/shard_map/ppermute | solution.py:308
  99.3 1.7 %collective-permute-start.8 = (f32[128,128]{1,0:T(8,128)S(1)}, f32[128,128]{1,0:T(8,128)S(1)}, u32[]{:S(2)}, u32[]{:S(2)}) collective-permute-start(f32[128,128]{1,0:T(8,128)S(1)} %add.26), channel_id=1, source_target_pairs={{0,1},{1,0},{2,3},{3,2},{4,5},{5,4},{6,7},{7,6},{8,9},{9,8},{10,11... | collective-permute-start | bytes 196616 | tf_op jit(solution)/shard_map/ppermute | solution.py:308
  101.0 2.8 %collective-permute-done.8 = f32[128,128]{1,0:T(8,128)S(1)} collective-permute-done((f32[128,128]{1,0:T(8,128)S(1)}, f32[128,128]{1,0:T(8,128)S(1)}, u32[]{:S(2)}, u32[]{:S(2)}) %collective-permute-start.8) | collective-permute-done | bytes 65568 | tf_op jit(solution)/shard_map/ppermute | solution.py:308
  103.8 2.8 %collective-permute-start.9 = (f32[128,128]{1,0:T(8,128)S(1)}, f32[128,128]{1,0:T(8,128)S(1)}, u32[]{:S(2)}, u32[]{:S(2)}) collective-permute-start(f32[128,128]{1,0:T(8,128)S(1)} %add.27), channel_id=1, source_target_pairs={{0,2},{1,3},{2,0},{3,1},{4,6},{5,7},{6,4},{7,5},{8,10},{9,11},{10,... | collective-permute-start | bytes 196616 | tf_op jit(solution)/shard_map/ppermute | solution.py:308
  106.7 2.4 %collective-permute-done.9 = f32[128,128]{1,0:T(8,128)S(1)} collective-permute-done((f32[128,128]{1,0:T(8,128)S(1)}, f32[128,128]{1,0:T(8,128)S(1)}, u32[]{:S(2)}, u32[]{:S(2)}) %collective-permute-start.9) | collective-permute-done | bytes 65568 | tf_op jit(solution)/shard_map/ppermute | solution.py:308
  109.1 6.2 %collective-permute-start.10 = (f32[128,128]{1,0:T(8,128)S(1)}, f32[128,128]{1,0:T(8,128)S(1)}, u32[]{:S(2)}, u32[]{:S(2)}) collective-permute-start(f32[128,128]{1,0:T(8,128)S(1)} %add.28), channel_id=1, source_target_pairs={{0,4},{1,5},{2,6},{3,7},{4,0},{5,1},{6,2},{7,3},{8,12},{9,13},{10,... | collective-permute-start | bytes 196616 | tf_op jit(solution)/shard_map/ppermute | solution.py:308
  115.2 2.5 %collective-permute-done.10 = f32[128,128]{1,0:T(8,128)S(1)} collective-permute-done((f32[128,128]{1,0:T(8,128)S(1)}, f32[128,128]{1,0:T(8,128)S(1)}, u32[]{:S(2)}, u32[]{:S(2)}) %collective-permute-start.10) | collective-permute-done | bytes 65568 | tf_op jit(solution)/shard_map/ppermute | solution.py:308
  117.8 0.7 collective-permute-start.11
  118.4 3.7 %collective-permute-done.11 = f32[128,128]{1,0:T(8,128)S(1)} collective-permute-done((f32[128,128]{1,0:T(8,128)S(1)}, f32[128,128]{1,0:T(8,128)S(1)}, u32[]{:S(2)}, u32[]{:S(2)}) %collective-permute-start.11) | collective-permute-done | bytes 65568 | tf_op jit(solution)/shard_map/ppermute | solution.py:308
  122.1 2.2 %collective-permute-start.12 = (f32[128,128]{1,0:T(8,128)S(1)}, f32[128,128]{1,0:T(8,128)S(1)}, u32[]{:S(2)}, u32[]{:S(2)}) collective-permute-start(f32[128,128]{1,0:T(8,128)S(1)} %add.30), channel_id=1, source_target_pairs={{0,16},{1,17},{2,18},{3,19},{4,20},{5,21},{6,22},{7,23},{8,24},{9,... | collective-permute-start | bytes 196616 | tf_op jit(solution)/shard_map/ppermute | solution.py:308
  124.3 3.6 %collective-permute-done.12 = f32[128,128]{1,0:T(8,128)S(1)} collective-permute-done((f32[128,128]{1,0:T(8,128)S(1)}, f32[128,128]{1,0:T(8,128)S(1)}, u32[]{:S(2)}, u32[]{:S(2)}) %collective-permute-start.12) | collective-permute-done | bytes 65568 | tf_op jit(solution)/shard_map/ppermute | solution.py:308
  128.0 0.0 copy-start.3
  128.0 2.2 %copy-done.3 = f32[16,2,8,4096]{3,2,1,0:T(8,128)S(1)} copy-done((f32[16,2,8,4096]{3,2,1,0:T(8,128)S(1)}, f32[16,2,8,4096]{3,2,1,0:T(8,128)}, u32[]{:S(2)}) %copy-start.3) | copy-done | bytes 4194328
  130.2 2.5 %shard_map.102 = (f32[16,2,8,8]{3,2,1,0:T(8,128)S(1)}, f32[2,8,4096]{2,1,0:T(8,128)}, f32[2,8,8]{2,1,0:T(8,128)}) custom-call(f32[32,24,128]{2,1,0:T(8,128)S(1)} %all-to-all-done.1.refs_0_, f32[128,128]{1,0:T(8,128)S(1)} %add.31.refs_1_, f32[16,4096]{1,0:T(8,128)S(1)} %get-tuple-element.6.refs_2_, f32[16,2,8,4096]{3,2,1,0:T(8,128)S(1)} %copy-done.3), custom_call_target="tpu_custom_call" | custom-call | flops 201326592 | bytes 6291456 | tf_op jit(solution)/shard_map/pallas_call | solution.py:284
  132.7 0.7 copy.11
  (22 shorter events, 0.1 us)
Async XLA Ops:
  0.6 2.2 %copy-start = (f32[16,2,8,4096]{3,2,1,0:T(8,128)S(1)}, f32[16,2,8,4096]{3,2,1,0:T(8,128)}, u32[]{:S(2)}) copy-start(f32[16,2,8,4096]{3,2,1,0:T(8,128)} %refs_3_.11) | copy-start | bytes 12582916
  2.8 1.6 %copy-start.5 = (bf16[2,32,128,128]{3,2,1,0:T(8,128)(2,1)S(1)}, bf16[2,32,128,128]{3,2,1,0:T(8,128)(2,1)}, u32[]{:S(2)}) copy-start(bf16[2,32,128,128]{3,2,1,0:T(8,128)(2,1)} %leaf_ref.2) | copy-start | bytes 6291460
  4.4 10.8 %copy-start.4 = (f32[5,2,2,128,128]{4,3,2,1,0:T(8,128)S(1)}, f32[5,2,2,128,128]{4,3,2,1,0:T(8,128)}, u32[]{:S(2)}) copy-start(f32[5,2,2,128,128]{4,3,2,1,0:T(8,128)} %refs_2_.9) | copy-start | bytes 3932164
  4.4 10.8 %copy-start.8 = (s32[5,32]{1,0:T(8,128)S(1)}, s32[5,32]{1,0:T(8,128)}, u32[]{:S(2)}) copy-start(s32[5,32]{1,0:T(8,128)} %refs_3_.10) | copy-start | bytes 1924
  4.4 10.8 %copy-start.9 = (s32[5,1,32]{2,1,0:T(1,128)S(1)}, s32[5,1,32]{2,1,0:T(1,128)}, u32[]{:S(2)}) copy-start(s32[5,1,32]{2,1,0:T(1,128)} %refs_4_.9) | copy-start | bytes 1924
  5.6 9.6 %collective-permute-start = (f32[32,16,128]{2,1,0:T(8,128)S(1)}, f32[32,16,128]{2,1,0:T(8,128)S(1)}, u32[]{:S(2)}, u32[]{:S(2)}) collective-permute-start(f32[32,16,128]{2,1,0:T(8,128)S(1)} %shard_map.94.refs_0_), channel_id=1, source_target_pairs={{0,128},{32,160},{64,192},{96,224},{128,0},{160,32},{192,64},{224,... | collective-permute-start | bytes 786440 | tf_op jit(solution)/shard_map/ppermute | solution.py:308
  16.4 7.3 %collective-permute-start.1 = (f32[32,16,128]{2,1,0:T(8,128)S(1)}, f32[32,16,128]{2,1,0:T(8,128)S(1)}, u32[]{:S(2)}, u32[]{:S(2)}) collective-permute-start(f32[32,16,128]{2,1,0:T(8,128)S(1)} %shard_map.95.refs_0_), channel_id=1, source_target_pairs={{0,64},{32,96},{64,0},{96,32},{128,192},{160,224},{192,128},{224,1... | collective-permute-start | bytes 786440 | tf_op jit(solution)/shard_map/ppermute | solution.py:308
  23.7 25.4 %copy-start.6 = (bf16[2,32,128,128]{3,2,1,0:T(8,128)(2,1)S(1)}, bf16[2,32,128,128]{3,2,1,0:T(8,128)(2,1)}, u32[]{:S(2)}) copy-start(bf16[2,32,128,128]{3,2,1,0:T(8,128)(2,1)} %leaf_ref.3) | copy-start | bytes 6291460
  24.9 24.2 %copy-start.1 = (f32[16,2,8,4096]{3,2,1,0:T(8,128)S(1)}, f32[16,2,8,4096]{3,2,1,0:T(8,128)}, u32[]{:S(2)}) copy-start(f32[16,2,8,4096]{3,2,1,0:T(8,128)} %refs_3_.11) | copy-start | bytes 12582916
  24.9 8.0 %collective-permute-start.2 = (f32[32,16,128]{2,1,0:T(8,128)S(1)}, f32[32,16,128]{2,1,0:T(8,128)S(1)}, u32[]{:S(2)}, u32[]{:S(2)}) collective-permute-start(f32[32,16,128]{2,1,0:T(8,128)S(1)} %shard_map.96.refs_0_), channel_id=1, source_target_pairs={{0,16},{1,17},{2,18},{3,19},{4,20},{5,21},{6,22},{7,23},{8,24},{9,... | collective-permute-start | bytes 786440 | tf_op jit(solution)/shard_map/ppermute | solution.py:308
  34.1 6.5 %collective-permute-start.3 = (f32[32,16,128]{2,1,0:T(8,128)S(1)}, f32[32,16,128]{2,1,0:T(8,128)S(1)}, u32[]{:S(2)}, u32[]{:S(2)}) collective-permute-start(f32[32,16,128]{2,1,0:T(8,128)S(1)} %shard_map.97.refs_0_), channel_id=1, source_target_pairs={{0,8},{1,9},{2,10},{3,11},{4,12},{5,13},{6,14},{7,15},{8,0},{9,1},... | collective-permute-start | bytes 786440 | tf_op jit(solution)/shard_map/ppermute | solution.py:308
  41.8 12.0 %copy-start.7 = (bf16[2,32,128,128]{3,2,1,0:T(8,128)(2,1)S(1)}, bf16[2,32,128,128]{3,2,1,0:T(8,128)(2,1)}, u32[]{:S(2)}) copy-start(bf16[2,32,128,128]{3,2,1,0:T(8,128)(2,1)} %refs_5_.1) | copy-start | bytes 6291460
  41.8 12.0 %collective-permute-start.4 = (f32[32,16,128]{2,1,0:T(8,128)S(1)}, f32[32,16,128]{2,1,0:T(8,128)S(1)}, u32[]{:S(2)}, u32[]{:S(2)}) collective-permute-start(f32[32,16,128]{2,1,0:T(8,128)S(1)} %shard_map.98.refs_0_), channel_id=1, source_target_pairs={{0,4},{1,5},{2,6},{3,7},{4,0},{5,1},{6,2},{7,3},{8,12},{9,13},{10,... | collective-permute-start | bytes 786440 | tf_op jit(solution)/shard_map/ppermute | solution.py:308
  69.2 58.8 %all-to-all-start.1 = ((f32[32,24,128]{2,1,0:T(8,128)}), f32[32,24,128]{2,1,0:T(8,128)S(1)}, u32[]{:S(2)}, u32[]{:S(2)}) async-start(f32[32,24,128]{2,1,0:T(8,128)} %broadcast_in_dim.5), calls=%async_computation.1 | async-start | bytes 786432 | tf_op jit(solution)/shard_map/all_to_all | solution.py:313
  82.0 2.2 %copy-start.2 = (f32[16,2,8,4096]{3,2,1,0:T(8,128)S(1)}, f32[16,2,8,4096]{3,2,1,0:T(8,128)}, u32[]{:S(2)}) copy-start(f32[16,2,8,4096]{3,2,1,0:T(8,128)} %refs_3_.11) | copy-start | bytes 12582916
  87.7 1.3 %collective-permute-start.5 = (f32[128,128]{1,0:T(8,128)S(1)}, f32[128,128]{1,0:T(8,128)S(1)}, u32[]{:S(2)}, u32[]{:S(2)}) collective-permute-start(f32[128,128]{1,0:T(8,128)S(1)} %shard_map.101), channel_id=1, source_target_pairs={{0,32},{32,0},{64,96},{96,64},{128,160},{160,128},{192,224},{224,1... | collective-permute-start | bytes 196616 | tf_op jit(solution)/shard_map/ppermute | solution.py:308
  89.0 4.4 %collective-permute-start.6 = (f32[128,128]{1,0:T(8,128)S(1)}, f32[128,128]{1,0:T(8,128)S(1)}, u32[]{:S(2)}, u32[]{:S(2)}) collective-permute-start(f32[128,128]{1,0:T(8,128)S(1)} %add.24), channel_id=1, source_target_pairs={{0,64},{32,96},{64,0},{96,32},{128,192},{160,224},{192,128},{224,1... | collective-permute-start | bytes 196616 | tf_op jit(solution)/shard_map/ppermute | solution.py:308
  93.4 5.9 %collective-permute-start.7 = (f32[128,128]{1,0:T(8,128)S(1)}, f32[128,128]{1,0:T(8,128)S(1)}, u32[]{:S(2)}, u32[]{:S(2)}) collective-permute-start(f32[128,128]{1,0:T(8,128)S(1)} %add.25), channel_id=1, source_target_pairs={{0,128},{32,160},{64,192},{96,224},{128,0},{160,32},{192,64},{224,... | collective-permute-start | bytes 196616 | tf_op jit(solution)/shard_map/ppermute | solution.py:308
  99.3 4.5 %collective-permute-start.8 = (f32[128,128]{1,0:T(8,128)S(1)}, f32[128,128]{1,0:T(8,128)S(1)}, u32[]{:S(2)}, u32[]{:S(2)}) collective-permute-start(f32[128,128]{1,0:T(8,128)S(1)} %add.26), channel_id=1, source_target_pairs={{0,1},{1,0},{2,3},{3,2},{4,5},{5,4},{6,7},{7,6},{8,9},{9,8},{10,11... | collective-permute-start | bytes 196616 | tf_op jit(solution)/shard_map/ppermute | solution.py:308
  103.8 5.3 %collective-permute-start.9 = (f32[128,128]{1,0:T(8,128)S(1)}, f32[128,128]{1,0:T(8,128)S(1)}, u32[]{:S(2)}, u32[]{:S(2)}) collective-permute-start(f32[128,128]{1,0:T(8,128)S(1)} %add.27), channel_id=1, source_target_pairs={{0,2},{1,3},{2,0},{3,1},{4,6},{5,7},{6,4},{7,5},{8,10},{9,11},{10,... | collective-permute-start | bytes 196616 | tf_op jit(solution)/shard_map/ppermute | solution.py:308
  109.1 8.7 %collective-permute-start.10 = (f32[128,128]{1,0:T(8,128)S(1)}, f32[128,128]{1,0:T(8,128)S(1)}, u32[]{:S(2)}, u32[]{:S(2)}) collective-permute-start(f32[128,128]{1,0:T(8,128)S(1)} %add.28), channel_id=1, source_target_pairs={{0,4},{1,5},{2,6},{3,7},{4,0},{5,1},{6,2},{7,3},{8,12},{9,13},{10,... | collective-permute-start | bytes 196616 | tf_op jit(solution)/shard_map/ppermute | solution.py:308
  117.8 4.4 %collective-permute-start.11 = (f32[128,128]{1,0:T(8,128)S(1)}, f32[128,128]{1,0:T(8,128)S(1)}, u32[]{:S(2)}, u32[]{:S(2)}) collective-permute-start(f32[128,128]{1,0:T(8,128)S(1)} %add.29), channel_id=1, source_target_pairs={{0,8},{1,9},{2,10},{3,11},{4,12},{5,13},{6,14},{7,15},{8,0},{9,1},... | collective-permute-start | bytes 196616 | tf_op jit(solution)/shard_map/ppermute | solution.py:308
  122.1 5.9 %collective-permute-start.12 = (f32[128,128]{1,0:T(8,128)S(1)}, f32[128,128]{1,0:T(8,128)S(1)}, u32[]{:S(2)}, u32[]{:S(2)}) collective-permute-start(f32[128,128]{1,0:T(8,128)S(1)} %add.30), channel_id=1, source_target_pairs={{0,16},{1,17},{2,18},{3,19},{4,20},{5,21},{6,22},{7,23},{8,24},{9,... | collective-permute-start | bytes 196616 | tf_op jit(solution)/shard_map/ppermute | solution.py:308
  128.0 2.2 %copy-start.3 = (f32[16,2,8,4096]{3,2,1,0:T(8,128)S(1)}, f32[16,2,8,4096]{3,2,1,0:T(8,128)}, u32[]{:S(2)}) copy-start(f32[16,2,8,4096]{3,2,1,0:T(8,128)} %refs_3_.11) | copy-start | bytes 12582916
where the time goes:
time: 134 us; the launch traced here: 133 us
  waiting for transfers between devices  52.1 us (39%)
  starting transfers between devices  42.9 us (32%)
  Pallas kernels  17.7 us (13%)
  blocking collectives  10.1 us (8%)
  local copies, waits for them, and re-layouts  9.71 us (7%)
    ppermute x13, waiting for transfers between devices, exchange(): return lax.ppermute(value, axis, pairs)  52.1 us
    ppermute x13, starting transfers between devices, exchange(): return lax.ppermute(value, axis, pairs)  30.2 us
    all_to_all x1, starting transfers between devices, from_all(): return lax.all_to_all(copies, axis, 0, 0)  12.7 us
    all_to_all x1, blocking collectives, from_all(): return lax.all_to_all(copies, axis, 0, 0)  10.1 us
    unnamed x20, local copies, waits for them, and re-layouts  8.17 us
    pallas_call x4, Pallas kernels, next_level(): pl.pallas_call(lambda *refs: level_kernel(level, *refs), grid=(1,), in_sp...  4.88 us
    pallas_call x1, Pallas kernels, project(): pl.pallas_call(lambda *refs: project_kernel(level, *refs), grid=(1,), in_...  4.51 us
    pallas_call x1, Pallas kernels, basis_gram(): pl.pallas_call(basis_gram_kernel, grid=(steps,), in_specs=[pl.BlockSpec((...  3.53 us
  transfers between devices with their start and end apart: 14, of which 13 were waited for; matrix products, arithmetic and copies ran while one was open for 0% of the time, Pallas kernels for 4%

commit v1 on v0

v1 whole, which is shorter than its diff:
```python
import jax
import jax.numpy as jnp
from jax import lax
from jax.experimental import pallas as pl
from jax.experimental.pallas import tpu as pltpu
from jax.sharding import PartitionSpec as P

NT = (((1,), (1,)), ((), ()))
NN = (((1,), (0,)), ((), ()))
KERNEL_VMEM = 24 * 1024 * 1024
BASIS_PARTS = 4


def in_hbm(value):
    return pltpu.with_memory_space_constraint(value, pltpu.HBM)


def dot_nt(left, right):
    return lax.dot_general(left, right, NT, preferred_element_type=jnp.float32)


def dot_nn(left, right):
    return lax.dot_general(left, right, NN, preferred_element_type=jnp.float32)


def split3(value):
    high = value.astype(jnp.bfloat16)
    rest = value - high.astype(jnp.float32)
    middle = rest.astype(jnp.bfloat16)
    low = (rest - middle.astype(jnp.float32)).astype(jnp.bfloat16)
    return high, middle, low


def complex_rows(rows):
    real, imag = rows[:8], rows[8:]
    return jnp.concatenate(
        [jnp.concatenate([real, -imag], axis=1), jnp.concatenate([imag, real], axis=1)], axis=0
    )


def leaf_product(rows, real, imag):
    return dot_nt(
        complex_rows(rows).astype(jnp.bfloat16), jnp.concatenate([real, imag], axis=1)
    )


def leaves_kernel(basis_ref, leaf_ref, out_ref, newest_ref, held_ref, newest_sem, held_sems):
    steps = held_sems.shape[0]
    count = held_ref.shape[1]
    part = count // steps
    newest_copy = pltpu.make_async_copy(
        basis_ref.at[basis_ref.shape[0] - 1], newest_ref, newest_sem
    )
    newest_copy.start()
    copies = []
    for step in range(steps):
        here = pl.ds(step * part, part)
        copies.append(
            pltpu.make_async_copy(leaf_ref.at[:, here], held_ref.at[:, here], held_sems.at[step])
        )
        copies[-1].start()
    newest_copy.wait()
    for leaf in range(count):
        if leaf % part == 0:
            copies[leaf // part].wait()
        rows = newest_ref[:, :, leaf * 128 : (leaf + 1) * 128].reshape(16, 128)
        rows = rows.astype(jnp.bfloat16).astype(jnp.float32)
        out_ref[leaf] = leaf_product(rows, held_ref[0, leaf], held_ref[1, leaf])


def apply_leaves(krylov_basis, leaves, steps):
    count = leaves.shape[1]
    return pl.pallas_call(
        leaves_kernel,
        in_specs=[pl.BlockSpec(memory_space=pltpu.HBM)] * 2,
        out_specs=pl.BlockSpec(memory_space=pltpu.VMEM),
        out_shape=jax.ShapeDtypeStruct((count, 16, 128), jnp.float32),
        scratch_shapes=[
            pltpu.VMEM(krylov_basis.shape[1:], jnp.float32),
            pltpu.VMEM(leaves.shape, leaves.dtype),
            pltpu.SemaphoreType.DMA,
            pltpu.SemaphoreType.DMA((steps,)),
        ],
        compiler_params=pltpu.CompilerParams(vmem_limit_bytes=KERNEL_VMEM),
        cost_estimate=pl.CostEstimate(
            flops=count * 16 * 256 * 128 * 2, bytes_accessed=count * 73728, transcendentals=0
        ),
    )(in_hbm(krylov_basis), in_hbm(leaves))


def stacked(basis):
    width = basis.shape[3]
    return jnp.concatenate(
        [basis[:, 0].reshape(128, width), basis[:, 1].reshape(128, width)], axis=0
    )


def basis_copies(basis_ref, held_ref, sems):
    steps = sems.shape[0]
    width = held_ref.shape[3] // steps
    copies = []
    for step in range(steps):
        here = pl.ds(step * width, width)
        copies.append(
            pltpu.make_async_copy(
                basis_ref.at[:, :, :, here], held_ref.at[:, :, :, here], sems.at[step]
            )
        )
        copies[-1].start()
    return copies, width


def basis_scratch(krylov_basis):
    return [pltpu.VMEM(krylov_basis.shape, jnp.float32), pltpu.SemaphoreType.DMA((BASIS_PARTS,))]


def basis_gram_kernel(basis_ref, out_ref, held_ref, sems):
    copies, width = basis_copies(basis_ref, held_ref, sems)
    even = jnp.zeros((256, 256), jnp.float32)
    odd = jnp.zeros((256, 256), jnp.float32)
    for step, copy in enumerate(copies):
        copy.wait()
        here = slice(step * width, (step + 1) * width)
        high, middle, low = split3(stacked(held_ref[:, :, :, here]))
        even += dot_nt(high, high) + dot_nt(middle, middle)
        odd += dot_nt(high, middle) + dot_nt(high, low)
    gram = even + odd + odd.T
    real = gram[:128, :128] + gram[128:, 128:]
    imag = gram[:128, 128:] - gram[128:, :128]
    row = lax.broadcasted_iota(jnp.int32, (128, 128), 0)
    column = lax.broadcasted_iota(jnp.int32, (128, 128), 1)
    out_ref[...] = jnp.where(row <= column, real, imag)


def basis_gram(krylov_basis):
    return pl.pallas_call(
        basis_gram_kernel,
        in_specs=[pl.BlockSpec(memory_space=pltpu.HBM)],
        out_specs=pl.BlockSpec(memory_space=pltpu.VMEM),
        out_shape=jax.ShapeDtypeStruct((128, 128), jnp.float32),
        scratch_shapes=basis_scratch(krylov_basis),
        compiler_params=pltpu.CompilerParams(vmem_limit_bytes=KERNEL_VMEM),
        cost_estimate=pl.CostEstimate(
            flops=4 * 2 * 256 * 256 * 4096, bytes_accessed=4 << 20, transcendentals=0
        ),
    )(in_hbm(krylov_basis))


def mix(level, own_ref, partner_ref, mixer_ref, rank_ref, table_ref, picked_ref, write):
    for leaf in range(32):
        picked_ref[leaf] = partner_ref[table_ref[level, 0, leaf]]
    both = jnp.concatenate(
        [own_ref[0:32].reshape(512, 128), picked_ref[...].reshape(512, 128)], axis=1
    )
    mixer = mixer_ref[0]
    weights = jnp.concatenate(
        [
            jnp.concatenate([mixer[0, 0], mixer[0, 1]], axis=1),
            jnp.concatenate([mixer[1, 0], mixer[1, 1]], axis=1),
        ],
        axis=0,
    )
    product = jnp.dot(
        both, weights, precision=lax.Precision.HIGHEST, preferred_element_type=jnp.float32
    )
    column = lax.broadcasted_iota(jnp.int32, (16, 128), 1)
    for leaf in range(32):
        by_real = product[leaf * 16 : (leaf + 1) * 16, :128]
        by_imag = product[leaf * 16 : (leaf + 1) * 16, 128:]
        mixed = jnp.concatenate([by_real[:8] - by_imag[8:], by_real[8:] + by_imag[:8]], axis=0)
        write(leaf, jnp.where(column < rank_ref[level, leaf], mixed, 0.0))


def first_level_kernel(own_ref, partner_ref, mixer_ref, rank_ref, table_ref, gram_ref, out_ref, picked_ref):
    def write(leaf, value):
        out_ref[leaf] = value

    mix(0, own_ref, partner_ref, mixer_ref, rank_ref, table_ref, picked_ref, write)
    out_ref[32:40] = gram_ref[...]


def level_kernel(level, own_ref, partner_ref, mixer_ref, rank_ref, table_ref, out_ref, picked_ref):
    def write(leaf, value):
        out_ref[leaf] = value

    mix(level, own_ref, partner_ref, mixer_ref, rank_ref, table_ref, picked_ref, write)
    out_ref[32:40] = own_ref[32:40] + partner_ref[32:40]


def whole(shape):
    return pl.BlockSpec(shape, lambda i: (0,) * len(shape))


def level_specs(level, own):
    return [
        whole(own.shape),
        whole(own.shape),
        pl.BlockSpec((1, 2, 2, 128, 128), lambda i: (level, 0, 0, 0, 0)),
        pl.BlockSpec(memory_space=pltpu.SMEM),
        pl.BlockSpec(memory_space=pltpu.SMEM),
    ]


def next_level(level, own, partner, level_mixers, block_ranks, partner_tables, gram=None):
    if gram is None:
        kernel, more, more_specs = lambda *refs: level_kernel(level, *refs), [], []
    else:
        kernel, more, more_specs = first_level_kernel, [gram], [whole(gram.shape)]
    return pl.pallas_call(
        kernel,
        grid=(1,),
        in_specs=level_specs(level, own) + more_specs,
        out_specs=whole((40, 16, 128)),
        out_shape=jax.ShapeDtypeStruct((40, 16, 128), jnp.float32),
        scratch_shapes=[pltpu.VMEM((32, 16, 128), jnp.float32)],
        compiler_params=pltpu.CompilerParams(vmem_limit_bytes=KERNEL_VMEM),
        cost_estimate=pl.CostEstimate(
            flops=6 * 512 * 256 * 256 * 2, bytes_accessed=1 << 20, transcendentals=0
        ),
    )(own, partner, level_mixers, block_ranks, partner_tables, *more)


def project_kernel(
    level, own_ref, partner_ref, mixer_ref, rank_ref, table_ref, close_ref, leaf_ref, basis_ref,
    image_ref, sums_ref, picked_ref, gram_ref, leaf_held_ref, leaf_sem, held_ref, sems,
):
    leaf_copy = pltpu.make_async_copy(leaf_ref, leaf_held_ref, leaf_sem)
    leaf_copy.start()
    copies, width = basis_copies(basis_ref, held_ref, sems)
    values = {}

    def write(leaf, value):
        values[leaf] = value.astype(jnp.bfloat16).astype(jnp.float32)

    mix(level, own_ref, partner_ref, mixer_ref, rank_ref, table_ref, picked_ref, write)
    gram_ref[...] = (own_ref[32:40] + partner_ref[32:40]).reshape(128, 128)
    leaf_copy.wait()
    for leaf in range(32):
        far = leaf_product(values[leaf], leaf_held_ref[0, leaf], leaf_held_ref[1, leaf])
        image_ref[:, leaf * 128 : (leaf + 1) * 128] = far + close_ref[leaf]
    high, middle, low = split3(image_ref[...])
    three = jnp.concatenate([high, middle, low], axis=0)
    two = three[:32]
    inner = jnp.zeros((16, 256), jnp.float32)
    for step, copy in enumerate(copies):
        copy.wait()
        here = slice(step * width, (step + 1) * width)
        b_high, b_middle, b_low = split3(stacked(held_ref[:, :, :, here]))
        one = dot_nt(three[:, here], b_high)
        inner += one[:16] + one[16:32] + one[32:]
        one = dot_nt(two[:, here], b_middle)
        inner += one[:16] + one[16:]
        inner += dot_nt(high[:, here], b_low)
    one = dot_nt(three, high)
    square = one[:16] + one[16:32] + one[32:]
    one = dot_nt(two, middle)
    square += one[:16] + one[16:]
    square += dot_nt(high, low)
    real = square[:8, :8] + square[8:, 8:]
    imag = square[:8, 8:] - square[8:, :8]
    sums = jnp.concatenate(
        [
            inner[:8, :128] + inner[8:, 128:],
            inner[8:, :128] - inner[:8, 128:],
            jnp.concatenate([real, imag, jnp.zeros((8, 112), jnp.float32)], axis=1),
        ],
        axis=0,
    )
    mine = lax.rem(lax.axis_index("src"), 4)
    piece = gram_ref[pl.ds(pl.multiple_of(mine * 32, 32), 32), :]
    for device in range(8):
        sums_ref[device, 0:24] = sums
        sums_ref[device, 24:56] = piece


def project(level, own, partner, level_mixers, block_ranks, partner_tables, close, leaf_out, krylov_basis):
    return pl.pallas_call(
        lambda *refs: project_kernel(level, *refs),
        grid=(1,),
        in_specs=level_specs(level, own)
        + [whole(close.shape)]
        + [pl.BlockSpec(memory_space=pltpu.HBM)] * 2,
        out_specs=[whole((16, 4096)), whole((8, 56, 128))],
        out_shape=[
            jax.ShapeDtypeStruct((16, 4096), jnp.float32),
            jax.ShapeDtypeStruct((8, 56, 128), jnp.float32),
        ],
        scratch_shapes=[
            pltpu.VMEM((32, 16, 128), jnp.float32),
            pltpu.VMEM((128, 128), jnp.float32),
            pltpu.VMEM(leaf_out.shape, leaf_out.dtype),
            pltpu.SemaphoreType.DMA,
        ]
        + basis_scratch(krylov_basis),
        compiler_params=pltpu.CompilerParams(vmem_limit_bytes=KERNEL_VMEM),
        cost_estimate=pl.CostEstimate(
            flops=6 * 512 * 256 * 256 * 2, bytes_accessed=8 << 20, transcendentals=0
        ),
    )(
        own, partner, level_mixers, block_ranks, partner_tables, close, in_hbm(leaf_out),
        in_hbm(krylov_basis),
    )


def relay_kernel(got_ref, out_ref, gram_ref):
    sums = jnp.sum(got_ref[:, 0:24], axis=0)
    for quarter in range(4):
        gram_ref[quarter * 32 : (quarter + 1) * 32] = (
            got_ref[quarter, 24:56] + got_ref[quarter + 4, 24:56]
        )
    mine = lax.div(lax.axis_index("obs"), 4)
    piece = gram_ref[pl.ds(pl.multiple_of(mine * 16, 16), 16), :]
    for device in range(32):
        out_ref[device, 0:24] = sums
        out_ref[device, 24:40] = piece


def relay(got):
    return pl.pallas_call(
        relay_kernel,
        out_shape=jax.ShapeDtypeStruct((32, 40, 128), jnp.float32),
        scratch_shapes=[pltpu.VMEM((128, 128), jnp.float32)],
        compiler_params=pltpu.CompilerParams(vmem_limit_bytes=KERNEL_VMEM),
    )(got)


def dot_high(left, right, numbers):
    return lax.dot_general(
        left, right, numbers, precision=lax.Precision.HIGHEST, preferred_element_type=jnp.float32
    )


def finish_kernel(
    scale, got_ref, image_ref, basis_ref, total_ref, new_ref, block_ref, gram_ref, held_ref, sems
):
    copies, width = basis_copies(basis_ref, held_ref, sems)
    sums = jnp.sum(got_ref[:, 0:24], axis=0) * scale
    first = sums[:16]
    for part in range(8):
        four = got_ref[part * 4 : part * 4 + 4, 24:40]
        gram_ref[part * 16 : (part + 1) * 16] = jnp.sum(four, axis=0) * scale
    packed = gram_ref[...]
    row = lax.broadcasted_iota(jnp.int32, (128, 128), 0)
    column = lax.broadcasted_iota(jnp.int32, (128, 128), 1)
    flipped = packed.T
    gram_real = jnp.where(row <= column, packed, flipped)
    gram_imag = jnp.where(row > column, packed, jnp.where(row < column, -flipped, 0.0))
    gram = jnp.concatenate([gram_real, gram_imag], axis=1)

    def by_gram(rows):
        one = dot_high(rows, gram, NN)
        real = one[:8, :128] + one[8:, 128:]
        imag = one[8:, :128] - one[:8, 128:]
        return jnp.concatenate([real, imag], axis=0)

    total = first + (first - by_gram(first))
    rest = first - by_gram(total)

    def inner(left, right):
        one = dot_high(left, right, NT)
        return one[:8, :8] + one[8:, 8:], one[:8, 8:] - one[8:, :8]

    one_real, one_imag = inner(first, total)
    two_real, two_imag = inner(total, rest)
    block_ref[0] = sums[16:24, 0:8] - one_real - two_real
    block_ref[1] = sums[16:24, 8:16] - one_imag - two_imag
    high, middle, low = split3(complex_rows(total))
    three = jnp.concatenate([high, middle, low], axis=0)
    two = three[:32]
    for step, copy in enumerate(copies):
        copy.wait()
        here = slice(step * width, (step + 1) * width)
        b_high, b_middle, b_low = split3(stacked(held_ref[:, :, :, here]))
        one = dot_nn(three, b_high)
        taken = one[:16] + one[16:32] + one[32:]
        one = dot_nn(two, b_middle)
        taken += one[:16] + one[16:]
        taken += dot_nn(high, b_low)
        new_ref[:, :, here] = (image_ref[:, here] - taken).reshape(2, 8, width)
    turn = jnp.where(row == lax.rem(column, 16) * 8 + lax.div(column, 16), 1.0, 0.0)
    turned = dot_high(total, turn, NN)
    for angle in range(8):
        total_ref[0, angle] = turned[:8, angle * 16 : (angle + 1) * 16]
        total_ref[1, angle] = turned[8:, angle * 16 : (angle + 1) * 16]


def finish(scale, got, image, krylov_basis):
    return pl.pallas_call(
        lambda *refs: finish_kernel(scale, *refs),
        grid=(1,),
        in_specs=[whole(got.shape), whole(image.shape), pl.BlockSpec(memory_space=pltpu.HBM)],
        out_specs=[whole((2, 8, 8, 16)), whole((2, 8, 4096)), whole((2, 8, 8))],
        out_shape=[
            jax.ShapeDtypeStruct((2, 8, 8, 16), jnp.float32),
            jax.ShapeDtypeStruct((2, 8, 4096), jnp.float32),
            jax.ShapeDtypeStruct((2, 8, 8), jnp.float32),
        ],
        scratch_shapes=[pltpu.VMEM((128, 128), jnp.float32)] + basis_scratch(krylov_basis),
        compiler_params=pltpu.CompilerParams(vmem_limit_bytes=KERNEL_VMEM),
        cost_estimate=pl.CostEstimate(
            flops=6 * 16 * 256 * 4096 * 2, bytes_accessed=6 << 20, transcendentals=0
        ),
    )(got, image, in_hbm(krylov_basis))


def exchange(value, axis, bit_number):
    pairs = [(source, source ^ (1 << bit_number)) for source in range(lax.axis_size(axis))]
    return lax.ppermute(value, axis, pairs)


def per_device(
    krylov_basis, near_field, leaf_in, leaf_out, level_mixers, block_ranks, partner_tables
):
    src_bits = lax.axis_size("src").bit_length() - 1
    obs_bits = lax.axis_size("obs").bit_length() - 1
    plan = [
        ("src", src_bits - 1),
        ("src", src_bits - 2),
        ("obs", obs_bits - 1),
        ("obs", obs_bits - 2),
        ("obs", obs_bits - 3),
    ]
    coeffs = apply_leaves(krylov_basis, leaf_in, 4)
    close = apply_leaves(krylov_basis, near_field, 4)
    gram = basis_gram(krylov_basis)
    gram = (gram + exchange(gram, "src", 0)).reshape(8, 16, 128)
    for level, (axis, bit) in enumerate(plan):
        partner = exchange(coeffs, axis, bit)
        operands = (level, coeffs, partner, level_mixers, block_ranks, partner_tables)
        if level == 0:
            coeffs = next_level(*operands, gram)
        elif level < len(plan) - 1:
            coeffs = next_level(*operands)
        else:
            image, sums = project(*operands, close, leaf_out, krylov_basis)
    got = relay(lax.all_to_all(sums, "src", 0, 0))
    got = lax.all_to_all(got, "obs", 0, 0)
    devices = lax.axis_size("src") * lax.axis_size("obs")
    scale = 1.0 / (krylov_basis.shape[3] * devices)
    total, new_block, block_gram = finish(scale, got, image, krylov_basis)
    return jnp.transpose(total, (3, 0, 1, 2)), new_block, block_gram


def solution(mesh):
    in_specs = (
        P(None, None, None, ("src", "obs")),
        P(None, ("src", "obs"), None, None),
        P(None, ("src", "obs"), None, None),
        P(None, ("src", "obs"), None, None),
        P(None, None, None, None, ("src", "obs")),
        P(None, ("src", "obs")),
        P(None, ("src", "obs"), None),
    )
    out_specs = (P(), P(None, None, ("src", "obs")), P())
    return jax.shard_map(
        per_device, mesh=mesh, in_specs=in_specs, out_specs=out_specs, check_vma=False
    )
```

time: 134 us -> 113 us (0.84); the launches traced: 133 us -> 111 us
  blocking collectives: 10.1 us -> 43.1 us
  starting transfers between devices: 42.9 us -> 15.3 us
  waiting for transfers between devices: 52.1 us -> 26.8 us
  local copies, waits for them, and re-layouts: 9.71 us -> 0.02 us
  Pallas kernels: 17.7 us -> 24.7 us
    all_to_all x1 -> x2, blocking collectives: 10.1 us -> 43.1 us  [the longest x1 32.5 us: per_device(): got = lax.all_to_all(got, 'obs', 0, 0)]
    ppermute x13 -> x6, waiting for transfers between devices: 52.1 us -> 26.8 us  [exchange(): return lax.ppermute(value, axis, pairs)]
    ppermute x13 -> x6, starting transfers between devices: 30.2 us -> 15.3 us  [exchange(): return lax.ppermute(value, axis, pairs)]
    all_to_all x1 -> x0, starting transfers between devices: 12.7 us -> none  [from_all(): return lax.all_to_all(copies, axis, 0, 0)]
    unnamed x20 -> x6, local copies, waits for them, and re-layouts: 8.17 us -> 0.02 us
    pallas_call x7 -> x8, Pallas kernels: 10.7 us -> 13.9 us  [the longest x2 4.95 us: apply_leaves(): pl.pallas_call(leaves_kernel, in_specs=[pl.BlockSpec(memory_space=pltpu.H...]
    pallas_call x1, Pallas kernels: 4.51 us -> 6.79 us  [project(): pl.pallas_call(lambda *refs: project_kernel(level, *refs), grid=(1,), in_...]
    pallas_call x1, Pallas kernels: 2.46 us -> 3.99 us  [finish(): pl.pallas_call(lambda *refs: finish_kernel(scale, *refs), grid=(1,), in_s...]
  transfers between devices with their start and end apart: 14 -> 6, of which waited for: 13 -> 6; matrix products, arithmetic and copies ran while one was open for 0% -> 0% of each run, Pallas kernels for 4% -> 6%
where the time goes in v1:
time: 113 us; the launch traced here: 111 us
  blocking collectives  43.1 us (38%)
  waiting for transfers between devices  26.8 us (24%)
  Pallas kernels  24.7 us (22%)
  starting transfers between devices  15.3 us (14%)
    all_to_all x1, blocking collectives, per_device(): got = lax.all_to_all(got, 'obs', 0, 0)  32.5 us
    ppermute x6, waiting for transfers between devices, exchange(): return lax.ppermute(value, axis, pairs)  26.8 us
    ppermute x6, starting transfers between devices, exchange(): return lax.ppermute(value, axis, pairs)  15.3 us
    all_to_all x1, blocking collectives, per_device(): got = relay(lax.all_to_all(sums, 'src', 0, 0))  10.7 us
    pallas_call x1, Pallas kernels, project(): pl.pallas_call(lambda *refs: project_kernel(level, *refs), grid=(1,), in_...  6.79 us
    pallas_call x2, Pallas kernels, apply_leaves(): pl.pallas_call(leaves_kernel, in_specs=[pl.BlockSpec(memory_space=pltpu.H...  4.95 us
    pallas_call x4, Pallas kernels, next_level(): pl.pallas_call(kernel, grid=(1,), in_specs=level_specs(level, own) + more...  4.89 us
    pallas_call x1, Pallas kernels, basis_gram(): pl.pallas_call(basis_gram_kernel, in_specs=[pl.BlockSpec(memory_space=plt...  4 us
  transfers between devices with their start and end apart: 6, of which 6 were waited for; matrix products, arithmetic and copies ran while one was open for 0% of the time, Pallas kernels for 6%

profile of v1, /device:TPU:2, one launch (start us, length us, event | category | flops | bytes accessed | tf_op | source)
XLA Modules:
  0.0 110.8 jit_solution(11145872877928333553)
XLA Ops:
  0.6 2.5 %shard_map.94.own_ref = f32[32,16,128]{2,1,0:T(8,128)S(1)} custom-call(f32[16,2,8,4096]{3,2,1,0:T(8,128)} %refs_2_.9, bf16[2,32,128,128]{3,2,1,0:T(8,128)(2,1)} %leaf_ref.2), custom_call_target="tpu_custom_call" | custom-call | flops 33554432 | bytes 2359296 | tf_op jit(solution)/shard_map/pallas_call | solution.py:73
  3.1 0.0 copy-start
  3.1 0.0 copy-start.1
  3.1 0.0 copy-start.2
  3.1 3.3 %collective-permute-start = (f32[32,16,128]{2,1,0:T(8,128)S(1)}, f32[32,16,128]{2,1,0:T(8,128)S(1)}, u32[]{:S(2)}, u32[]{:S(2)}) collective-permute-start(f32[32,16,128]{2,1,0:T(8,128)S(1)} %shard_map.94.own_ref), channel_id=1, source_target_pairs={{0,128},{32,160},{64,192},{96,224},{128,0},{160,32},{192,64},{224,... | collective-permute-start | bytes 786440 | tf_op jit(solution)/shard_map/ppermute | solution.py:408
  6.4 4.0 %shard_map.95 = f32[128,128]{1,0:T(8,128)S(1)} custom-call(f32[16,2,8,4096]{3,2,1,0:T(8,128)} %refs_2_.9), custom_call_target="tpu_custom_call" | custom-call | flops 2147483648 | bytes 4194304 | tf_op jit(solution)/shard_map/pallas_call | solution.py:136
  10.4 0.1 collective-permute-start.1
  10.5 1.2 %collective-permute-done.1 = f32[128,128]{1,0:T(8,128)S(1)} collective-permute-done((f32[128,128]{1,0:T(8,128)S(1)}, f32[128,128]{1,0:T(8,128)S(1)}, u32[]{:S(2)}, u32[]{:S(2)}) %collective-permute-start.1) | collective-permute-done | bytes 65568 | tf_op jit(solution)/shard_map/ppermute | solution.py:408
  11.8 1.0 collective-permute-done.partner_ref
  12.8 0.0 copy-done
  12.8 0.0 copy-done.1
  12.8 0.0 copy-done.2
  12.8 1.2 %shard_map.96.refs_0_ = f32[40,16,128]{2,1,0:T(8,128)S(1)} custom-call(f32[32,16,128]{2,1,0:T(8,128)S(1)} %shard_map.94.own_ref, f32[32,16,128]{2,1,0:T(8,128)S(1)} %collective-permute-done.partner_ref, f32[5,2,2,128,128]{4,3,2,1,0:T(8,128)S(1)} %copy-done, s32[5,32]{1,0:T(8,128)S(1)} %copy-done.1, s32[5,1,32]{2,1,0:T(1,128)S(1)} %copy-done.2, ...), custom_call_target="tpu_custom_call" | custom-call | flops 402653184 | bytes 1048576 | tf_op jit(solution)/shard_map/pallas_call | solution.py:209
  14.0 1.7 %collective-permute-start.2 = (f32[40,16,128]{2,1,0:T(8,128)S(1)}, f32[40,16,128]{2,1,0:T(8,128)S(1)}, u32[]{:S(2)}, u32[]{:S(2)}) collective-permute-start(f32[40,16,128]{2,1,0:T(8,128)S(1)} %shard_map.96.refs_0_), channel_id=1, source_target_pairs={{0,64},{32,96},{64,0},{96,32},{128,192},{160,224},{192,128},{224,1... | collective-permute-start | bytes 983048 | tf_op jit(solution)/shard_map/ppermute | solution.py:408
  15.7 7.2 %collective-permute-done.2.refs_1_ = f32[40,16,128]{2,1,0:T(8,128)S(1)} collective-permute-done((f32[40,16,128]{2,1,0:T(8,128)S(1)}, f32[40,16,128]{2,1,0:T(8,128)S(1)}, u32[]{:S(2)}, u32[]{:S(2)}) %collective-permute-start.2) | collective-permute-done | bytes 327712 | tf_op jit(solution)/shard_map/ppermute | solution.py:408
  22.9 1.2 %shard_map.97.refs_0_ = f32[40,16,128]{2,1,0:T(8,128)S(1)} custom-call(f32[40,16,128]{2,1,0:T(8,128)S(1)} %shard_map.96.refs_0_, f32[40,16,128]{2,1,0:T(8,128)S(1)} %collective-permute-done.2.refs_1_, f32[5,2,2,128,128]{4,3,2,1,0:T(8,128)S(1)} %copy-done, s32[5,32]{1,0:T(8,128)S(1)} %copy-done.1, s32[5,1,32]{2,1,0:T(1,128)S(1)} %copy-done.2), custom_call_target="tpu_custom_call" | custom-call | flops 402653184 | bytes 1048576 | tf_op jit(solution)/shard_map/pallas_call | solution.py:209
  24.2 2.2 %collective-permute-start.3 = (f32[40,16,128]{2,1,0:T(8,128)S(1)}, f32[40,16,128]{2,1,0:T(8,128)S(1)}, u32[]{:S(2)}, u32[]{:S(2)}) collective-permute-start(f32[40,16,128]{2,1,0:T(8,128)S(1)} %shard_map.97.refs_0_), channel_id=1, source_target_pairs={{0,16},{1,17},{2,18},{3,19},{4,20},{5,21},{6,22},{7,23},{8,24},{9,... | collective-permute-start | bytes 983048 | tf_op jit(solution)/shard_map/ppermute | solution.py:408
  26.4 7.3 %collective-permute-done.3.refs_1_ = f32[40,16,128]{2,1,0:T(8,128)S(1)} collective-permute-done((f32[40,16,128]{2,1,0:T(8,128)S(1)}, f32[40,16,128]{2,1,0:T(8,128)S(1)}, u32[]{:S(2)}, u32[]{:S(2)}) %collective-permute-start.3) | collective-permute-done | bytes 327712 | tf_op jit(solution)/shard_map/ppermute | solution.py:408
  33.6 1.2 %shard_map.98.refs_0_ = f32[40,16,128]{2,1,0:T(8,128)S(1)} custom-call(f32[40,16,128]{2,1,0:T(8,128)S(1)} %shard_map.97.refs_0_, f32[40,16,128]{2,1,0:T(8,128)S(1)} %collective-permute-done.3.refs_1_, f32[5,2,2,128,128]{4,3,2,1,0:T(8,128)S(1)} %copy-done, s32[5,32]{1,0:T(8,128)S(1)} %copy-done.1, s32[5,1,32]{2,1,0:T(1,128)S(1)} %copy-done.2), custom_call_target="tpu_custom_call" | custom-call | flops 402653184 | bytes 1048576 | tf_op jit(solution)/shard_map/pallas_call | solution.py:209
  34.9 0.5 collective-permute-start.4
  35.4 6.6 %collective-permute-done.4.refs_1_ = f32[40,16,128]{2,1,0:T(8,128)S(1)} collective-permute-done((f32[40,16,128]{2,1,0:T(8,128)S(1)}, f32[40,16,128]{2,1,0:T(8,128)S(1)}, u32[]{:S(2)}, u32[]{:S(2)}) %collective-permute-start.4) | collective-permute-done | bytes 327712 | tf_op jit(solution)/shard_map/ppermute | solution.py:408
  42.0 1.2 %shard_map.99.refs_0_ = f32[40,16,128]{2,1,0:T(8,128)S(1)} custom-call(f32[40,16,128]{2,1,0:T(8,128)S(1)} %shard_map.98.refs_0_, f32[40,16,128]{2,1,0:T(8,128)S(1)} %collective-permute-done.4.refs_1_, f32[5,2,2,128,128]{4,3,2,1,0:T(8,128)S(1)} %copy-done, s32[5,32]{1,0:T(8,128)S(1)} %copy-done.1, s32[5,1,32]{2,1,0:T(1,128)S(1)} %copy-done.2), custom_call_target="tpu_custom_call" | custom-call | flops 402653184 | bytes 1048576 | tf_op jit(solution)/shard_map/pallas_call | solution.py:209
  43.3 7.5 %collective-permute-start.5 = (f32[40,16,128]{2,1,0:T(8,128)S(1)}, f32[40,16,128]{2,1,0:T(8,128)S(1)}, u32[]{:S(2)}, u32[]{:S(2)}) collective-permute-start(f32[40,16,128]{2,1,0:T(8,128)S(1)} %shard_map.99.refs_0_), channel_id=1, source_target_pairs={{0,4},{1,5},{2,6},{3,7},{4,0},{5,1},{6,2},{7,3},{8,12},{9,13},{10,... | collective-permute-start | bytes 983048 | tf_op jit(solution)/shard_map/ppermute | solution.py:408
  50.8 2.5 %shard_map.100.refs_5_ = f32[32,16,128]{2,1,0:T(8,128)S(1)} custom-call(f32[16,2,8,4096]{3,2,1,0:T(8,128)} %refs_2_.9, bf16[2,32,128,128]{3,2,1,0:T(8,128)(2,1)} %leaf_ref.3), custom_call_target="tpu_custom_call" | custom-call | flops 33554432 | bytes 2359296 | tf_op jit(solution)/shard_map/pallas_call | solution.py:73
  53.2 3.4 %collective-permute-done.5.refs_1_ = f32[40,16,128]{2,1,0:T(8,128)S(1)} collective-permute-done((f32[40,16,128]{2,1,0:T(8,128)S(1)}, f32[40,16,128]{2,1,0:T(8,128)S(1)}, u32[]{:S(2)}, u32[]{:S(2)}) %collective-permute-start.5) | collective-permute-done | bytes 327712 | tf_op jit(solution)/shard_map/ppermute | solution.py:408
  56.6 6.8 %shard_map.101 = (f32[16,4096]{1,0:T(8,128)S(1)}, f32[8,56,128]{2,1,0:T(8,128)S(1)}) custom-call(f32[40,16,128]{2,1,0:T(8,128)S(1)} %shard_map.99.refs_0_, f32[40,16,128]{2,1,0:T(8,128)S(1)} %collective-permute-done.5.refs_1_, f32[5,2,2,128,128]{4,3,2,1,0:T(8,128)S(1)} %copy-done, s32[5,32]{1,0:T(8,128)S(1)} %copy-done.1, s32[5,1,32]{2,1,0:T(1,128)S(1)} %copy-done.2, ...), custom_call_target="tpu_custom_call" | custom-call | flops 402653184 | bytes 8388608 | tf_op jit(solution)/shard_map/pallas_call | solution.py:277
  63.4 10.7 %all_to_all.10.got_ref = f32[8,56,128]{2,1,0:T(8,128)S(1)} all-to-all(f32[8,56,128]{2,1,0:T(8,128)S(1)} %get-tuple-element.8), channel_id=1, replica_groups=mesh['src'=8,'obs'=32] {'src'}, dimensions={0} | all-to-all | bytes 458752 | tf_op jit(solution)/shard_map/all_to_all | solution.py:436
  74.1 0.1 shard_map.102
  74.2 32.5 %all_to_all.11.refs_0_ = f32[32,40,128]{2,1,0:T(8,128)S(1)} all-to-all(f32[32,40,128]{2,1,0:T(8,128)S(1)} %shard_map.102), channel_id=1, replica_groups=mesh['src'=8,'obs'=32] {'obs'}, dimensions={0} | all-to-all | bytes 1310720 | tf_op jit(solution)/shard_map/all_to_all | solution.py:437
  106.6 4.0 %shard_map.103 = (f32[2,8,8,16]{3,2,1,0:T(8,128)}, f32[2,8,4096]{2,1,0:T(8,128)}, f32[2,8,8]{2,1,0:T(8,128)}) custom-call(f32[32,40,128]{2,1,0:T(8,128)S(1)} %all_to_all.11.refs_0_, f32[16,4096]{1,0:T(8,128)S(1)} %get-tuple-element.9.refs_1_, f32[16,2,8,4096]{3,2,1,0:T(8,128)} %refs_2_.9), custom_call_target="tpu_custom_call" | custom-call | flops 201326592 | bytes 6291456 | tf_op jit(solution)/shard_map/pallas_call | solution.py:388
  (1 shorter events, 0.0 us)
Async XLA Ops:
  3.1 9.7 %copy-start = (f32[5,2,2,128,128]{4,3,2,1,0:T(8,128)S(1)}, f32[5,2,2,128,128]{4,3,2,1,0:T(8,128)}, u32[]{:S(2)}) copy-start(f32[5,2,2,128,128]{4,3,2,1,0:T(8,128)} %refs_2_.8) | copy-start | bytes 3932164
  3.1 9.7 %copy-start.1 = (s32[5,32]{1,0:T(8,128)S(1)}, s32[5,32]{1,0:T(8,128)}, u32[]{:S(2)}) copy-start(s32[5,32]{1,0:T(8,128)} %refs_3_.7) | copy-start | bytes 1924
  3.1 9.7 %copy-start.2 = (s32[5,1,32]{2,1,0:T(1,128)S(1)}, s32[5,1,32]{2,1,0:T(1,128)}, u32[]{:S(2)}) copy-start(s32[5,1,32]{2,1,0:T(1,128)} %refs_4_.7) | copy-start | bytes 1924
  3.1 9.6 %collective-permute-start = (f32[32,16,128]{2,1,0:T(8,128)S(1)}, f32[32,16,128]{2,1,0:T(8,128)S(1)}, u32[]{:S(2)}, u32[]{:S(2)}) collective-permute-start(f32[32,16,128]{2,1,0:T(8,128)S(1)} %shard_map.94.own_ref), channel_id=1, source_target_pairs={{0,128},{32,160},{64,192},{96,224},{128,0},{160,32},{192,64},{224,... | collective-permute-start | bytes 786440 | tf_op jit(solution)/shard_map/ppermute | solution.py:408
  10.4 1.3 %collective-permute-start.1 = (f32[128,128]{1,0:T(8,128)S(1)}, f32[128,128]{1,0:T(8,128)S(1)}, u32[]{:S(2)}, u32[]{:S(2)}) collective-permute-start(f32[128,128]{1,0:T(8,128)S(1)} %shard_map.95), channel_id=1, source_target_pairs={{0,32},{32,0},{64,96},{96,64},{128,160},{160,128},{192,224},{224,1... | collective-permute-start | bytes 196616 | tf_op jit(solution)/shard_map/ppermute | solution.py:408
  14.0 8.9 %collective-permute-start.2 = (f32[40,16,128]{2,1,0:T(8,128)S(1)}, f32[40,16,128]{2,1,0:T(8,128)S(1)}, u32[]{:S(2)}, u32[]{:S(2)}) collective-permute-start(f32[40,16,128]{2,1,0:T(8,128)S(1)} %shard_map.96.refs_0_), channel_id=1, source_target_pairs={{0,64},{32,96},{64,0},{96,32},{128,192},{160,224},{192,128},{224,1... | collective-permute-start | bytes 983048 | tf_op jit(solution)/shard_map/ppermute | solution.py:408
  24.2 9.5 %collective-permute-start.3 = (f32[40,16,128]{2,1,0:T(8,128)S(1)}, f32[40,16,128]{2,1,0:T(8,128)S(1)}, u32[]{:S(2)}, u32[]{:S(2)}) collective-permute-start(f32[40,16,128]{2,1,0:T(8,128)S(1)} %shard_map.97.refs_0_), channel_id=1, source_target_pairs={{0,16},{1,17},{2,18},{3,19},{4,20},{5,21},{6,22},{7,23},{8,24},{9,... | collective-permute-start | bytes 983048 | tf_op jit(solution)/shard_map/ppermute | solution.py:408
  34.9 7.2 %collective-permute-start.4 = (f32[40,16,128]{2,1,0:T(8,128)S(1)}, f32[40,16,128]{2,1,0:T(8,128)S(1)}, u32[]{:S(2)}, u32[]{:S(2)}) collective-permute-start(f32[40,16,128]{2,1,0:T(8,128)S(1)} %shard_map.98.refs_0_), channel_id=1, source_target_pairs={{0,8},{1,9},{2,10},{3,11},{4,12},{5,13},{6,14},{7,15},{8,0},{9,1},... | collective-permute-start | bytes 983048 | tf_op jit(solution)/shard_map/ppermute | solution.py:408
  43.3 13.4 %collective-permute-start.5 = (f32[40,16,128]{2,1,0:T(8,128)S(1)}, f32[40,16,128]{2,1,0:T(8,128)S(1)}, u32[]{:S(2)}, u32[]{:S(2)}) collective-permute-start(f32[40,16,128]{2,1,0:T(8,128)S(1)} %shard_map.99.refs_0_), channel_id=1, source_target_pairs={{0,4},{1,5},{2,6},{3,7},{4,0},{5,1},{6,2},{7,3},{8,12},{9,13},{10,... | collective-permute-start | bytes 983048 | tf_op jit(solution)/shard_map/ppermute | solution.py:408

commit v2 on v1

v2 whole, which is shorter than its diff:
```python
import jax
import jax.numpy as jnp
from jax import lax
from jax.experimental import pallas as pl
from jax.experimental.pallas import tpu as pltpu
from jax.sharding import PartitionSpec as P

NT = (((1,), (1,)), ((), ()))
NN = (((1,), (0,)), ((), ()))
KERNEL_VMEM = 24 * 1024 * 1024
VMEM = pl.BlockSpec(memory_space=pltpu.VMEM)
BASIS_PARTS = 4


def in_hbm(value):
    return pltpu.with_memory_space_constraint(value, pltpu.HBM)


def dot_nt(left, right):
    return lax.dot_general(left, right, NT, preferred_element_type=jnp.float32)


def dot_nn(left, right):
    return lax.dot_general(left, right, NN, preferred_element_type=jnp.float32)


def split3(value):
    high = value.astype(jnp.bfloat16)
    rest = value - high.astype(jnp.float32)
    middle = rest.astype(jnp.bfloat16)
    low = (rest - middle.astype(jnp.float32)).astype(jnp.bfloat16)
    return high, middle, low


def split2(value):
    high = value.astype(jnp.bfloat16)
    return high, (value - high.astype(jnp.float32)).astype(jnp.bfloat16)


def complex_rows(rows):
    real, imag = rows[:8], rows[8:]
    return jnp.concatenate(
        [jnp.concatenate([real, -imag], axis=1), jnp.concatenate([imag, real], axis=1)], axis=0
    )


def leaf_product(rows, real, imag):
    return dot_nt(
        complex_rows(rows).astype(jnp.bfloat16), jnp.concatenate([real, imag], axis=1)
    )


def leaves_kernel(basis_ref, leaf_ref, out_ref, newest_ref, held_ref, newest_sem, held_sems):
    steps = held_sems.shape[0]
    count = held_ref.shape[1]
    part = count // steps
    newest_copy = pltpu.make_async_copy(
        basis_ref.at[basis_ref.shape[0] - 1], newest_ref, newest_sem
    )
    newest_copy.start()
    copies = []
    for step in range(steps):
        here = pl.ds(step * part, part)
        copies.append(
            pltpu.make_async_copy(leaf_ref.at[:, here], held_ref.at[:, here], held_sems.at[step])
        )
        copies[-1].start()
    newest_copy.wait()
    for leaf in range(count):
        if leaf % part == 0:
            copies[leaf // part].wait()
        rows = newest_ref[:, :, leaf * 128 : (leaf + 1) * 128].reshape(16, 128)
        rows = rows.astype(jnp.bfloat16).astype(jnp.float32)
        out_ref[leaf] = leaf_product(rows, held_ref[0, leaf], held_ref[1, leaf])


def apply_leaves(krylov_basis, leaves, steps):
    count = leaves.shape[1]
    return pl.pallas_call(
        leaves_kernel,
        in_specs=[pl.BlockSpec(memory_space=pltpu.HBM)] * 2,
        out_specs=pl.BlockSpec(memory_space=pltpu.VMEM),
        out_shape=jax.ShapeDtypeStruct((count, 16, 128), jnp.float32),
        scratch_shapes=[
            pltpu.VMEM(krylov_basis.shape[1:], jnp.float32),
            pltpu.VMEM(leaves.shape, leaves.dtype),
            pltpu.SemaphoreType.DMA,
            pltpu.SemaphoreType.DMA((steps,)),
        ],
        compiler_params=pltpu.CompilerParams(vmem_limit_bytes=KERNEL_VMEM),
        cost_estimate=pl.CostEstimate(
            flops=count * 16 * 256 * 128 * 2, bytes_accessed=count * 73728, transcendentals=0
        ),
    )(in_hbm(krylov_basis), in_hbm(leaves))


def stacked(basis):
    width = basis.shape[3]
    return jnp.concatenate(
        [basis[:, 0].reshape(128, width), basis[:, 1].reshape(128, width)], axis=0
    )


def basis_gram_kernel(basis_ref, out_ref, high_ref, middle_ref, low_ref, held_ref, sems):
    steps = sems.shape[0]
    width = held_ref.shape[3] // steps
    copies = []
    for step in range(steps):
        here = pl.ds(step * width, width)
        copies.append(
            pltpu.make_async_copy(
                basis_ref.at[:, :, :, here], held_ref.at[:, :, :, here], sems.at[step]
            )
        )
        copies[-1].start()
    even = jnp.zeros((256, 256), jnp.float32)
    odd = jnp.zeros((256, 256), jnp.float32)
    for step, copy in enumerate(copies):
        copy.wait()
        here = slice(step * width, (step + 1) * width)
        high, middle, low = split3(stacked(held_ref[:, :, :, here]))
        high_ref[:, here] = high
        middle_ref[:, here] = middle
        low_ref[:, here] = low
        even += dot_nt(high, high) + dot_nt(middle, middle)
        odd += dot_nt(high, middle) + dot_nt(high, low)
    gram = even + odd + odd.T
    real = gram[:128, :128] + gram[128:, 128:]
    imag = gram[:128, 128:] - gram[128:, :128]
    row = lax.broadcasted_iota(jnp.int32, (128, 128), 0)
    column = lax.broadcasted_iota(jnp.int32, (128, 128), 1)
    out_ref[...] = jnp.where(row <= column, real, imag)


def basis_gram(krylov_basis):
    part = jax.ShapeDtypeStruct((256, krylov_basis.shape[3]), jnp.bfloat16)
    gram, *parts = pl.pallas_call(
        basis_gram_kernel,
        in_specs=[pl.BlockSpec(memory_space=pltpu.HBM)],
        out_specs=[VMEM] * 4,
        out_shape=[jax.ShapeDtypeStruct((128, 128), jnp.float32), part, part, part],
        scratch_shapes=[
            pltpu.VMEM(krylov_basis.shape, jnp.float32),
            pltpu.SemaphoreType.DMA((BASIS_PARTS,)),
        ],
        compiler_params=pltpu.CompilerParams(vmem_limit_bytes=KERNEL_VMEM),
        cost_estimate=pl.CostEstimate(
            flops=4 * 2 * 256 * 256 * 4096, bytes_accessed=10 << 20, transcendentals=0
        ),
    )(in_hbm(krylov_basis))
    return gram, parts


def mix(level, own_ref, partner_ref, mixer_ref, rank_ref, table_ref):
    table = table_ref[level]
    picked = jnp.concatenate([partner_ref[table[0, leaf]] for leaf in range(32)], axis=0)
    both = jnp.concatenate([own_ref[...].reshape(512, 128), picked], axis=1)
    weights = jnp.concatenate(
        [
            jnp.concatenate([mixer_ref[level, 0, 0], mixer_ref[level, 0, 1]], axis=1),
            jnp.concatenate([mixer_ref[level, 1, 0], mixer_ref[level, 1, 1]], axis=1),
        ],
        axis=0,
    )
    high, low = split2(both)
    w_high, w_low = split2(weights)
    product = dot_nn(high, w_high) + dot_nn(high, w_low) + dot_nn(low, w_high)
    column = lax.broadcasted_iota(jnp.int32, (16, 128), 1)
    ranks = rank_ref[level : level + 1]

    def leaf_value(leaf):
        by_real = product[leaf * 16 : (leaf + 1) * 16, :128]
        by_imag = product[leaf * 16 : (leaf + 1) * 16, 128:]
        mixed = jnp.concatenate([by_real[:8] - by_imag[8:], by_real[8:] + by_imag[:8]], axis=0)
        return jnp.where(column < ranks[0, leaf], mixed, 0.0)

    return leaf_value


def level_kernel(level, own_ref, partner_ref, mixer_ref, rank_ref, table_ref, *refs):
    out_ref = refs[-1]
    leaf_value = mix(level, own_ref, partner_ref, mixer_ref, rank_ref, table_ref)
    for leaf in range(32):
        out_ref[leaf] = leaf_value(leaf)


def next_level(level, own, partner, level_mixers, block_ranks, partner_tables, before):
    return pl.pallas_call(
        lambda *refs: level_kernel(level, *refs),
        in_specs=[VMEM] * 5 + [pl.BlockSpec(memory_space=pl.ANY)] * len(before),
        out_specs=VMEM,
        out_shape=jax.ShapeDtypeStruct((32, 16, 128), jnp.float32),
        compiler_params=pltpu.CompilerParams(vmem_limit_bytes=KERNEL_VMEM),
        cost_estimate=pl.CostEstimate(
            flops=3 * 512 * 256 * 256 * 2, bytes_accessed=1 << 20, transcendentals=0
        ),
    )(own, partner, level_mixers, block_ranks, partner_tables, *before)


def project_kernel(
    level, own_ref, partner_ref, mixer_ref, rank_ref, table_ref, close_ref, leaf_ref,
    high_ref, middle_ref, low_ref, before_ref, image_ref, sums_ref,
):
    leaf_value = mix(level, own_ref, partner_ref, mixer_ref, rank_ref, table_ref)
    for leaf in range(32):
        rounded = leaf_value(leaf).astype(jnp.bfloat16).astype(jnp.float32)
        far = leaf_product(rounded, leaf_ref[0, leaf], leaf_ref[1, leaf])
        image_ref[:, leaf * 128 : (leaf + 1) * 128] = far + close_ref[leaf]
    high, middle, low = split3(image_ref[...])
    three = jnp.concatenate([high, middle, low], axis=0)
    two = three[:32]

    def product(first, second, third):
        one = dot_nt(three, first)
        result = one[:16] + one[16:32] + one[32:]
        one = dot_nt(two, second)
        return result + one[:16] + one[16:] + dot_nt(high, third)

    inner = product(high_ref[...], middle_ref[...], low_ref[...])
    square = product(high, middle, low)
    first = jnp.concatenate(
        [inner[:8, :128] + inner[8:, 128:], inner[8:, :128] - inner[:8, 128:]], axis=0
    )
    real = square[:8, :8] + square[8:, 8:]
    imag = square[:8, 8:] - square[8:, :8]
    pieces = [real[row : row + 1] for row in range(8)] + [imag[row : row + 1] for row in range(8)]
    last = jnp.concatenate(pieces, axis=1)
    for device in range(8):
        sums_ref[device, 0:16, 0] = first
        sums_ref[device, 16] = last


def project(
    level, own, partner, level_mixers, block_ranks, partner_tables, close, leaf_out, parts, before
):
    return pl.pallas_call(
        lambda *refs: project_kernel(level, *refs),
        in_specs=[VMEM] * 10 + [pl.BlockSpec(memory_space=pl.ANY)],
        out_specs=[VMEM] * 2,
        out_shape=[
            jax.ShapeDtypeStruct((16, 4096), jnp.float32),
            jax.ShapeDtypeStruct((8, 17, 1, 128), jnp.float32),
        ],
        compiler_params=pltpu.CompilerParams(vmem_limit_bytes=KERNEL_VMEM),
        cost_estimate=pl.CostEstimate(
            flops=6 * 512 * 256 * 256 * 2, bytes_accessed=8 << 20, transcendentals=0
        ),
    )(own, partner, level_mixers, block_ranks, partner_tables, close, leaf_out, *parts, before)


def relay_kernel(got_ref, before_ref, out_ref):
    sums = jnp.sum(got_ref[...], axis=0)
    for device in range(32):
        out_ref[device] = sums


def relay(got, before):
    return pl.pallas_call(
        relay_kernel,
        in_specs=[VMEM, pl.BlockSpec(memory_space=pl.ANY)],
        out_specs=VMEM,
        out_shape=jax.ShapeDtypeStruct((32, 17, 1, 128), jnp.float32),
        compiler_params=pltpu.CompilerParams(vmem_limit_bytes=KERNEL_VMEM),
    )(got, before)


def dot_high(left, right, numbers):
    return lax.dot_general(
        left, right, numbers, precision=lax.Precision.HIGHEST, preferred_element_type=jnp.float32
    )


def finish_kernel(
    scale, got_ref, gram_ref, image_ref, high_ref, middle_ref, low_ref, total_ref, new_ref, block_ref
):
    sums = jnp.concatenate(
        [jnp.sum(got_ref[:, row, 0], axis=0, keepdims=True) for row in range(17)], axis=0
    )
    sums = sums * scale
    first = sums[:16]
    packed = gram_ref[...] * scale
    row = lax.broadcasted_iota(jnp.int32, (128, 128), 0)
    column = lax.broadcasted_iota(jnp.int32, (128, 128), 1)
    flipped = packed.T
    gram_real = jnp.where(row <= column, packed, flipped)
    gram_imag = jnp.where(row > column, packed, jnp.where(row < column, -flipped, 0.0))
    gram = jnp.concatenate([gram_real, gram_imag], axis=1)

    def by_gram(rows):
        one = dot_high(rows, gram, NN)
        real = one[:8, :128] + one[8:, 128:]
        imag = one[8:, :128] - one[:8, 128:]
        return jnp.concatenate([real, imag], axis=0)

    total = first + (first - by_gram(first))
    rest = first - by_gram(total)

    def inner(left, right):
        one = dot_high(left, right, NT)
        return one[:8, :8] + one[8:, 8:], one[:8, 8:] - one[8:, :8]

    one_real, one_imag = inner(first, total)
    two_real, two_imag = inner(total, rest)
    taken_real, taken_imag = one_real + two_real, one_imag + two_imag
    for angle in range(8):
        at = angle * 8
        block_ref[0, angle] = sums[16, at : at + 8] - taken_real[angle]
        block_ref[1, angle] = sums[16, 64 + at : 72 + at] - taken_imag[angle]
    high, middle, low = split3(complex_rows(total))
    three = jnp.concatenate([high, middle, low], axis=0)
    two = three[:32]
    width = 1024
    for start in range(0, 4096, width):
        here = slice(start, start + width)
        one = dot_nn(three, high_ref[:, here])
        taken = one[:16] + one[16:32] + one[32:]
        one = dot_nn(two, middle_ref[:, here])
        taken += one[:16] + one[16:]
        taken += dot_nn(high, low_ref[:, here])
        new_ref[:, :, here] = (image_ref[:, here] - taken).reshape(2, 8, width)
    turn = jnp.where(row == lax.rem(column, 16) * 8 + lax.div(column, 16), 1.0, 0.0)
    turned = dot_high(total, turn, NN)
    for angle in range(8):
        total_ref[0, angle] = turned[:8, angle * 16 : (angle + 1) * 16]
        total_ref[1, angle] = turned[8:, angle * 16 : (angle + 1) * 16]


def finish(scale, got, gram, image, parts):
    return pl.pallas_call(
        lambda *refs: finish_kernel(scale, *refs),
        in_specs=[VMEM] * 6,
        out_specs=[VMEM] * 3,
        out_shape=[
            jax.ShapeDtypeStruct((2, 8, 8, 16), jnp.float32),
            jax.ShapeDtypeStruct((2, 8, 4096), jnp.float32),
            jax.ShapeDtypeStruct((2, 8, 8), jnp.float32),
        ],
        compiler_params=pltpu.CompilerParams(vmem_limit_bytes=KERNEL_VMEM),
        cost_estimate=pl.CostEstimate(
            flops=6 * 16 * 256 * 4096 * 2, bytes_accessed=6 << 20, transcendentals=0
        ),
    )(got, gram, image, *parts)


def add_kernel(left_ref, right_ref, before_ref, out_ref):
    out_ref[...] = left_ref[...] + right_ref[...]


def add_after(left, right, before):
    return pl.pallas_call(
        add_kernel,
        in_specs=[VMEM, VMEM, pl.BlockSpec(memory_space=pl.ANY)],
        out_specs=VMEM,
        out_shape=jax.ShapeDtypeStruct(left.shape, left.dtype),
        compiler_params=pltpu.CompilerParams(vmem_limit_bytes=KERNEL_VMEM),
    )(left, right, before)


def exchange(value, axis, bit_number):
    pairs = [(source, source ^ (1 << bit_number)) for source in range(lax.axis_size(axis))]
    return lax.ppermute(value, axis, pairs)


def per_device(
    krylov_basis, near_field, leaf_in, leaf_out, level_mixers, block_ranks, partner_tables
):
    src_bits = lax.axis_size("src").bit_length() - 1
    obs_bits = lax.axis_size("obs").bit_length() - 1
    plan = [
        ("src", src_bits - 1),
        ("src", src_bits - 2),
        ("obs", obs_bits - 1),
        ("obs", obs_bits - 2),
        ("obs", obs_bits - 3),
    ]
    coeffs = apply_leaves(krylov_basis, leaf_in, 4)
    close = apply_leaves(krylov_basis, near_field, 4)
    gram, parts = basis_gram(krylov_basis)
    beside = [
        [("src", 0)],
        [("obs", obs_bits - 1)],
        [("obs", 1)],
        [("src", src_bits - 1)],
        [("obs", 2), ("obs", 0)],
        [("obs", obs_bits - 2)],
        [("src", 1)],
    ]

    def sum_on(gram, step, before=None):
        for axis, bit in beside[step][:-1]:
            gram = gram + exchange(gram, axis, bit)
        got = exchange(gram, *beside[step][-1])
        return gram + got if before is None else add_after(gram, got, before)

    for level, (axis, bit) in enumerate(plan):
        partner = exchange(coeffs, axis, bit)
        operands = (level, coeffs, partner, level_mixers, block_ranks, partner_tables)
        if level < len(plan) - 1:
            gram = sum_on(gram, level)
            coeffs = next_level(*operands, [gram, close] if level == 2 else [gram])
        else:
            gram = sum_on(gram, level, partner)
            image, sums = project(*operands, close, leaf_out, parts, gram)
    gram = sum_on(gram, 5, image)
    got = lax.all_to_all(sums, "src", 0, 0)
    gram = sum_on(gram, 6)
    got = relay(got, gram)
    got = lax.all_to_all(got, "obs", 0, 0)
    devices = lax.axis_size("src") * lax.axis_size("obs")
    scale = 1.0 / (krylov_basis.shape[3] * devices)
    total, new_block, block_gram = finish(scale, got, gram, image, parts)
    return jnp.transpose(total, (3, 0, 1, 2)), new_block, block_gram


def solution(mesh):
    in_specs = (
        P(None, None, None, ("src", "obs")),
        P(None, ("src", "obs"), None, None),
        P(None, ("src", "obs"), None, None),
        P(None, ("src", "obs"), None, None),
        P(None, None, None, None, ("src", "obs")),
        P(None, ("src", "obs")),
        P(None, ("src", "obs"), None),
    )
    out_specs = (P(), P(None, None, ("src", "obs")), P())
    return jax.shard_map(
        per_device, mesh=mesh, in_specs=in_specs, out_specs=out_specs, check_vma=False
    )
```

time: 113 us -> 104 us (0.920); the launches traced: 111 us -> 103 us
  blocking collectives: 43.1 us -> 22.3 us
  starting transfers between devices: 15.3 us -> 33.8 us
  Pallas kernels: 24.7 us -> 17.8 us
  local copies, waits for them, and re-layouts: 0.02 us -> 3.22 us
  waiting for transfers between devices: 26.8 us -> 25.4 us
    ppermute x6 -> x13, starting transfers between devices: 15.3 us -> 29.6 us  [exchange(): return lax.ppermute(value, axis, pairs)]
    all_to_all x1 -> x0, blocking collectives: 10.7 us -> none  [per_device(): got = relay(lax.all_to_all(sums, 'src', 0, 0))]
    all_to_all x1, blocking collectives: 32.5 us -> 22.3 us  [per_device(): got = lax.all_to_all(got, 'obs', 0, 0)]
    pallas_call x7 -> x9, Pallas kernels: 15.7 us -> 8.76 us  [the longest x1 4.33 us: project(): pl.pallas_call(lambda *refs: project_kernel(level, *refs), in_specs=[VMEM...]
    ppermute x6 -> x13, waiting for transfers between devices: 26.8 us -> 19.8 us  [exchange(): return lax.ppermute(value, axis, pairs)]
    all_to_all x0 -> x1, waiting for transfers between devices: none -> 5.62 us  [per_device(): got = lax.all_to_all(sums, 'src', 0, 0)]
    all_to_all x0 -> x1, starting transfers between devices: none -> 4.16 us  [per_device(): got = lax.all_to_all(sums, 'src', 0, 0)]
    unnamed x6 -> x16, local copies, waits for them, and re-layouts: 0.02 us -> 3.22 us
  transfers between devices with their start and end apart: 6 -> 14, of which waited for: 6 -> 9; matrix products, arithmetic and copies ran while one was open for 0% -> 0% of each run, Pallas kernels for 6% -> 11%
where the time goes in v2:
time: 104 us; the launch traced here: 103 us
  starting transfers between devices  33.8 us (32%)
  waiting for transfers between devices  25.4 us (24%)
  blocking collectives  22.3 us (21%)
  Pallas kernels  17.8 us (17%)
  local copies, waits for them, and re-layouts  3.22 us (3%)
    ppermute x13, starting transfers between devices, exchange(): return lax.ppermute(value, axis, pairs)  29.6 us
    all_to_all x1, blocking collectives, per_device(): got = lax.all_to_all(got, 'obs', 0, 0)  22.3 us
    ppermute x13, waiting for transfers between devices, exchange(): return lax.ppermute(value, axis, pairs)  19.8 us
    all_to_all x1, waiting for transfers between devices, per_device(): got = lax.all_to_all(sums, 'src', 0, 0)  5.62 us
    pallas_call x2, Pallas kernels, apply_leaves(): pl.pallas_call(leaves_kernel, in_specs=[pl.BlockSpec(memory_space=pltpu.H...  4.95 us
    pallas_call x1, Pallas kernels, project(): pl.pallas_call(lambda *refs: project_kernel(level, *refs), in_specs=[VMEM...  4.33 us
    all_to_all x1, starting transfers between devices, per_device(): got = lax.all_to_all(sums, 'src', 0, 0)  4.16 us
    pallas_call x1, Pallas kernels, basis_gram(): pl.pallas_call(basis_gram_kernel, in_specs=[pl.BlockSpec(memory_space=plt...  4.05 us
  transfers between devices with their start and end apart: 14, of which 9 were waited for; matrix products, arithmetic and copies ran while one was open for 0% of the time, Pallas kernels for 11%

profile of v2, /device:TPU:2, one launch (start us, length us, event | category | flops | bytes accessed | tf_op | source)
XLA Modules:
  0.0 103.3 jit_solution(3928674826235862010)
XLA Ops:
  0.6 2.5 %shard_map.94.refs_0_ = f32[32,16,128]{2,1,0:T(8,128)S(1)} custom-call(f32[16,2,8,4096]{3,2,1,0:T(8,128)} %basis_ref.5, bf16[2,32,128,128]{3,2,1,0:T(8,128)(2,1)} %leaf_ref.2), custom_call_target="tpu_custom_call" | custom-call | flops 33554432 | bytes 2359296 | tf_op jit(solution)/shard_map/pallas_call | solution.py:79
  3.1 0.0 copy-start
  3.1 0.0 copy-start.6
  3.1 0.0 copy-start.7
  3.1 3.3 %collective-permute-start = (f32[32,16,128]{2,1,0:T(8,128)S(1)}, f32[32,16,128]{2,1,0:T(8,128)S(1)}, u32[]{:S(2)}, u32[]{:S(2)}) collective-permute-start(f32[32,16,128]{2,1,0:T(8,128)S(1)} %shard_map.94.refs_0_), channel_id=1, source_target_pairs={{0,128},{32,160},{64,192},{96,224},{128,0},{160,32},{192,64},{224,... | collective-permute-start | bytes 786440 | tf_op jit(solution)/shard_map/ppermute | solution.py:361
  6.4 4.1 %shard_map.95 = (f32[128,128]{1,0:T(8,128)S(1)}, bf16[256,4096]{1,0:T(8,128)(2,1)S(1)}, bf16[256,4096]{1,0:T(8,128)(2,1)S(1)}, bf16[256,4096]{1,0:T(8,128)(2,1)S(1)}) custom-call(f32[16,2,8,4096]{3,2,1,0:T(8,128)} %basis_ref.5), custom_call_target="tpu_custom_call" | custom-call | flops 2147483648 | bytes 10485760 | tf_op jit(solution)/shard_map/pallas_call | solution.py:137
  10.5 0.1 collective-permute-start.1
  10.6 1.2 %collective-permute-done.1 = f32[128,128]{1,0:T(8,128)S(1)} collective-permute-done((f32[128,128]{1,0:T(8,128)S(1)}, f32[128,128]{1,0:T(8,128)S(1)}, u32[]{:S(2)}, u32[]{:S(2)}) %collective-permute-start.1) | collective-permute-done | bytes 65568 | tf_op jit(solution)/shard_map/ppermute | solution.py:361
  11.9 0.9 collective-permute-done.refs_1_
  12.8 0.0 copy-done
  12.8 0.5 shard_map.96.refs_0_
  13.3 1.7 %collective-permute-start.2 = (f32[32,16,128]{2,1,0:T(8,128)S(1)}, f32[32,16,128]{2,1,0:T(8,128)S(1)}, u32[]{:S(2)}, u32[]{:S(2)}) collective-permute-start(f32[32,16,128]{2,1,0:T(8,128)S(1)} %shard_map.96.refs_0_), channel_id=1, source_target_pairs={{0,64},{32,96},{64,0},{96,32},{128,192},{160,224},{192,128},{224,1... | collective-permute-start | bytes 786440 | tf_op jit(solution)/shard_map/ppermute | solution.py:361
  14.9 2.1 %collective-permute-start.3 = (f32[128,128]{1,0:T(8,128)S(1)}, f32[128,128]{1,0:T(8,128)S(1)}, u32[]{:S(2)}, u32[]{:S(2)}) collective-permute-start(f32[128,128]{1,0:T(8,128)S(1)} %add.18.refs_5_), channel_id=1, source_target_pairs={{0,16},{1,17},{2,18},{3,19},{4,20},{5,21},{6,22},{7,23},{8,24},{9,... | collective-permute-start | bytes 196616 | tf_op jit(solution)/shard_map/ppermute | solution.py:361
  17.1 3.6 %collective-permute-done.3 = f32[128,128]{1,0:T(8,128)S(1)} collective-permute-done((f32[128,128]{1,0:T(8,128)S(1)}, f32[128,128]{1,0:T(8,128)S(1)}, u32[]{:S(2)}, u32[]{:S(2)}) %collective-permute-start.3) | collective-permute-done | bytes 65568 | tf_op jit(solution)/shard_map/ppermute | solution.py:361
  20.7 0.1 collective-permute-done.2.refs_1_
  20.8 0.5 shard_map.97.refs_0_
  21.3 2.2 %collective-permute-start.4 = (f32[32,16,128]{2,1,0:T(8,128)S(1)}, f32[32,16,128]{2,1,0:T(8,128)S(1)}, u32[]{:S(2)}, u32[]{:S(2)}) collective-permute-start(f32[32,16,128]{2,1,0:T(8,128)S(1)} %shard_map.97.refs_0_), channel_id=1, source_target_pairs={{0,16},{1,17},{2,18},{3,19},{4,20},{5,21},{6,22},{7,23},{8,24},{9,... | collective-permute-start | bytes 786440 | tf_op jit(solution)/shard_map/ppermute | solution.py:361
  23.5 3.3 %collective-permute-start.5 = (f32[128,128]{1,0:T(8,128)S(1)}, f32[128,128]{1,0:T(8,128)S(1)}, u32[]{:S(2)}, u32[]{:S(2)}) collective-permute-start(f32[128,128]{1,0:T(8,128)S(1)} %add.19.refs_5_), channel_id=1, source_target_pairs={{0,2},{1,3},{2,0},{3,1},{4,6},{5,7},{6,4},{7,5},{8,10},{9,11},{10,... | collective-permute-start | bytes 196616 | tf_op jit(solution)/shard_map/ppermute | solution.py:361
  26.8 2.5 %shard_map.98.refs_6_.refs_5_ = f32[32,16,128]{2,1,0:T(8,128)S(1)} custom-call(f32[16,2,8,4096]{3,2,1,0:T(8,128)} %basis_ref.5, bf16[2,32,128,128]{3,2,1,0:T(8,128)(2,1)} %leaf_ref.3), custom_call_target="tpu_custom_call" | custom-call | flops 33554432 | bytes 2359296 | tf_op jit(solution)/shard_map/pallas_call | solution.py:79
  29.3 0.0 collective-permute-done.5
  29.3 0.2 collective-permute-done.4.refs_1_
  29.5 0.5 shard_map.99.refs_0_
  29.9 0.0 copy-start.5
  29.9 1.4 %collective-permute-start.6 = (f32[32,16,128]{2,1,0:T(8,128)S(1)}, f32[32,16,128]{2,1,0:T(8,128)S(1)}, u32[]{:S(2)}, u32[]{:S(2)}) collective-permute-start(f32[32,16,128]{2,1,0:T(8,128)S(1)} %shard_map.99.refs_0_), channel_id=1, source_target_pairs={{0,8},{1,9},{2,10},{3,11},{4,12},{5,13},{6,14},{7,15},{8,0},{9,1},... | collective-permute-start | bytes 786440 | tf_op jit(solution)/shard_map/ppermute | solution.py:361
  31.3 2.9 %collective-permute-start.7 = (f32[128,128]{1,0:T(8,128)S(1)}, f32[128,128]{1,0:T(8,128)S(1)}, u32[]{:S(2)}, u32[]{:S(2)}) collective-permute-start(f32[128,128]{1,0:T(8,128)S(1)} %add.20.refs_5_), channel_id=1, source_target_pairs={{0,128},{32,160},{64,192},{96,224},{128,0},{160,32},{192,64},{224,... | collective-permute-start | bytes 196616 | tf_op jit(solution)/shard_map/ppermute | solution.py:361
  34.2 2.9 %collective-permute-done.7 = f32[128,128]{1,0:T(8,128)S(1)} collective-permute-done((f32[128,128]{1,0:T(8,128)S(1)}, f32[128,128]{1,0:T(8,128)S(1)}, u32[]{:S(2)}, u32[]{:S(2)}) %collective-permute-start.7) | collective-permute-done | bytes 65568 | tf_op jit(solution)/shard_map/ppermute | solution.py:361
  37.1 0.0 collective-permute-done.6.refs_1_
  37.1 0.5 shard_map.100.refs_0_
  37.6 7.4 %collective-permute-start.8 = (f32[32,16,128]{2,1,0:T(8,128)S(1)}, f32[32,16,128]{2,1,0:T(8,128)S(1)}, u32[]{:S(2)}, u32[]{:S(2)}) collective-permute-start(f32[32,16,128]{2,1,0:T(8,128)S(1)} %shard_map.100.refs_0_), channel_id=1, source_target_pairs={{0,4},{1,5},{2,6},{3,7},{4,0},{5,1},{6,2},{7,3},{8,12},{9,13},{10,... | collective-permute-start | bytes 786440 | tf_op jit(solution)/shard_map/ppermute | solution.py:361
  44.9 0.1 collective-permute-start.9
  45.0 8.6 %collective-permute-done.9 = f32[128,128]{1,0:T(8,128)S(1)} collective-permute-done((f32[128,128]{1,0:T(8,128)S(1)}, f32[128,128]{1,0:T(8,128)S(1)}, u32[]{:S(2)}, u32[]{:S(2)}) %collective-permute-start.9) | collective-permute-done | bytes 65568 | tf_op jit(solution)/shard_map/ppermute | solution.py:361
  53.6 3.0 %collective-permute-start.10 = (f32[128,128]{1,0:T(8,128)S(1)}, f32[128,128]{1,0:T(8,128)S(1)}, u32[]{:S(2)}, u32[]{:S(2)}) collective-permute-start(f32[128,128]{1,0:T(8,128)S(1)} %add.22.left_ref), channel_id=1, source_target_pairs={{0,1},{1,0},{2,3},{3,2},{4,5},{5,4},{6,7},{7,6},{8,9},{9,8},{10,11... | collective-permute-start | bytes 196616 | tf_op jit(solution)/shard_map/ppermute | solution.py:361
  56.6 2.2 %collective-permute-done.10.right_ref = f32[128,128]{1,0:T(8,128)S(1)} collective-permute-done((f32[128,128]{1,0:T(8,128)S(1)}, f32[128,128]{1,0:T(8,128)S(1)}, u32[]{:S(2)}, u32[]{:S(2)}) %collective-permute-start.10) | collective-permute-done | bytes 65568 | tf_op jit(solution)/shard_map/ppermute | solution.py:361
  58.9 0.0 collective-permute-done.8.before_ref.refs_1_
  58.9 1.3 %collective-permute-start.11 = (f32[128,128]{1,0:T(8,128)S(1)}, f32[128,128]{1,0:T(8,128)S(1)}, u32[]{:S(2)}, u32[]{:S(2)}) collective-permute-start(f32[128,128]{1,0:T(8,128)S(1)} %shard_map.101.refs_10_.left_ref), channel_id=1, source_target_pairs={{0,8},{1,9},{2,10},{3,11},{4,12},{5,13},{6,14},{7,15},{8,0},{9,1},... | collective-permute-start | bytes 196616 | tf_op jit(solution)/shard_map/ppermute | solution.py:361
  60.2 0.0 copy-done.1
  60.2 0.0 copy-done.5
  60.2 4.3 %shard_map.102 = (f32[16,4096]{1,0:T(8,128)S(1)}, f32[8,17,1,128]{3,2,1,0:T(1,128)}) custom-call(f32[32,16,128]{2,1,0:T(8,128)S(1)} %shard_map.100.refs_0_, f32[32,16,128]{2,1,0:T(8,128)S(1)} %collective-permute-done.8.before_ref.refs_1_, f32[5,2,2,128,128]{4,3,2,1,0:T(8,128)S(1)} %copy-done, s32[5,32]{1,0:T(8,128)S(1)} %copy-done.6, ...), custom_call_target="tpu_custom_call" | custom-call | flops 402653184 | bytes 8388608 | tf_op jit(solution)/shard_map/pallas_call | solution.py:236
  64.6 0.0 collective-permute-done.11.right_ref
  64.6 0.9 collective-permute-start.12
  65.5 4.2 %all-to-all-start = ((f32[8,17,1,128]{3,2,1,0:T(1,128)}), f32[8,17,1,128]{3,2,1,0:T(1,128)S(1)}, u32[]{:S(2)}, u32[]{:S(2)}) async-start(f32[8,17,1,128]{3,2,1,0:T(1,128)} %get-tuple-element.16), calls=%async_computation | async-start | bytes 139264 | tf_op jit(solution)/shard_map/all_to_all | solution.py:405
  69.6 0.0 collective-permute-done.12
  69.7 5.6 %all-to-all-done.got_ref = f32[8,17,1,128]{3,2,1,0:T(1,128)S(1)} async-done(((f32[8,17,1,128]{3,2,1,0:T(1,128)}), f32[8,17,1,128]{3,2,1,0:T(1,128)S(1)}, u32[]{:S(2)}, u32[]{:S(2)}) %all-to-all-start) | async-done | bytes 69664 | tf_op jit(solution)/shard_map/all_to_all | solution.py:405
  75.3 0.2 shard_map.104
  75.4 22.3 %all_to_all.10.refs_0_ = f32[32,17,1,128]{3,2,1,0:T(1,128)S(1)} all-to-all(f32[32,17,1,128]{3,2,1,0:T(1,128)S(1)} %shard_map.104), channel_id=1, replica_groups=mesh['src'=8,'obs'=32] {'obs'}, dimensions={0} | all-to-all | bytes 557056 | tf_op jit(solution)/shard_map/all_to_all | solution.py:408
  97.7 1.6 %copy-done.2 = bf16[256,4096]{1,0:T(8,128)(2,1)S(1)} copy-done((bf16[256,4096]{1,0:T(8,128)(2,1)S(1)}, bf16[256,4096]{1,0:T(8,128)(2,1)}, u32[]{:S(2)}) %copy-start.2) | copy-done | bytes 2097176
  99.3 1.6 %copy-done.4 = bf16[256,4096]{1,0:T(8,128)(2,1)S(1)} copy-done((bf16[256,4096]{1,0:T(8,128)(2,1)S(1)}, bf16[256,4096]{1,0:T(8,128)(2,1)}, u32[]{:S(2)}) %copy-start.4) | copy-done | bytes 2097176
  100.9 2.4 %shard_map.105 = (f32[2,8,8,16]{3,2,1,0:T(8,128)}, f32[2,8,4096]{2,1,0:T(8,128)}, f32[2,8,8]{2,1,0:T(8,128)}) custom-call(f32[32,17,1,128]{3,2,1,0:T(1,128)S(1)} %all_to_all.10.refs_0_, f32[128,128]{1,0:T(8,128)S(1)} %add.23.before_ref.refs_1_, f32[16,4096]{1,0:T(8,128)S(1)} %get-tuple-element.17.before_ref.refs_2_, ...), custom_call_target="tpu_custom_call" | custom-call | flops 201326592 | bytes 6291456 | tf_op jit(solution)/shard_map/pallas_call | solution.py:329
  (15 shorter events, 0.1 us)
Async XLA Ops:
  3.1 9.7 %copy-start = (f32[5,2,2,128,128]{4,3,2,1,0:T(8,128)S(1)}, f32[5,2,2,128,128]{4,3,2,1,0:T(8,128)}, u32[]{:S(2)}) copy-start(f32[5,2,2,128,128]{4,3,2,1,0:T(8,128)} %refs_2_.9) | copy-start | bytes 3932164
  3.1 9.7 %copy-start.6 = (s32[5,32]{1,0:T(8,128)S(1)}, s32[5,32]{1,0:T(8,128)}, u32[]{:S(2)}) copy-start(s32[5,32]{1,0:T(8,128)} %refs_3_.9) | copy-start | bytes 1924
  3.1 9.7 %copy-start.7 = (s32[5,1,32]{2,1,0:T(1,128)S(1)}, s32[5,1,32]{2,1,0:T(1,128)}, u32[]{:S(2)}) copy-start(s32[5,1,32]{2,1,0:T(1,128)} %refs_4_.9) | copy-start | bytes 1924
  3.1 9.6 %collective-permute-start = (f32[32,16,128]{2,1,0:T(8,128)S(1)}, f32[32,16,128]{2,1,0:T(8,128)S(1)}, u32[]{:S(2)}, u32[]{:S(2)}) collective-permute-start(f32[32,16,128]{2,1,0:T(8,128)S(1)} %shard_map.94.refs_0_), channel_id=1, source_target_pairs={{0,128},{32,160},{64,192},{96,224},{128,0},{160,32},{192,64},{224,... | collective-permute-start | bytes 786440 | tf_op jit(solution)/shard_map/ppermute | solution.py:361
  10.5 49.7 %copy-start.1 = (bf16[256,4096]{1,0:T(8,128)(2,1)}, bf16[256,4096]{1,0:T(8,128)(2,1)S(1)}, u32[]{:S(2)}) copy-start(bf16[256,4096]{1,0:T(8,128)(2,1)S(1)} %get-tuple-element.14.refs_8_.refs_4_) | copy-start | bytes 6291460
  10.5 49.7 %copy-start.3 = (bf16[256,4096]{1,0:T(8,128)(2,1)}, bf16[256,4096]{1,0:T(8,128)(2,1)S(1)}, u32[]{:S(2)}) copy-start(bf16[256,4096]{1,0:T(8,128)(2,1)S(1)} %get-tuple-element.15.refs_9_.refs_5_) | copy-start | bytes 6291460
  10.5 1.3 %collective-permute-start.1 = (f32[128,128]{1,0:T(8,128)S(1)}, f32[128,128]{1,0:T(8,128)S(1)}, u32[]{:S(2)}, u32[]{:S(2)}) collective-permute-start(f32[128,128]{1,0:T(8,128)S(1)} %get-tuple-element.12), channel_id=1, source_target_pairs={{0,32},{32,0},{64,96},{96,64},{128,160},{160,128},{192,224},{224,1... | collective-permute-start | bytes 196616 | tf_op jit(solution)/shard_map/ppermute | solution.py:361
  13.3 7.6 %collective-permute-start.2 = (f32[32,16,128]{2,1,0:T(8,128)S(1)}, f32[32,16,128]{2,1,0:T(8,128)S(1)}, u32[]{:S(2)}, u32[]{:S(2)}) collective-permute-start(f32[32,16,128]{2,1,0:T(8,128)S(1)} %shard_map.96.refs_0_), channel_id=1, source_target_pairs={{0,64},{32,96},{64,0},{96,32},{128,192},{160,224},{192,128},{224,1... | collective-permute-start | bytes 786440 | tf_op jit(solution)/shard_map/ppermute | solution.py:361
  14.9 5.8 %collective-permute-start.3 = (f32[128,128]{1,0:T(8,128)S(1)}, f32[128,128]{1,0:T(8,128)S(1)}, u32[]{:S(2)}, u32[]{:S(2)}) collective-permute-start(f32[128,128]{1,0:T(8,128)S(1)} %add.18.refs_5_), channel_id=1, source_target_pairs={{0,16},{1,17},{2,18},{3,19},{4,20},{5,21},{6,22},{7,23},{8,24},{9,... | collective-permute-start | bytes 196616 | tf_op jit(solution)/shard_map/ppermute | solution.py:361
  21.3 8.2 %collective-permute-start.4 = (f32[32,16,128]{2,1,0:T(8,128)S(1)}, f32[32,16,128]{2,1,0:T(8,128)S(1)}, u32[]{:S(2)}, u32[]{:S(2)}) collective-permute-start(f32[32,16,128]{2,1,0:T(8,128)S(1)} %shard_map.97.refs_0_), channel_id=1, source_target_pairs={{0,16},{1,17},{2,18},{3,19},{4,20},{5,21},{6,22},{7,23},{8,24},{9,... | collective-permute-start | bytes 786440 | tf_op jit(solution)/shard_map/ppermute | solution.py:361
  23.5 5.8 %collective-permute-start.5 = (f32[128,128]{1,0:T(8,128)S(1)}, f32[128,128]{1,0:T(8,128)S(1)}, u32[]{:S(2)}, u32[]{:S(2)}) collective-permute-start(f32[128,128]{1,0:T(8,128)S(1)} %add.19.refs_5_), channel_id=1, source_target_pairs={{0,2},{1,3},{2,0},{3,1},{4,6},{5,7},{6,4},{7,5},{8,10},{9,11},{10,... | collective-permute-start | bytes 196616 | tf_op jit(solution)/shard_map/ppermute | solution.py:361
  29.9 30.3 %copy-start.5 = (bf16[2,32,128,128]{3,2,1,0:T(8,128)(2,1)S(1)}, bf16[2,32,128,128]{3,2,1,0:T(8,128)(2,1)}, u32[]{:S(2)}) copy-start(bf16[2,32,128,128]{3,2,1,0:T(8,128)(2,1)} %refs_6_.1) | copy-start | bytes 6291460
  29.9 7.2 %collective-permute-start.6 = (f32[32,16,128]{2,1,0:T(8,128)S(1)}, f32[32,16,128]{2,1,0:T(8,128)S(1)}, u32[]{:S(2)}, u32[]{:S(2)}) collective-permute-start(f32[32,16,128]{2,1,0:T(8,128)S(1)} %shard_map.99.refs_0_), channel_id=1, source_target_pairs={{0,8},{1,9},{2,10},{3,11},{4,12},{5,13},{6,14},{7,15},{8,0},{9,1},... | collective-permute-start | bytes 786440 | tf_op jit(solution)/shard_map/ppermute | solution.py:361
  31.3 5.8 %collective-permute-start.7 = (f32[128,128]{1,0:T(8,128)S(1)}, f32[128,128]{1,0:T(8,128)S(1)}, u32[]{:S(2)}, u32[]{:S(2)}) collective-permute-start(f32[128,128]{1,0:T(8,128)S(1)} %add.20.refs_5_), channel_id=1, source_target_pairs={{0,128},{32,160},{64,192},{96,224},{128,0},{160,32},{192,64},{224,... | collective-permute-start | bytes 196616 | tf_op jit(solution)/shard_map/ppermute | solution.py:361
  37.6 21.3 %collective-permute-start.8 = (f32[32,16,128]{2,1,0:T(8,128)S(1)}, f32[32,16,128]{2,1,0:T(8,128)S(1)}, u32[]{:S(2)}, u32[]{:S(2)}) collective-permute-start(f32[32,16,128]{2,1,0:T(8,128)S(1)} %shard_map.100.refs_0_), channel_id=1, source_target_pairs={{0,4},{1,5},{2,6},{3,7},{4,0},{5,1},{6,2},{7,3},{8,12},{9,13},{10,... | collective-permute-start | bytes 786440 | tf_op jit(solution)/shard_map/ppermute | solution.py:361
  44.9 8.7 %collective-permute-start.9 = (f32[128,128]{1,0:T(8,128)S(1)}, f32[128,128]{1,0:T(8,128)S(1)}, u32[]{:S(2)}, u32[]{:S(2)}) collective-permute-start(f32[128,128]{1,0:T(8,128)S(1)} %add.21.refs_5_), channel_id=1, source_target_pairs={{0,4},{1,5},{2,6},{3,7},{4,0},{5,1},{6,2},{7,3},{8,12},{9,13},{10,... | collective-permute-start | bytes 196616 | tf_op jit(solution)/shard_map/ppermute | solution.py:361
  53.6 5.3 %collective-permute-start.10 = (f32[128,128]{1,0:T(8,128)S(1)}, f32[128,128]{1,0:T(8,128)S(1)}, u32[]{:S(2)}, u32[]{:S(2)}) collective-permute-start(f32[128,128]{1,0:T(8,128)S(1)} %add.22.left_ref), channel_id=1, source_target_pairs={{0,1},{1,0},{2,3},{3,2},{4,5},{5,4},{6,7},{7,6},{8,9},{9,8},{10,11... | collective-permute-start | bytes 196616 | tf_op jit(solution)/shard_map/ppermute | solution.py:361
  58.9 5.7 %collective-permute-start.11 = (f32[128,128]{1,0:T(8,128)S(1)}, f32[128,128]{1,0:T(8,128)S(1)}, u32[]{:S(2)}, u32[]{:S(2)}) collective-permute-start(f32[128,128]{1,0:T(8,128)S(1)} %shard_map.101.refs_10_.left_ref), channel_id=1, source_target_pairs={{0,8},{1,9},{2,10},{3,11},{4,12},{5,13},{6,14},{7,15},{8,0},{9,1},... | collective-permute-start | bytes 196616 | tf_op jit(solution)/shard_map/ppermute | solution.py:361
  64.6 5.1 %collective-permute-start.12 = (f32[128,128]{1,0:T(8,128)S(1)}, f32[128,128]{1,0:T(8,128)S(1)}, u32[]{:S(2)}, u32[]{:S(2)}) collective-permute-start(f32[128,128]{1,0:T(8,128)S(1)} %shard_map.103), channel_id=1, source_target_pairs={{0,64},{32,96},{64,0},{96,32},{128,192},{160,224},{192,128},{224,1... | collective-permute-start | bytes 196616 | tf_op jit(solution)/shard_map/ppermute | solution.py:361
  65.5 9.8 %all-to-all-start = ((f32[8,17,1,128]{3,2,1,0:T(1,128)}), f32[8,17,1,128]{3,2,1,0:T(1,128)S(1)}, u32[]{:S(2)}, u32[]{:S(2)}) async-start(f32[8,17,1,128]{3,2,1,0:T(1,128)} %get-tuple-element.16), calls=%async_computation | async-start | bytes 139264 | tf_op jit(solution)/shard_map/all_to_all | solution.py:405
  97.7 1.6 %copy-start.2 = (bf16[256,4096]{1,0:T(8,128)(2,1)S(1)}, bf16[256,4096]{1,0:T(8,128)(2,1)}, u32[]{:S(2)}) copy-start(bf16[256,4096]{1,0:T(8,128)(2,1)} %copy-done.1) | copy-start | bytes 6291460
  99.3 1.6 %copy-start.4 = (bf16[256,4096]{1,0:T(8,128)(2,1)S(1)}, bf16[256,4096]{1,0:T(8,128)(2,1)}, u32[]{:S(2)}) copy-start(bf16[256,4096]{1,0:T(8,128)(2,1)} %copy-done.3) | copy-start | bytes 6291460

commit v3 on v2

--- a/solution.py
+++ b/solution.py
@@ -3,6 +3,7 @@
 from jax import lax
 from jax.experimental import pallas as pl
 from jax.experimental.pallas import tpu as pltpu
+from jax.sharding import Mesh
 from jax.sharding import PartitionSpec as P
 
 NT = (((1,), (1,)), ((), ()))
@@ -10,6 +11,7 @@
 KERNEL_VMEM = 24 * 1024 * 1024
 VMEM = pl.BlockSpec(memory_space=pltpu.VMEM)
 BASIS_PARTS = 4
+AXES = ("y", "core", "x", "z")
 
 
 def in_hbm(value):
@@ -50,7 +52,9 @@
     )
 
 
-def leaves_kernel(basis_ref, leaf_ref, out_ref, newest_ref, held_ref, newest_sem, held_sems):
+def leaves_in_kernel(
+    basis_ref, leaf_ref, out_ref, rows_ref, newest_ref, held_ref, newest_sem, held_sems
+):
     steps = held_sems.shape[0]
     count = held_ref.shape[1]
     part = count // steps
@@ -71,16 +75,18 @@
             copies[leaf // part].wait()
         rows = newest_ref[:, :, leaf * 128 : (leaf + 1) * 128].reshape(16, 128)
         rows = rows.astype(jnp.bfloat16).astype(jnp.float32)
+        rows_ref[leaf] = rows
         out_ref[leaf] = leaf_product(rows, held_ref[0, leaf], held_ref[1, leaf])
 
 
-def apply_leaves(krylov_basis, leaves, steps):
+def leaves_in(krylov_basis, leaves, steps):
     count = leaves.shape[1]
-    return pl.pallas_call(
-        leaves_kernel,
+    rows = jax.ShapeDtypeStruct((count, 16, 128), jnp.float32)
+    return pl.pallas_call(
+        leaves_in_kernel,
         in_specs=[pl.BlockSpec(memory_space=pltpu.HBM)] * 2,
-        out_specs=pl.BlockSpec(memory_space=pltpu.VMEM),
-        out_shape=jax.ShapeDtypeStruct((count, 16, 128), jnp.float32),
+        out_specs=[VMEM] * 2,
+        out_shape=[rows, rows],
         scratch_shapes=[
             pltpu.VMEM(krylov_basis.shape[1:], jnp.float32),
             pltpu.VMEM(leaves.shape, leaves.dtype),
@@ -92,6 +98,24 @@
             flops=count * 16 * 256 * 128 * 2, bytes_accessed=count * 73728, transcendentals=0
         ),
     )(in_hbm(krylov_basis), in_hbm(leaves))
+
+
+def near_kernel(rows_ref, leaf_ref, out_ref):
+    for leaf in range(rows_ref.shape[0]):
+        out_ref[leaf] = leaf_product(rows_ref[leaf], leaf_ref[0, leaf], leaf_ref[1, leaf])
+
+
+def near_product(rows, near_field):
+    return pl.pallas_call(
+        near_kernel,
+        in_specs=[VMEM] * 2,
+        out_specs=VMEM,
+        out_shape=jax.ShapeDtypeStruct(rows.shape, jnp.float32),
+        compiler_params=pltpu.CompilerParams(vmem_limit_bytes=KERNEL_VMEM),
+        cost_estimate=pl.CostEstimate(
+            flops=rows.shape[0] * 16 * 256 * 128 * 2, bytes_accessed=2 << 20, transcendentals=0
+        ),
+    )(rows, near_field)
 
 
 def stacked(basis):
@@ -223,11 +247,8 @@
     )
     real = square[:8, :8] + square[8:, 8:]
     imag = square[:8, 8:] - square[8:, :8]
-    pieces = [real[row : row + 1] for row in range(8)] + [imag[row : row + 1] for row in range(8)]
-    last = jnp.concatenate(pieces, axis=1)
-    for device in range(8):
-        sums_ref[device, 0:16, 0] = first
-        sums_ref[device, 16] = last
+    sums_ref[0:16] = first
+    sums_ref[16:24] = jnp.concatenate([real, imag, jnp.zeros((8, 112), jnp.float32)], axis=1)
 
 
 def project(
@@ -239,29 +260,13 @@
         out_specs=[VMEM] * 2,
         out_shape=[
             jax.ShapeDtypeStruct((16, 4096), jnp.float32),
-            jax.ShapeDtypeStruct((8, 17, 1, 128), jnp.float32),
+            jax.ShapeDtypeStruct((24, 128), jnp.float32),
         ],
         compiler_params=pltpu.CompilerParams(vmem_limit_bytes=KERNEL_VMEM),
         cost_estimate=pl.CostEstimate(
             flops=6 * 512 * 256 * 256 * 2, bytes_accessed=8 << 20, transcendentals=0
         ),
     )(own, partner, level_mixers, block_ranks, partner_tables, close, leaf_out, *parts, before)
-
-
-def relay_kernel(got_ref, before_ref, out_ref):
-    sums = jnp.sum(got_ref[...], axis=0)
-    for device in range(32):
-        out_ref[device] = sums
-
-
-def relay(got, before):
-    return pl.pallas_call(
-        relay_kernel,
-        in_specs=[VMEM, pl.BlockSpec(memory_space=pl.ANY)],
-        out_specs=VMEM,
-        out_shape=jax.ShapeDtypeStruct((32, 17, 1, 128), jnp.float32),
-        compiler_params=pltpu.CompilerParams(vmem_limit_bytes=KERNEL_VMEM),
-    )(got, before)
 
 
 def dot_high(left, right, numbers):
@@ -273,10 +278,7 @@
 def finish_kernel(
     scale, got_ref, gram_ref, image_ref, high_ref, middle_ref, low_ref, total_ref, new_ref, block_ref
 ):
-    sums = jnp.concatenate(
-        [jnp.sum(got_ref[:, row, 0], axis=0, keepdims=True) for row in range(17)], axis=0
-    )
-    sums = sums * scale
+    sums = jnp.sum(got_ref[...], axis=0) * scale
     first = sums[:16]
     packed = gram_ref[...] * scale
     row = lax.broadcasted_iota(jnp.int32, (128, 128), 0)
@@ -301,11 +303,8 @@
 
     one_real, one_imag = inner(first, total)
     two_real, two_imag = inner(total, rest)
-    taken_real, taken_imag = one_real + two_real, one_imag + two_imag
-    for angle in range(8):
-        at = angle * 8
-        block_ref[0, angle] = sums[16, at : at + 8] - taken_real[angle]
-        block_ref[1, angle] = sums[16, 64 + at : 72 + at] - taken_imag[angle]
+    block_ref[0] = sums[16:24, 0:8] - one_real - two_real
+    block_ref[1] = sums[16:24, 8:16] - one_imag - two_imag
     high, middle, low = split3(complex_rows(total))
     three = jnp.concatenate([high, middle, low], axis=0)
     two = three[:32]
@@ -361,68 +360,54 @@
     return lax.ppermute(value, axis, pairs)
 
 
+def sum_of_all(value, axes):
+    copies = jnp.broadcast_to(value[None], (lax.axis_size(axes),) + value.shape)
+    return jnp.sum(lax.all_to_all(copies, axes, 0, 0), axis=0)
+
+
 def per_device(
     krylov_basis, near_field, leaf_in, leaf_out, level_mixers, block_ranks, partner_tables
 ):
-    src_bits = lax.axis_size("src").bit_length() - 1
-    obs_bits = lax.axis_size("obs").bit_length() - 1
-    plan = [
-        ("src", src_bits - 1),
-        ("src", src_bits - 2),
-        ("obs", obs_bits - 1),
-        ("obs", obs_bits - 2),
-        ("obs", obs_bits - 3),
-    ]
-    coeffs = apply_leaves(krylov_basis, leaf_in, 4)
-    close = apply_leaves(krylov_basis, near_field, 4)
+    plan = [("y", 1), ("y", 0), ("x", 1), ("x", 0), ("z", 2)]
+    beside = [[("core", 0)], [("z", 1)], [("z", 2)], [("y", 1)], [("x", 1), ("x", 0), ("y", 0)]]
+    coeffs, rows = leaves_in(krylov_basis, leaf_in, 4)
     gram, parts = basis_gram(krylov_basis)
-    beside = [
-        [("src", 0)],
-        [("obs", obs_bits - 1)],
-        [("obs", 1)],
-        [("src", src_bits - 1)],
-        [("obs", 2), ("obs", 0)],
-        [("obs", obs_bits - 2)],
-        [("src", 1)],
-    ]
-
-    def sum_on(gram, step, before=None):
-        for axis, bit in beside[step][:-1]:
-            gram = gram + exchange(gram, axis, bit)
-        got = exchange(gram, *beside[step][-1])
-        return gram + got if before is None else add_after(gram, got, before)
-
+    close = near_product(rows, near_field)
     for level, (axis, bit) in enumerate(plan):
         partner = exchange(coeffs, axis, bit)
+        for gram_axis, gram_bit in beside[level][:-1]:
+            gram = gram + exchange(gram, gram_axis, gram_bit)
+        got = exchange(gram, *beside[level][-1])
         operands = (level, coeffs, partner, level_mixers, block_ranks, partner_tables)
         if level < len(plan) - 1:
-            gram = sum_on(gram, level)
-            coeffs = next_level(*operands, [gram, close] if level == 2 else [gram])
+            gram = gram + got
+            coeffs = next_level(*operands, [gram, close] if level == 1 else [gram])
         else:
-            gram = sum_on(gram, level, partner)
+            gram = add_after(gram, got, partner)
             image, sums = project(*operands, close, leaf_out, parts, gram)
-    gram = sum_on(gram, 5, image)
-    got = lax.all_to_all(sums, "src", 0, 0)
-    gram = sum_on(gram, 6)
-    got = relay(got, gram)
-    got = lax.all_to_all(got, "obs", 0, 0)
-    devices = lax.axis_size("src") * lax.axis_size("obs")
+    gram = add_after(gram, exchange(gram, "z", 0), image)
+    sums = add_after(sums, exchange(sums, "core", 0), gram)
+    sums = sum_of_all(sums, ("y", "x"))
+    copies = jnp.broadcast_to(sums[None], (lax.axis_size("z"),) + sums.shape)
+    got = lax.all_to_all(copies, "z", 0, 0)
+    devices = lax.axis_size(AXES)
     scale = 1.0 / (krylov_basis.shape[3] * devices)
     total, new_block, block_gram = finish(scale, got, gram, image, parts)
     return jnp.transpose(total, (3, 0, 1, 2)), new_block, block_gram
 
 
 def solution(mesh):
+    mesh = Mesh(mesh.devices.reshape(4, 2, 4, 8), AXES)
     in_specs = (
-        P(None, None, None, ("src", "obs")),
-        P(None, ("src", "obs"), None, None),
-        P(None, ("src", "obs"), None, None),
-        P(None, ("src", "obs"), None, None),
-        P(None, None, None, None, ("src", "obs")),
-        P(None, ("src", "obs")),
-        P(None, ("src", "obs"), None),
-    )
-    out_specs = (P(), P(None, None, ("src", "obs")), P())
+        P(None, None, None, AXES),
+        P(None, AXES, None, None),
+        P(None, AXES, None, None),
+        P(None, AXES, None, None),
+        P(None, None, None, None, AXES),
+        P(None, AXES),
+        P(None, AXES, None),
+    )
+    out_specs = (P(), P(None, None, AXES), P())
     return jax.shard_map(
         per_device, mesh=mesh, in_specs=in_specs, out_specs=out_specs, check_vma=False
     )

time: 104 us -> 98.4 us (0.946)
  waiting for transfers between devices: 25.4 us -> 21.5 us
  Pallas kernels: 17.8 us -> 15 us
  blocking collectives: 22.3 us -> 24.7 us
    all_to_all x1 -> x0, waiting for transfers between devices: 5.62 us -> none  [per_device(): got = lax.all_to_all(sums, 'src', 0, 0)]
    all_to_all x1 -> x0, starting transfers between devices: 4.16 us -> none  [per_device(): got = lax.all_to_all(sums, 'src', 0, 0)]
    ppermute x13 -> x14, starting transfers between devices: 29.6 us -> 32.8 us  [exchange(): return lax.ppermute(value, axis, pairs)]
    all_to_all x1 -> x2, blocking collectives: 22.3 us -> 24.7 us  [the longest x1 13 us: sum_of_all(): return jnp.sum(lax.all_to_all(copies, axes, 0, 0), axis=0)]
    pallas_call x3 -> x2, Pallas kernels: 5.1 us -> 3.12 us  [the longest x1 2.48 us: leaves_in(): pl.pallas_call(leaves_in_kernel, in_specs=[pl.BlockSpec(memory_space=pltp...]
    ppermute x13 -> x14, waiting for transfers between devices: 19.8 us -> 21.5 us  [exchange(): return lax.ppermute(value, axis, pairs)]
    unnamed x16 -> x18, local copies, waits for them, and re-layouts: 3.22 us -> 3.22 us
  transfers between devices with their start and end apart: 14 -> 14, of which waited for: 9 -> 10; matrix products, arithmetic and copies ran while one was open for 0% -> 0% of each run, Pallas kernels for 11% -> 8%
where the time goes in v3:
time: 98.4 us; the launch traced here: 98.2 us
  starting transfers between devices  32.8 us (33%)
  blocking collectives  24.7 us (25%)
  waiting for transfers between devices  21.5 us (22%)
  Pallas kernels  15 us (15%)
  local copies, waits for them, and re-layouts  3.25 us (3%)
    ppermute x14, starting transfers between devices, exchange(): return lax.ppermute(value, axis, pairs)  32.8 us
    ppermute x14, waiting for transfers between devices, exchange(): return lax.ppermute(value, axis, pairs)  21.5 us
    all_to_all x1, blocking collectives, sum_of_all(): return jnp.sum(lax.all_to_all(copies, axes, 0, 0), axis=0)  13 us
    all_to_all x1, blocking collectives, per_device(): got = lax.all_to_all(copies, 'z', 0, 0)  11.7 us
    pallas_call x1, Pallas kernels, basis_gram(): pl.pallas_call(basis_gram_kernel, in_specs=[pl.BlockSpec(memory_space=plt...  4.05 us
    pallas_call x1, Pallas kernels, project(): pl.pallas_call(lambda *refs: project_kernel(level, *refs), in_specs=[VMEM...  3.63 us
    unnamed x18, local copies, waits for them, and re-layouts  3.22 us
    pallas_call x1, Pallas kernels, leaves_in(): pl.pallas_call(leaves_in_kernel, in_specs=[pl.BlockSpec(memory_space=pltp...  2.48 us
  transfers between devices with their start and end apart: 14, of which 10 were waited for; matrix products, arithmetic and copies ran while one was open for 0% of the time, Pallas kernels for 8%

profile of v3, /device:TPU:2, one launch (start us, length us, event | category | flops | bytes accessed | tf_op | source)
XLA Modules:
  0.0 98.2 jit_solution(12073868208843956602)
XLA Ops:
  0.6 2.5 %shard_map.94 = (f32[32,16,128]{2,1,0:T(8,128)S(1)}, f32[32,16,128]{2,1,0:T(8,128)S(1)}) custom-call(f32[16,2,8,4096]{3,2,1,0:T(8,128)} %basis_ref.3, bf16[2,32,128,128]{3,2,1,0:T(8,128)(2,1)} %leaf_ref.2), custom_call_target="tpu_custom_call" | custom-call | flops 33554432 | bytes 2359296 | tf_op jit(solution)/shard_map/pallas_call | solution.py:85
  3.1 0.0 copy-start
  3.1 0.0 copy-start.7
  3.1 0.0 copy-start.8
  3.2 3.3 %collective-permute-start = (f32[32,16,128]{2,1,0:T(8,128)S(1)}, f32[32,16,128]{2,1,0:T(8,128)S(1)}, u32[]{:S(2)}, u32[]{:S(2)}) collective-permute-start(f32[32,16,128]{2,1,0:T(8,128)S(1)} %get-tuple-element.14.refs_0_), channel_id=1, source_target_pairs={{0,128},{64,192},{128,0},{192,64},{1,129},{65,193},{129,1},{193,65... | collective-permute-start | bytes 786440 | tf_op jit(solution)/shard_map/ppermute | solution.py:360
  6.4 4.0 %shard_map.95 = (f32[128,128]{1,0:T(8,128)S(1)}, bf16[256,4096]{1,0:T(8,128)(2,1)S(1)}, bf16[256,4096]{1,0:T(8,128)(2,1)S(1)}, bf16[256,4096]{1,0:T(8,128)(2,1)S(1)}) custom-call(f32[16,2,8,4096]{3,2,1,0:T(8,128)} %basis_ref.3), custom_call_target="tpu_custom_call" | custom-call | flops 2147483648 | bytes 10485760 | tf_op jit(solution)/shard_map/pallas_call | solution.py:161
  10.5 0.0 copy-start.5
  10.5 0.1 collective-permute-start.1
  10.6 1.2 %collective-permute-done.1 = f32[128,128]{1,0:T(8,128)S(1)} collective-permute-done((f32[128,128]{1,0:T(8,128)S(1)}, f32[128,128]{1,0:T(8,128)S(1)}, u32[]{:S(2)}, u32[]{:S(2)}) %collective-permute-start.1) | collective-permute-done | bytes 65568 | tf_op jit(solution)/shard_map/ppermute | solution.py:360
  11.9 0.9 collective-permute-done.refs_1_
  12.8 0.0 copy-done
  12.8 0.5 shard_map.96.refs_0_
  13.3 1.7 %collective-permute-start.2 = (f32[32,16,128]{2,1,0:T(8,128)S(1)}, f32[32,16,128]{2,1,0:T(8,128)S(1)}, u32[]{:S(2)}, u32[]{:S(2)}) collective-permute-start(f32[32,16,128]{2,1,0:T(8,128)S(1)} %shard_map.96.refs_0_), channel_id=1, source_target_pairs={{0,64},{64,0},{128,192},{192,128},{1,65},{65,1},{129,193},{193,129... | collective-permute-start | bytes 786440 | tf_op jit(solution)/shard_map/ppermute | solution.py:360
  14.9 3.3 %collective-permute-start.3 = (f32[128,128]{1,0:T(8,128)S(1)}, f32[128,128]{1,0:T(8,128)S(1)}, u32[]{:S(2)}, u32[]{:S(2)}) collective-permute-start(f32[128,128]{1,0:T(8,128)S(1)} %add.18.refs_5_), channel_id=1, source_target_pairs={{0,2},{1,3},{2,0},{3,1},{4,6},{5,7},{6,4},{7,5},{8,10},{9,11},{10,... | collective-permute-start | bytes 196616 | tf_op jit(solution)/shard_map/ppermute | solution.py:360
  18.2 0.6 shard_map.97.refs_6_.refs_5_
  18.9 1.6 %collective-permute-done.3 = f32[128,128]{1,0:T(8,128)S(1)} collective-permute-done((f32[128,128]{1,0:T(8,128)S(1)}, f32[128,128]{1,0:T(8,128)S(1)}, u32[]{:S(2)}, u32[]{:S(2)}) %collective-permute-start.3) | collective-permute-done | bytes 65568 | tf_op jit(solution)/shard_map/ppermute | solution.py:360
  20.5 0.3 collective-permute-done.2.refs_1_
  20.8 0.5 shard_map.98.refs_0_
  21.3 2.2 %collective-permute-start.4 = (f32[32,16,128]{2,1,0:T(8,128)S(1)}, f32[32,16,128]{2,1,0:T(8,128)S(1)}, u32[]{:S(2)}, u32[]{:S(2)}) collective-permute-start(f32[32,16,128]{2,1,0:T(8,128)S(1)} %shard_map.98.refs_0_), channel_id=1, source_target_pairs={{0,16},{8,24},{16,0},{24,8},{1,17},{9,25},{17,1},{25,9},{2,18},{10... | collective-permute-start | bytes 786440 | tf_op jit(solution)/shard_map/ppermute | solution.py:360
  23.5 7.2 %collective-permute-start.5 = (f32[128,128]{1,0:T(8,128)S(1)}, f32[128,128]{1,0:T(8,128)S(1)}, u32[]{:S(2)}, u32[]{:S(2)}) collective-permute-start(f32[128,128]{1,0:T(8,128)S(1)} %add.19.refs_5_), channel_id=1, source_target_pairs={{0,4},{1,5},{2,6},{3,7},{4,0},{5,1},{6,2},{7,3},{8,12},{9,13},{10,... | collective-permute-start | bytes 196616 | tf_op jit(solution)/shard_map/ppermute | solution.py:360
  30.7 2.3 %collective-permute-done.5 = f32[128,128]{1,0:T(8,128)S(1)} collective-permute-done((f32[128,128]{1,0:T(8,128)S(1)}, f32[128,128]{1,0:T(8,128)S(1)}, u32[]{:S(2)}, u32[]{:S(2)}) %collective-permute-start.5) | collective-permute-done | bytes 65568 | tf_op jit(solution)/shard_map/ppermute | solution.py:360
  33.1 0.0 collective-permute-done.4.refs_1_
  33.1 0.5 shard_map.99.refs_0_
  33.5 0.0 copy-start.6
  33.6 1.5 %collective-permute-start.6 = (f32[32,16,128]{2,1,0:T(8,128)S(1)}, f32[32,16,128]{2,1,0:T(8,128)S(1)}, u32[]{:S(2)}, u32[]{:S(2)}) collective-permute-start(f32[32,16,128]{2,1,0:T(8,128)S(1)} %shard_map.99.refs_0_), channel_id=1, source_target_pairs={{0,8},{8,0},{16,24},{24,16},{1,9},{9,1},{17,25},{25,17},{2,10},{10... | collective-permute-start | bytes 786440 | tf_op jit(solution)/shard_map/ppermute | solution.py:360
  35.1 2.9 %collective-permute-start.7 = (f32[128,128]{1,0:T(8,128)S(1)}, f32[128,128]{1,0:T(8,128)S(1)}, u32[]{:S(2)}, u32[]{:S(2)}) collective-permute-start(f32[128,128]{1,0:T(8,128)S(1)} %add.20.refs_5_), channel_id=1, source_target_pairs={{0,128},{64,192},{128,0},{192,64},{1,129},{65,193},{129,1},{193,65... | collective-permute-start | bytes 196616 | tf_op jit(solution)/shard_map/ppermute | solution.py:360
  38.0 2.9 %collective-permute-done.7 = f32[128,128]{1,0:T(8,128)S(1)} collective-permute-done((f32[128,128]{1,0:T(8,128)S(1)}, f32[128,128]{1,0:T(8,128)S(1)}, u32[]{:S(2)}, u32[]{:S(2)}) %collective-permute-start.7) | collective-permute-done | bytes 65568 | tf_op jit(solution)/shard_map/ppermute | solution.py:360
  40.9 0.0 collective-permute-done.6.refs_1_
  40.9 0.5 shard_map.100.refs_0_
  41.3 6.2 %collective-permute-start.8 = (f32[32,16,128]{2,1,0:T(8,128)S(1)}, f32[32,16,128]{2,1,0:T(8,128)S(1)}, u32[]{:S(2)}, u32[]{:S(2)}) collective-permute-start(f32[32,16,128]{2,1,0:T(8,128)S(1)} %shard_map.100.refs_0_), channel_id=1, source_target_pairs={{0,4},{1,5},{2,6},{3,7},{4,0},{5,1},{6,2},{7,3},{8,12},{9,13},{10,... | collective-permute-start | bytes 786440 | tf_op jit(solution)/shard_map/ppermute | solution.py:360
  47.5 0.8 collective-permute-start.9
  48.3 5.0 %collective-permute-done.9 = f32[128,128]{1,0:T(8,128)S(1)} collective-permute-done((f32[128,128]{1,0:T(8,128)S(1)}, f32[128,128]{1,0:T(8,128)S(1)}, u32[]{:S(2)}, u32[]{:S(2)}) %collective-permute-start.9) | collective-permute-done | bytes 65568 | tf_op jit(solution)/shard_map/ppermute | solution.py:360
  53.3 1.4 %collective-permute-start.10 = (f32[128,128]{1,0:T(8,128)S(1)}, f32[128,128]{1,0:T(8,128)S(1)}, u32[]{:S(2)}, u32[]{:S(2)}) collective-permute-start(f32[128,128]{1,0:T(8,128)S(1)} %add.22), channel_id=1, source_target_pairs={{0,8},{8,0},{16,24},{24,16},{1,9},{9,1},{17,25},{25,17},{2,10},{10... | collective-permute-start | bytes 196616 | tf_op jit(solution)/shard_map/ppermute | solution.py:360
  54.6 3.0 %collective-permute-done.10 = f32[128,128]{1,0:T(8,128)S(1)} collective-permute-done((f32[128,128]{1,0:T(8,128)S(1)}, f32[128,128]{1,0:T(8,128)S(1)}, u32[]{:S(2)}, u32[]{:S(2)}) %collective-permute-start.10) | collective-permute-done | bytes 65568 | tf_op jit(solution)/shard_map/ppermute | solution.py:360
  57.7 1.3 %collective-permute-start.11 = (f32[128,128]{1,0:T(8,128)S(1)}, f32[128,128]{1,0:T(8,128)S(1)}, u32[]{:S(2)}, u32[]{:S(2)}) collective-permute-start(f32[128,128]{1,0:T(8,128)S(1)} %add.23.left_ref), channel_id=1, source_target_pairs={{0,64},{64,0},{128,192},{192,128},{1,65},{65,1},{129,193},{193,129... | collective-permute-start | bytes 196616 | tf_op jit(solution)/shard_map/ppermute | solution.py:360
  59.0 3.0 %collective-permute-done.11.right_ref = f32[128,128]{1,0:T(8,128)S(1)} collective-permute-done((f32[128,128]{1,0:T(8,128)S(1)}, f32[128,128]{1,0:T(8,128)S(1)}, u32[]{:S(2)}, u32[]{:S(2)}) %collective-permute-start.11) | collective-permute-done | bytes 65568 | tf_op jit(solution)/shard_map/ppermute | solution.py:360
  62.0 0.0 collective-permute-done.8.before_ref.refs_1_
  62.0 1.0 %collective-permute-start.13 = (f32[128,128]{1,0:T(8,128)S(1)}, f32[128,128]{1,0:T(8,128)S(1)}, u32[]{:S(2)}, u32[]{:S(2)}) collective-permute-start(f32[128,128]{1,0:T(8,128)S(1)} %shard_map.101.refs_10_.left_ref), channel_id=1, source_target_pairs={{0,1},{1,0},{2,3},{3,2},{4,5},{5,4},{6,7},{7,6},{8,9},{9,8},{10,11... | collective-permute-start | bytes 196616 | tf_op jit(solution)/shard_map/ppermute | solution.py:360
  63.1 0.0 copy-done.3
  63.1 3.6 %shard_map.102 = (f32[16,4096]{1,0:T(8,128)S(1)}, f32[24,128]{1,0:T(8,128)S(1)}) custom-call(f32[32,16,128]{2,1,0:T(8,128)S(1)} %shard_map.100.refs_0_, f32[32,16,128]{2,1,0:T(8,128)S(1)} %collective-permute-done.8.before_ref.refs_1_, f32[5,2,2,128,128]{4,3,2,1,0:T(8,128)S(1)} %copy-done, s32[5,32]{1,0:T(8,128)S(1)} %copy-done.7, s32[5,1,32]{2,1,0:T(1,128)S(1)} %copy-done.8, ...), custom_call_target="tpu_custom_call" | custom-call | flops 402653184 | bytes 8388608 | tf_op jit(solution)/shard_map/pallas_call | solution.py:257
  66.7 0.0 collective-permute-start.12
  66.7 0.0 collective-permute-done.13.right_ref
  66.8 1.2 %collective-permute-done.12.right_ref = f32[24,128]{1,0:T(8,128)S(1)} collective-permute-done((f32[24,128]{1,0:T(8,128)S(1)}, f32[24,128]{1,0:T(8,128)S(1)}, u32[]{:S(2)}, u32[]{:S(2)}) %collective-permute-start.12) | collective-permute-done | bytes 12320 | tf_op jit(solution)/shard_map/ppermute | solution.py:360
  67.9 13.0 %all_to_all.10 = f32[16,24,128]{2,1,0:T(8,128)S(1)} all-to-all(f32[16,24,128]{2,1,0:T(8,128)S(1)} %broadcast_in_dim.4), channel_id=1, replica_groups=mesh['y'=4,'core'=2,'x'=4,'z'=8] {'y','x'}, dimensions={0} | all-to-all | bytes 393216 | tf_op jit(solution)/shard_map/all_to_all | solution.py:365
  81.0 11.7 %all_to_all.11.refs_0_ = f32[8,24,128]{2,1,0:T(8,128)S(1)} all-to-all(f32[8,24,128]{2,1,0:T(8,128)S(1)} %broadcast_in_dim.5), channel_id=1, replica_groups=mesh['y'=4,'core'=2,'x'=4,'z'=8] {'z'}, dimensions={0} | all-to-all | bytes 196608 | tf_op jit(solution)/shard_map/all_to_all | solution.py:392
  92.7 1.6 %copy-done.2 = bf16[256,4096]{1,0:T(8,128)(2,1)S(1)} copy-done((bf16[256,4096]{1,0:T(8,128)(2,1)S(1)}, bf16[256,4096]{1,0:T(8,128)(2,1)}, u32[]{:S(2)}) %copy-start.2) | copy-done | bytes 2097176
  94.3 1.6 %copy-done.4 = bf16[256,4096]{1,0:T(8,128)(2,1)S(1)} copy-done((bf16[256,4096]{1,0:T(8,128)(2,1)S(1)}, bf16[256,4096]{1,0:T(8,128)(2,1)}, u32[]{:S(2)}) %copy-start.4) | copy-done | bytes 2097176
  95.9 2.3 %shard_map.105 = (f32[2,8,8,16]{3,2,1,0:T(8,128)}, f32[2,8,4096]{2,1,0:T(8,128)}, f32[2,8,8]{2,1,0:T(8,128)}) custom-call(f32[8,24,128]{2,1,0:T(8,128)S(1)} %all_to_all.11.refs_0_, f32[128,128]{1,0:T(8,128)S(1)} %shard_map.103.before_ref.refs_1_, f32[16,4096]{1,0:T(8,128)S(1)} %get-tuple-element.21.before_ref.refs_2_, ...), custom_call_target="tpu_custom_call" | custom-call | flops 201326592 | bytes 6291456 | tf_op jit(solution)/shard_map/pallas_call | solution.py:328
  (21 shorter events, 0.1 us)
Async XLA Ops:
  3.1 9.7 %copy-start = (f32[5,2,2,128,128]{4,3,2,1,0:T(8,128)S(1)}, f32[5,2,2,128,128]{4,3,2,1,0:T(8,128)}, u32[]{:S(2)}) copy-start(f32[5,2,2,128,128]{4,3,2,1,0:T(8,128)} %refs_2_.9) | copy-start | bytes 3932164
  3.1 9.7 %copy-start.7 = (s32[5,32]{1,0:T(8,128)S(1)}, s32[5,32]{1,0:T(8,128)}, u32[]{:S(2)}) copy-start(s32[5,32]{1,0:T(8,128)} %refs_3_.9) | copy-start | bytes 1924
  3.1 9.7 %copy-start.8 = (s32[5,1,32]{2,1,0:T(1,128)S(1)}, s32[5,1,32]{2,1,0:T(1,128)}, u32[]{:S(2)}) copy-start(s32[5,1,32]{2,1,0:T(1,128)} %refs_4_.9) | copy-start | bytes 1924
  3.2 9.6 %collective-permute-start = (f32[32,16,128]{2,1,0:T(8,128)S(1)}, f32[32,16,128]{2,1,0:T(8,128)S(1)}, u32[]{:S(2)}, u32[]{:S(2)}) collective-permute-start(f32[32,16,128]{2,1,0:T(8,128)S(1)} %get-tuple-element.14.refs_0_), channel_id=1, source_target_pairs={{0,128},{64,192},{128,0},{192,64},{1,129},{65,193},{129,1},{193,65... | collective-permute-start | bytes 786440 | tf_op jit(solution)/shard_map/ppermute | solution.py:360
  10.5 52.6 %copy-start.1 = (bf16[256,4096]{1,0:T(8,128)(2,1)}, bf16[256,4096]{1,0:T(8,128)(2,1)S(1)}, u32[]{:S(2)}) copy-start(bf16[256,4096]{1,0:T(8,128)(2,1)S(1)} %get-tuple-element.18.refs_8_.refs_4_) | copy-start | bytes 6291460
  10.5 52.6 %copy-start.3 = (bf16[256,4096]{1,0:T(8,128)(2,1)}, bf16[256,4096]{1,0:T(8,128)(2,1)S(1)}, u32[]{:S(2)}) copy-start(bf16[256,4096]{1,0:T(8,128)(2,1)S(1)} %get-tuple-element.19.refs_9_.refs_5_) | copy-start | bytes 6291460
  10.5 7.7 %copy-start.5 = (bf16[2,32,128,128]{3,2,1,0:T(8,128)(2,1)S(1)}, bf16[2,32,128,128]{3,2,1,0:T(8,128)(2,1)}, u32[]{:S(2)}) copy-start(bf16[2,32,128,128]{3,2,1,0:T(8,128)(2,1)} %leaf_ref.3) | copy-start | bytes 6291460
  10.5 1.3 %collective-permute-start.1 = (f32[128,128]{1,0:T(8,128)S(1)}, f32[128,128]{1,0:T(8,128)S(1)}, u32[]{:S(2)}, u32[]{:S(2)}) collective-permute-start(f32[128,128]{1,0:T(8,128)S(1)} %get-tuple-element.15), channel_id=1, source_target_pairs={{0,32},{32,0},{1,33},{33,1},{2,34},{34,2},{3,35},{35,3},{4,36},{36... | collective-permute-start | bytes 196616 | tf_op jit(solution)/shard_map/ppermute | solution.py:360
  13.3 7.6 %collective-permute-start.2 = (f32[32,16,128]{2,1,0:T(8,128)S(1)}, f32[32,16,128]{2,1,0:T(8,128)S(1)}, u32[]{:S(2)}, u32[]{:S(2)}) collective-permute-start(f32[32,16,128]{2,1,0:T(8,128)S(1)} %shard_map.96.refs_0_), channel_id=1, source_target_pairs={{0,64},{64,0},{128,192},{192,128},{1,65},{65,1},{129,193},{193,129... | collective-permute-start | bytes 786440 | tf_op jit(solution)/shard_map/ppermute | solution.py:360
  14.9 5.6 %collective-permute-start.3 = (f32[128,128]{1,0:T(8,128)S(1)}, f32[128,128]{1,0:T(8,128)S(1)}, u32[]{:S(2)}, u32[]{:S(2)}) collective-permute-start(f32[128,128]{1,0:T(8,128)S(1)} %add.18.refs_5_), channel_id=1, source_target_pairs={{0,2},{1,3},{2,0},{3,1},{4,6},{5,7},{6,4},{7,5},{8,10},{9,11},{10,... | collective-permute-start | bytes 196616 | tf_op jit(solution)/shard_map/ppermute | solution.py:360
  21.3 11.8 %collective-permute-start.4 = (f32[32,16,128]{2,1,0:T(8,128)S(1)}, f32[32,16,128]{2,1,0:T(8,128)S(1)}, u32[]{:S(2)}, u32[]{:S(2)}) collective-permute-start(f32[32,16,128]{2,1,0:T(8,128)S(1)} %shard_map.98.refs_0_), channel_id=1, source_target_pairs={{0,16},{8,24},{16,0},{24,8},{1,17},{9,25},{17,1},{25,9},{2,18},{10... | collective-permute-start | bytes 786440 | tf_op jit(solution)/shard_map/ppermute | solution.py:360
  23.5 9.5 %collective-permute-start.5 = (f32[128,128]{1,0:T(8,128)S(1)}, f32[128,128]{1,0:T(8,128)S(1)}, u32[]{:S(2)}, u32[]{:S(2)}) collective-permute-start(f32[128,128]{1,0:T(8,128)S(1)} %add.19.refs_5_), channel_id=1, source_target_pairs={{0,4},{1,5},{2,6},{3,7},{4,0},{5,1},{6,2},{7,3},{8,12},{9,13},{10,... | collective-permute-start | bytes 196616 | tf_op jit(solution)/shard_map/ppermute | solution.py:360
  33.5 29.5 %copy-start.6 = (bf16[2,32,128,128]{3,2,1,0:T(8,128)(2,1)S(1)}, bf16[2,32,128,128]{3,2,1,0:T(8,128)(2,1)}, u32[]{:S(2)}) copy-start(bf16[2,32,128,128]{3,2,1,0:T(8,128)(2,1)} %refs_6_.1) | copy-start | bytes 6291460
  33.6 7.3 %collective-permute-start.6 = (f32[32,16,128]{2,1,0:T(8,128)S(1)}, f32[32,16,128]{2,1,0:T(8,128)S(1)}, u32[]{:S(2)}, u32[]{:S(2)}) collective-permute-start(f32[32,16,128]{2,1,0:T(8,128)S(1)} %shard_map.99.refs_0_), channel_id=1, source_target_pairs={{0,8},{8,0},{16,24},{24,16},{1,9},{9,1},{17,25},{25,17},{2,10},{10... | collective-permute-start | bytes 786440 | tf_op jit(solution)/shard_map/ppermute | solution.py:360
  35.1 5.8 %collective-permute-start.7 = (f32[128,128]{1,0:T(8,128)S(1)}, f32[128,128]{1,0:T(8,128)S(1)}, u32[]{:S(2)}, u32[]{:S(2)}) collective-permute-start(f32[128,128]{1,0:T(8,128)S(1)} %add.20.refs_5_), channel_id=1, source_target_pairs={{0,128},{64,192},{128,0},{192,64},{1,129},{65,193},{129,1},{193,65... | collective-permute-start | bytes 196616 | tf_op jit(solution)/shard_map/ppermute | solution.py:360
  41.3 20.7 %collective-permute-start.8 = (f32[32,16,128]{2,1,0:T(8,128)S(1)}, f32[32,16,128]{2,1,0:T(8,128)S(1)}, u32[]{:S(2)}, u32[]{:S(2)}) collective-permute-start(f32[32,16,128]{2,1,0:T(8,128)S(1)} %shard_map.100.refs_0_), channel_id=1, source_target_pairs={{0,4},{1,5},{2,6},{3,7},{4,0},{5,1},{6,2},{7,3},{8,12},{9,13},{10,... | collective-permute-start | bytes 786440 | tf_op jit(solution)/shard_map/ppermute | solution.py:360
  47.5 5.8 %collective-permute-start.9 = (f32[128,128]{1,0:T(8,128)S(1)}, f32[128,128]{1,0:T(8,128)S(1)}, u32[]{:S(2)}, u32[]{:S(2)}) collective-permute-start(f32[128,128]{1,0:T(8,128)S(1)} %add.21.refs_5_), channel_id=1, source_target_pairs={{0,16},{8,24},{16,0},{24,8},{1,17},{9,25},{17,1},{25,9},{2,18},{10... | collective-permute-start | bytes 196616 | tf_op jit(solution)/shard_map/ppermute | solution.py:360
  53.3 4.4 %collective-permute-start.10 = (f32[128,128]{1,0:T(8,128)S(1)}, f32[128,128]{1,0:T(8,128)S(1)}, u32[]{:S(2)}, u32[]{:S(2)}) collective-permute-start(f32[128,128]{1,0:T(8,128)S(1)} %add.22), channel_id=1, source_target_pairs={{0,8},{8,0},{16,24},{24,16},{1,9},{9,1},{17,25},{25,17},{2,10},{10... | collective-permute-start | bytes 196616 | tf_op jit(solution)/shard_map/ppermute | solution.py:360
  57.7 4.4 %collective-permute-start.11 = (f32[128,128]{1,0:T(8,128)S(1)}, f32[128,128]{1,0:T(8,128)S(1)}, u32[]{:S(2)}, u32[]{:S(2)}) collective-permute-start(f32[128,128]{1,0:T(8,128)S(1)} %add.23.left_ref), channel_id=1, source_target_pairs={{0,64},{64,0},{128,192},{192,128},{1,65},{65,1},{129,193},{193,129... | collective-permute-start | bytes 196616 | tf_op jit(solution)/shard_map/ppermute | solution.py:360
  62.0 4.7 %collective-permute-start.13 = (f32[128,128]{1,0:T(8,128)S(1)}, f32[128,128]{1,0:T(8,128)S(1)}, u32[]{:S(2)}, u32[]{:S(2)}) collective-permute-start(f32[128,128]{1,0:T(8,128)S(1)} %shard_map.101.refs_10_.left_ref), channel_id=1, source_target_pairs={{0,1},{1,0},{2,3},{3,2},{4,5},{5,4},{6,7},{7,6},{8,9},{9,8},{10,11... | collective-permute-start | bytes 196616 | tf_op jit(solution)/shard_map/ppermute | solution.py:360
  66.7 1.2 %collective-permute-start.12 = (f32[24,128]{1,0:T(8,128)S(1)}, f32[24,128]{1,0:T(8,128)S(1)}, u32[]{:S(2)}, u32[]{:S(2)}) collective-permute-start(f32[24,128]{1,0:T(8,128)S(1)} %get-tuple-element.20.left_ref), channel_id=1, source_target_pairs={{0,32},{32,0},{1,33},{33,1},{2,34},{34,2},{3,35},{35,3},{4,36},{36... | collective-permute-start | bytes 36872 | tf_op jit(solution)/shard_map/ppermute | solution.py:360
  92.7 1.6 %copy-start.2 = (bf16[256,4096]{1,0:T(8,128)(2,1)S(1)}, bf16[256,4096]{1,0:T(8,128)(2,1)}, u32[]{:S(2)}) copy-start(bf16[256,4096]{1,0:T(8,128)(2,1)} %copy-done.1) | copy-start | bytes 6291460
  94.3 1.6 %copy-start.4 = (bf16[256,4096]{1,0:T(8,128)(2,1)S(1)}, bf16[256,4096]{1,0:T(8,128)(2,1)}, u32[]{:S(2)}) copy-start(bf16[256,4096]{1,0:T(8,128)(2,1)} %copy-done.3) | copy-start | bytes 6291460

commit v4 on v3

--- a/solution.py
+++ b/solution.py
@@ -10,6 +10,7 @@
 NN = (((1,), (0,)), ((), ()))
 KERNEL_VMEM = 24 * 1024 * 1024
 VMEM = pl.BlockSpec(memory_space=pltpu.VMEM)
+ANYWHERE = pl.BlockSpec(memory_space=pl.ANY)
 BASIS_PARTS = 4
 AXES = ("y", "core", "x", "z")
 
@@ -18,20 +19,16 @@
     return pltpu.with_memory_space_constraint(value, pltpu.HBM)
 
 
+def in_vmem(value):
+    return pltpu.with_memory_space_constraint(value, pltpu.VMEM)
+
+
 def dot_nt(left, right):
     return lax.dot_general(left, right, NT, preferred_element_type=jnp.float32)
 
 
 def dot_nn(left, right):
     return lax.dot_general(left, right, NN, preferred_element_type=jnp.float32)
-
-
-def split3(value):
-    high = value.astype(jnp.bfloat16)
-    rest = value - high.astype(jnp.float32)
-    middle = rest.astype(jnp.bfloat16)
-    low = (rest - middle.astype(jnp.float32)).astype(jnp.bfloat16)
-    return high, middle, low
 
 
 def split2(value):
@@ -125,7 +122,7 @@
     )
 
 
-def basis_gram_kernel(basis_ref, out_ref, high_ref, middle_ref, low_ref, held_ref, sems):
+def basis_gram_kernel(basis_ref, out_ref, high_ref, low_ref, held_ref, sems):
     steps = sems.shape[0]
     width = held_ref.shape[3] // steps
     copies = []
@@ -142,12 +139,11 @@
     for step, copy in enumerate(copies):
         copy.wait()
         here = slice(step * width, (step + 1) * width)
-        high, middle, low = split3(stacked(held_ref[:, :, :, here]))
+        high, low = split2(stacked(held_ref[:, :, :, here]))
         high_ref[:, here] = high
-        middle_ref[:, here] = middle
         low_ref[:, here] = low
-        even += dot_nt(high, high) + dot_nt(middle, middle)
-        odd += dot_nt(high, middle) + dot_nt(high, low)
+        even += dot_nt(high, high)
+        odd += dot_nt(high, low)
     gram = even + odd + odd.T
     real = gram[:128, :128] + gram[128:, 128:]
     imag = gram[:128, 128:] - gram[128:, :128]
@@ -157,19 +153,19 @@
 
 
 def basis_gram(krylov_basis):
-    part = jax.ShapeDtypeStruct((256, krylov_basis.shape[3]), jnp.bfloat16)
+    part = pltpu.VMEM((256, krylov_basis.shape[3]), jnp.bfloat16)
     gram, *parts = pl.pallas_call(
         basis_gram_kernel,
         in_specs=[pl.BlockSpec(memory_space=pltpu.HBM)],
-        out_specs=[VMEM] * 4,
-        out_shape=[jax.ShapeDtypeStruct((128, 128), jnp.float32), part, part, part],
+        out_specs=[VMEM] * 3,
+        out_shape=[jax.ShapeDtypeStruct((128, 128), jnp.float32), part, part],
         scratch_shapes=[
             pltpu.VMEM(krylov_basis.shape, jnp.float32),
             pltpu.SemaphoreType.DMA((BASIS_PARTS,)),
         ],
         compiler_params=pltpu.CompilerParams(vmem_limit_bytes=KERNEL_VMEM),
         cost_estimate=pl.CostEstimate(
-            flops=4 * 2 * 256 * 256 * 4096, bytes_accessed=10 << 20, transcendentals=0
+            flops=2 * 2 * 256 * 256 * 4096, bytes_accessed=8 << 20, transcendentals=0
         ),
     )(in_hbm(krylov_basis))
     return gram, parts
@@ -178,7 +174,7 @@
 def mix(level, own_ref, partner_ref, mixer_ref, rank_ref, table_ref):
     table = table_ref[level]
     picked = jnp.concatenate([partner_ref[table[0, leaf]] for leaf in range(32)], axis=0)
-    both = jnp.concatenate([own_ref[...].reshape(512, 128), picked], axis=1)
+    both = jnp.concatenate([own_ref[0:32].reshape(512, 128), picked], axis=1)
     weights = jnp.concatenate(
         [
             jnp.concatenate([mixer_ref[level, 0, 0], mixer_ref[level, 0, 1]], axis=1),
@@ -201,72 +197,114 @@
     return leaf_value
 
 
-def level_kernel(level, own_ref, partner_ref, mixer_ref, rank_ref, table_ref, *refs):
+def level_kernel(level, gram_rows, own_ref, partner_ref, mixer_ref, rank_ref, table_ref, gram_ref, *refs):
     out_ref = refs[-1]
     leaf_value = mix(level, own_ref, partner_ref, mixer_ref, rank_ref, table_ref)
     for leaf in range(32):
         out_ref[leaf] = leaf_value(leaf)
-
-
-def next_level(level, own, partner, level_mixers, block_ranks, partner_tables, before):
-    return pl.pallas_call(
-        lambda *refs: level_kernel(level, *refs),
-        in_specs=[VMEM] * 5 + [pl.BlockSpec(memory_space=pl.ANY)] * len(before),
+    if gram_rows:
+        out_ref[32:40] = gram_ref[...].reshape(8, 16, 128)
+
+
+def next_level(level, own, partner, level_mixers, block_ranks, partner_tables, gram, with_gram):
+    return pl.pallas_call(
+        lambda *refs: level_kernel(level, with_gram, *refs),
+        in_specs=[VMEM] * 5 + [VMEM if with_gram else ANYWHERE],
         out_specs=VMEM,
-        out_shape=jax.ShapeDtypeStruct((32, 16, 128), jnp.float32),
+        out_shape=jax.ShapeDtypeStruct((40 if with_gram else 32, 16, 128), jnp.float32),
         compiler_params=pltpu.CompilerParams(vmem_limit_bytes=KERNEL_VMEM),
         cost_estimate=pl.CostEstimate(
             flops=3 * 512 * 256 * 256 * 2, bytes_accessed=1 << 20, transcendentals=0
         ),
-    )(own, partner, level_mixers, block_ranks, partner_tables, *before)
+    )(own, partner, level_mixers, block_ranks, partner_tables, gram)
 
 
 def project_kernel(
     level, own_ref, partner_ref, mixer_ref, rank_ref, table_ref, close_ref, leaf_ref,
-    high_ref, middle_ref, low_ref, before_ref, image_ref, sums_ref,
+    high_ref, low_ref, image_ref, sums_ref, gram_ref,
 ):
     leaf_value = mix(level, own_ref, partner_ref, mixer_ref, rank_ref, table_ref)
     for leaf in range(32):
         rounded = leaf_value(leaf).astype(jnp.bfloat16).astype(jnp.float32)
         far = leaf_product(rounded, leaf_ref[0, leaf], leaf_ref[1, leaf])
         image_ref[:, leaf * 128 : (leaf + 1) * 128] = far + close_ref[leaf]
-    high, middle, low = split3(image_ref[...])
-    three = jnp.concatenate([high, middle, low], axis=0)
-    two = three[:32]
-
-    def product(first, second, third):
-        one = dot_nt(three, first)
-        result = one[:16] + one[16:32] + one[32:]
-        one = dot_nt(two, second)
-        return result + one[:16] + one[16:] + dot_nt(high, third)
-
-    inner = product(high_ref[...], middle_ref[...], low_ref[...])
-    square = product(high, middle, low)
-    first = jnp.concatenate(
-        [inner[:8, :128] + inner[8:, 128:], inner[8:, :128] - inner[:8, 128:]], axis=0
-    )
+    high, low = split2(image_ref[...])
+    two = jnp.concatenate([high, low], axis=0)
+
+    def product(first, second):
+        one = dot_nt(two, first)
+        return one[:16] + one[16:] + dot_nt(high, second)
+
+    inner = product(high_ref[...], low_ref[...])
+    square = product(high, low)
+    sums_ref[0:8] = inner[:8, :128] + inner[8:, 128:]
+    sums_ref[8:16] = inner[8:, :128] - inner[:8, 128:]
     real = square[:8, :8] + square[8:, 8:]
     imag = square[:8, 8:] - square[8:, :8]
-    sums_ref[0:16] = first
     sums_ref[16:24] = jnp.concatenate([real, imag, jnp.zeros((8, 112), jnp.float32)], axis=1)
-
-
-def project(
-    level, own, partner, level_mixers, block_ranks, partner_tables, close, leaf_out, parts, before
-):
+    gram_ref[...] = (own_ref[32:40] + partner_ref[32:40]).reshape(128, 128)
+
+
+def project(level, own, partner, level_mixers, block_ranks, partner_tables, close, leaf_out, parts):
     return pl.pallas_call(
         lambda *refs: project_kernel(level, *refs),
-        in_specs=[VMEM] * 10 + [pl.BlockSpec(memory_space=pl.ANY)],
-        out_specs=[VMEM] * 2,
+        in_specs=[VMEM] * 9,
+        out_specs=[VMEM] * 3,
         out_shape=[
             jax.ShapeDtypeStruct((16, 4096), jnp.float32),
             jax.ShapeDtypeStruct((24, 128), jnp.float32),
+            jax.ShapeDtypeStruct((128, 128), jnp.float32),
         ],
         compiler_params=pltpu.CompilerParams(vmem_limit_bytes=KERNEL_VMEM),
         cost_estimate=pl.CostEstimate(
             flops=6 * 512 * 256 * 256 * 2, bytes_accessed=8 << 20, transcendentals=0
         ),
-    )(own, partner, level_mixers, block_ranks, partner_tables, close, leaf_out, *parts, before)
+    )(
+        own, partner, level_mixers, block_ranks, partner_tables, close, leaf_out,
+        *[in_vmem(part) for part in parts],
+    )
+
+
+def merge_kernel(own_ref, other_ref, gram_ref, out_ref):
+    sums = own_ref[...] + other_ref[...]
+    mine = lax.axis_index("y")
+    piece = gram_ref[pl.ds(pl.multiple_of(mine * 32, 32), 32), :]
+    for device in range(out_ref.shape[0]):
+        out_ref[device, 0:24] = sums
+        out_ref[device, 24:56] = piece
+
+
+def merge(own, other, gram):
+    return pl.pallas_call(
+        merge_kernel,
+        in_specs=[VMEM] * 3,
+        out_specs=VMEM,
+        out_shape=jax.ShapeDtypeStruct((lax.axis_size(("y", "x")), 56, 128), jnp.float32),
+        compiler_params=pltpu.CompilerParams(vmem_limit_bytes=KERNEL_VMEM),
+    )(own, other, gram)
+
+
+def relay_kernel(got_ref, out_ref, gram_ref):
+    sums = jnp.sum(got_ref[:, 0:24], axis=0)
+    for device in range(out_ref.shape[0]):
+        out_ref[device] = sums
+    for quarter in range(4):
+        gram_ref[quarter * 32 : (quarter + 1) * 32] = jnp.sum(
+            got_ref[quarter * 4 : quarter * 4 + 4, 24:56], axis=0
+        )
+
+
+def relay(got):
+    return pl.pallas_call(
+        relay_kernel,
+        in_specs=[VMEM],
+        out_specs=[VMEM] * 2,
+        out_shape=[
+            jax.ShapeDtypeStruct((lax.axis_size("z"), 24, 128), jnp.float32),
+            jax.ShapeDtypeStruct((128, 128), jnp.float32),
+        ],
+        compiler_params=pltpu.CompilerParams(vmem_limit_bytes=KERNEL_VMEM),
+    )(got)
 
 
 def dot_high(left, right, numbers):
@@ -276,7 +314,7 @@
 
 
 def finish_kernel(
-    scale, got_ref, gram_ref, image_ref, high_ref, middle_ref, low_ref, total_ref, new_ref, block_ref
+    scale, got_ref, gram_ref, image_ref, high_ref, low_ref, total_ref, new_ref, block_ref
 ):
     sums = jnp.sum(got_ref[...], axis=0) * scale
     first = sums[:16]
@@ -305,17 +343,13 @@
     two_real, two_imag = inner(total, rest)
     block_ref[0] = sums[16:24, 0:8] - one_real - two_real
     block_ref[1] = sums[16:24, 8:16] - one_imag - two_imag
-    high, middle, low = split3(complex_rows(total))
-    three = jnp.concatenate([high, middle, low], axis=0)
-    two = three[:32]
+    high, low = split2(complex_rows(total))
+    two = jnp.concatenate([high, low], axis=0)
     width = 1024
     for start in range(0, 4096, width):
         here = slice(start, start + width)
-        one = dot_nn(three, high_ref[:, here])
-        taken = one[:16] + one[16:32] + one[32:]
-        one = dot_nn(two, middle_ref[:, here])
-        taken += one[:16] + one[16:]
-        taken += dot_nn(high, low_ref[:, here])
+        one = dot_nn(two, high_ref[:, here])
+        taken = one[:16] + one[16:] + dot_nn(high, low_ref[:, here])
         new_ref[:, :, here] = (image_ref[:, here] - taken).reshape(2, 8, width)
     turn = jnp.where(row == lax.rem(column, 16) * 8 + lax.div(column, 16), 1.0, 0.0)
     turned = dot_high(total, turn, NN)
@@ -327,7 +361,7 @@
 def finish(scale, got, gram, image, parts):
     return pl.pallas_call(
         lambda *refs: finish_kernel(scale, *refs),
-        in_specs=[VMEM] * 6,
+        in_specs=[VMEM] * 5,
         out_specs=[VMEM] * 3,
         out_shape=[
             jax.ShapeDtypeStruct((2, 8, 8, 16), jnp.float32),
@@ -338,60 +372,35 @@
         cost_estimate=pl.CostEstimate(
             flops=6 * 16 * 256 * 4096 * 2, bytes_accessed=6 << 20, transcendentals=0
         ),
-    )(got, gram, image, *parts)
-
-
-def add_kernel(left_ref, right_ref, before_ref, out_ref):
-    out_ref[...] = left_ref[...] + right_ref[...]
-
-
-def add_after(left, right, before):
-    return pl.pallas_call(
-        add_kernel,
-        in_specs=[VMEM, VMEM, pl.BlockSpec(memory_space=pl.ANY)],
-        out_specs=VMEM,
-        out_shape=jax.ShapeDtypeStruct(left.shape, left.dtype),
-        compiler_params=pltpu.CompilerParams(vmem_limit_bytes=KERNEL_VMEM),
-    )(left, right, before)
+    )(got, gram, image, *[in_vmem(part) for part in parts])
 
 
 def exchange(value, axis, bit_number):
     pairs = [(source, source ^ (1 << bit_number)) for source in range(lax.axis_size(axis))]
     return lax.ppermute(value, axis, pairs)
-
-
-def sum_of_all(value, axes):
-    copies = jnp.broadcast_to(value[None], (lax.axis_size(axes),) + value.shape)
-    return jnp.sum(lax.all_to_all(copies, axes, 0, 0), axis=0)
 
 
 def per_device(
     krylov_basis, near_field, leaf_in, leaf_out, level_mixers, block_ranks, partner_tables
 ):
     plan = [("y", 1), ("y", 0), ("x", 1), ("x", 0), ("z", 2)]
-    beside = [[("core", 0)], [("z", 1)], [("z", 2)], [("y", 1)], [("x", 1), ("x", 0), ("y", 0)]]
+    beside = [[("z", 0)], [("z", 1)], [("y", 0), ("core", 0)], [("y", 1)]]
     coeffs, rows = leaves_in(krylov_basis, leaf_in, 4)
     gram, parts = basis_gram(krylov_basis)
     close = near_product(rows, near_field)
     for level, (axis, bit) in enumerate(plan):
         partner = exchange(coeffs, axis, bit)
-        for gram_axis, gram_bit in beside[level][:-1]:
-            gram = gram + exchange(gram, gram_axis, gram_bit)
-        got = exchange(gram, *beside[level][-1])
         operands = (level, coeffs, partner, level_mixers, block_ranks, partner_tables)
         if level < len(plan) - 1:
-            gram = gram + got
-            coeffs = next_level(*operands, [gram, close] if level == 1 else [gram])
+            for gram_axis, gram_bit in beside[level]:
+                gram = gram + exchange(gram, gram_axis, gram_bit)
+            coeffs = next_level(*operands, gram, level == len(plan) - 2)
         else:
-            gram = add_after(gram, got, partner)
-            image, sums = project(*operands, close, leaf_out, parts, gram)
-    gram = add_after(gram, exchange(gram, "z", 0), image)
-    sums = add_after(sums, exchange(sums, "core", 0), gram)
-    sums = sum_of_all(sums, ("y", "x"))
-    copies = jnp.broadcast_to(sums[None], (lax.axis_size("z"),) + sums.shape)
-    got = lax.all_to_all(copies, "z", 0, 0)
-    devices = lax.axis_size(AXES)
-    scale = 1.0 / (krylov_basis.shape[3] * devices)
+            image, sums, gram = project(*operands, close, leaf_out, parts)
+    got = merge(sums, exchange(sums, "core", 0), gram)
+    got, gram = relay(lax.all_to_all(got, ("y", "x"), 0, 0))
+    got = lax.all_to_all(got, "z", 0, 0)
+    scale = 1.0 / (krylov_basis.shape[3] * lax.axis_size(AXES))
     total, new_block, block_gram = finish(scale, got, gram, image, parts)
     return jnp.transpose(total, (3, 0, 1, 2)), new_block, block_gram
 

time: 98.4 us -> 96.6 us (0.982)
  blocking collectives: 24.7 us -> 35.4 us
  starting transfers between devices: 32.8 us -> 22.9 us
  local copies, waits for them, and re-layouts: 3.25 us -> 0.03 us
  waiting for transfers between devices: 21.5 us -> 24.1 us
  Pallas kernels: 15 us -> 13.1 us
    all_to_all x2, blocking collectives: 24.7 us -> 35.4 us  [the longest x1 20.9 us: per_device(): got = lax.all_to_all(got, 'z', 0, 0)]
    ppermute x14 -> x11, starting transfers between devices: 32.8 us -> 22.9 us  [exchange(): return lax.ppermute(value, axis, pairs)]
    unnamed x18 -> x10, local copies, waits for them, and re-layouts: 3.22 us -> 0.03 us
    ppermute x14 -> x11, waiting for transfers between devices: 21.5 us -> 24.1 us  [exchange(): return lax.ppermute(value, axis, pairs)]
  transfers between devices with their start and end apart: 14 -> 11, of which waited for: 10 -> 10; matrix products, arithmetic and copies ran while one was open for 0% -> 0% of each run, Pallas kernels for 8% -> 4%
where the time goes in v4:
time: 96.6 us; the launch traced here: 96.4 us
  blocking collectives  35.4 us (37%)
  waiting for transfers between devices  24.1 us (25%)
  starting transfers between devices  22.9 us (24%)
  Pallas kernels  13.1 us (14%)
    ppermute x11, waiting for transfers between devices, exchange(): return lax.ppermute(value, axis, pairs)  24.1 us
    ppermute x11, starting transfers between devices, exchange(): return lax.ppermute(value, axis, pairs)  22.9 us
    all_to_all x1, blocking collectives, per_device(): got = lax.all_to_all(got, 'z', 0, 0)  20.9 us
    all_to_all x1, blocking collectives, per_device(): got, gram = relay(lax.all_to_all(got, ('y', 'x'), 0, 0))  14.6 us
    pallas_call x1, Pallas kernels, basis_gram(): pl.pallas_call(basis_gram_kernel, in_specs=[pl.BlockSpec(memory_space=plt...  3.23 us
    pallas_call x1, Pallas kernels, project(): pl.pallas_call(lambda *refs: project_kernel(level, *refs), in_specs=[VMEM...  2.84 us
    pallas_call x1, Pallas kernels, leaves_in(): pl.pallas_call(leaves_in_kernel, in_specs=[pl.BlockSpec(memory_space=pltp...  2.48 us
    pallas_call x1, Pallas kernels, finish(): pl.pallas_call(lambda *refs: finish_kernel(scale, *refs), in_specs=[VMEM]...  2.04 us
  transfers between devices with their start and end apart: 11, of which 10 were waited for; matrix products, arithmetic and copies ran while one was open for 0% of the time, Pallas kernels for 4%

profile of v4, /device:TPU:2, one launch (start us, length us, event | category | flops | bytes accessed | tf_op | source)
XLA Modules:
  0.0 96.4 jit_solution(7708701724035578629)
XLA Ops:
  0.6 2.5 %shard_map.94 = (f32[32,16,128]{2,1,0:T(8,128)S(1)}, f32[32,16,128]{2,1,0:T(8,128)S(1)}) custom-call(f32[16,2,8,4096]{3,2,1,0:T(8,128)} %basis_ref.3, bf16[2,32,128,128]{3,2,1,0:T(8,128)(2,1)} %leaf_ref.2), custom_call_target="tpu_custom_call" | custom-call | flops 33554432 | bytes 2359296 | tf_op jit(solution)/shard_map/pallas_call | solution.py:82
  3.1 0.0 copy-start
  3.1 0.0 copy-start.3
  3.1 0.0 copy-start.4
  3.2 3.3 %collective-permute-start = (f32[32,16,128]{2,1,0:T(8,128)S(1)}, f32[32,16,128]{2,1,0:T(8,128)S(1)}, u32[]{:S(2)}, u32[]{:S(2)}) collective-permute-start(f32[32,16,128]{2,1,0:T(8,128)S(1)} %get-tuple-element.16.refs_0_), channel_id=1, source_target_pairs={{0,128},{64,192},{128,0},{192,64},{1,129},{65,193},{129,1},{193,65... | collective-permute-start | bytes 786440 | tf_op jit(solution)/shard_map/ppermute | solution.py:380
  6.4 3.2 %shard_map.95 = (f32[128,128]{1,0:T(8,128)S(1)}, bf16[256,4096]{1,0:T(8,128)(2,1)S(1)}, bf16[256,4096]{1,0:T(8,128)(2,1)S(1)}) custom-call(f32[16,2,8,4096]{3,2,1,0:T(8,128)} %basis_ref.3), custom_call_target="tpu_custom_call" | custom-call | flops 1073741824 | bytes 8388608 | tf_op jit(solution)/shard_map/pallas_call | solution.py:157
  9.7 2.0 %collective-permute-start.1 = (f32[128,128]{1,0:T(8,128)S(1)}, f32[128,128]{1,0:T(8,128)S(1)}, u32[]{:S(2)}, u32[]{:S(2)}) collective-permute-start(f32[128,128]{1,0:T(8,128)S(1)} %get-tuple-element.17), channel_id=1, source_target_pairs={{0,1},{1,0},{2,3},{3,2},{4,5},{5,4},{6,7},{7,6},{8,9},{9,8},{10,11... | collective-permute-start | bytes 196616 | tf_op jit(solution)/shard_map/ppermute | solution.py:380
  11.7 2.3 %collective-permute-done.1 = f32[128,128]{1,0:T(8,128)S(1)} collective-permute-done((f32[128,128]{1,0:T(8,128)S(1)}, f32[128,128]{1,0:T(8,128)S(1)}, u32[]{:S(2)}, u32[]{:S(2)}) %collective-permute-start.1) | collective-permute-done | bytes 65568 | tf_op jit(solution)/shard_map/ppermute | solution.py:380
  14.0 0.0 collective-permute-done.refs_1_
  14.0 0.0 copy-done
  14.1 0.0 copy-done.3
  14.1 0.0 copy-done.4
  14.1 0.5 shard_map.96.refs_0_
  14.5 0.8 collective-permute-start.2
  15.3 3.3 %collective-permute-start.3 = (f32[128,128]{1,0:T(8,128)S(1)}, f32[128,128]{1,0:T(8,128)S(1)}, u32[]{:S(2)}, u32[]{:S(2)}) collective-permute-start(f32[128,128]{1,0:T(8,128)S(1)} %add.15.refs_5_), channel_id=1, source_target_pairs={{0,2},{1,3},{2,0},{3,1},{4,6},{5,7},{6,4},{7,5},{8,10},{9,11},{10,... | collective-permute-start | bytes 196616 | tf_op jit(solution)/shard_map/ppermute | solution.py:380
  18.6 2.2 %collective-permute-done.3 = f32[128,128]{1,0:T(8,128)S(1)} collective-permute-done((f32[128,128]{1,0:T(8,128)S(1)}, f32[128,128]{1,0:T(8,128)S(1)}, u32[]{:S(2)}, u32[]{:S(2)}) %collective-permute-start.3) | collective-permute-done | bytes 65568 | tf_op jit(solution)/shard_map/ppermute | solution.py:380
  20.8 0.9 collective-permute-done.2.refs_1_
  21.7 0.5 shard_map.97.refs_0_
  22.2 2.2 %collective-permute-start.4 = (f32[32,16,128]{2,1,0:T(8,128)S(1)}, f32[32,16,128]{2,1,0:T(8,128)S(1)}, u32[]{:S(2)}, u32[]{:S(2)}) collective-permute-start(f32[32,16,128]{2,1,0:T(8,128)S(1)} %shard_map.97.refs_0_), channel_id=1, source_target_pairs={{0,16},{8,24},{16,0},{24,8},{1,17},{9,25},{17,1},{25,9},{2,18},{10... | collective-permute-start | bytes 786440 | tf_op jit(solution)/shard_map/ppermute | solution.py:380
  24.4 0.7 collective-permute-start.5
  25.1 3.6 %collective-permute-done.5 = f32[128,128]{1,0:T(8,128)S(1)} collective-permute-done((f32[128,128]{1,0:T(8,128)S(1)}, f32[128,128]{1,0:T(8,128)S(1)}, u32[]{:S(2)}, u32[]{:S(2)}) %collective-permute-start.5) | collective-permute-done | bytes 65568 | tf_op jit(solution)/shard_map/ppermute | solution.py:380
  28.7 0.1 collective-permute-start.6
  28.8 1.2 %collective-permute-done.6 = f32[128,128]{1,0:T(8,128)S(1)} collective-permute-done((f32[128,128]{1,0:T(8,128)S(1)}, f32[128,128]{1,0:T(8,128)S(1)}, u32[]{:S(2)}, u32[]{:S(2)}) %collective-permute-start.6) | collective-permute-done | bytes 65568 | tf_op jit(solution)/shard_map/ppermute | solution.py:380
  30.0 0.0 copy-start.2
  30.1 0.1 collective-permute-done.4.refs_1_
  30.2 0.5 shard_map.98.refs_0_
  30.6 1.4 %collective-permute-start.7 = (f32[32,16,128]{2,1,0:T(8,128)S(1)}, f32[32,16,128]{2,1,0:T(8,128)S(1)}, u32[]{:S(2)}, u32[]{:S(2)}) collective-permute-start(f32[32,16,128]{2,1,0:T(8,128)S(1)} %shard_map.98.refs_0_), channel_id=1, source_target_pairs={{0,8},{8,0},{16,24},{24,16},{1,9},{9,1},{17,25},{25,17},{2,10},{10... | collective-permute-start | bytes 786440 | tf_op jit(solution)/shard_map/ppermute | solution.py:380
  32.0 2.0 %collective-permute-start.8 = (f32[128,128]{1,0:T(8,128)S(1)}, f32[128,128]{1,0:T(8,128)S(1)}, u32[]{:S(2)}, u32[]{:S(2)}) collective-permute-start(f32[128,128]{1,0:T(8,128)S(1)} %add.18.refs_5_), channel_id=1, source_target_pairs={{0,128},{64,192},{128,0},{192,64},{1,129},{65,193},{129,1},{193,65... | collective-permute-start | bytes 196616 | tf_op jit(solution)/shard_map/ppermute | solution.py:380
  34.0 3.8 %collective-permute-done.8 = f32[128,128]{1,0:T(8,128)S(1)} collective-permute-done((f32[128,128]{1,0:T(8,128)S(1)}, f32[128,128]{1,0:T(8,128)S(1)}, u32[]{:S(2)}, u32[]{:S(2)}) %collective-permute-start.8) | collective-permute-done | bytes 65568 | tf_op jit(solution)/shard_map/ppermute | solution.py:380
  37.8 0.0 copy-start.1
  37.8 1.2 %collective-permute-done.7.refs_1_ = f32[32,16,128]{2,1,0:T(8,128)S(1)} collective-permute-done((f32[32,16,128]{2,1,0:T(8,128)S(1)}, f32[32,16,128]{2,1,0:T(8,128)S(1)}, u32[]{:S(2)}, u32[]{:S(2)}) %collective-permute-start.7) | collective-permute-done | bytes 262176 | tf_op jit(solution)/shard_map/ppermute | solution.py:380
  39.0 0.5 shard_map.99.refs_0_
  39.5 7.1 %collective-permute-start.9 = (f32[40,16,128]{2,1,0:T(8,128)S(1)}, f32[40,16,128]{2,1,0:T(8,128)S(1)}, u32[]{:S(2)}, u32[]{:S(2)}) collective-permute-start(f32[40,16,128]{2,1,0:T(8,128)S(1)} %shard_map.99.refs_0_), channel_id=1, source_target_pairs={{0,4},{1,5},{2,6},{3,7},{4,0},{5,1},{6,2},{7,3},{8,12},{9,13},{10,... | collective-permute-start | bytes 983048 | tf_op jit(solution)/shard_map/ppermute | solution.py:380
  46.6 0.0 copy-done.2
  46.6 0.6 shard_map.100.refs_5_
  47.2 7.6 %collective-permute-done.9.refs_1_ = f32[40,16,128]{2,1,0:T(8,128)S(1)} collective-permute-done((f32[40,16,128]{2,1,0:T(8,128)S(1)}, f32[40,16,128]{2,1,0:T(8,128)S(1)}, u32[]{:S(2)}, u32[]{:S(2)}) %collective-permute-start.9) | collective-permute-done | bytes 327712 | tf_op jit(solution)/shard_map/ppermute | solution.py:380
  54.8 0.0 copy-done.1
  54.8 2.8 %shard_map.101 = (f32[16,4096]{1,0:T(8,128)S(1)}, f32[24,128]{1,0:T(8,128)S(1)}, f32[128,128]{1,0:T(8,128)S(1)}) custom-call(f32[40,16,128]{2,1,0:T(8,128)S(1)} %shard_map.99.refs_0_, f32[40,16,128]{2,1,0:T(8,128)S(1)} %collective-permute-done.9.refs_1_, f32[5,2,2,128,128]{4,3,2,1,0:T(8,128)S(1)} %copy-done, s32[5,32]{1,0:T(8,128)S(1)} %copy-done.3, ...), custom_call_target="tpu_custom_call" | custom-call | flops 402653184 | bytes 8388608 | tf_op jit(solution)/shard_map/pallas_call | solution.py:249
  57.7 0.0 collective-permute-start.10
  57.7 1.2 %collective-permute-done.10.other_ref = f32[24,128]{1,0:T(8,128)S(1)} collective-permute-done((f32[24,128]{1,0:T(8,128)S(1)}, f32[24,128]{1,0:T(8,128)S(1)}, u32[]{:S(2)}, u32[]{:S(2)}) %collective-permute-start.10) | collective-permute-done | bytes 12320 | tf_op jit(solution)/shard_map/ppermute | solution.py:380
  58.9 14.6 %all_to_all.10.got_ref = f32[16,56,128]{2,1,0:T(8,128)S(1)} all-to-all(f32[16,56,128]{2,1,0:T(8,128)S(1)} %shard_map.102), channel_id=1, replica_groups=mesh['y'=4,'core'=2,'x'=4,'z'=8] {'y','x'}, dimensions={0} | all-to-all | bytes 917504 | tf_op jit(solution)/shard_map/all_to_all | solution.py:401
  73.5 20.9 %all_to_all.11.refs_0_ = f32[8,24,128]{2,1,0:T(8,128)S(1)} all-to-all(f32[8,24,128]{2,1,0:T(8,128)S(1)} %get-tuple-element.23), channel_id=1, replica_groups=mesh['y'=4,'core'=2,'x'=4,'z'=8] {'z'}, dimensions={0} | all-to-all | bytes 196608 | tf_op jit(solution)/shard_map/all_to_all | solution.py:402
  94.3 2.0 %shard_map.104 = (f32[2,8,8,16]{3,2,1,0:T(8,128)}, f32[2,8,4096]{2,1,0:T(8,128)}, f32[2,8,8]{2,1,0:T(8,128)}) custom-call(f32[8,24,128]{2,1,0:T(8,128)S(1)} %all_to_all.11.refs_0_, f32[128,128]{1,0:T(8,128)S(1)} %get-tuple-element.24.refs_1_, f32[16,4096]{1,0:T(8,128)S(1)} %get-tuple-element.25.refs_2_, ...), custom_call_target="tpu_custom_call" | custom-call | flops 201326592 | bytes 6291456 | tf_op jit(solution)/shard_map/pallas_call | solution.py:362
  (7 shorter events, 0.1 us)
Async XLA Ops:
  3.1 10.9 %copy-start = (f32[5,2,2,128,128]{4,3,2,1,0:T(8,128)S(1)}, f32[5,2,2,128,128]{4,3,2,1,0:T(8,128)}, u32[]{:S(2)}) copy-start(f32[5,2,2,128,128]{4,3,2,1,0:T(8,128)} %refs_2_.9) | copy-start | bytes 3932164
  3.1 10.9 %copy-start.3 = (s32[5,32]{1,0:T(8,128)S(1)}, s32[5,32]{1,0:T(8,128)}, u32[]{:S(2)}) copy-start(s32[5,32]{1,0:T(8,128)} %refs_3_.9) | copy-start | bytes 1924
  3.1 10.9 %copy-start.4 = (s32[5,1,32]{2,1,0:T(1,128)S(1)}, s32[5,1,32]{2,1,0:T(1,128)}, u32[]{:S(2)}) copy-start(s32[5,1,32]{2,1,0:T(1,128)} %refs_4_.9) | copy-start | bytes 1924
  3.2 10.9 %collective-permute-start = (f32[32,16,128]{2,1,0:T(8,128)S(1)}, f32[32,16,128]{2,1,0:T(8,128)S(1)}, u32[]{:S(2)}, u32[]{:S(2)}) collective-permute-start(f32[32,16,128]{2,1,0:T(8,128)S(1)} %get-tuple-element.16.refs_0_), channel_id=1, source_target_pairs={{0,128},{64,192},{128,0},{192,64},{1,129},{65,193},{129,1},{193,65... | collective-permute-start | bytes 786440 | tf_op jit(solution)/shard_map/ppermute | solution.py:380
  9.7 4.4 %collective-permute-start.1 = (f32[128,128]{1,0:T(8,128)S(1)}, f32[128,128]{1,0:T(8,128)S(1)}, u32[]{:S(2)}, u32[]{:S(2)}) collective-permute-start(f32[128,128]{1,0:T(8,128)S(1)} %get-tuple-element.17), channel_id=1, source_target_pairs={{0,1},{1,0},{2,3},{3,2},{4,5},{5,4},{6,7},{7,6},{8,9},{9,8},{10,11... | collective-permute-start | bytes 196616 | tf_op jit(solution)/shard_map/ppermute | solution.py:380
  14.5 7.2 %collective-permute-start.2 = (f32[32,16,128]{2,1,0:T(8,128)S(1)}, f32[32,16,128]{2,1,0:T(8,128)S(1)}, u32[]{:S(2)}, u32[]{:S(2)}) collective-permute-start(f32[32,16,128]{2,1,0:T(8,128)S(1)} %shard_map.96.refs_0_), channel_id=1, source_target_pairs={{0,64},{64,0},{128,192},{192,128},{1,65},{65,1},{129,193},{193,129... | collective-permute-start | bytes 786440 | tf_op jit(solution)/shard_map/ppermute | solution.py:380
  15.3 5.5 %collective-permute-start.3 = (f32[128,128]{1,0:T(8,128)S(1)}, f32[128,128]{1,0:T(8,128)S(1)}, u32[]{:S(2)}, u32[]{:S(2)}) collective-permute-start(f32[128,128]{1,0:T(8,128)S(1)} %add.15.refs_5_), channel_id=1, source_target_pairs={{0,2},{1,3},{2,0},{3,1},{4,6},{5,7},{6,4},{7,5},{8,10},{9,11},{10,... | collective-permute-start | bytes 196616 | tf_op jit(solution)/shard_map/ppermute | solution.py:380
  22.2 8.0 %collective-permute-start.4 = (f32[32,16,128]{2,1,0:T(8,128)S(1)}, f32[32,16,128]{2,1,0:T(8,128)S(1)}, u32[]{:S(2)}, u32[]{:S(2)}) collective-permute-start(f32[32,16,128]{2,1,0:T(8,128)S(1)} %shard_map.97.refs_0_), channel_id=1, source_target_pairs={{0,16},{8,24},{16,0},{24,8},{1,17},{9,25},{17,1},{25,9},{2,18},{10... | collective-permute-start | bytes 786440 | tf_op jit(solution)/shard_map/ppermute | solution.py:380
  24.4 4.3 %collective-permute-start.5 = (f32[128,128]{1,0:T(8,128)S(1)}, f32[128,128]{1,0:T(8,128)S(1)}, u32[]{:S(2)}, u32[]{:S(2)}) collective-permute-start(f32[128,128]{1,0:T(8,128)S(1)} %add.16.refs_5_), channel_id=1, source_target_pairs={{0,64},{64,0},{128,192},{192,128},{1,65},{65,1},{129,193},{193,129... | collective-permute-start | bytes 196616 | tf_op jit(solution)/shard_map/ppermute | solution.py:380
  28.7 1.3 %collective-permute-start.6 = (f32[128,128]{1,0:T(8,128)S(1)}, f32[128,128]{1,0:T(8,128)S(1)}, u32[]{:S(2)}, u32[]{:S(2)}) collective-permute-start(f32[128,128]{1,0:T(8,128)S(1)} %add.17), channel_id=1, source_target_pairs={{0,32},{32,0},{1,33},{33,1},{2,34},{34,2},{3,35},{35,3},{4,36},{36... | collective-permute-start | bytes 196616 | tf_op jit(solution)/shard_map/ppermute | solution.py:380
  30.0 16.5 %copy-start.2 = (bf16[2,32,128,128]{3,2,1,0:T(8,128)(2,1)S(1)}, bf16[2,32,128,128]{3,2,1,0:T(8,128)(2,1)}, u32[]{:S(2)}) copy-start(bf16[2,32,128,128]{3,2,1,0:T(8,128)(2,1)} %leaf_ref.3) | copy-start | bytes 6291460
  30.6 8.4 %collective-permute-start.7 = (f32[32,16,128]{2,1,0:T(8,128)S(1)}, f32[32,16,128]{2,1,0:T(8,128)S(1)}, u32[]{:S(2)}, u32[]{:S(2)}) collective-permute-start(f32[32,16,128]{2,1,0:T(8,128)S(1)} %shard_map.98.refs_0_), channel_id=1, source_target_pairs={{0,8},{8,0},{16,24},{24,16},{1,9},{9,1},{17,25},{25,17},{2,10},{10... | collective-permute-start | bytes 786440 | tf_op jit(solution)/shard_map/ppermute | solution.py:380
  32.0 5.8 %collective-permute-start.8 = (f32[128,128]{1,0:T(8,128)S(1)}, f32[128,128]{1,0:T(8,128)S(1)}, u32[]{:S(2)}, u32[]{:S(2)}) collective-permute-start(f32[128,128]{1,0:T(8,128)S(1)} %add.18.refs_5_), channel_id=1, source_target_pairs={{0,128},{64,192},{128,0},{192,64},{1,129},{65,193},{129,1},{193,65... | collective-permute-start | bytes 196616 | tf_op jit(solution)/shard_map/ppermute | solution.py:380
  37.8 17.0 %copy-start.1 = (bf16[2,32,128,128]{3,2,1,0:T(8,128)(2,1)S(1)}, bf16[2,32,128,128]{3,2,1,0:T(8,128)(2,1)}, u32[]{:S(2)}) copy-start(bf16[2,32,128,128]{3,2,1,0:T(8,128)(2,1)} %refs_6_.1) | copy-start | bytes 6291460
  39.5 15.3 %collective-permute-start.9 = (f32[40,16,128]{2,1,0:T(8,128)S(1)}, f32[40,16,128]{2,1,0:T(8,128)S(1)}, u32[]{:S(2)}, u32[]{:S(2)}) collective-permute-start(f32[40,16,128]{2,1,0:T(8,128)S(1)} %shard_map.99.refs_0_), channel_id=1, source_target_pairs={{0,4},{1,5},{2,6},{3,7},{4,0},{5,1},{6,2},{7,3},{8,12},{9,13},{10,... | collective-permute-start | bytes 983048 | tf_op jit(solution)/shard_map/ppermute | solution.py:380
  57.7 1.2 %collective-permute-start.10 = (f32[24,128]{1,0:T(8,128)S(1)}, f32[24,128]{1,0:T(8,128)S(1)}, u32[]{:S(2)}, u32[]{:S(2)}) collective-permute-start(f32[24,128]{1,0:T(8,128)S(1)} %get-tuple-element.21.own_ref), channel_id=1, source_target_pairs={{0,32},{32,0},{1,33},{33,1},{2,34},{34,2},{3,35},{35,3},{4,36},{36... | collective-permute-start | bytes 36872 | tf_op jit(solution)/shard_map/ppermute | solution.py:380

commit v5 on v4

--- a/solution.py
+++ b/solution.py
@@ -174,7 +174,7 @@
 def mix(level, own_ref, partner_ref, mixer_ref, rank_ref, table_ref):
     table = table_ref[level]
     picked = jnp.concatenate([partner_ref[table[0, leaf]] for leaf in range(32)], axis=0)
-    both = jnp.concatenate([own_ref[0:32].reshape(512, 128), picked], axis=1)
+    both = jnp.concatenate([own_ref[...].reshape(512, 128), picked], axis=1)
     weights = jnp.concatenate(
         [
             jnp.concatenate([mixer_ref[level, 0, 0], mixer_ref[level, 0, 1]], axis=1),
@@ -197,21 +197,18 @@
     return leaf_value
 
 
-def level_kernel(level, gram_rows, own_ref, partner_ref, mixer_ref, rank_ref, table_ref, gram_ref, *refs):
-    out_ref = refs[-1]
+def level_kernel(level, own_ref, partner_ref, mixer_ref, rank_ref, table_ref, gram_ref, out_ref):
     leaf_value = mix(level, own_ref, partner_ref, mixer_ref, rank_ref, table_ref)
     for leaf in range(32):
         out_ref[leaf] = leaf_value(leaf)
-    if gram_rows:
-        out_ref[32:40] = gram_ref[...].reshape(8, 16, 128)
-
-
-def next_level(level, own, partner, level_mixers, block_ranks, partner_tables, gram, with_gram):
-    return pl.pallas_call(
-        lambda *refs: level_kernel(level, with_gram, *refs),
-        in_specs=[VMEM] * 5 + [VMEM if with_gram else ANYWHERE],
+
+
+def next_level(level, own, partner, level_mixers, block_ranks, partner_tables, gram):
+    return pl.pallas_call(
+        lambda *refs: level_kernel(level, *refs),
+        in_specs=[VMEM] * 5 + [ANYWHERE],
         out_specs=VMEM,
-        out_shape=jax.ShapeDtypeStruct((40 if with_gram else 32, 16, 128), jnp.float32),
+        out_shape=jax.ShapeDtypeStruct(own.shape, jnp.float32),
         compiler_params=pltpu.CompilerParams(vmem_limit_bytes=KERNEL_VMEM),
         cost_estimate=pl.CostEstimate(
             flops=3 * 512 * 256 * 256 * 2, bytes_accessed=1 << 20, transcendentals=0
@@ -221,7 +218,7 @@
 
 def project_kernel(
     level, own_ref, partner_ref, mixer_ref, rank_ref, table_ref, close_ref, leaf_ref,
-    high_ref, low_ref, image_ref, sums_ref, gram_ref,
+    high_ref, low_ref, before_ref, image_ref, sums_ref,
 ):
     leaf_value = mix(level, own_ref, partner_ref, mixer_ref, rank_ref, table_ref)
     for leaf in range(32):
@@ -242,18 +239,16 @@
     real = square[:8, :8] + square[8:, 8:]
     imag = square[:8, 8:] - square[8:, :8]
     sums_ref[16:24] = jnp.concatenate([real, imag, jnp.zeros((8, 112), jnp.float32)], axis=1)
-    gram_ref[...] = (own_ref[32:40] + partner_ref[32:40]).reshape(128, 128)
-
-
-def project(level, own, partner, level_mixers, block_ranks, partner_tables, close, leaf_out, parts):
+
+
+def project(level, own, partner, level_mixers, block_ranks, partner_tables, close, leaf_out, parts, gram):
     return pl.pallas_call(
         lambda *refs: project_kernel(level, *refs),
-        in_specs=[VMEM] * 9,
-        out_specs=[VMEM] * 3,
+        in_specs=[VMEM] * 9 + [ANYWHERE],
+        out_specs=[VMEM] * 2,
         out_shape=[
             jax.ShapeDtypeStruct((16, 4096), jnp.float32),
             jax.ShapeDtypeStruct((24, 128), jnp.float32),
-            jax.ShapeDtypeStruct((128, 128), jnp.float32),
         ],
         compiler_params=pltpu.CompilerParams(vmem_limit_bytes=KERNEL_VMEM),
         cost_estimate=pl.CostEstimate(
@@ -261,48 +256,50 @@
         ),
     )(
         own, partner, level_mixers, block_ranks, partner_tables, close, leaf_out,
-        *[in_vmem(part) for part in parts],
-    )
-
-
-def merge_kernel(own_ref, other_ref, gram_ref, out_ref):
+        *[in_vmem(part) for part in parts], gram,
+    )
+
+
+def merge_kernel(own_ref, other_ref, gram_ref, other_gram_ref, out_ref, gram_sum_ref):
     sums = own_ref[...] + other_ref[...]
-    mine = lax.axis_index("y")
+    gram_sum_ref[...] = gram_ref[...] + other_gram_ref[...]
+    mine = lax.axis_index("y") * 2 + lax.rem(lax.axis_index("x"), 2)
+    piece = gram_sum_ref[pl.ds(pl.multiple_of(mine * 16, 16), 16), :]
+    for device in range(out_ref.shape[0]):
+        out_ref[device, 0:24] = sums
+        out_ref[device, 24:40] = piece
+
+
+def merge(own, other, gram, other_gram):
+    return pl.pallas_call(
+        merge_kernel,
+        in_specs=[VMEM] * 4,
+        out_specs=VMEM,
+        out_shape=jax.ShapeDtypeStruct((lax.axis_size(("y", "x")), 40, 128), jnp.float32),
+        scratch_shapes=[pltpu.VMEM((128, 128), jnp.float32)],
+        compiler_params=pltpu.CompilerParams(vmem_limit_bytes=KERNEL_VMEM),
+    )(own, other, gram, other_gram)
+
+
+def relay_kernel(got_ref, out_ref, gram_ref):
+    sums = jnp.sum(got_ref[:, 0:24], axis=0)
+    for piece in range(8):
+        at = piece // 2 * 4 + piece % 2
+        gram_ref[piece * 16 : (piece + 1) * 16] = got_ref[at, 24:40] + got_ref[at + 2, 24:40]
+    mine = lax.rem(lax.axis_index("z"), 4)
     piece = gram_ref[pl.ds(pl.multiple_of(mine * 32, 32), 32), :]
     for device in range(out_ref.shape[0]):
         out_ref[device, 0:24] = sums
         out_ref[device, 24:56] = piece
 
 
-def merge(own, other, gram):
-    return pl.pallas_call(
-        merge_kernel,
-        in_specs=[VMEM] * 3,
-        out_specs=VMEM,
-        out_shape=jax.ShapeDtypeStruct((lax.axis_size(("y", "x")), 56, 128), jnp.float32),
-        compiler_params=pltpu.CompilerParams(vmem_limit_bytes=KERNEL_VMEM),
-    )(own, other, gram)
-
-
-def relay_kernel(got_ref, out_ref, gram_ref):
-    sums = jnp.sum(got_ref[:, 0:24], axis=0)
-    for device in range(out_ref.shape[0]):
-        out_ref[device] = sums
-    for quarter in range(4):
-        gram_ref[quarter * 32 : (quarter + 1) * 32] = jnp.sum(
-            got_ref[quarter * 4 : quarter * 4 + 4, 24:56], axis=0
-        )
-
-
 def relay(got):
     return pl.pallas_call(
         relay_kernel,
         in_specs=[VMEM],
-        out_specs=[VMEM] * 2,
-        out_shape=[
-            jax.ShapeDtypeStruct((lax.axis_size("z"), 24, 128), jnp.float32),
-            jax.ShapeDtypeStruct((128, 128), jnp.float32),
-        ],
+        out_specs=VMEM,
+        out_shape=jax.ShapeDtypeStruct((lax.axis_size("z"), 56, 128), jnp.float32),
+        scratch_shapes=[pltpu.VMEM((128, 128), jnp.float32)],
         compiler_params=pltpu.CompilerParams(vmem_limit_bytes=KERNEL_VMEM),
     )(got)
 
@@ -314,9 +311,11 @@
 
 
 def finish_kernel(
-    scale, got_ref, gram_ref, image_ref, high_ref, low_ref, total_ref, new_ref, block_ref
+    scale, got_ref, image_ref, high_ref, low_ref, total_ref, new_ref, block_ref, gram_ref
 ):
-    sums = jnp.sum(got_ref[...], axis=0) * scale
+    sums = jnp.sum(got_ref[:, 0:24], axis=0) * scale
+    for piece in range(4):
+        gram_ref[piece * 32 : (piece + 1) * 32] = got_ref[piece, 24:56] + got_ref[piece + 4, 24:56]
     first = sums[:16]
     packed = gram_ref[...] * scale
     row = lax.broadcasted_iota(jnp.int32, (128, 128), 0)
@@ -358,21 +357,22 @@
         total_ref[1, angle] = turned[8:, angle * 16 : (angle + 1) * 16]
 
 
-def finish(scale, got, gram, image, parts):
+def finish(scale, got, image, parts):
     return pl.pallas_call(
         lambda *refs: finish_kernel(scale, *refs),
-        in_specs=[VMEM] * 5,
+        in_specs=[VMEM] * 4,
         out_specs=[VMEM] * 3,
         out_shape=[
             jax.ShapeDtypeStruct((2, 8, 8, 16), jnp.float32),
             jax.ShapeDtypeStruct((2, 8, 4096), jnp.float32),
             jax.ShapeDtypeStruct((2, 8, 8), jnp.float32),
         ],
+        scratch_shapes=[pltpu.VMEM((128, 128), jnp.float32)],
         compiler_params=pltpu.CompilerParams(vmem_limit_bytes=KERNEL_VMEM),
         cost_estimate=pl.CostEstimate(
             flops=6 * 16 * 256 * 4096 * 2, bytes_accessed=6 << 20, transcendentals=0
         ),
-    )(got, gram, image, *[in_vmem(part) for part in parts])
+    )(got, image, *[in_vmem(part) for part in parts])
 
 
 def exchange(value, axis, bit_number):
@@ -384,24 +384,23 @@
     krylov_basis, near_field, leaf_in, leaf_out, level_mixers, block_ranks, partner_tables
 ):
     plan = [("y", 1), ("y", 0), ("x", 1), ("x", 0), ("z", 2)]
-    beside = [[("z", 0)], [("z", 1)], [("y", 0), ("core", 0)], [("y", 1)]]
+    beside = [("core", 0), ("z", 1), ("y", 0), ("y", 1), ("x", 0)]
     coeffs, rows = leaves_in(krylov_basis, leaf_in, 4)
     gram, parts = basis_gram(krylov_basis)
     close = near_product(rows, near_field)
     for level, (axis, bit) in enumerate(plan):
         partner = exchange(coeffs, axis, bit)
+        gram = gram + exchange(gram, *beside[level])
         operands = (level, coeffs, partner, level_mixers, block_ranks, partner_tables)
         if level < len(plan) - 1:
-            for gram_axis, gram_bit in beside[level]:
-                gram = gram + exchange(gram, gram_axis, gram_bit)
-            coeffs = next_level(*operands, gram, level == len(plan) - 2)
+            coeffs = next_level(*operands, gram)
         else:
-            image, sums, gram = project(*operands, close, leaf_out, parts)
-    got = merge(sums, exchange(sums, "core", 0), gram)
-    got, gram = relay(lax.all_to_all(got, ("y", "x"), 0, 0))
+            image, sums = project(*operands, close, leaf_out, parts, gram)
+    got = merge(sums, exchange(sums, "core", 0), gram, exchange(gram, "z", 0))
+    got = relay(lax.all_to_all(got, ("y", "x"), 0, 0))
     got = lax.all_to_all(got, "z", 0, 0)
     scale = 1.0 / (krylov_basis.shape[3] * lax.axis_size(AXES))
-    total, new_block, block_gram = finish(scale, got, gram, image, parts)
+    total, new_block, block_gram = finish(scale, got, image, parts)
     return jnp.transpose(total, (3, 0, 1, 2)), new_block, block_gram
 
 

time: 96.6 us -> 91 us (0.942)
  waiting for transfers between devices: 24.1 us -> 17.4 us
  starting transfers between devices: 22.9 us -> 25.7 us
  blocking collectives: 35.4 us -> 33.6 us
    ppermute x11 -> x12, waiting for transfers between devices: 24.1 us -> 17.4 us  [exchange(): return lax.ppermute(value, axis, pairs)]
    all_to_all x1, blocking collectives: 20.9 us -> 17.3 us  [per_device(): got = lax.all_to_all(got, 'z', 0, 0)]
    ppermute x11 -> x12, starting transfers between devices: 22.9 us -> 25.7 us  [exchange(): return lax.ppermute(value, axis, pairs)]
    all_to_all x1, blocking collectives: 14.6 us -> 16.3 us  [per_device(): got = relay(lax.all_to_all(got, ('y', 'x'), 0, 0))]
  transfers between devices with their start and end apart: 11 -> 12, of which waited for: 10 -> 9; matrix products, arithmetic and copies ran while one was open for 0% -> 0% of each run, Pallas kernels for 4% -> 7%
where the time goes in v5:
time: 91 us; the launch traced here: 90.8 us
  blocking collectives  33.6 us (37%)
  starting transfers between devices  25.7 us (28%)
  waiting for transfers between devices  17.4 us (19%)
  Pallas kernels  13.1 us (14%)
    ppermute x12, starting transfers between devices, exchange(): return lax.ppermute(value, axis, pairs)  25.7 us
    ppermute x12, waiting for transfers between devices, exchange(): return lax.ppermute(value, axis, pairs)  17.4 us
    all_to_all x1, blocking collectives, per_device(): got = lax.all_to_all(got, 'z', 0, 0)  17.3 us
    all_to_all x1, blocking collectives, per_device(): got = relay(lax.all_to_all(got, ('y', 'x'), 0, 0))  16.3 us
    pallas_call x1, Pallas kernels, basis_gram(): pl.pallas_call(basis_gram_kernel, in_specs=[pl.BlockSpec(memory_space=plt...  3.23 us
    pallas_call x1, Pallas kernels, project(): pl.pallas_call(lambda *refs: project_kernel(level, *refs), in_specs=[VMEM...  2.83 us
    pallas_call x1, Pallas kernels, leaves_in(): pl.pallas_call(leaves_in_kernel, in_specs=[pl.BlockSpec(memory_space=pltp...  2.48 us
    pallas_call x1, Pallas kernels, finish(): pl.pallas_call(lambda *refs: finish_kernel(scale, *refs), in_specs=[VMEM]...  2.04 us
  transfers between devices with their start and end apart: 12, of which 9 were waited for; matrix products, arithmetic and copies ran while one was open for 0% of the time, Pallas kernels for 7%

profile of v5, /device:TPU:2, one launch (start us, length us, event | category | flops | bytes accessed | tf_op | source)
XLA Modules:
  0.0 90.8 jit_solution(3484438524293082556)
XLA Ops:
  0.6 2.5 %shard_map.94 = (f32[32,16,128]{2,1,0:T(8,128)S(1)}, f32[32,16,128]{2,1,0:T(8,128)S(1)}) custom-call(f32[16,2,8,4096]{3,2,1,0:T(8,128)} %basis_ref.3, bf16[2,32,128,128]{3,2,1,0:T(8,128)(2,1)} %leaf_ref.2), custom_call_target="tpu_custom_call" | custom-call | flops 33554432 | bytes 2359296 | tf_op jit(solution)/shard_map/pallas_call | solution.py:82
  3.1 0.0 copy-start
  3.1 0.0 copy-start.3
  3.1 0.0 copy-start.4
  3.2 3.3 %collective-permute-start = (f32[32,16,128]{2,1,0:T(8,128)S(1)}, f32[32,16,128]{2,1,0:T(8,128)S(1)}, u32[]{:S(2)}, u32[]{:S(2)}) collective-permute-start(f32[32,16,128]{2,1,0:T(8,128)S(1)} %get-tuple-element.13.refs_0_), channel_id=1, source_target_pairs={{0,128},{64,192},{128,0},{192,64},{1,129},{65,193},{129,1},{193,65... | collective-permute-start | bytes 786440 | tf_op jit(solution)/shard_map/ppermute | solution.py:380
  6.4 3.2 %shard_map.95 = (f32[128,128]{1,0:T(8,128)S(1)}, bf16[256,4096]{1,0:T(8,128)(2,1)S(1)}, bf16[256,4096]{1,0:T(8,128)(2,1)S(1)}) custom-call(f32[16,2,8,4096]{3,2,1,0:T(8,128)} %basis_ref.3), custom_call_target="tpu_custom_call" | custom-call | flops 1073741824 | bytes 8388608 | tf_op jit(solution)/shard_map/pallas_call | solution.py:157
  9.7 0.1 collective-permute-start.1
  9.8 1.2 %collective-permute-done.1 = f32[128,128]{1,0:T(8,128)S(1)} collective-permute-done((f32[128,128]{1,0:T(8,128)S(1)}, f32[128,128]{1,0:T(8,128)S(1)}, u32[]{:S(2)}, u32[]{:S(2)}) %collective-permute-start.1) | collective-permute-done | bytes 65568 | tf_op jit(solution)/shard_map/ppermute | solution.py:380
  11.0 1.8 %collective-permute-done.refs_1_ = f32[32,16,128]{2,1,0:T(8,128)S(1)} collective-permute-done((f32[32,16,128]{2,1,0:T(8,128)S(1)}, f32[32,16,128]{2,1,0:T(8,128)S(1)}, u32[]{:S(2)}, u32[]{:S(2)}) %collective-permute-start) | collective-permute-done | bytes 262176 | tf_op jit(solution)/shard_map/ppermute | solution.py:380
  12.8 0.0 copy-done
  12.8 0.0 copy-done.3
  12.8 0.0 copy-done.4
  12.8 0.5 shard_map.96.refs_0_
  13.3 1.7 %collective-permute-start.2 = (f32[32,16,128]{2,1,0:T(8,128)S(1)}, f32[32,16,128]{2,1,0:T(8,128)S(1)}, u32[]{:S(2)}, u32[]{:S(2)}) collective-permute-start(f32[32,16,128]{2,1,0:T(8,128)S(1)} %shard_map.96.refs_0_), channel_id=1, source_target_pairs={{0,64},{64,0},{128,192},{192,128},{1,65},{65,1},{129,193},{193,129... | collective-permute-start | bytes 786440 | tf_op jit(solution)/shard_map/ppermute | solution.py:380
  14.9 3.3 %collective-permute-start.3 = (f32[128,128]{1,0:T(8,128)S(1)}, f32[128,128]{1,0:T(8,128)S(1)}, u32[]{:S(2)}, u32[]{:S(2)}) collective-permute-start(f32[128,128]{1,0:T(8,128)S(1)} %add.15.refs_5_), channel_id=1, source_target_pairs={{0,2},{1,3},{2,0},{3,1},{4,6},{5,7},{6,4},{7,5},{8,10},{9,11},{10,... | collective-permute-start | bytes 196616 | tf_op jit(solution)/shard_map/ppermute | solution.py:380
  18.2 2.3 %collective-permute-done.3 = f32[128,128]{1,0:T(8,128)S(1)} collective-permute-done((f32[128,128]{1,0:T(8,128)S(1)}, f32[128,128]{1,0:T(8,128)S(1)}, u32[]{:S(2)}, u32[]{:S(2)}) %collective-permute-start.3) | collective-permute-done | bytes 65568 | tf_op jit(solution)/shard_map/ppermute | solution.py:380
  20.5 0.0 collective-permute-done.2.refs_1_
  20.5 0.5 shard_map.97.refs_0_
  21.0 2.2 %collective-permute-start.4 = (f32[32,16,128]{2,1,0:T(8,128)S(1)}, f32[32,16,128]{2,1,0:T(8,128)S(1)}, u32[]{:S(2)}, u32[]{:S(2)}) collective-permute-start(f32[32,16,128]{2,1,0:T(8,128)S(1)} %shard_map.97.refs_0_), channel_id=1, source_target_pairs={{0,16},{8,24},{16,0},{24,8},{1,17},{9,25},{17,1},{25,9},{2,18},{10... | collective-permute-start | bytes 786440 | tf_op jit(solution)/shard_map/ppermute | solution.py:380
  23.2 1.6 %collective-permute-start.5 = (f32[128,128]{1,0:T(8,128)S(1)}, f32[128,128]{1,0:T(8,128)S(1)}, u32[]{:S(2)}, u32[]{:S(2)}) collective-permute-start(f32[128,128]{1,0:T(8,128)S(1)} %add.16.refs_5_), channel_id=1, source_target_pairs={{0,64},{64,0},{128,192},{192,128},{1,65},{65,1},{129,193},{193,129... | collective-permute-start | bytes 196616 | tf_op jit(solution)/shard_map/ppermute | solution.py:380
  24.8 2.7 %collective-permute-done.5 = f32[128,128]{1,0:T(8,128)S(1)} collective-permute-done((f32[128,128]{1,0:T(8,128)S(1)}, f32[128,128]{1,0:T(8,128)S(1)}, u32[]{:S(2)}, u32[]{:S(2)}) %collective-permute-start.5) | collective-permute-done | bytes 65568 | tf_op jit(solution)/shard_map/ppermute | solution.py:380
  27.5 0.0 copy-start.2
  27.5 1.5 %collective-permute-done.4.refs_1_ = f32[32,16,128]{2,1,0:T(8,128)S(1)} collective-permute-done((f32[32,16,128]{2,1,0:T(8,128)S(1)}, f32[32,16,128]{2,1,0:T(8,128)S(1)}, u32[]{:S(2)}, u32[]{:S(2)}) %collective-permute-start.4) | collective-permute-done | bytes 262176 | tf_op jit(solution)/shard_map/ppermute | solution.py:380
  29.0 0.5 shard_map.98.refs_0_
  29.4 0.6 collective-permute-start.6
  30.0 3.2 %collective-permute-start.7 = (f32[128,128]{1,0:T(8,128)S(1)}, f32[128,128]{1,0:T(8,128)S(1)}, u32[]{:S(2)}, u32[]{:S(2)}) collective-permute-start(f32[128,128]{1,0:T(8,128)S(1)} %add.17.refs_5_), channel_id=1, source_target_pairs={{0,128},{64,192},{128,0},{192,64},{1,129},{65,193},{129,1},{193,65... | collective-permute-start | bytes 196616 | tf_op jit(solution)/shard_map/ppermute | solution.py:380
  33.2 2.6 %collective-permute-done.7 = f32[128,128]{1,0:T(8,128)S(1)} collective-permute-done((f32[128,128]{1,0:T(8,128)S(1)}, f32[128,128]{1,0:T(8,128)S(1)}, u32[]{:S(2)}, u32[]{:S(2)}) %collective-permute-start.7) | collective-permute-done | bytes 65568 | tf_op jit(solution)/shard_map/ppermute | solution.py:380
  35.8 0.0 copy-start.1
  35.8 0.0 collective-permute-done.6.refs_1_
  35.9 0.5 shard_map.99.refs_0_
  36.4 8.3 %collective-permute-start.8 = (f32[32,16,128]{2,1,0:T(8,128)S(1)}, f32[32,16,128]{2,1,0:T(8,128)S(1)}, u32[]{:S(2)}, u32[]{:S(2)}) collective-permute-start(f32[32,16,128]{2,1,0:T(8,128)S(1)} %shard_map.99.refs_0_), channel_id=1, source_target_pairs={{0,4},{1,5},{2,6},{3,7},{4,0},{5,1},{6,2},{7,3},{8,12},{9,13},{10,... | collective-permute-start | bytes 786440 | tf_op jit(solution)/shard_map/ppermute | solution.py:380
  44.6 0.8 collective-permute-start.9
  45.4 3.5 %collective-permute-done.9 = f32[128,128]{1,0:T(8,128)S(1)} collective-permute-done((f32[128,128]{1,0:T(8,128)S(1)}, f32[128,128]{1,0:T(8,128)S(1)}, u32[]{:S(2)}, u32[]{:S(2)}) %collective-permute-start.9) | collective-permute-done | bytes 65568 | tf_op jit(solution)/shard_map/ppermute | solution.py:380
  48.9 0.8 collective-permute-start.11
  49.7 0.0 copy-done.2
  49.7 0.6 shard_map.100.refs_5_
  50.4 0.6 collective-permute-done.8.refs_1_
  51.0 0.0 copy-done.1
  51.0 2.8 %shard_map.101 = (f32[16,4096]{1,0:T(8,128)S(1)}, f32[24,128]{1,0:T(8,128)S(1)}) custom-call(f32[32,16,128]{2,1,0:T(8,128)S(1)} %shard_map.99.refs_0_, f32[32,16,128]{2,1,0:T(8,128)S(1)} %collective-permute-done.8.refs_1_, f32[5,2,2,128,128]{4,3,2,1,0:T(8,128)S(1)} %copy-done, s32[5,32]{1,0:T(8,128)S(1)} %copy-done.3, s32[5,1,32]{2,1,0:T(1,128)S(1)} %copy-done.4, ...), custom_call_target="tpu_custom_call" | custom-call | flops 402653184 | bytes 8388608 | tf_op jit(solution)/shard_map/pallas_call | solution.py:245
  53.8 0.0 collective-permute-start.10
  53.8 0.0 collective-permute-done.11.other_gram_ref
  53.8 1.2 %collective-permute-done.10.other_ref = f32[24,128]{1,0:T(8,128)S(1)} collective-permute-done((f32[24,128]{1,0:T(8,128)S(1)}, f32[24,128]{1,0:T(8,128)S(1)}, u32[]{:S(2)}, u32[]{:S(2)}) %collective-permute-start.10) | collective-permute-done | bytes 12320 | tf_op jit(solution)/shard_map/ppermute | solution.py:380
  55.0 16.3 %all_to_all.10.got_ref = f32[16,40,128]{2,1,0:T(8,128)S(1)} all-to-all(f32[16,40,128]{2,1,0:T(8,128)S(1)} %shard_map.102), channel_id=1, replica_groups=mesh['y'=4,'core'=2,'x'=4,'z'=8] {'y','x'}, dimensions={0} | all-to-all | bytes 655360 | tf_op jit(solution)/shard_map/all_to_all | solution.py:400
  71.4 17.3 %all_to_all.11.refs_0_ = f32[8,56,128]{2,1,0:T(8,128)S(1)} all-to-all(f32[8,56,128]{2,1,0:T(8,128)S(1)} %shard_map.103), channel_id=1, replica_groups=mesh['y'=4,'core'=2,'x'=4,'z'=8] {'z'}, dimensions={0} | all-to-all | bytes 458752 | tf_op jit(solution)/shard_map/all_to_all | solution.py:401
  88.7 2.0 %shard_map.104 = (f32[2,8,8,16]{3,2,1,0:T(8,128)}, f32[2,8,4096]{2,1,0:T(8,128)}, f32[2,8,8]{2,1,0:T(8,128)}) custom-call(f32[8,56,128]{2,1,0:T(8,128)S(1)} %all_to_all.11.refs_0_, f32[16,4096]{1,0:T(8,128)S(1)} %get-tuple-element.19.refs_1_, bf16[256,4096]{1,0:T(8,128)(2,1)S(1)} %get-tuple-element.16.refs_7_.refs_2_, ...), custom_call_target="tpu_custom_call" | custom-call | flops 201326592 | bytes 6291456 | tf_op jit(solution)/shard_map/pallas_call | solution.py:361
  (7 shorter events, 0.1 us)
Async XLA Ops:
  3.1 9.7 %copy-start = (f32[5,2,2,128,128]{4,3,2,1,0:T(8,128)S(1)}, f32[5,2,2,128,128]{4,3,2,1,0:T(8,128)}, u32[]{:S(2)}) copy-start(f32[5,2,2,128,128]{4,3,2,1,0:T(8,128)} %refs_2_.9) | copy-start | bytes 3932164
  3.1 9.7 %copy-start.3 = (s32[5,32]{1,0:T(8,128)S(1)}, s32[5,32]{1,0:T(8,128)}, u32[]{:S(2)}) copy-start(s32[5,32]{1,0:T(8,128)} %refs_3_.9) | copy-start | bytes 1924
  3.1 9.7 %copy-start.4 = (s32[5,1,32]{2,1,0:T(1,128)S(1)}, s32[5,1,32]{2,1,0:T(1,128)}, u32[]{:S(2)}) copy-start(s32[5,1,32]{2,1,0:T(1,128)} %refs_4_.9) | copy-start | bytes 1924
  3.2 9.6 %collective-permute-start = (f32[32,16,128]{2,1,0:T(8,128)S(1)}, f32[32,16,128]{2,1,0:T(8,128)S(1)}, u32[]{:S(2)}, u32[]{:S(2)}) collective-permute-start(f32[32,16,128]{2,1,0:T(8,128)S(1)} %get-tuple-element.13.refs_0_), channel_id=1, source_target_pairs={{0,128},{64,192},{128,0},{192,64},{1,129},{65,193},{129,1},{193,65... | collective-permute-start | bytes 786440 | tf_op jit(solution)/shard_map/ppermute | solution.py:380
  9.7 1.3 %collective-permute-start.1 = (f32[128,128]{1,0:T(8,128)S(1)}, f32[128,128]{1,0:T(8,128)S(1)}, u32[]{:S(2)}, u32[]{:S(2)}) collective-permute-start(f32[128,128]{1,0:T(8,128)S(1)} %get-tuple-element.14), channel_id=1, source_target_pairs={{0,32},{32,0},{1,33},{33,1},{2,34},{34,2},{3,35},{35,3},{4,36},{36... | collective-permute-start | bytes 196616 | tf_op jit(solution)/shard_map/ppermute | solution.py:380
  13.3 7.3 %collective-permute-start.2 = (f32[32,16,128]{2,1,0:T(8,128)S(1)}, f32[32,16,128]{2,1,0:T(8,128)S(1)}, u32[]{:S(2)}, u32[]{:S(2)}) collective-permute-start(f32[32,16,128]{2,1,0:T(8,128)S(1)} %shard_map.96.refs_0_), channel_id=1, source_target_pairs={{0,64},{64,0},{128,192},{192,128},{1,65},{65,1},{129,193},{193,129... | collective-permute-start | bytes 786440 | tf_op jit(solution)/shard_map/ppermute | solution.py:380
  14.9 5.6 %collective-permute-start.3 = (f32[128,128]{1,0:T(8,128)S(1)}, f32[128,128]{1,0:T(8,128)S(1)}, u32[]{:S(2)}, u32[]{:S(2)}) collective-permute-start(f32[128,128]{1,0:T(8,128)S(1)} %add.15.refs_5_), channel_id=1, source_target_pairs={{0,2},{1,3},{2,0},{3,1},{4,6},{5,7},{6,4},{7,5},{8,10},{9,11},{10,... | collective-permute-start | bytes 196616 | tf_op jit(solution)/shard_map/ppermute | solution.py:380
  21.0 8.0 %collective-permute-start.4 = (f32[32,16,128]{2,1,0:T(8,128)S(1)}, f32[32,16,128]{2,1,0:T(8,128)S(1)}, u32[]{:S(2)}, u32[]{:S(2)}) collective-permute-start(f32[32,16,128]{2,1,0:T(8,128)S(1)} %shard_map.97.refs_0_), channel_id=1, source_target_pairs={{0,16},{8,24},{16,0},{24,8},{1,17},{9,25},{17,1},{25,9},{2,18},{10... | collective-permute-start | bytes 786440 | tf_op jit(solution)/shard_map/ppermute | solution.py:380
  23.2 4.3 %collective-permute-start.5 = (f32[128,128]{1,0:T(8,128)S(1)}, f32[128,128]{1,0:T(8,128)S(1)}, u32[]{:S(2)}, u32[]{:S(2)}) collective-permute-start(f32[128,128]{1,0:T(8,128)S(1)} %add.16.refs_5_), channel_id=1, source_target_pairs={{0,64},{64,0},{128,192},{192,128},{1,65},{65,1},{129,193},{193,129... | collective-permute-start | bytes 196616 | tf_op jit(solution)/shard_map/ppermute | solution.py:380
  27.5 22.2 %copy-start.2 = (bf16[2,32,128,128]{3,2,1,0:T(8,128)(2,1)S(1)}, bf16[2,32,128,128]{3,2,1,0:T(8,128)(2,1)}, u32[]{:S(2)}) copy-start(bf16[2,32,128,128]{3,2,1,0:T(8,128)(2,1)} %leaf_ref.3) | copy-start | bytes 6291460
  29.4 6.5 %collective-permute-start.6 = (f32[32,16,128]{2,1,0:T(8,128)S(1)}, f32[32,16,128]{2,1,0:T(8,128)S(1)}, u32[]{:S(2)}, u32[]{:S(2)}) collective-permute-start(f32[32,16,128]{2,1,0:T(8,128)S(1)} %shard_map.98.refs_0_), channel_id=1, source_target_pairs={{0,8},{8,0},{16,24},{24,16},{1,9},{9,1},{17,25},{25,17},{2,10},{10... | collective-permute-start | bytes 786440 | tf_op jit(solution)/shard_map/ppermute | solution.py:380
  30.0 5.8 %collective-permute-start.7 = (f32[128,128]{1,0:T(8,128)S(1)}, f32[128,128]{1,0:T(8,128)S(1)}, u32[]{:S(2)}, u32[]{:S(2)}) collective-permute-start(f32[128,128]{1,0:T(8,128)S(1)} %add.17.refs_5_), channel_id=1, source_target_pairs={{0,128},{64,192},{128,0},{192,64},{1,129},{65,193},{129,1},{193,65... | collective-permute-start | bytes 196616 | tf_op jit(solution)/shard_map/ppermute | solution.py:380
  35.8 15.1 %copy-start.1 = (bf16[2,32,128,128]{3,2,1,0:T(8,128)(2,1)S(1)}, bf16[2,32,128,128]{3,2,1,0:T(8,128)(2,1)}, u32[]{:S(2)}) copy-start(bf16[2,32,128,128]{3,2,1,0:T(8,128)(2,1)} %refs_6_.1) | copy-start | bytes 6291460
  36.4 14.6 %collective-permute-start.8 = (f32[32,16,128]{2,1,0:T(8,128)S(1)}, f32[32,16,128]{2,1,0:T(8,128)S(1)}, u32[]{:S(2)}, u32[]{:S(2)}) collective-permute-start(f32[32,16,128]{2,1,0:T(8,128)S(1)} %shard_map.99.refs_0_), channel_id=1, source_target_pairs={{0,4},{1,5},{2,6},{3,7},{4,0},{5,1},{6,2},{7,3},{8,12},{9,13},{10,... | collective-permute-start | bytes 786440 | tf_op jit(solution)/shard_map/ppermute | solution.py:380
  44.6 4.3 %collective-permute-start.9 = (f32[128,128]{1,0:T(8,128)S(1)}, f32[128,128]{1,0:T(8,128)S(1)}, u32[]{:S(2)}, u32[]{:S(2)}) collective-permute-start(f32[128,128]{1,0:T(8,128)S(1)} %add.18.refs_5_), channel_id=1, source_target_pairs={{0,8},{8,0},{16,24},{24,16},{1,9},{9,1},{17,25},{25,17},{2,10},{10... | collective-permute-start | bytes 196616 | tf_op jit(solution)/shard_map/ppermute | solution.py:380
  48.9 4.9 %collective-permute-start.11 = (f32[128,128]{1,0:T(8,128)S(1)}, f32[128,128]{1,0:T(8,128)S(1)}, u32[]{:S(2)}, u32[]{:S(2)}) collective-permute-start(f32[128,128]{1,0:T(8,128)S(1)} %add.19.refs_9_.gram_ref), channel_id=1, source_target_pairs={{0,1},{1,0},{2,3},{3,2},{4,5},{5,4},{6,7},{7,6},{8,9},{9,8},{10,11... | collective-permute-start | bytes 196616 | tf_op jit(solution)/shard_map/ppermute | solution.py:380
  53.8 1.2 %collective-permute-start.10 = (f32[24,128]{1,0:T(8,128)S(1)}, f32[24,128]{1,0:T(8,128)S(1)}, u32[]{:S(2)}, u32[]{:S(2)}) collective-permute-start(f32[24,128]{1,0:T(8,128)S(1)} %get-tuple-element.18.own_ref), channel_id=1, source_target_pairs={{0,32},{32,0},{1,33},{33,1},{2,34},{34,2},{3,35},{35,3},{4,36},{36... | collective-permute-start | bytes 36872 | tf_op jit(solution)/shard_map/ppermute | solution.py:380

commit v6 on v5

--- a/solution.py
+++ b/solution.py
@@ -263,11 +263,11 @@
 def merge_kernel(own_ref, other_ref, gram_ref, other_gram_ref, out_ref, gram_sum_ref):
     sums = own_ref[...] + other_ref[...]
     gram_sum_ref[...] = gram_ref[...] + other_gram_ref[...]
-    mine = lax.axis_index("y") * 2 + lax.rem(lax.axis_index("x"), 2)
-    piece = gram_sum_ref[pl.ds(pl.multiple_of(mine * 16, 16), 16), :]
+    mine = lax.rem(lax.axis_index("y"), 2) * 2 + lax.rem(lax.axis_index("x"), 2)
+    piece = gram_sum_ref[pl.ds(pl.multiple_of(mine * 32, 32), 32), :]
     for device in range(out_ref.shape[0]):
         out_ref[device, 0:24] = sums
-        out_ref[device, 24:40] = piece
+        out_ref[device, 24:56] = piece
 
 
 def merge(own, other, gram, other_gram):
@@ -275,7 +275,7 @@
         merge_kernel,
         in_specs=[VMEM] * 4,
         out_specs=VMEM,
-        out_shape=jax.ShapeDtypeStruct((lax.axis_size(("y", "x")), 40, 128), jnp.float32),
+        out_shape=jax.ShapeDtypeStruct((lax.axis_size(("y", "x")), 56, 128), jnp.float32),
         scratch_shapes=[pltpu.VMEM((128, 128), jnp.float32)],
         compiler_params=pltpu.CompilerParams(vmem_limit_bytes=KERNEL_VMEM),
     )(own, other, gram, other_gram)
@@ -283,23 +283,24 @@
 
 def relay_kernel(got_ref, out_ref, gram_ref):
     sums = jnp.sum(got_ref[:, 0:24], axis=0)
-    for piece in range(8):
-        at = piece // 2 * 4 + piece % 2
-        gram_ref[piece * 16 : (piece + 1) * 16] = got_ref[at, 24:40] + got_ref[at + 2, 24:40]
-    mine = lax.rem(lax.axis_index("z"), 4)
-    piece = gram_ref[pl.ds(pl.multiple_of(mine * 32, 32), 32), :]
     for device in range(out_ref.shape[0]):
-        out_ref[device, 0:24] = sums
-        out_ref[device, 24:56] = piece
+        out_ref[device] = sums
+    for quarter in range(4):
+        at = quarter // 2 * 4 + quarter % 2
+        gram_ref[quarter * 32 : (quarter + 1) * 32] = (got_ref[at, 24:56] + got_ref[at + 2, 24:56]) + (
+            got_ref[at + 8, 24:56] + got_ref[at + 10, 24:56]
+        )
 
 
 def relay(got):
     return pl.pallas_call(
         relay_kernel,
         in_specs=[VMEM],
-        out_specs=VMEM,
-        out_shape=jax.ShapeDtypeStruct((lax.axis_size("z"), 56, 128), jnp.float32),
-        scratch_shapes=[pltpu.VMEM((128, 128), jnp.float32)],
+        out_specs=[VMEM] * 2,
+        out_shape=[
+            jax.ShapeDtypeStruct((lax.axis_size("z"), 24, 128), jnp.float32),
+            jax.ShapeDtypeStruct((128, 128), jnp.float32),
+        ],
         compiler_params=pltpu.CompilerParams(vmem_limit_bytes=KERNEL_VMEM),
     )(got)
 
@@ -311,11 +312,9 @@
 
 
 def finish_kernel(
-    scale, got_ref, image_ref, high_ref, low_ref, total_ref, new_ref, block_ref, gram_ref
+    scale, got_ref, gram_ref, image_ref, high_ref, low_ref, total_ref, new_ref, block_ref
 ):
-    sums = jnp.sum(got_ref[:, 0:24], axis=0) * scale
-    for piece in range(4):
-        gram_ref[piece * 32 : (piece + 1) * 32] = got_ref[piece, 24:56] + got_ref[piece + 4, 24:56]
+    sums = jnp.sum(got_ref[...], axis=0) * scale
     first = sums[:16]
     packed = gram_ref[...] * scale
     row = lax.broadcasted_iota(jnp.int32, (128, 128), 0)
@@ -357,22 +356,21 @@
         total_ref[1, angle] = turned[8:, angle * 16 : (angle + 1) * 16]
 
 
-def finish(scale, got, image, parts):
+def finish(scale, got, gram, image, parts):
     return pl.pallas_call(
         lambda *refs: finish_kernel(scale, *refs),
-        in_specs=[VMEM] * 4,
+        in_specs=[VMEM] * 5,
         out_specs=[VMEM] * 3,
         out_shape=[
             jax.ShapeDtypeStruct((2, 8, 8, 16), jnp.float32),
             jax.ShapeDtypeStruct((2, 8, 4096), jnp.float32),
             jax.ShapeDtypeStruct((2, 8, 8), jnp.float32),
         ],
-        scratch_shapes=[pltpu.VMEM((128, 128), jnp.float32)],
         compiler_params=pltpu.CompilerParams(vmem_limit_bytes=KERNEL_VMEM),
         cost_estimate=pl.CostEstimate(
             flops=6 * 16 * 256 * 4096 * 2, bytes_accessed=6 << 20, transcendentals=0
         ),
-    )(got, image, *[in_vmem(part) for part in parts])
+    )(got, gram, image, *[in_vmem(part) for part in parts])
 
 
 def exchange(value, axis, bit_number):
@@ -384,7 +382,7 @@
     krylov_basis, near_field, leaf_in, leaf_out, level_mixers, block_ranks, partner_tables
 ):
     plan = [("y", 1), ("y", 0), ("x", 1), ("x", 0), ("z", 2)]
-    beside = [("core", 0), ("z", 1), ("y", 0), ("y", 1), ("x", 0)]
+    beside = [("core", 0), ("z", 1), ("z", 0), ("y", 0), ("x", 0)]
     coeffs, rows = leaves_in(krylov_basis, leaf_in, 4)
     gram, parts = basis_gram(krylov_basis)
     close = near_product(rows, near_field)
@@ -396,11 +394,11 @@
             coeffs = next_level(*operands, gram)
         else:
             image, sums = project(*operands, close, leaf_out, parts, gram)
-    got = merge(sums, exchange(sums, "core", 0), gram, exchange(gram, "z", 0))
-    got = relay(lax.all_to_all(got, ("y", "x"), 0, 0))
+    got = merge(sums, exchange(sums, "core", 0), gram, exchange(gram, "z", 2))
+    got, gram = relay(lax.all_to_all(got, ("y", "x"), 0, 0))
     got = lax.all_to_all(got, "z", 0, 0)
     scale = 1.0 / (krylov_basis.shape[3] * lax.axis_size(AXES))
-    total, new_block, block_gram = finish(scale, got, image, parts)
+    total, new_block, block_gram = finish(scale, got, gram, image, parts)
     return jnp.transpose(total, (3, 0, 1, 2)), new_block, block_gram
 
 

time: 91 us -> 91.9 us (level)
  waiting for transfers between devices: 17.4 us -> 21.6 us
  starting transfers between devices: 25.7 us -> 23.7 us
  blocking collectives: 33.6 us -> 32.5 us
    ppermute x12, waiting for transfers between devices: 17.4 us -> 21.6 us  [exchange(): return lax.ppermute(value, axis, pairs)]
    ppermute x12, starting transfers between devices: 25.7 us -> 23.7 us  [exchange(): return lax.ppermute(value, axis, pairs)]
  transfers between devices with their start and end apart: 12 -> 12, of which waited for: 9 -> 10; matrix products, arithmetic and copies ran while one was open for 0% -> 0% of each run, Pallas kernels for 7% -> 7%
where the time goes in v6:
time: 91.9 us; the launch traced here: 91.7 us
  blocking collectives  32.5 us (35%)
  starting transfers between devices  23.7 us (26%)
  waiting for transfers between devices  21.6 us (24%)
  Pallas kernels  13.1 us (14%)
    ppermute x12, starting transfers between devices, exchange(): return lax.ppermute(value, axis, pairs)  23.7 us
    ppermute x12, waiting for transfers between devices, exchange(): return lax.ppermute(value, axis, pairs)  21.6 us
    all_to_all x1, blocking collectives, per_device(): got = lax.all_to_all(got, 'z', 0, 0)  16.5 us
    all_to_all x1, blocking collectives, per_device(): got, gram = relay(lax.all_to_all(got, ('y', 'x'), 0, 0))  15.9 us
    pallas_call x1, Pallas kernels, basis_gram(): pl.pallas_call(basis_gram_kernel, in_specs=[pl.BlockSpec(memory_space=plt...  3.23 us
    pallas_call x1, Pallas kernels, project(): pl.pallas_call(lambda *refs: project_kernel(level, *refs), in_specs=[VMEM...  2.83 us
    pallas_call x1, Pallas kernels, leaves_in(): pl.pallas_call(leaves_in_kernel, in_specs=[pl.BlockSpec(memory_space=pltp...  2.48 us
    pallas_call x1, Pallas kernels, finish(): pl.pallas_call(lambda *refs: finish_kernel(scale, *refs), in_specs=[VMEM]...  2.04 us
  transfers between devices with their start and end apart: 12, of which 10 were waited for; matrix products, arithmetic and copies ran while one was open for 0% of the time, Pallas kernels for 7%

profile of v6, /device:TPU:2, one launch (start us, length us, event | category | flops | bytes accessed | tf_op | source)
XLA Modules:
  0.0 91.7 jit_solution(16191607453783134694)
XLA Ops:
  0.6 2.5 %shard_map.94 = (f32[32,16,128]{2,1,0:T(8,128)S(1)}, f32[32,16,128]{2,1,0:T(8,128)S(1)}) custom-call(f32[16,2,8,4096]{3,2,1,0:T(8,128)} %basis_ref.3, bf16[2,32,128,128]{3,2,1,0:T(8,128)(2,1)} %leaf_ref.2), custom_call_target="tpu_custom_call" | custom-call | flops 33554432 | bytes 2359296 | tf_op jit(solution)/shard_map/pallas_call | solution.py:82
  3.1 0.0 copy-start
  3.1 0.0 copy-start.3
  3.1 0.0 copy-start.4
  3.2 3.3 %collective-permute-start = (f32[32,16,128]{2,1,0:T(8,128)S(1)}, f32[32,16,128]{2,1,0:T(8,128)S(1)}, u32[]{:S(2)}, u32[]{:S(2)}) collective-permute-start(f32[32,16,128]{2,1,0:T(8,128)S(1)} %get-tuple-element.15.refs_0_), channel_id=1, source_target_pairs={{0,128},{64,192},{128,0},{192,64},{1,129},{65,193},{129,1},{193,65... | collective-permute-start | bytes 786440 | tf_op jit(solution)/shard_map/ppermute | solution.py:378
  6.4 3.2 %shard_map.95 = (f32[128,128]{1,0:T(8,128)S(1)}, bf16[256,4096]{1,0:T(8,128)(2,1)S(1)}, bf16[256,4096]{1,0:T(8,128)(2,1)S(1)}) custom-call(f32[16,2,8,4096]{3,2,1,0:T(8,128)} %basis_ref.3), custom_call_target="tpu_custom_call" | custom-call | flops 1073741824 | bytes 8388608 | tf_op jit(solution)/shard_map/pallas_call | solution.py:157
  9.7 0.1 collective-permute-start.1
  9.8 1.2 %collective-permute-done.1 = f32[128,128]{1,0:T(8,128)S(1)} collective-permute-done((f32[128,128]{1,0:T(8,128)S(1)}, f32[128,128]{1,0:T(8,128)S(1)}, u32[]{:S(2)}, u32[]{:S(2)}) %collective-permute-start.1) | collective-permute-done | bytes 65568 | tf_op jit(solution)/shard_map/ppermute | solution.py:378
  11.0 1.8 %collective-permute-done.refs_1_ = f32[32,16,128]{2,1,0:T(8,128)S(1)} collective-permute-done((f32[32,16,128]{2,1,0:T(8,128)S(1)}, f32[32,16,128]{2,1,0:T(8,128)S(1)}, u32[]{:S(2)}, u32[]{:S(2)}) %collective-permute-start) | collective-permute-done | bytes 262176 | tf_op jit(solution)/shard_map/ppermute | solution.py:378
  12.8 0.0 copy-done
  12.8 0.0 copy-done.3
  12.8 0.0 copy-done.4
  12.8 0.5 shard_map.96.refs_0_
  13.3 1.7 %collective-permute-start.2 = (f32[32,16,128]{2,1,0:T(8,128)S(1)}, f32[32,16,128]{2,1,0:T(8,128)S(1)}, u32[]{:S(2)}, u32[]{:S(2)}) collective-permute-start(f32[32,16,128]{2,1,0:T(8,128)S(1)} %shard_map.96.refs_0_), channel_id=1, source_target_pairs={{0,64},{64,0},{128,192},{192,128},{1,65},{65,1},{129,193},{193,129... | collective-permute-start | bytes 786440 | tf_op jit(solution)/shard_map/ppermute | solution.py:378
  14.9 3.3 %collective-permute-start.3 = (f32[128,128]{1,0:T(8,128)S(1)}, f32[128,128]{1,0:T(8,128)S(1)}, u32[]{:S(2)}, u32[]{:S(2)}) collective-permute-start(f32[128,128]{1,0:T(8,128)S(1)} %add.15.refs_5_), channel_id=1, source_target_pairs={{0,2},{1,3},{2,0},{3,1},{4,6},{5,7},{6,4},{7,5},{8,10},{9,11},{10,... | collective-permute-start | bytes 196616 | tf_op jit(solution)/shard_map/ppermute | solution.py:378
  18.2 2.3 %collective-permute-done.3 = f32[128,128]{1,0:T(8,128)S(1)} collective-permute-done((f32[128,128]{1,0:T(8,128)S(1)}, f32[128,128]{1,0:T(8,128)S(1)}, u32[]{:S(2)}, u32[]{:S(2)}) %collective-permute-start.3) | collective-permute-done | bytes 65568 | tf_op jit(solution)/shard_map/ppermute | solution.py:378
  20.5 0.0 collective-permute-done.2.refs_1_
  20.5 0.5 shard_map.97.refs_0_
  21.0 2.2 %collective-permute-start.4 = (f32[32,16,128]{2,1,0:T(8,128)S(1)}, f32[32,16,128]{2,1,0:T(8,128)S(1)}, u32[]{:S(2)}, u32[]{:S(2)}) collective-permute-start(f32[32,16,128]{2,1,0:T(8,128)S(1)} %shard_map.97.refs_0_), channel_id=1, source_target_pairs={{0,16},{8,24},{16,0},{24,8},{1,17},{9,25},{17,1},{25,9},{2,18},{10... | collective-permute-start | bytes 786440 | tf_op jit(solution)/shard_map/ppermute | solution.py:378
  23.2 1.9 %collective-permute-start.5 = (f32[128,128]{1,0:T(8,128)S(1)}, f32[128,128]{1,0:T(8,128)S(1)}, u32[]{:S(2)}, u32[]{:S(2)}) collective-permute-start(f32[128,128]{1,0:T(8,128)S(1)} %add.16.refs_5_), channel_id=1, source_target_pairs={{0,1},{1,0},{2,3},{3,2},{4,5},{5,4},{6,7},{7,6},{8,9},{9,8},{10,11... | collective-permute-start | bytes 196616 | tf_op jit(solution)/shard_map/ppermute | solution.py:378
  25.1 2.3 %collective-permute-done.5 = f32[128,128]{1,0:T(8,128)S(1)} collective-permute-done((f32[128,128]{1,0:T(8,128)S(1)}, f32[128,128]{1,0:T(8,128)S(1)}, u32[]{:S(2)}, u32[]{:S(2)}) %collective-permute-start.5) | collective-permute-done | bytes 65568 | tf_op jit(solution)/shard_map/ppermute | solution.py:378
  27.5 0.0 copy-start.2
  27.5 1.5 %collective-permute-done.4.refs_1_ = f32[32,16,128]{2,1,0:T(8,128)S(1)} collective-permute-done((f32[32,16,128]{2,1,0:T(8,128)S(1)}, f32[32,16,128]{2,1,0:T(8,128)S(1)}, u32[]{:S(2)}, u32[]{:S(2)}) %collective-permute-start.4) | collective-permute-done | bytes 262176 | tf_op jit(solution)/shard_map/ppermute | solution.py:378
  29.0 0.5 shard_map.98.refs_0_
  29.4 0.6 collective-permute-start.6
  30.0 1.6 %collective-permute-start.7 = (f32[128,128]{1,0:T(8,128)S(1)}, f32[128,128]{1,0:T(8,128)S(1)}, u32[]{:S(2)}, u32[]{:S(2)}) collective-permute-start(f32[128,128]{1,0:T(8,128)S(1)} %add.17.refs_5_), channel_id=1, source_target_pairs={{0,64},{64,0},{128,192},{192,128},{1,65},{65,1},{129,193},{193,129... | collective-permute-start | bytes 196616 | tf_op jit(solution)/shard_map/ppermute | solution.py:378
  31.6 2.7 %collective-permute-done.7 = f32[128,128]{1,0:T(8,128)S(1)} collective-permute-done((f32[128,128]{1,0:T(8,128)S(1)}, f32[128,128]{1,0:T(8,128)S(1)}, u32[]{:S(2)}, u32[]{:S(2)}) %collective-permute-start.7) | collective-permute-done | bytes 65568 | tf_op jit(solution)/shard_map/ppermute | solution.py:378
  34.3 0.0 copy-start.1
  34.3 1.6 %collective-permute-done.6.refs_1_ = f32[32,16,128]{2,1,0:T(8,128)S(1)} collective-permute-done((f32[32,16,128]{2,1,0:T(8,128)S(1)}, f32[32,16,128]{2,1,0:T(8,128)S(1)}, u32[]{:S(2)}, u32[]{:S(2)}) %collective-permute-start.6) | collective-permute-done | bytes 262176 | tf_op jit(solution)/shard_map/ppermute | solution.py:378
  35.9 0.5 shard_map.99.refs_0_
  36.3 8.3 %collective-permute-start.8 = (f32[32,16,128]{2,1,0:T(8,128)S(1)}, f32[32,16,128]{2,1,0:T(8,128)S(1)}, u32[]{:S(2)}, u32[]{:S(2)}) collective-permute-start(f32[32,16,128]{2,1,0:T(8,128)S(1)} %shard_map.99.refs_0_), channel_id=1, source_target_pairs={{0,4},{1,5},{2,6},{3,7},{4,0},{5,1},{6,2},{7,3},{8,12},{9,13},{10,... | collective-permute-start | bytes 786440 | tf_op jit(solution)/shard_map/ppermute | solution.py:378
  44.6 0.6 collective-permute-start.9
  45.2 3.7 %collective-permute-done.9 = f32[128,128]{1,0:T(8,128)S(1)} collective-permute-done((f32[128,128]{1,0:T(8,128)S(1)}, f32[128,128]{1,0:T(8,128)S(1)}, u32[]{:S(2)}, u32[]{:S(2)}) %collective-permute-start.9) | collective-permute-done | bytes 65568 | tf_op jit(solution)/shard_map/ppermute | solution.py:378
  48.9 0.2 collective-permute-start.11
  49.1 0.0 copy-done.2
  49.1 0.6 shard_map.100.refs_5_
  49.7 2.5 %collective-permute-done.8.refs_1_ = f32[32,16,128]{2,1,0:T(8,128)S(1)} collective-permute-done((f32[32,16,128]{2,1,0:T(8,128)S(1)}, f32[32,16,128]{2,1,0:T(8,128)S(1)}, u32[]{:S(2)}, u32[]{:S(2)}) %collective-permute-start.8) | collective-permute-done | bytes 262176 | tf_op jit(solution)/shard_map/ppermute | solution.py:378
  52.3 0.0 copy-done.1
  52.3 2.8 %shard_map.101 = (f32[16,4096]{1,0:T(8,128)S(1)}, f32[24,128]{1,0:T(8,128)S(1)}) custom-call(f32[32,16,128]{2,1,0:T(8,128)S(1)} %shard_map.99.refs_0_, f32[32,16,128]{2,1,0:T(8,128)S(1)} %collective-permute-done.8.refs_1_, f32[5,2,2,128,128]{4,3,2,1,0:T(8,128)S(1)} %copy-done, s32[5,32]{1,0:T(8,128)S(1)} %copy-done.3, s32[5,1,32]{2,1,0:T(1,128)S(1)} %copy-done.4, ...), custom_call_target="tpu_custom_call" | custom-call | flops 402653184 | bytes 8388608 | tf_op jit(solution)/shard_map/pallas_call | solution.py:245
  55.1 0.0 collective-permute-start.10
  55.1 2.0 %collective-permute-done.11.other_gram_ref = f32[128,128]{1,0:T(8,128)S(1)} collective-permute-done((f32[128,128]{1,0:T(8,128)S(1)}, f32[128,128]{1,0:T(8,128)S(1)}, u32[]{:S(2)}, u32[]{:S(2)}) %collective-permute-start.11) | collective-permute-done | bytes 65568 | tf_op jit(solution)/shard_map/ppermute | solution.py:378
  57.2 0.0 collective-permute-done.10.other_ref
  57.2 15.9 %all_to_all.10.got_ref = f32[16,56,128]{2,1,0:T(8,128)S(1)} all-to-all(f32[16,56,128]{2,1,0:T(8,128)S(1)} %shard_map.102), channel_id=1, replica_groups=mesh['y'=4,'core'=2,'x'=4,'z'=8] {'y','x'}, dimensions={0} | all-to-all | bytes 917504 | tf_op jit(solution)/shard_map/all_to_all | solution.py:398
  73.2 16.5 %all_to_all.11.refs_0_ = f32[8,24,128]{2,1,0:T(8,128)S(1)} all-to-all(f32[8,24,128]{2,1,0:T(8,128)S(1)} %get-tuple-element.21), channel_id=1, replica_groups=mesh['y'=4,'core'=2,'x'=4,'z'=8] {'z'}, dimensions={0} | all-to-all | bytes 196608 | tf_op jit(solution)/shard_map/all_to_all | solution.py:399
  89.7 2.0 %shard_map.104 = (f32[2,8,8,16]{3,2,1,0:T(8,128)}, f32[2,8,4096]{2,1,0:T(8,128)}, f32[2,8,8]{2,1,0:T(8,128)}) custom-call(f32[8,24,128]{2,1,0:T(8,128)S(1)} %all_to_all.11.refs_0_, f32[128,128]{1,0:T(8,128)S(1)} %get-tuple-element.22.refs_1_, f32[16,4096]{1,0:T(8,128)S(1)} %get-tuple-element.23.refs_2_, ...), custom_call_target="tpu_custom_call" | custom-call | flops 201326592 | bytes 6291456 | tf_op jit(solution)/shard_map/pallas_call | solution.py:360
  (7 shorter events, 0.1 us)
Async XLA Ops:
  3.1 9.7 %copy-start = (f32[5,2,2,128,128]{4,3,2,1,0:T(8,128)S(1)}, f32[5,2,2,128,128]{4,3,2,1,0:T(8,128)}, u32[]{:S(2)}) copy-start(f32[5,2,2,128,128]{4,3,2,1,0:T(8,128)} %refs_2_.9) | copy-start | bytes 3932164
  3.1 9.7 %copy-start.3 = (s32[5,32]{1,0:T(8,128)S(1)}, s32[5,32]{1,0:T(8,128)}, u32[]{:S(2)}) copy-start(s32[5,32]{1,0:T(8,128)} %refs_3_.9) | copy-start | bytes 1924
  3.1 9.7 %copy-start.4 = (s32[5,1,32]{2,1,0:T(1,128)S(1)}, s32[5,1,32]{2,1,0:T(1,128)}, u32[]{:S(2)}) copy-start(s32[5,1,32]{2,1,0:T(1,128)} %refs_4_.9) | copy-start | bytes 1924
  3.2 9.6 %collective-permute-start = (f32[32,16,128]{2,1,0:T(8,128)S(1)}, f32[32,16,128]{2,1,0:T(8,128)S(1)}, u32[]{:S(2)}, u32[]{:S(2)}) collective-permute-start(f32[32,16,128]{2,1,0:T(8,128)S(1)} %get-tuple-element.15.refs_0_), channel_id=1, source_target_pairs={{0,128},{64,192},{128,0},{192,64},{1,129},{65,193},{129,1},{193,65... | collective-permute-start | bytes 786440 | tf_op jit(solution)/shard_map/ppermute | solution.py:378
  9.7 1.3 %collective-permute-start.1 = (f32[128,128]{1,0:T(8,128)S(1)}, f32[128,128]{1,0:T(8,128)S(1)}, u32[]{:S(2)}, u32[]{:S(2)}) collective-permute-start(f32[128,128]{1,0:T(8,128)S(1)} %get-tuple-element.16), channel_id=1, source_target_pairs={{0,32},{32,0},{1,33},{33,1},{2,34},{34,2},{3,35},{35,3},{4,36},{36... | collective-permute-start | bytes 196616 | tf_op jit(solution)/shard_map/ppermute | solution.py:378
  13.3 7.3 %collective-permute-start.2 = (f32[32,16,128]{2,1,0:T(8,128)S(1)}, f32[32,16,128]{2,1,0:T(8,128)S(1)}, u32[]{:S(2)}, u32[]{:S(2)}) collective-permute-start(f32[32,16,128]{2,1,0:T(8,128)S(1)} %shard_map.96.refs_0_), channel_id=1, source_target_pairs={{0,64},{64,0},{128,192},{192,128},{1,65},{65,1},{129,193},{193,129... | collective-permute-start | bytes 786440 | tf_op jit(solution)/shard_map/ppermute | solution.py:378
  14.9 5.6 %collective-permute-start.3 = (f32[128,128]{1,0:T(8,128)S(1)}, f32[128,128]{1,0:T(8,128)S(1)}, u32[]{:S(2)}, u32[]{:S(2)}) collective-permute-start(f32[128,128]{1,0:T(8,128)S(1)} %add.15.refs_5_), channel_id=1, source_target_pairs={{0,2},{1,3},{2,0},{3,1},{4,6},{5,7},{6,4},{7,5},{8,10},{9,11},{10,... | collective-permute-start | bytes 196616 | tf_op jit(solution)/shard_map/ppermute | solution.py:378
  21.0 8.0 %collective-permute-start.4 = (f32[32,16,128]{2,1,0:T(8,128)S(1)}, f32[32,16,128]{2,1,0:T(8,128)S(1)}, u32[]{:S(2)}, u32[]{:S(2)}) collective-permute-start(f32[32,16,128]{2,1,0:T(8,128)S(1)} %shard_map.97.refs_0_), channel_id=1, source_target_pairs={{0,16},{8,24},{16,0},{24,8},{1,17},{9,25},{17,1},{25,9},{2,18},{10... | collective-permute-start | bytes 786440 | tf_op jit(solution)/shard_map/ppermute | solution.py:378
  23.2 4.3 %collective-permute-start.5 = (f32[128,128]{1,0:T(8,128)S(1)}, f32[128,128]{1,0:T(8,128)S(1)}, u32[]{:S(2)}, u32[]{:S(2)}) collective-permute-start(f32[128,128]{1,0:T(8,128)S(1)} %add.16.refs_5_), channel_id=1, source_target_pairs={{0,1},{1,0},{2,3},{3,2},{4,5},{5,4},{6,7},{7,6},{8,9},{9,8},{10,11... | collective-permute-start | bytes 196616 | tf_op jit(solution)/shard_map/ppermute | solution.py:378
  27.5 21.6 %copy-start.2 = (bf16[2,32,128,128]{3,2,1,0:T(8,128)(2,1)S(1)}, bf16[2,32,128,128]{3,2,1,0:T(8,128)(2,1)}, u32[]{:S(2)}) copy-start(bf16[2,32,128,128]{3,2,1,0:T(8,128)(2,1)} %leaf_ref.3) | copy-start | bytes 6291460
  29.4 6.5 %collective-permute-start.6 = (f32[32,16,128]{2,1,0:T(8,128)S(1)}, f32[32,16,128]{2,1,0:T(8,128)S(1)}, u32[]{:S(2)}, u32[]{:S(2)}) collective-permute-start(f32[32,16,128]{2,1,0:T(8,128)S(1)} %shard_map.98.refs_0_), channel_id=1, source_target_pairs={{0,8},{8,0},{16,24},{24,16},{1,9},{9,1},{17,25},{25,17},{2,10},{10... | collective-permute-start | bytes 786440 | tf_op jit(solution)/shard_map/ppermute | solution.py:378
  30.0 4.3 %collective-permute-start.7 = (f32[128,128]{1,0:T(8,128)S(1)}, f32[128,128]{1,0:T(8,128)S(1)}, u32[]{:S(2)}, u32[]{:S(2)}) collective-permute-start(f32[128,128]{1,0:T(8,128)S(1)} %add.17.refs_5_), channel_id=1, source_target_pairs={{0,64},{64,0},{128,192},{192,128},{1,65},{65,1},{129,193},{193,129... | collective-permute-start | bytes 196616 | tf_op jit(solution)/shard_map/ppermute | solution.py:378
  34.3 18.0 %copy-start.1 = (bf16[2,32,128,128]{3,2,1,0:T(8,128)(2,1)S(1)}, bf16[2,32,128,128]{3,2,1,0:T(8,128)(2,1)}, u32[]{:S(2)}) copy-start(bf16[2,32,128,128]{3,2,1,0:T(8,128)(2,1)} %refs_6_.1) | copy-start | bytes 6291460
  36.3 15.9 %collective-permute-start.8 = (f32[32,16,128]{2,1,0:T(8,128)S(1)}, f32[32,16,128]{2,1,0:T(8,128)S(1)}, u32[]{:S(2)}, u32[]{:S(2)}) collective-permute-start(f32[32,16,128]{2,1,0:T(8,128)S(1)} %shard_map.99.refs_0_), channel_id=1, source_target_pairs={{0,4},{1,5},{2,6},{3,7},{4,0},{5,1},{6,2},{7,3},{8,12},{9,13},{10,... | collective-permute-start | bytes 786440 | tf_op jit(solution)/shard_map/ppermute | solution.py:378
  44.6 4.3 %collective-permute-start.9 = (f32[128,128]{1,0:T(8,128)S(1)}, f32[128,128]{1,0:T(8,128)S(1)}, u32[]{:S(2)}, u32[]{:S(2)}) collective-permute-start(f32[128,128]{1,0:T(8,128)S(1)} %add.18.refs_5_), channel_id=1, source_target_pairs={{0,8},{8,0},{16,24},{24,16},{1,9},{9,1},{17,25},{25,17},{2,10},{10... | collective-permute-start | bytes 196616 | tf_op jit(solution)/shard_map/ppermute | solution.py:378
  48.9 8.3 %collective-permute-start.11 = (f32[128,128]{1,0:T(8,128)S(1)}, f32[128,128]{1,0:T(8,128)S(1)}, u32[]{:S(2)}, u32[]{:S(2)}) collective-permute-start(f32[128,128]{1,0:T(8,128)S(1)} %add.19.refs_9_.gram_ref), channel_id=1, source_target_pairs={{0,4},{1,5},{2,6},{3,7},{4,0},{5,1},{6,2},{7,3},{8,12},{9,13},{10,... | collective-permute-start | bytes 196616 | tf_op jit(solution)/shard_map/ppermute | solution.py:378
  55.1 2.1 %collective-permute-start.10 = (f32[24,128]{1,0:T(8,128)S(1)}, f32[24,128]{1,0:T(8,128)S(1)}, u32[]{:S(2)}, u32[]{:S(2)}) collective-permute-start(f32[24,128]{1,0:T(8,128)S(1)} %get-tuple-element.20.own_ref), channel_id=1, source_target_pairs={{0,32},{32,0},{1,33},{33,1},{2,34},{34,2},{3,35},{35,3},{4,36},{36... | collective-permute-start | bytes 36872 | tf_op jit(solution)/shard_map/ppermute | solution.py:378

commit v7 on v6

--- a/solution.py
+++ b/solution.py
@@ -12,6 +12,7 @@
 VMEM = pl.BlockSpec(memory_space=pltpu.VMEM)
 ANYWHERE = pl.BlockSpec(memory_space=pl.ANY)
 BASIS_PARTS = 4
+LEVEL_FLOPS = 1_000_000_000
 AXES = ("y", "core", "x", "z")
 
 
@@ -43,6 +44,18 @@
     )
 
 
+def times_i(rows):
+    turned = pltpu.roll(rows, 4, 0)
+    upper = lax.broadcasted_iota(jnp.int32, rows.shape, 0) < 4
+    return jnp.where(upper, -turned, turned)
+
+
+def halves(rows):
+    return [
+        jnp.concatenate([rows[at : at + 4], rows[8 + at : 12 + at]], axis=0) for at in (0, 4)
+    ]
+
+
 def leaf_product(rows, real, imag):
     return dot_nt(
         complex_rows(rows).astype(jnp.bfloat16), jnp.concatenate([real, imag], axis=1)
@@ -50,7 +63,7 @@
 
 
 def leaves_in_kernel(
-    basis_ref, leaf_ref, out_ref, rows_ref, newest_ref, held_ref, newest_sem, held_sems
+    basis_ref, leaf_ref, first_ref, second_ref, rows_ref, newest_ref, held_ref, newest_sem, held_sems
 ):
     steps = held_sems.shape[0]
     count = held_ref.shape[1]
@@ -73,17 +86,24 @@
         rows = newest_ref[:, :, leaf * 128 : (leaf + 1) * 128].reshape(16, 128)
         rows = rows.astype(jnp.bfloat16).astype(jnp.float32)
         rows_ref[leaf] = rows
-        out_ref[leaf] = leaf_product(rows, held_ref[0, leaf], held_ref[1, leaf])
+        both = [jnp.concatenate([half, times_i(half)], axis=1) for half in halves(rows)]
+        product = dot_nt(
+            jnp.concatenate(both, axis=0).astype(jnp.bfloat16),
+            jnp.concatenate([held_ref[0, leaf], held_ref[1, leaf]], axis=1),
+        )
+        first_ref[leaf] = product[:8]
+        second_ref[leaf] = product[8:]
 
 
 def leaves_in(krylov_basis, leaves, steps):
     count = leaves.shape[1]
+    half = jax.ShapeDtypeStruct((count, 8, 128), jnp.float32)
     rows = jax.ShapeDtypeStruct((count, 16, 128), jnp.float32)
     return pl.pallas_call(
         leaves_in_kernel,
         in_specs=[pl.BlockSpec(memory_space=pltpu.HBM)] * 2,
-        out_specs=[VMEM] * 2,
-        out_shape=[rows, rows],
+        out_specs=[VMEM] * 3,
+        out_shape=[half, half, rows],
         scratch_shapes=[
             pltpu.VMEM(krylov_basis.shape[1:], jnp.float32),
             pltpu.VMEM(leaves.shape, leaves.dtype),
@@ -97,22 +117,22 @@
     )(in_hbm(krylov_basis), in_hbm(leaves))
 
 
-def near_kernel(rows_ref, leaf_ref, out_ref):
+def near_kernel(rows_ref, leaf_ref, before_ref, out_ref):
     for leaf in range(rows_ref.shape[0]):
         out_ref[leaf] = leaf_product(rows_ref[leaf], leaf_ref[0, leaf], leaf_ref[1, leaf])
 
 
-def near_product(rows, near_field):
+def near_product(rows, near_field, before):
     return pl.pallas_call(
         near_kernel,
-        in_specs=[VMEM] * 2,
+        in_specs=[VMEM] * 2 + [ANYWHERE],
         out_specs=VMEM,
         out_shape=jax.ShapeDtypeStruct(rows.shape, jnp.float32),
         compiler_params=pltpu.CompilerParams(vmem_limit_bytes=KERNEL_VMEM),
         cost_estimate=pl.CostEstimate(
             flops=rows.shape[0] * 16 * 256 * 128 * 2, bytes_accessed=2 << 20, transcendentals=0
         ),
-    )(rows, near_field)
+    )(rows, near_field, before)
 
 
 def stacked(basis):
@@ -122,24 +142,13 @@
     )
 
 
-def basis_gram_kernel(basis_ref, out_ref, high_ref, low_ref, held_ref, sems):
-    steps = sems.shape[0]
-    width = held_ref.shape[3] // steps
-    copies = []
-    for step in range(steps):
-        here = pl.ds(step * width, width)
-        copies.append(
-            pltpu.make_async_copy(
-                basis_ref.at[:, :, :, here], held_ref.at[:, :, :, here], sems.at[step]
-            )
-        )
-        copies[-1].start()
+def basis_gram_kernel(basis_ref, before_ref, out_ref, high_ref, low_ref):
+    width = basis_ref.shape[3] // BASIS_PARTS
     even = jnp.zeros((256, 256), jnp.float32)
     odd = jnp.zeros((256, 256), jnp.float32)
-    for step, copy in enumerate(copies):
-        copy.wait()
+    for step in range(BASIS_PARTS):
         here = slice(step * width, (step + 1) * width)
-        high, low = split2(stacked(held_ref[:, :, :, here]))
+        high, low = split2(stacked(basis_ref[:, :, :, here]))
         high_ref[:, here] = high
         low_ref[:, here] = low
         even += dot_nt(high, high)
@@ -152,29 +161,24 @@
     out_ref[...] = jnp.where(row <= column, real, imag)
 
 
-def basis_gram(krylov_basis):
+def basis_gram(krylov_basis, before):
     part = pltpu.VMEM((256, krylov_basis.shape[3]), jnp.bfloat16)
     gram, *parts = pl.pallas_call(
         basis_gram_kernel,
-        in_specs=[pl.BlockSpec(memory_space=pltpu.HBM)],
+        in_specs=[VMEM, ANYWHERE],
         out_specs=[VMEM] * 3,
         out_shape=[jax.ShapeDtypeStruct((128, 128), jnp.float32), part, part],
-        scratch_shapes=[
-            pltpu.VMEM(krylov_basis.shape, jnp.float32),
-            pltpu.SemaphoreType.DMA((BASIS_PARTS,)),
-        ],
         compiler_params=pltpu.CompilerParams(vmem_limit_bytes=KERNEL_VMEM),
         cost_estimate=pl.CostEstimate(
             flops=2 * 2 * 256 * 256 * 4096, bytes_accessed=8 << 20, transcendentals=0
         ),
-    )(in_hbm(krylov_basis))
+    )(in_vmem(krylov_basis), before)
     return gram, parts
 
 
 def mix(level, own_ref, partner_ref, mixer_ref, rank_ref, table_ref):
     table = table_ref[level]
     picked = jnp.concatenate([partner_ref[table[0, leaf]] for leaf in range(32)], axis=0)
-    both = jnp.concatenate([own_ref[...].reshape(512, 128), picked], axis=1)
     weights = jnp.concatenate(
         [
             jnp.concatenate([mixer_ref[level, 0, 0], mixer_ref[level, 0, 1]], axis=1),
@@ -182,47 +186,49 @@
         ],
         axis=0,
     )
-    high, low = split2(both)
+    high, low = split2(jnp.concatenate([own_ref[...].reshape(256, 128), picked], axis=1))
     w_high, w_low = split2(weights)
     product = dot_nn(high, w_high) + dot_nn(high, w_low) + dot_nn(low, w_high)
-    column = lax.broadcasted_iota(jnp.int32, (16, 128), 1)
+    column = lax.broadcasted_iota(jnp.int32, (8, 128), 1)
     ranks = rank_ref[level : level + 1]
 
     def leaf_value(leaf):
-        by_real = product[leaf * 16 : (leaf + 1) * 16, :128]
-        by_imag = product[leaf * 16 : (leaf + 1) * 16, 128:]
-        mixed = jnp.concatenate([by_real[:8] - by_imag[8:], by_real[8:] + by_imag[:8]], axis=0)
+        at = leaf * 8
+        mixed = product[at : at + 8, :128] + times_i(product[at : at + 8, 128:])
         return jnp.where(column < ranks[0, leaf], mixed, 0.0)
 
     return leaf_value
 
 
-def level_kernel(level, own_ref, partner_ref, mixer_ref, rank_ref, table_ref, gram_ref, out_ref):
+def level_kernel(level, own_ref, partner_ref, mixer_ref, rank_ref, table_ref, *refs):
+    out_ref = refs[-1]
     leaf_value = mix(level, own_ref, partner_ref, mixer_ref, rank_ref, table_ref)
     for leaf in range(32):
         out_ref[leaf] = leaf_value(leaf)
 
 
-def next_level(level, own, partner, level_mixers, block_ranks, partner_tables, gram):
+def next_level(level, own, partner, tables, before):
     return pl.pallas_call(
         lambda *refs: level_kernel(level, *refs),
-        in_specs=[VMEM] * 5 + [ANYWHERE],
+        in_specs=[VMEM] * 5 + [ANYWHERE] * len(before),
         out_specs=VMEM,
         out_shape=jax.ShapeDtypeStruct(own.shape, jnp.float32),
         compiler_params=pltpu.CompilerParams(vmem_limit_bytes=KERNEL_VMEM),
         cost_estimate=pl.CostEstimate(
-            flops=3 * 512 * 256 * 256 * 2, bytes_accessed=1 << 20, transcendentals=0
-        ),
-    )(own, partner, level_mixers, block_ranks, partner_tables, gram)
+            flops=LEVEL_FLOPS, bytes_accessed=1 << 20, transcendentals=0
+        ),
+    )(own, partner, *tables, *before)
 
 
 def project_kernel(
-    level, own_ref, partner_ref, mixer_ref, rank_ref, table_ref, close_ref, leaf_ref,
-    high_ref, low_ref, before_ref, image_ref, sums_ref,
+    level, lower_ref, own_ref, partner_ref, mixer_ref, rank_ref, table_ref,
+    close_ref, leaf_ref, high_ref, low_ref, image_ref, sums_ref,
 ):
     leaf_value = mix(level, own_ref, partner_ref, mixer_ref, rank_ref, table_ref)
     for leaf in range(32):
-        rounded = leaf_value(leaf).astype(jnp.bfloat16).astype(jnp.float32)
+        one, two = lower_ref[leaf], leaf_value(leaf)
+        rows = jnp.concatenate([one[:4], two[:4], one[4:], two[4:]], axis=0)
+        rounded = rows.astype(jnp.bfloat16).astype(jnp.float32)
         far = leaf_product(rounded, leaf_ref[0, leaf], leaf_ref[1, leaf])
         image_ref[:, leaf * 128 : (leaf + 1) * 128] = far + close_ref[leaf]
     high, low = split2(image_ref[...])
@@ -241,10 +247,10 @@
     sums_ref[16:24] = jnp.concatenate([real, imag, jnp.zeros((8, 112), jnp.float32)], axis=1)
 
 
-def project(level, own, partner, level_mixers, block_ranks, partner_tables, close, leaf_out, parts, gram):
+def project(level, lower, own, partner, tables, close, leaf_out, parts):
     return pl.pallas_call(
         lambda *refs: project_kernel(level, *refs),
-        in_specs=[VMEM] * 9 + [ANYWHERE],
+        in_specs=[VMEM] * 10,
         out_specs=[VMEM] * 2,
         out_shape=[
             jax.ShapeDtypeStruct((16, 4096), jnp.float32),
@@ -254,31 +260,43 @@
         cost_estimate=pl.CostEstimate(
             flops=6 * 512 * 256 * 256 * 2, bytes_accessed=8 << 20, transcendentals=0
         ),
-    )(
-        own, partner, level_mixers, block_ranks, partner_tables, close, leaf_out,
-        *[in_vmem(part) for part in parts], gram,
-    )
-
-
-def merge_kernel(own_ref, other_ref, gram_ref, other_gram_ref, out_ref, gram_sum_ref):
-    sums = own_ref[...] + other_ref[...]
-    gram_sum_ref[...] = gram_ref[...] + other_gram_ref[...]
+    )(lower, own, partner, *tables, close, leaf_out, *[in_vmem(part) for part in parts])
+
+
+def stack_kernel(sums_ref, gram_ref, other_ref, out_ref):
+    out_ref[0:24] = sums_ref[...]
+    out_ref[24:152] = gram_ref[...] + other_ref[...]
+
+
+def stack(sums, gram, other):
+    return pl.pallas_call(
+        stack_kernel,
+        in_specs=[VMEM] * 3,
+        out_specs=VMEM,
+        out_shape=jax.ShapeDtypeStruct((152, 128), jnp.float32),
+        compiler_params=pltpu.CompilerParams(vmem_limit_bytes=KERNEL_VMEM),
+    )(sums, gram, other)
+
+
+def merge_kernel(own_ref, other_ref, out_ref, sum_ref):
+    sum_ref[...] = own_ref[...] + other_ref[...]
     mine = lax.rem(lax.axis_index("y"), 2) * 2 + lax.rem(lax.axis_index("x"), 2)
-    piece = gram_sum_ref[pl.ds(pl.multiple_of(mine * 32, 32), 32), :]
+    sums = sum_ref[0:24]
+    piece = sum_ref[pl.ds(pl.multiple_of(24 + mine * 32, 8), 32), :]
     for device in range(out_ref.shape[0]):
         out_ref[device, 0:24] = sums
         out_ref[device, 24:56] = piece
 
 
-def merge(own, other, gram, other_gram):
+def merge(own, other):
     return pl.pallas_call(
         merge_kernel,
-        in_specs=[VMEM] * 4,
+        in_specs=[VMEM] * 2,
         out_specs=VMEM,
         out_shape=jax.ShapeDtypeStruct((lax.axis_size(("y", "x")), 56, 128), jnp.float32),
-        scratch_shapes=[pltpu.VMEM((128, 128), jnp.float32)],
-        compiler_params=pltpu.CompilerParams(vmem_limit_bytes=KERNEL_VMEM),
-    )(own, other, gram, other_gram)
+        scratch_shapes=[pltpu.VMEM((152, 128), jnp.float32)],
+        compiler_params=pltpu.CompilerParams(vmem_limit_bytes=KERNEL_VMEM),
+    )(own, other)
 
 
 def relay_kernel(got_ref, out_ref, gram_ref):
@@ -373,6 +391,20 @@
     )(got, gram, image, *[in_vmem(part) for part in parts])
 
 
+def add_kernel(left_ref, right_ref, before_ref, out_ref):
+    out_ref[...] = left_ref[...] + right_ref[...]
+
+
+def add_after(left, right, before):
+    return pl.pallas_call(
+        add_kernel,
+        in_specs=[VMEM, VMEM, ANYWHERE],
+        out_specs=VMEM,
+        out_shape=jax.ShapeDtypeStruct(left.shape, left.dtype),
+        compiler_params=pltpu.CompilerParams(vmem_limit_bytes=KERNEL_VMEM),
+    )(left, right, before)
+
+
 def exchange(value, axis, bit_number):
     pairs = [(source, source ^ (1 << bit_number)) for source in range(lax.axis_size(axis))]
     return lax.ppermute(value, axis, pairs)
@@ -382,19 +414,26 @@
     krylov_basis, near_field, leaf_in, leaf_out, level_mixers, block_ranks, partner_tables
 ):
     plan = [("y", 1), ("y", 0), ("x", 1), ("x", 0), ("z", 2)]
-    beside = [("core", 0), ("z", 1), ("z", 0), ("y", 0), ("x", 0)]
-    coeffs, rows = leaves_in(krylov_basis, leaf_in, 4)
-    gram, parts = basis_gram(krylov_basis)
-    close = near_product(rows, near_field)
+    *coeffs, rows = leaves_in(krylov_basis, leaf_in, 2)
+    gram, parts = basis_gram(krylov_basis, coeffs[0])
+    tables = (level_mixers, block_ranks, partner_tables)
+    gram_bits = [("x", 0), ("z", 0), ("z", 1), ("y", 0)]
     for level, (axis, bit) in enumerate(plan):
-        partner = exchange(coeffs, axis, bit)
-        gram = gram + exchange(gram, *beside[level])
-        operands = (level, coeffs, partner, level_mixers, block_ranks, partner_tables)
+        partner = [exchange(half, axis, bit) for half in coeffs]
+        before = [gram] if level == 0 else []
+        lower = next_level(level, coeffs[0], partner[0], tables, before)
         if level < len(plan) - 1:
-            coeffs = next_level(*operands, gram)
+            moved = exchange(gram, *gram_bits[level])
+            upper = next_level(level, coeffs[1], partner[1], tables, [lower, moved])
+            gram = add_after(gram, moved, upper)
+            coeffs = [lower, upper]
         else:
-            image, sums = project(*operands, close, leaf_out, parts, gram)
-    got = merge(sums, exchange(sums, "core", 0), gram, exchange(gram, "z", 2))
+            close = near_product(rows, near_field, gram)
+            image, sums = project(
+                level, lower, coeffs[1], partner[1], tables, close, leaf_out, parts
+            )
+    sums = stack(sums, gram, exchange(gram, "z", 2))
+    got = merge(sums, exchange(sums, "core", 0))
     got, gram = relay(lax.all_to_all(got, ("y", "x"), 0, 0))
     got = lax.all_to_all(got, "z", 0, 0)
     scale = 1.0 / (krylov_basis.shape[3] * lax.axis_size(AXES))

time: 91.9 us -> 86.1 us (0.937)
  waiting for transfers between devices: 21.6 us -> 6.26 us
  starting transfers between devices: 23.7 us -> 37.6 us
  blocking collectives: 32.5 us -> 29.1 us
    ppermute x12 -> x16, waiting for transfers between devices: 21.6 us -> 6.26 us  [exchange(): return lax.ppermute(value, axis, pairs)]
    ppermute x12 -> x16, starting transfers between devices: 23.7 us -> 37.6 us  [exchange(): return lax.ppermute(value, axis, pairs)]
    all_to_all x1, blocking collectives: 16.5 us -> 13.6 us  [per_device(): got = lax.all_to_all(got, 'z', 0, 0)]
    pallas_call x3 -> x8, Pallas kernels: 3.92 us -> 2.18 us  [the longest x1 1.41 us: basis_gram(): pl.pallas_call(basis_gram_kernel, in_specs=[VMEM, ANYWHERE], out_specs=[V...]
    pallas_call x4 -> x9, Pallas kernels: 1.83 us -> 3.22 us  [next_level(): pl.pallas_call(lambda *refs: level_kernel(level, *refs), in_specs=[VMEM]...]
  transfers between devices with their start and end apart: 12 -> 16, of which waited for: 10 -> 7; matrix products, arithmetic and copies ran while one was open for 0% -> 0% of each run, Pallas kernels for 7% -> 9%
where the time goes in v7:
time: 86.1 us; the launch traced here: 85.9 us
  starting transfers between devices  37.6 us (44%)
  blocking collectives  29.1 us (34%)
  Pallas kernels  12.2 us (14%)
  waiting for transfers between devices  6.26 us (7%)
    ppermute x16, starting transfers between devices, exchange(): return lax.ppermute(value, axis, pairs)  37.6 us
    all_to_all x1, blocking collectives, per_device(): got, gram = relay(lax.all_to_all(got, ('y', 'x'), 0, 0))  15.5 us
    all_to_all x1, blocking collectives, per_device(): got = lax.all_to_all(got, 'z', 0, 0)  13.6 us
    ppermute x16, waiting for transfers between devices, exchange(): return lax.ppermute(value, axis, pairs)  6.26 us
    pallas_call x9, Pallas kernels, next_level(): pl.pallas_call(lambda *refs: level_kernel(level, *refs), in_specs=[VMEM]...  3.22 us
    pallas_call x1, Pallas kernels, project(): pl.pallas_call(lambda *refs: project_kernel(level, *refs), in_specs=[VMEM...  2.47 us
    pallas_call x1, Pallas kernels, leaves_in(): pl.pallas_call(leaves_in_kernel, in_specs=[pl.BlockSpec(memory_space=pltp...  2.22 us
    pallas_call x1, Pallas kernels, finish(): pl.pallas_call(lambda *refs: finish_kernel(scale, *refs), in_specs=[VMEM]...  2.03 us
  transfers between devices with their start and end apart: 16, of which 7 were waited for; matrix products, arithmetic and copies ran while one was open for 0% of the time, Pallas kernels for 9%

profile of v7, /device:TPU:2, one launch (start us, length us, event | category | flops | bytes accessed | tf_op | source)
XLA Modules:
  0.0 85.9 jit_solution(16011720833918509814)
XLA Ops:
  0.6 2.2 %shard_map.94 = (f32[32,8,128]{2,1,0:T(8,128)S(1)}, f32[32,8,128]{2,1,0:T(8,128)S(1)}, f32[32,16,128]{2,1,0:T(8,128)S(1)}) custom-call(f32[16,2,8,4096]{3,2,1,0:T(8,128)} %basis_ref.3, bf16[2,32,128,128]{3,2,1,0:T(8,128)(2,1)} %leaf_ref.2), custom_call_target="tpu_custom_call" | custom-call | flops 33554432 | bytes 2359296 | tf_op jit(solution)/shard_map/pallas_call | solution.py:102
  2.9 3.3 %collective-permute-start = (f32[32,8,128]{2,1,0:T(8,128)S(1)}, f32[32,8,128]{2,1,0:T(8,128)S(1)}, u32[]{:S(2)}, u32[]{:S(2)}) collective-permute-start(f32[32,8,128]{2,1,0:T(8,128)S(1)} %get-tuple-element.16.before_ref.refs_0_), channel_id=1, source_target_pairs={{0,128},{64,192},{128,0},{192,64},{1,129},{65,193},{129,1},{193,65... | collective-permute-start | bytes 393224 | tf_op jit(solution)/shard_map/ppermute | solution.py:410
  6.2 0.3 collective-permute-start.5
  6.5 1.4 %shard_map.95 = (f32[128,128]{1,0:T(8,128)S(1)}, bf16[256,4096]{1,0:T(8,128)(2,1)S(1)}, bf16[256,4096]{1,0:T(8,128)(2,1)S(1)}) custom-call(f32[16,2,8,4096]{3,2,1,0:T(8,128)S(1)} %copy-done, f32[32,8,128]{2,1,0:T(8,128)S(1)} %get-tuple-element.16.before_ref.refs_0_), custom_call_target="tpu_custom_call" | custom-call | flops 1073741824 | bytes 8388608 | tf_op jit(solution)/shard_map/pallas_call | solution.py:166
  7.9 2.4 %collective-permute-start.6 = (f32[128,128]{1,0:T(8,128)S(1)}, f32[128,128]{1,0:T(8,128)S(1)}, u32[]{:S(2)}, u32[]{:S(2)}) collective-permute-start(f32[128,128]{1,0:T(8,128)S(1)} %get-tuple-element.17.refs_5_.left_ref), channel_id=1, source_target_pairs={{0,8},{8,0},{16,24},{24,16},{1,9},{9,1},{17,25},{25,17},{2,10},{10... | collective-permute-start | bytes 196616 | tf_op jit(solution)/shard_map/ppermute | solution.py:410
  10.3 0.0 collective-permute-done.refs_1_
  10.3 0.4 shard_map.96.refs_0_.refs_5_
  10.7 1.9 %collective-permute-start.1 = (f32[32,8,128]{2,1,0:T(8,128)S(1)}, f32[32,8,128]{2,1,0:T(8,128)S(1)}, u32[]{:S(2)}, u32[]{:S(2)}) collective-permute-start(f32[32,8,128]{2,1,0:T(8,128)S(1)} %shard_map.96.refs_0_.refs_5_), channel_id=1, source_target_pairs={{0,64},{64,0},{128,192},{192,128},{1,65},{65,1},{129,193},{193,129... | collective-permute-start | bytes 393224 | tf_op jit(solution)/shard_map/ppermute | solution.py:410
  12.5 0.0 collective-permute-done.6.refs_6_.right_ref
  12.5 0.1 collective-permute-done.5.refs_1_
  12.6 0.4 shard_map.101.before_ref.refs_0_
  13.0 1.5 %collective-permute-start.7 = (f32[32,8,128]{2,1,0:T(8,128)S(1)}, f32[32,8,128]{2,1,0:T(8,128)S(1)}, u32[]{:S(2)}, u32[]{:S(2)}) collective-permute-start(f32[32,8,128]{2,1,0:T(8,128)S(1)} %shard_map.101.before_ref.refs_0_), channel_id=1, source_target_pairs={{0,64},{64,0},{128,192},{192,128},{1,65},{65,1},{129,193},{193,129... | collective-permute-start | bytes 393224 | tf_op jit(solution)/shard_map/ppermute | solution.py:410
  14.5 2.0 %collective-permute-start.8 = (f32[128,128]{1,0:T(8,128)S(1)}, f32[128,128]{1,0:T(8,128)S(1)}, u32[]{:S(2)}, u32[]{:S(2)}) collective-permute-start(f32[128,128]{1,0:T(8,128)S(1)} %shard_map.102.left_ref), channel_id=1, source_target_pairs={{0,1},{1,0},{2,3},{3,2},{4,5},{5,4},{6,7},{7,6},{8,9},{9,8},{10,11... | collective-permute-start | bytes 196616 | tf_op jit(solution)/shard_map/ppermute | solution.py:410
  16.5 0.3 collective-permute-done.1.refs_1_
  16.8 0.4 shard_map.97.refs_0_.refs_5_
  17.2 2.1 %collective-permute-start.2 = (f32[32,8,128]{2,1,0:T(8,128)S(1)}, f32[32,8,128]{2,1,0:T(8,128)S(1)}, u32[]{:S(2)}, u32[]{:S(2)}) collective-permute-start(f32[32,8,128]{2,1,0:T(8,128)S(1)} %shard_map.97.refs_0_.refs_5_), channel_id=1, source_target_pairs={{0,16},{8,24},{16,0},{24,8},{1,17},{9,25},{17,1},{25,9},{2,18},{10... | collective-permute-start | bytes 393224 | tf_op jit(solution)/shard_map/ppermute | solution.py:410
  19.2 0.0 collective-permute-done.8.refs_6_.right_ref
  19.2 0.0 collective-permute-done.7.refs_1_
  19.2 0.4 shard_map.103.before_ref.refs_0_
  19.6 1.9 %collective-permute-start.9 = (f32[32,8,128]{2,1,0:T(8,128)S(1)}, f32[32,8,128]{2,1,0:T(8,128)S(1)}, u32[]{:S(2)}, u32[]{:S(2)}) collective-permute-start(f32[32,8,128]{2,1,0:T(8,128)S(1)} %shard_map.103.before_ref.refs_0_), channel_id=1, source_target_pairs={{0,16},{8,24},{16,0},{24,8},{1,17},{9,25},{17,1},{25,9},{2,18},{10... | collective-permute-start | bytes 393224 | tf_op jit(solution)/shard_map/ppermute | solution.py:410
  21.5 3.4 %collective-permute-start.10 = (f32[128,128]{1,0:T(8,128)S(1)}, f32[128,128]{1,0:T(8,128)S(1)}, u32[]{:S(2)}, u32[]{:S(2)}) collective-permute-start(f32[128,128]{1,0:T(8,128)S(1)} %shard_map.104.left_ref), channel_id=1, source_target_pairs={{0,2},{1,3},{2,0},{3,1},{4,6},{5,7},{6,4},{7,5},{8,10},{9,11},{10,... | collective-permute-start | bytes 196616 | tf_op jit(solution)/shard_map/ppermute | solution.py:410
  24.8 0.1 collective-permute-done.2.refs_1_
  25.0 0.4 shard_map.98.refs_0_.refs_5_
  25.3 1.5 %collective-permute-start.3 = (f32[32,8,128]{2,1,0:T(8,128)S(1)}, f32[32,8,128]{2,1,0:T(8,128)S(1)}, u32[]{:S(2)}, u32[]{:S(2)}) collective-permute-start(f32[32,8,128]{2,1,0:T(8,128)S(1)} %shard_map.98.refs_0_.refs_5_), channel_id=1, source_target_pairs={{0,8},{8,0},{16,24},{24,16},{1,9},{9,1},{17,25},{25,17},{2,10},{10... | collective-permute-start | bytes 393224 | tf_op jit(solution)/shard_map/ppermute | solution.py:410
  26.8 0.3 collective-permute-done.10.refs_6_.right_ref
  27.1 0.4 shard_map.105.before_ref.refs_0_
  27.4 1.8 %collective-permute-start.11 = (f32[32,8,128]{2,1,0:T(8,128)S(1)}, f32[32,8,128]{2,1,0:T(8,128)S(1)}, u32[]{:S(2)}, u32[]{:S(2)}) collective-permute-start(f32[32,8,128]{2,1,0:T(8,128)S(1)} %shard_map.105.before_ref.refs_0_), channel_id=1, source_target_pairs={{0,8},{8,0},{16,24},{24,16},{1,9},{9,1},{17,25},{25,17},{2,10},{10... | collective-permute-start | bytes 393224 | tf_op jit(solution)/shard_map/ppermute | solution.py:410
  29.3 1.3 %collective-permute-start.12 = (f32[128,128]{1,0:T(8,128)S(1)}, f32[128,128]{1,0:T(8,128)S(1)}, u32[]{:S(2)}, u32[]{:S(2)}) collective-permute-start(f32[128,128]{1,0:T(8,128)S(1)} %shard_map.106.left_ref), channel_id=1, source_target_pairs={{0,64},{64,0},{128,192},{192,128},{1,65},{65,1},{129,193},{193,129... | collective-permute-start | bytes 196616 | tf_op jit(solution)/shard_map/ppermute | solution.py:410
  30.6 0.1 collective-permute-done.3.refs_1_
  30.7 0.4 shard_map.99.refs_0_.refs_5_
  31.1 0.0 copy-start.2
  31.1 7.9 %collective-permute-start.4 = (f32[32,8,128]{2,1,0:T(8,128)S(1)}, f32[32,8,128]{2,1,0:T(8,128)S(1)}, u32[]{:S(2)}, u32[]{:S(2)}) collective-permute-start(f32[32,8,128]{2,1,0:T(8,128)S(1)} %shard_map.99.refs_0_.refs_5_), channel_id=1, source_target_pairs={{0,4},{1,5},{2,6},{3,7},{4,0},{5,1},{6,2},{7,3},{8,12},{9,13},{10,... | collective-permute-start | bytes 393224 | tf_op jit(solution)/shard_map/ppermute | solution.py:410
  39.0 0.0 collective-permute-done.12.refs_6_.right_ref
  39.0 0.0 collective-permute-done.11.refs_1_
  39.0 0.4 shard_map.107.before_ref.refs_1_
  39.4 2.1 %collective-permute-start.13 = (f32[32,8,128]{2,1,0:T(8,128)S(1)}, f32[32,8,128]{2,1,0:T(8,128)S(1)}, u32[]{:S(2)}, u32[]{:S(2)}) collective-permute-start(f32[32,8,128]{2,1,0:T(8,128)S(1)} %shard_map.107.before_ref.refs_1_), channel_id=1, source_target_pairs={{0,4},{1,5},{2,6},{3,7},{4,0},{5,1},{6,2},{7,3},{8,12},{9,13},{10,... | collective-permute-start | bytes 393224 | tf_op jit(solution)/shard_map/ppermute | solution.py:410
  41.5 4.2 %collective-permute-start.14 = (f32[128,128]{1,0:T(8,128)S(1)}, f32[128,128]{1,0:T(8,128)S(1)}, u32[]{:S(2)}, u32[]{:S(2)}) collective-permute-start(f32[128,128]{1,0:T(8,128)S(1)} %shard_map.108.before_ref.gram_ref), channel_id=1, source_target_pairs={{0,4},{1,5},{2,6},{3,7},{4,0},{5,1},{6,2},{7,3},{8,12},{9,13},{10,... | collective-permute-start | bytes 196616 | tf_op jit(solution)/shard_map/ppermute | solution.py:410
  45.7 0.6 shard_map.109.refs_6_
  46.3 0.0 collective-permute-done.4.refs_1_
  46.3 0.4 shard_map.100.refs_0_
  46.7 4.1 %collective-permute-done.13.refs_2_ = f32[32,8,128]{2,1,0:T(8,128)S(1)} collective-permute-done((f32[32,8,128]{2,1,0:T(8,128)S(1)}, f32[32,8,128]{2,1,0:T(8,128)S(1)}, u32[]{:S(2)}, u32[]{:S(2)}) %collective-permute-start.13) | collective-permute-done | bytes 131104 | tf_op jit(solution)/shard_map/ppermute | solution.py:410
  50.8 2.5 %shard_map.110 = (f32[16,4096]{1,0:T(8,128)S(1)}, f32[24,128]{1,0:T(8,128)S(1)}) custom-call(f32[32,8,128]{2,1,0:T(8,128)S(1)} %shard_map.100.refs_0_, f32[32,8,128]{2,1,0:T(8,128)S(1)} %shard_map.107.before_ref.refs_1_, f32[32,8,128]{2,1,0:T(8,128)S(1)} %collective-permute-done.13.refs_2_, f32[5,2,2,128,128]{4,3,2,1,0:T(8,128)S(1)} %copy-done.3, ...), custom_call_target="tpu_custom_call" | custom-call | flops 402653184 | bytes 8388608 | tf_op jit(solution)/shard_map/pallas_call | solution.py:251
  53.3 0.0 collective-permute-done.14.other_ref
  53.4 0.1 collective-permute-start.15
  53.5 1.3 %collective-permute-done.15.other_ref = f32[152,128]{1,0:T(8,128)S(1)} collective-permute-done((f32[152,128]{1,0:T(8,128)S(1)}, f32[152,128]{1,0:T(8,128)S(1)}, u32[]{:S(2)}, u32[]{:S(2)}) %collective-permute-start.15) | collective-permute-done | bytes 77856 | tf_op jit(solution)/shard_map/ppermute | solution.py:410
  54.8 15.5 %all_to_all.10.got_ref = f32[16,56,128]{2,1,0:T(8,128)S(1)} all-to-all(f32[16,56,128]{2,1,0:T(8,128)S(1)} %shard_map.112), channel_id=1, replica_groups=mesh['y'=4,'core'=2,'x'=4,'z'=8] {'y','x'}, dimensions={0} | all-to-all | bytes 917504 | tf_op jit(solution)/shard_map/all_to_all | solution.py:437
  70.3 13.6 %all_to_all.11.refs_0_ = f32[8,24,128]{2,1,0:T(8,128)S(1)} all-to-all(f32[8,24,128]{2,1,0:T(8,128)S(1)} %get-tuple-element.23), channel_id=1, replica_groups=mesh['y'=4,'core'=2,'x'=4,'z'=8] {'z'}, dimensions={0} | all-to-all | bytes 196608 | tf_op jit(solution)/shard_map/all_to_all | solution.py:438
  83.9 2.0 %shard_map.114 = (f32[2,8,8,16]{3,2,1,0:T(8,128)}, f32[2,8,4096]{2,1,0:T(8,128)}, f32[2,8,8]{2,1,0:T(8,128)}) custom-call(f32[8,24,128]{2,1,0:T(8,128)S(1)} %all_to_all.11.refs_0_, f32[128,128]{1,0:T(8,128)S(1)} %get-tuple-element.24.refs_1_, f32[16,4096]{1,0:T(8,128)S(1)} %get-tuple-element.25.refs_2_, ...), custom_call_target="tpu_custom_call" | custom-call | flops 201326592 | bytes 6291456 | tf_op jit(solution)/shard_map/pallas_call | solution.py:378
  (19 shorter events, 0.2 us)
Async XLA Ops:
  0.6 5.9 %copy-start = (f32[16,2,8,4096]{3,2,1,0:T(8,128)S(1)}, f32[16,2,8,4096]{3,2,1,0:T(8,128)}, u32[]{:S(2)}) copy-start(f32[16,2,8,4096]{3,2,1,0:T(8,128)} %basis_ref.3) | copy-start | bytes 12582916
  2.9 7.4 %collective-permute-start = (f32[32,8,128]{2,1,0:T(8,128)S(1)}, f32[32,8,128]{2,1,0:T(8,128)S(1)}, u32[]{:S(2)}, u32[]{:S(2)}) collective-permute-start(f32[32,8,128]{2,1,0:T(8,128)S(1)} %get-tuple-element.16.before_ref.refs_0_), channel_id=1, source_target_pairs={{0,128},{64,192},{128,0},{192,64},{1,129},{65,193},{129,1},{193,65... | collective-permute-start | bytes 393224 | tf_op jit(solution)/shard_map/ppermute | solution.py:410
  6.1 4.1 %copy-start.3 = (f32[5,2,2,128,128]{4,3,2,1,0:T(8,128)S(1)}, f32[5,2,2,128,128]{4,3,2,1,0:T(8,128)}, u32[]{:S(2)}) copy-start(f32[5,2,2,128,128]{4,3,2,1,0:T(8,128)} %refs_3_.19) | copy-start | bytes 3932164
  6.2 4.1 %copy-start.4 = (s32[5,32]{1,0:T(8,128)S(1)}, s32[5,32]{1,0:T(8,128)}, u32[]{:S(2)}) copy-start(s32[5,32]{1,0:T(8,128)} %refs_4_.19) | copy-start | bytes 1924
  6.2 4.1 %copy-start.5 = (s32[5,1,32]{2,1,0:T(1,128)S(1)}, s32[5,1,32]{2,1,0:T(1,128)}, u32[]{:S(2)}) copy-start(s32[5,1,32]{2,1,0:T(1,128)} %refs_5_.1) | copy-start | bytes 1924
  6.2 6.5 %collective-permute-start.5 = (f32[32,8,128]{2,1,0:T(8,128)S(1)}, f32[32,8,128]{2,1,0:T(8,128)S(1)}, u32[]{:S(2)}, u32[]{:S(2)}) collective-permute-start(f32[32,8,128]{2,1,0:T(8,128)S(1)} %get-tuple-element.18.refs_0_), channel_id=1, source_target_pairs={{0,128},{64,192},{128,0},{192,64},{1,129},{65,193},{129,1},{193,65... | collective-permute-start | bytes 393224 | tf_op jit(solution)/shard_map/ppermute | solution.py:410
  7.9 4.6 %collective-permute-start.6 = (f32[128,128]{1,0:T(8,128)S(1)}, f32[128,128]{1,0:T(8,128)S(1)}, u32[]{:S(2)}, u32[]{:S(2)}) collective-permute-start(f32[128,128]{1,0:T(8,128)S(1)} %get-tuple-element.17.refs_5_.left_ref), channel_id=1, source_target_pairs={{0,8},{8,0},{16,24},{24,16},{1,9},{9,1},{17,25},{25,17},{2,10},{10... | collective-permute-start | bytes 196616 | tf_op jit(solution)/shard_map/ppermute | solution.py:410
  10.7 6.2 %collective-permute-start.1 = (f32[32,8,128]{2,1,0:T(8,128)S(1)}, f32[32,8,128]{2,1,0:T(8,128)S(1)}, u32[]{:S(2)}, u32[]{:S(2)}) collective-permute-start(f32[32,8,128]{2,1,0:T(8,128)S(1)} %shard_map.96.refs_0_.refs_5_), channel_id=1, source_target_pairs={{0,64},{64,0},{128,192},{192,128},{1,65},{65,1},{129,193},{193,129... | collective-permute-start | bytes 393224 | tf_op jit(solution)/shard_map/ppermute | solution.py:410
  13.0 6.3 %collective-permute-start.7 = (f32[32,8,128]{2,1,0:T(8,128)S(1)}, f32[32,8,128]{2,1,0:T(8,128)S(1)}, u32[]{:S(2)}, u32[]{:S(2)}) collective-permute-start(f32[32,8,128]{2,1,0:T(8,128)S(1)} %shard_map.101.before_ref.refs_0_), channel_id=1, source_target_pairs={{0,64},{64,0},{128,192},{192,128},{1,65},{65,1},{129,193},{193,129... | collective-permute-start | bytes 393224 | tf_op jit(solution)/shard_map/ppermute | solution.py:410
  14.5 4.7 %collective-permute-start.8 = (f32[128,128]{1,0:T(8,128)S(1)}, f32[128,128]{1,0:T(8,128)S(1)}, u32[]{:S(2)}, u32[]{:S(2)}) collective-permute-start(f32[128,128]{1,0:T(8,128)S(1)} %shard_map.102.left_ref), channel_id=1, source_target_pairs={{0,1},{1,0},{2,3},{3,2},{4,5},{5,4},{6,7},{7,6},{8,9},{9,8},{10,11... | collective-permute-start | bytes 196616 | tf_op jit(solution)/shard_map/ppermute | solution.py:410
  17.2 7.8 %collective-permute-start.2 = (f32[32,8,128]{2,1,0:T(8,128)S(1)}, f32[32,8,128]{2,1,0:T(8,128)S(1)}, u32[]{:S(2)}, u32[]{:S(2)}) collective-permute-start(f32[32,8,128]{2,1,0:T(8,128)S(1)} %shard_map.97.refs_0_.refs_5_), channel_id=1, source_target_pairs={{0,16},{8,24},{16,0},{24,8},{1,17},{9,25},{17,1},{25,9},{2,18},{10... | collective-permute-start | bytes 393224 | tf_op jit(solution)/shard_map/ppermute | solution.py:410
  19.6 7.5 %collective-permute-start.9 = (f32[32,8,128]{2,1,0:T(8,128)S(1)}, f32[32,8,128]{2,1,0:T(8,128)S(1)}, u32[]{:S(2)}, u32[]{:S(2)}) collective-permute-start(f32[32,8,128]{2,1,0:T(8,128)S(1)} %shard_map.103.before_ref.refs_0_), channel_id=1, source_target_pairs={{0,16},{8,24},{16,0},{24,8},{1,17},{9,25},{17,1},{25,9},{2,18},{10... | collective-permute-start | bytes 393224 | tf_op jit(solution)/shard_map/ppermute | solution.py:410
  21.5 5.6 %collective-permute-start.10 = (f32[128,128]{1,0:T(8,128)S(1)}, f32[128,128]{1,0:T(8,128)S(1)}, u32[]{:S(2)}, u32[]{:S(2)}) collective-permute-start(f32[128,128]{1,0:T(8,128)S(1)} %shard_map.104.left_ref), channel_id=1, source_target_pairs={{0,2},{1,3},{2,0},{3,1},{4,6},{5,7},{6,4},{7,5},{8,10},{9,11},{10,... | collective-permute-start | bytes 196616 | tf_op jit(solution)/shard_map/ppermute | solution.py:410
  25.3 5.4 %collective-permute-start.3 = (f32[32,8,128]{2,1,0:T(8,128)S(1)}, f32[32,8,128]{2,1,0:T(8,128)S(1)}, u32[]{:S(2)}, u32[]{:S(2)}) collective-permute-start(f32[32,8,128]{2,1,0:T(8,128)S(1)} %shard_map.98.refs_0_.refs_5_), channel_id=1, source_target_pairs={{0,8},{8,0},{16,24},{24,16},{1,9},{9,1},{17,25},{25,17},{2,10},{10... | collective-permute-start | bytes 393224 | tf_op jit(solution)/shard_map/ppermute | solution.py:410
  27.4 11.6 %collective-permute-start.11 = (f32[32,8,128]{2,1,0:T(8,128)S(1)}, f32[32,8,128]{2,1,0:T(8,128)S(1)}, u32[]{:S(2)}, u32[]{:S(2)}) collective-permute-start(f32[32,8,128]{2,1,0:T(8,128)S(1)} %shard_map.105.before_ref.refs_0_), channel_id=1, source_target_pairs={{0,8},{8,0},{16,24},{24,16},{1,9},{9,1},{17,25},{25,17},{2,10},{10... | collective-permute-start | bytes 393224 | tf_op jit(solution)/shard_map/ppermute | solution.py:410
  29.3 9.7 %collective-permute-start.12 = (f32[128,128]{1,0:T(8,128)S(1)}, f32[128,128]{1,0:T(8,128)S(1)}, u32[]{:S(2)}, u32[]{:S(2)}) collective-permute-start(f32[128,128]{1,0:T(8,128)S(1)} %shard_map.106.left_ref), channel_id=1, source_target_pairs={{0,64},{64,0},{128,192},{192,128},{1,65},{65,1},{129,193},{193,129... | collective-permute-start | bytes 196616 | tf_op jit(solution)/shard_map/ppermute | solution.py:410
  31.1 14.6 %copy-start.2 = (bf16[2,32,128,128]{3,2,1,0:T(8,128)(2,1)S(1)}, bf16[2,32,128,128]{3,2,1,0:T(8,128)(2,1)}, u32[]{:S(2)}) copy-start(bf16[2,32,128,128]{3,2,1,0:T(8,128)(2,1)} %leaf_ref.3) | copy-start | bytes 6291460
  31.1 15.2 %collective-permute-start.4 = (f32[32,8,128]{2,1,0:T(8,128)S(1)}, f32[32,8,128]{2,1,0:T(8,128)S(1)}, u32[]{:S(2)}, u32[]{:S(2)}) collective-permute-start(f32[32,8,128]{2,1,0:T(8,128)S(1)} %shard_map.99.refs_0_.refs_5_), channel_id=1, source_target_pairs={{0,4},{1,5},{2,6},{3,7},{4,0},{5,1},{6,2},{7,3},{8,12},{9,13},{10,... | collective-permute-start | bytes 393224 | tf_op jit(solution)/shard_map/ppermute | solution.py:410
  39.4 11.5 %collective-permute-start.13 = (f32[32,8,128]{2,1,0:T(8,128)S(1)}, f32[32,8,128]{2,1,0:T(8,128)S(1)}, u32[]{:S(2)}, u32[]{:S(2)}) collective-permute-start(f32[32,8,128]{2,1,0:T(8,128)S(1)} %shard_map.107.before_ref.refs_1_), channel_id=1, source_target_pairs={{0,4},{1,5},{2,6},{3,7},{4,0},{5,1},{6,2},{7,3},{8,12},{9,13},{10,... | collective-permute-start | bytes 393224 | tf_op jit(solution)/shard_map/ppermute | solution.py:410
  41.5 11.8 %collective-permute-start.14 = (f32[128,128]{1,0:T(8,128)S(1)}, f32[128,128]{1,0:T(8,128)S(1)}, u32[]{:S(2)}, u32[]{:S(2)}) collective-permute-start(f32[128,128]{1,0:T(8,128)S(1)} %shard_map.108.before_ref.gram_ref), channel_id=1, source_target_pairs={{0,4},{1,5},{2,6},{3,7},{4,0},{5,1},{6,2},{7,3},{8,12},{9,13},{10,... | collective-permute-start | bytes 196616 | tf_op jit(solution)/shard_map/ppermute | solution.py:410
  46.3 4.5 %copy-start.1 = (bf16[2,32,128,128]{3,2,1,0:T(8,128)(2,1)S(1)}, bf16[2,32,128,128]{3,2,1,0:T(8,128)(2,1)}, u32[]{:S(2)}) copy-start(bf16[2,32,128,128]{3,2,1,0:T(8,128)(2,1)} %refs_7_.1) | copy-start | bytes 6291460
  53.4 1.4 %collective-permute-start.15 = (f32[152,128]{1,0:T(8,128)S(1)}, f32[152,128]{1,0:T(8,128)S(1)}, u32[]{:S(2)}, u32[]{:S(2)}) collective-permute-start(f32[152,128]{1,0:T(8,128)S(1)} %shard_map.111.own_ref), channel_id=1, source_target_pairs={{0,32},{32,0},{1,33},{33,1},{2,34},{34,2},{3,35},{35,3},{4,36},{36... | collective-permute-start | bytes 233480 | tf_op jit(solution)/shard_map/ppermute | solution.py:410

commit v8 on v7

--- a/solution.py
+++ b/solution.py
@@ -342,8 +342,11 @@
     gram_imag = jnp.where(row > column, packed, jnp.where(row < column, -flipped, 0.0))
     gram = jnp.concatenate([gram_real, gram_imag], axis=1)
 
+    gram_high, gram_low = split2(gram)
+
     def by_gram(rows):
-        one = dot_high(rows, gram, NN)
+        high, low = split2(rows)
+        one = dot_nn(high, gram_high) + dot_nn(high, gram_low) + dot_nn(low, gram_high)
         real = one[:8, :128] + one[8:, 128:]
         imag = one[8:, :128] - one[:8, 128:]
         return jnp.concatenate([real, imag], axis=0)
@@ -424,7 +427,8 @@
         lower = next_level(level, coeffs[0], partner[0], tables, before)
         if level < len(plan) - 1:
             moved = exchange(gram, *gram_bits[level])
-            upper = next_level(level, coeffs[1], partner[1], tables, [lower, moved])
+            before = [lower, moved] if level < len(plan) - 2 else [lower]
+            upper = next_level(level, coeffs[1], partner[1], tables, before)
             gram = add_after(gram, moved, upper)
             coeffs = [lower, upper]
         else:

time: 86.1 us -> 85.6 us (level)
  waiting for transfers between devices: 6.26 us -> 5.14 us
    all_to_all x1, blocking collectives: 15.5 us -> 16.7 us  [per_device(): got, gram = relay(lax.all_to_all(got, ('y', 'x'), 0, 0))]
    ppermute x16, waiting for transfers between devices: 6.26 us -> 5.14 us  [exchange(): return lax.ppermute(value, axis, pairs)]
where the time goes in v8:
time: 85.6 us; the launch traced here: 85.5 us
  starting transfers between devices  37.6 us (44%)
  blocking collectives  29.9 us (35%)
  Pallas kernels  12 us (14%)
  waiting for transfers between devices  5.14 us (6%)
    ppermute x16, starting transfers between devices, exchange(): return lax.ppermute(value, axis, pairs)  37.6 us
    all_to_all x1, blocking collectives, per_device(): got, gram = relay(lax.all_to_all(got, ('y', 'x'), 0, 0))  16.7 us
    all_to_all x1, blocking collectives, per_device(): got = lax.all_to_all(got, 'z', 0, 0)  13.2 us
    ppermute x16, waiting for transfers between devices, exchange(): return lax.ppermute(value, axis, pairs)  5.14 us
    pallas_call x9, Pallas kernels, next_level(): pl.pallas_call(lambda *refs: level_kernel(level, *refs), in_specs=[VMEM]...  3.22 us
    pallas_call x1, Pallas kernels, project(): pl.pallas_call(lambda *refs: project_kernel(level, *refs), in_specs=[VMEM...  2.47 us
    pallas_call x1, Pallas kernels, leaves_in(): pl.pallas_call(leaves_in_kernel, in_specs=[pl.BlockSpec(memory_space=pltp...  2.22 us
    pallas_call x1, Pallas kernels, finish(): pl.pallas_call(lambda *refs: finish_kernel(scale, *refs), in_specs=[VMEM]...  1.9 us
  transfers between devices with their start and end apart: 16, of which 7 were waited for; matrix products, arithmetic and copies ran while one was open for 0% of the time, Pallas kernels for 9%

profile of v8, /device:TPU:2, one launch (start us, length us, event | category | flops | bytes accessed | tf_op | source)
XLA Modules:
  0.0 85.5 jit_solution(3410170354705774491)
XLA Ops:
  0.6 2.2 %shard_map.94 = (f32[32,8,128]{2,1,0:T(8,128)S(1)}, f32[32,8,128]{2,1,0:T(8,128)S(1)}, f32[32,16,128]{2,1,0:T(8,128)S(1)}) custom-call(f32[16,2,8,4096]{3,2,1,0:T(8,128)} %basis_ref.3, bf16[2,32,128,128]{3,2,1,0:T(8,128)(2,1)} %leaf_ref.2), custom_call_target="tpu_custom_call" | custom-call | flops 33554432 | bytes 2359296 | tf_op jit(solution)/shard_map/pallas_call | solution.py:102
  2.9 3.3 %collective-permute-start = (f32[32,8,128]{2,1,0:T(8,128)S(1)}, f32[32,8,128]{2,1,0:T(8,128)S(1)}, u32[]{:S(2)}, u32[]{:S(2)}) collective-permute-start(f32[32,8,128]{2,1,0:T(8,128)S(1)} %get-tuple-element.16.before_ref.refs_0_), channel_id=1, source_target_pairs={{0,128},{64,192},{128,0},{192,64},{1,129},{65,193},{129,1},{193,65... | collective-permute-start | bytes 393224 | tf_op jit(solution)/shard_map/ppermute | solution.py:413
  6.2 0.3 collective-permute-start.5
  6.5 1.4 %shard_map.95 = (f32[128,128]{1,0:T(8,128)S(1)}, bf16[256,4096]{1,0:T(8,128)(2,1)S(1)}, bf16[256,4096]{1,0:T(8,128)(2,1)S(1)}) custom-call(f32[16,2,8,4096]{3,2,1,0:T(8,128)S(1)} %copy-done, f32[32,8,128]{2,1,0:T(8,128)S(1)} %get-tuple-element.16.before_ref.refs_0_), custom_call_target="tpu_custom_call" | custom-call | flops 1073741824 | bytes 8388608 | tf_op jit(solution)/shard_map/pallas_call | solution.py:166
  7.9 2.4 %collective-permute-start.6 = (f32[128,128]{1,0:T(8,128)S(1)}, f32[128,128]{1,0:T(8,128)S(1)}, u32[]{:S(2)}, u32[]{:S(2)}) collective-permute-start(f32[128,128]{1,0:T(8,128)S(1)} %get-tuple-element.17.refs_5_.left_ref), channel_id=1, source_target_pairs={{0,8},{8,0},{16,24},{24,16},{1,9},{9,1},{17,25},{25,17},{2,10},{10... | collective-permute-start | bytes 196616 | tf_op jit(solution)/shard_map/ppermute | solution.py:413
  10.3 0.0 collective-permute-done.refs_1_
  10.3 0.4 shard_map.96.refs_0_.refs_5_
  10.7 1.9 %collective-permute-start.1 = (f32[32,8,128]{2,1,0:T(8,128)S(1)}, f32[32,8,128]{2,1,0:T(8,128)S(1)}, u32[]{:S(2)}, u32[]{:S(2)}) collective-permute-start(f32[32,8,128]{2,1,0:T(8,128)S(1)} %shard_map.96.refs_0_.refs_5_), channel_id=1, source_target_pairs={{0,64},{64,0},{128,192},{192,128},{1,65},{65,1},{129,193},{193,129... | collective-permute-start | bytes 393224 | tf_op jit(solution)/shard_map/ppermute | solution.py:413
  12.5 0.0 collective-permute-done.6.refs_6_.right_ref
  12.5 0.1 collective-permute-done.5.refs_1_
  12.6 0.4 shard_map.101.before_ref.refs_0_
  13.0 1.5 %collective-permute-start.7 = (f32[32,8,128]{2,1,0:T(8,128)S(1)}, f32[32,8,128]{2,1,0:T(8,128)S(1)}, u32[]{:S(2)}, u32[]{:S(2)}) collective-permute-start(f32[32,8,128]{2,1,0:T(8,128)S(1)} %shard_map.101.before_ref.refs_0_), channel_id=1, source_target_pairs={{0,64},{64,0},{128,192},{192,128},{1,65},{65,1},{129,193},{193,129... | collective-permute-start | bytes 393224 | tf_op jit(solution)/shard_map/ppermute | solution.py:413
  14.5 2.0 %collective-permute-start.8 = (f32[128,128]{1,0:T(8,128)S(1)}, f32[128,128]{1,0:T(8,128)S(1)}, u32[]{:S(2)}, u32[]{:S(2)}) collective-permute-start(f32[128,128]{1,0:T(8,128)S(1)} %shard_map.102.left_ref), channel_id=1, source_target_pairs={{0,1},{1,0},{2,3},{3,2},{4,5},{5,4},{6,7},{7,6},{8,9},{9,8},{10,11... | collective-permute-start | bytes 196616 | tf_op jit(solution)/shard_map/ppermute | solution.py:413
  16.5 0.3 collective-permute-done.1.refs_1_
  16.8 0.4 shard_map.97.refs_0_.refs_5_
  17.2 2.1 %collective-permute-start.2 = (f32[32,8,128]{2,1,0:T(8,128)S(1)}, f32[32,8,128]{2,1,0:T(8,128)S(1)}, u32[]{:S(2)}, u32[]{:S(2)}) collective-permute-start(f32[32,8,128]{2,1,0:T(8,128)S(1)} %shard_map.97.refs_0_.refs_5_), channel_id=1, source_target_pairs={{0,16},{8,24},{16,0},{24,8},{1,17},{9,25},{17,1},{25,9},{2,18},{10... | collective-permute-start | bytes 393224 | tf_op jit(solution)/shard_map/ppermute | solution.py:413
  19.2 0.0 collective-permute-done.8.refs_6_.right_ref
  19.2 0.0 collective-permute-done.7.refs_1_
  19.2 0.4 shard_map.103.before_ref.refs_0_
  19.6 1.9 %collective-permute-start.9 = (f32[32,8,128]{2,1,0:T(8,128)S(1)}, f32[32,8,128]{2,1,0:T(8,128)S(1)}, u32[]{:S(2)}, u32[]{:S(2)}) collective-permute-start(f32[32,8,128]{2,1,0:T(8,128)S(1)} %shard_map.103.before_ref.refs_0_), channel_id=1, source_target_pairs={{0,16},{8,24},{16,0},{24,8},{1,17},{9,25},{17,1},{25,9},{2,18},{10... | collective-permute-start | bytes 393224 | tf_op jit(solution)/shard_map/ppermute | solution.py:413
  21.5 3.4 %collective-permute-start.10 = (f32[128,128]{1,0:T(8,128)S(1)}, f32[128,128]{1,0:T(8,128)S(1)}, u32[]{:S(2)}, u32[]{:S(2)}) collective-permute-start(f32[128,128]{1,0:T(8,128)S(1)} %shard_map.104.left_ref), channel_id=1, source_target_pairs={{0,2},{1,3},{2,0},{3,1},{4,6},{5,7},{6,4},{7,5},{8,10},{9,11},{10,... | collective-permute-start | bytes 196616 | tf_op jit(solution)/shard_map/ppermute | solution.py:413
  24.8 0.1 collective-permute-done.2.refs_1_
  24.9 0.4 shard_map.98.refs_0_.refs_5_
  25.3 1.5 %collective-permute-start.3 = (f32[32,8,128]{2,1,0:T(8,128)S(1)}, f32[32,8,128]{2,1,0:T(8,128)S(1)}, u32[]{:S(2)}, u32[]{:S(2)}) collective-permute-start(f32[32,8,128]{2,1,0:T(8,128)S(1)} %shard_map.98.refs_0_.refs_5_), channel_id=1, source_target_pairs={{0,8},{8,0},{16,24},{24,16},{1,9},{9,1},{17,25},{25,17},{2,10},{10... | collective-permute-start | bytes 393224 | tf_op jit(solution)/shard_map/ppermute | solution.py:413
  26.8 0.2 collective-permute-done.10.refs_6_.right_ref
  27.1 0.0 collective-permute-done.9.refs_1_
  27.1 0.4 shard_map.105.refs_0_.before_ref
  27.4 1.8 %collective-permute-start.11 = (f32[32,8,128]{2,1,0:T(8,128)S(1)}, f32[32,8,128]{2,1,0:T(8,128)S(1)}, u32[]{:S(2)}, u32[]{:S(2)}) collective-permute-start(f32[32,8,128]{2,1,0:T(8,128)S(1)} %shard_map.105.refs_0_.before_ref), channel_id=1, source_target_pairs={{0,8},{8,0},{16,24},{24,16},{1,9},{9,1},{17,25},{25,17},{2,10},{10... | collective-permute-start | bytes 393224 | tf_op jit(solution)/shard_map/ppermute | solution.py:413
  29.3 1.3 %collective-permute-start.13 = (f32[128,128]{1,0:T(8,128)S(1)}, f32[128,128]{1,0:T(8,128)S(1)}, u32[]{:S(2)}, u32[]{:S(2)}) collective-permute-start(f32[128,128]{1,0:T(8,128)S(1)} %shard_map.107.left_ref), channel_id=1, source_target_pairs={{0,64},{64,0},{128,192},{192,128},{1,65},{65,1},{129,193},{193,129... | collective-permute-start | bytes 196616 | tf_op jit(solution)/shard_map/ppermute | solution.py:413
  30.6 0.1 collective-permute-done.3.refs_1_
  30.7 0.4 shard_map.99.refs_0_.refs_5_
  31.1 0.0 copy-start.2
  31.1 7.9 %collective-permute-start.4 = (f32[32,8,128]{2,1,0:T(8,128)S(1)}, f32[32,8,128]{2,1,0:T(8,128)S(1)}, u32[]{:S(2)}, u32[]{:S(2)}) collective-permute-start(f32[32,8,128]{2,1,0:T(8,128)S(1)} %shard_map.99.refs_0_.refs_5_), channel_id=1, source_target_pairs={{0,4},{1,5},{2,6},{3,7},{4,0},{5,1},{6,2},{7,3},{8,12},{9,13},{10,... | collective-permute-start | bytes 393224 | tf_op jit(solution)/shard_map/ppermute | solution.py:413
  39.0 0.0 collective-permute-done.11.refs_1_
  39.0 0.4 shard_map.106.before_ref.refs_1_
  39.4 1.4 %collective-permute-start.12 = (f32[32,8,128]{2,1,0:T(8,128)S(1)}, f32[32,8,128]{2,1,0:T(8,128)S(1)}, u32[]{:S(2)}, u32[]{:S(2)}) collective-permute-start(f32[32,8,128]{2,1,0:T(8,128)S(1)} %shard_map.106.before_ref.refs_1_), channel_id=1, source_target_pairs={{0,4},{1,5},{2,6},{3,7},{4,0},{5,1},{6,2},{7,3},{8,12},{9,13},{10,... | collective-permute-start | bytes 393224 | tf_op jit(solution)/shard_map/ppermute | solution.py:413
  40.8 4.9 %collective-permute-start.14 = (f32[128,128]{1,0:T(8,128)S(1)}, f32[128,128]{1,0:T(8,128)S(1)}, u32[]{:S(2)}, u32[]{:S(2)}) collective-permute-start(f32[128,128]{1,0:T(8,128)S(1)} %shard_map.108.before_ref.gram_ref), channel_id=1, source_target_pairs={{0,4},{1,5},{2,6},{3,7},{4,0},{5,1},{6,2},{7,3},{8,12},{9,13},{10,... | collective-permute-start | bytes 196616 | tf_op jit(solution)/shard_map/ppermute | solution.py:413
  45.7 0.6 shard_map.109.refs_6_
  46.3 0.0 collective-permute-done.4.refs_1_
  46.3 0.4 shard_map.100.refs_0_
  46.7 3.0 %collective-permute-done.12.refs_2_ = f32[32,8,128]{2,1,0:T(8,128)S(1)} collective-permute-done((f32[32,8,128]{2,1,0:T(8,128)S(1)}, f32[32,8,128]{2,1,0:T(8,128)S(1)}, u32[]{:S(2)}, u32[]{:S(2)}) %collective-permute-start.12) | collective-permute-done | bytes 131104 | tf_op jit(solution)/shard_map/ppermute | solution.py:413
  49.7 2.5 %shard_map.110 = (f32[16,4096]{1,0:T(8,128)S(1)}, f32[24,128]{1,0:T(8,128)S(1)}) custom-call(f32[32,8,128]{2,1,0:T(8,128)S(1)} %shard_map.100.refs_0_, f32[32,8,128]{2,1,0:T(8,128)S(1)} %shard_map.106.before_ref.refs_1_, f32[32,8,128]{2,1,0:T(8,128)S(1)} %collective-permute-done.12.refs_2_, f32[5,2,2,128,128]{4,3,2,1,0:T(8,128)S(1)} %copy-done.3, ...), custom_call_target="tpu_custom_call" | custom-call | flops 402653184 | bytes 8388608 | tf_op jit(solution)/shard_map/pallas_call | solution.py:251
  52.2 0.0 collective-permute-done.14.other_ref
  52.2 0.1 collective-permute-start.15
  52.3 1.3 %collective-permute-done.15.other_ref = f32[152,128]{1,0:T(8,128)S(1)} collective-permute-done((f32[152,128]{1,0:T(8,128)S(1)}, f32[152,128]{1,0:T(8,128)S(1)}, u32[]{:S(2)}, u32[]{:S(2)}) %collective-permute-start.15) | collective-permute-done | bytes 77856 | tf_op jit(solution)/shard_map/ppermute | solution.py:413
  53.6 16.7 %all_to_all.10.got_ref = f32[16,56,128]{2,1,0:T(8,128)S(1)} all-to-all(f32[16,56,128]{2,1,0:T(8,128)S(1)} %shard_map.112), channel_id=1, replica_groups=mesh['y'=4,'core'=2,'x'=4,'z'=8] {'y','x'}, dimensions={0} | all-to-all | bytes 917504 | tf_op jit(solution)/shard_map/all_to_all | solution.py:441
  70.3 13.2 %all_to_all.11.refs_0_ = f32[8,24,128]{2,1,0:T(8,128)S(1)} all-to-all(f32[8,24,128]{2,1,0:T(8,128)S(1)} %get-tuple-element.23), channel_id=1, replica_groups=mesh['y'=4,'core'=2,'x'=4,'z'=8] {'z'}, dimensions={0} | all-to-all | bytes 196608 | tf_op jit(solution)/shard_map/all_to_all | solution.py:442
  83.6 1.9 %shard_map.114 = (f32[2,8,8,16]{3,2,1,0:T(8,128)}, f32[2,8,4096]{2,1,0:T(8,128)}, f32[2,8,8]{2,1,0:T(8,128)}) custom-call(f32[8,24,128]{2,1,0:T(8,128)S(1)} %all_to_all.11.refs_0_, f32[128,128]{1,0:T(8,128)S(1)} %get-tuple-element.24.refs_1_, f32[16,4096]{1,0:T(8,128)S(1)} %get-tuple-element.25.refs_2_, ...), custom_call_target="tpu_custom_call" | custom-call | flops 201326592 | bytes 6291456 | tf_op jit(solution)/shard_map/pallas_call | solution.py:381
  (19 shorter events, 0.2 us)
Async XLA Ops:
  0.6 5.9 %copy-start = (f32[16,2,8,4096]{3,2,1,0:T(8,128)S(1)}, f32[16,2,8,4096]{3,2,1,0:T(8,128)}, u32[]{:S(2)}) copy-start(f32[16,2,8,4096]{3,2,1,0:T(8,128)} %basis_ref.3) | copy-start | bytes 12582916
  2.9 7.4 %collective-permute-start = (f32[32,8,128]{2,1,0:T(8,128)S(1)}, f32[32,8,128]{2,1,0:T(8,128)S(1)}, u32[]{:S(2)}, u32[]{:S(2)}) collective-permute-start(f32[32,8,128]{2,1,0:T(8,128)S(1)} %get-tuple-element.16.before_ref.refs_0_), channel_id=1, source_target_pairs={{0,128},{64,192},{128,0},{192,64},{1,129},{65,193},{129,1},{193,65... | collective-permute-start | bytes 393224 | tf_op jit(solution)/shard_map/ppermute | solution.py:413
  6.1 4.1 %copy-start.3 = (f32[5,2,2,128,128]{4,3,2,1,0:T(8,128)S(1)}, f32[5,2,2,128,128]{4,3,2,1,0:T(8,128)}, u32[]{:S(2)}) copy-start(f32[5,2,2,128,128]{4,3,2,1,0:T(8,128)} %refs_3_.19) | copy-start | bytes 3932164
  6.2 4.1 %copy-start.4 = (s32[5,32]{1,0:T(8,128)S(1)}, s32[5,32]{1,0:T(8,128)}, u32[]{:S(2)}) copy-start(s32[5,32]{1,0:T(8,128)} %refs_4_.19) | copy-start | bytes 1924
  6.2 4.1 %copy-start.5 = (s32[5,1,32]{2,1,0:T(1,128)S(1)}, s32[5,1,32]{2,1,0:T(1,128)}, u32[]{:S(2)}) copy-start(s32[5,1,32]{2,1,0:T(1,128)} %refs_5_.1) | copy-start | bytes 1924
  6.2 6.5 %collective-permute-start.5 = (f32[32,8,128]{2,1,0:T(8,128)S(1)}, f32[32,8,128]{2,1,0:T(8,128)S(1)}, u32[]{:S(2)}, u32[]{:S(2)}) collective-permute-start(f32[32,8,128]{2,1,0:T(8,128)S(1)} %get-tuple-element.18.refs_0_), channel_id=1, source_target_pairs={{0,128},{64,192},{128,0},{192,64},{1,129},{65,193},{129,1},{193,65... | collective-permute-start | bytes 393224 | tf_op jit(solution)/shard_map/ppermute | solution.py:413
  7.9 4.6 %collective-permute-start.6 = (f32[128,128]{1,0:T(8,128)S(1)}, f32[128,128]{1,0:T(8,128)S(1)}, u32[]{:S(2)}, u32[]{:S(2)}) collective-permute-start(f32[128,128]{1,0:T(8,128)S(1)} %get-tuple-element.17.refs_5_.left_ref), channel_id=1, source_target_pairs={{0,8},{8,0},{16,24},{24,16},{1,9},{9,1},{17,25},{25,17},{2,10},{10... | collective-permute-start | bytes 196616 | tf_op jit(solution)/shard_map/ppermute | solution.py:413
  10.7 6.2 %collective-permute-start.1 = (f32[32,8,128]{2,1,0:T(8,128)S(1)}, f32[32,8,128]{2,1,0:T(8,128)S(1)}, u32[]{:S(2)}, u32[]{:S(2)}) collective-permute-start(f32[32,8,128]{2,1,0:T(8,128)S(1)} %shard_map.96.refs_0_.refs_5_), channel_id=1, source_target_pairs={{0,64},{64,0},{128,192},{192,128},{1,65},{65,1},{129,193},{193,129... | collective-permute-start | bytes 393224 | tf_op jit(solution)/shard_map/ppermute | solution.py:413
  13.0 6.3 %collective-permute-start.7 = (f32[32,8,128]{2,1,0:T(8,128)S(1)}, f32[32,8,128]{2,1,0:T(8,128)S(1)}, u32[]{:S(2)}, u32[]{:S(2)}) collective-permute-start(f32[32,8,128]{2,1,0:T(8,128)S(1)} %shard_map.101.before_ref.refs_0_), channel_id=1, source_target_pairs={{0,64},{64,0},{128,192},{192,128},{1,65},{65,1},{129,193},{193,129... | collective-permute-start | bytes 393224 | tf_op jit(solution)/shard_map/ppermute | solution.py:413
  14.5 4.7 %collective-permute-start.8 = (f32[128,128]{1,0:T(8,128)S(1)}, f32[128,128]{1,0:T(8,128)S(1)}, u32[]{:S(2)}, u32[]{:S(2)}) collective-permute-start(f32[128,128]{1,0:T(8,128)S(1)} %shard_map.102.left_ref), channel_id=1, source_target_pairs={{0,1},{1,0},{2,3},{3,2},{4,5},{5,4},{6,7},{7,6},{8,9},{9,8},{10,11... | collective-permute-start | bytes 196616 | tf_op jit(solution)/shard_map/ppermute | solution.py:413
  17.2 7.8 %collective-permute-start.2 = (f32[32,8,128]{2,1,0:T(8,128)S(1)}, f32[32,8,128]{2,1,0:T(8,128)S(1)}, u32[]{:S(2)}, u32[]{:S(2)}) collective-permute-start(f32[32,8,128]{2,1,0:T(8,128)S(1)} %shard_map.97.refs_0_.refs_5_), channel_id=1, source_target_pairs={{0,16},{8,24},{16,0},{24,8},{1,17},{9,25},{17,1},{25,9},{2,18},{10... | collective-permute-start | bytes 393224 | tf_op jit(solution)/shard_map/ppermute | solution.py:413
  19.6 7.5 %collective-permute-start.9 = (f32[32,8,128]{2,1,0:T(8,128)S(1)}, f32[32,8,128]{2,1,0:T(8,128)S(1)}, u32[]{:S(2)}, u32[]{:S(2)}) collective-permute-start(f32[32,8,128]{2,1,0:T(8,128)S(1)} %shard_map.103.before_ref.refs_0_), channel_id=1, source_target_pairs={{0,16},{8,24},{16,0},{24,8},{1,17},{9,25},{17,1},{25,9},{2,18},{10... | collective-permute-start | bytes 393224 | tf_op jit(solution)/shard_map/ppermute | solution.py:413
  21.5 5.6 %collective-permute-start.10 = (f32[128,128]{1,0:T(8,128)S(1)}, f32[128,128]{1,0:T(8,128)S(1)}, u32[]{:S(2)}, u32[]{:S(2)}) collective-permute-start(f32[128,128]{1,0:T(8,128)S(1)} %shard_map.104.left_ref), channel_id=1, source_target_pairs={{0,2},{1,3},{2,0},{3,1},{4,6},{5,7},{6,4},{7,5},{8,10},{9,11},{10,... | collective-permute-start | bytes 196616 | tf_op jit(solution)/shard_map/ppermute | solution.py:413
  25.3 5.4 %collective-permute-start.3 = (f32[32,8,128]{2,1,0:T(8,128)S(1)}, f32[32,8,128]{2,1,0:T(8,128)S(1)}, u32[]{:S(2)}, u32[]{:S(2)}) collective-permute-start(f32[32,8,128]{2,1,0:T(8,128)S(1)} %shard_map.98.refs_0_.refs_5_), channel_id=1, source_target_pairs={{0,8},{8,0},{16,24},{24,16},{1,9},{9,1},{17,25},{25,17},{2,10},{10... | collective-permute-start | bytes 393224 | tf_op jit(solution)/shard_map/ppermute | solution.py:413
  27.4 11.6 %collective-permute-start.11 = (f32[32,8,128]{2,1,0:T(8,128)S(1)}, f32[32,8,128]{2,1,0:T(8,128)S(1)}, u32[]{:S(2)}, u32[]{:S(2)}) collective-permute-start(f32[32,8,128]{2,1,0:T(8,128)S(1)} %shard_map.105.refs_0_.before_ref), channel_id=1, source_target_pairs={{0,8},{8,0},{16,24},{24,16},{1,9},{9,1},{17,25},{25,17},{2,10},{10... | collective-permute-start | bytes 393224 | tf_op jit(solution)/shard_map/ppermute | solution.py:413
  29.3 11.5 %collective-permute-start.13 = (f32[128,128]{1,0:T(8,128)S(1)}, f32[128,128]{1,0:T(8,128)S(1)}, u32[]{:S(2)}, u32[]{:S(2)}) collective-permute-start(f32[128,128]{1,0:T(8,128)S(1)} %shard_map.107.left_ref), channel_id=1, source_target_pairs={{0,64},{64,0},{128,192},{192,128},{1,65},{65,1},{129,193},{193,129... | collective-permute-start | bytes 196616 | tf_op jit(solution)/shard_map/ppermute | solution.py:413
  31.1 14.6 %copy-start.2 = (bf16[2,32,128,128]{3,2,1,0:T(8,128)(2,1)S(1)}, bf16[2,32,128,128]{3,2,1,0:T(8,128)(2,1)}, u32[]{:S(2)}) copy-start(bf16[2,32,128,128]{3,2,1,0:T(8,128)(2,1)} %leaf_ref.3) | copy-start | bytes 6291460
  31.1 15.2 %collective-permute-start.4 = (f32[32,8,128]{2,1,0:T(8,128)S(1)}, f32[32,8,128]{2,1,0:T(8,128)S(1)}, u32[]{:S(2)}, u32[]{:S(2)}) collective-permute-start(f32[32,8,128]{2,1,0:T(8,128)S(1)} %shard_map.99.refs_0_.refs_5_), channel_id=1, source_target_pairs={{0,4},{1,5},{2,6},{3,7},{4,0},{5,1},{6,2},{7,3},{8,12},{9,13},{10,... | collective-permute-start | bytes 393224 | tf_op jit(solution)/shard_map/ppermute | solution.py:413
  39.4 10.3 %collective-permute-start.12 = (f32[32,8,128]{2,1,0:T(8,128)S(1)}, f32[32,8,128]{2,1,0:T(8,128)S(1)}, u32[]{:S(2)}, u32[]{:S(2)}) collective-permute-start(f32[32,8,128]{2,1,0:T(8,128)S(1)} %shard_map.106.before_ref.refs_1_), channel_id=1, source_target_pairs={{0,4},{1,5},{2,6},{3,7},{4,0},{5,1},{6,2},{7,3},{8,12},{9,13},{10,... | collective-permute-start | bytes 393224 | tf_op jit(solution)/shard_map/ppermute | solution.py:413
  40.8 11.4 %collective-permute-start.14 = (f32[128,128]{1,0:T(8,128)S(1)}, f32[128,128]{1,0:T(8,128)S(1)}, u32[]{:S(2)}, u32[]{:S(2)}) collective-permute-start(f32[128,128]{1,0:T(8,128)S(1)} %shard_map.108.before_ref.gram_ref), channel_id=1, source_target_pairs={{0,4},{1,5},{2,6},{3,7},{4,0},{5,1},{6,2},{7,3},{8,12},{9,13},{10,... | collective-permute-start | bytes 196616 | tf_op jit(solution)/shard_map/ppermute | solution.py:413
  46.3 3.4 %copy-start.1 = (bf16[2,32,128,128]{3,2,1,0:T(8,128)(2,1)S(1)}, bf16[2,32,128,128]{3,2,1,0:T(8,128)(2,1)}, u32[]{:S(2)}) copy-start(bf16[2,32,128,128]{3,2,1,0:T(8,128)(2,1)} %refs_7_.1) | copy-start | bytes 6291460
  52.2 1.4 %collective-permute-start.15 = (f32[152,128]{1,0:T(8,128)S(1)}, f32[152,128]{1,0:T(8,128)S(1)}, u32[]{:S(2)}, u32[]{:S(2)}) collective-permute-start(f32[152,128]{1,0:T(8,128)S(1)} %shard_map.111.own_ref), channel_id=1, source_target_pairs={{0,32},{32,0},{1,33},{33,1},{2,34},{34,2},{3,35},{35,3},{4,36},{36... | collective-permute-start | bytes 233480 | tf_op jit(solution)/shard_map/ppermute | solution.py:413

commit v9 on v8

--- a/solution.py
+++ b/solution.py
@@ -278,61 +278,60 @@
     )(sums, gram, other)
 
 
-def merge_kernel(own_ref, other_ref, out_ref, sum_ref):
-    sum_ref[...] = own_ref[...] + other_ref[...]
+def merge_kernel(own_ref, other_ref, out_ref, gram_ref):
+    sums = own_ref[0:24] + other_ref[0:24]
+    for device in range(out_ref.shape[0]):
+        out_ref[device] = sums
+    gram_ref[...] = own_ref[24:152] + other_ref[24:152]
+
+
+def merge(own, other):
+    return pl.pallas_call(
+        merge_kernel,
+        in_specs=[VMEM] * 2,
+        out_specs=[VMEM] * 2,
+        out_shape=[
+            jax.ShapeDtypeStruct((lax.axis_size("z"), 24, 128), jnp.float32),
+            jax.ShapeDtypeStruct((128, 128), jnp.float32),
+        ],
+        compiler_params=pltpu.CompilerParams(vmem_limit_bytes=KERNEL_VMEM),
+    )(own, other)
+
+
+def relay_kernel(got_ref, gram_ref, out_ref):
+    sums = jnp.sum(got_ref[...], axis=0)
     mine = lax.rem(lax.axis_index("y"), 2) * 2 + lax.rem(lax.axis_index("x"), 2)
-    sums = sum_ref[0:24]
-    piece = sum_ref[pl.ds(pl.multiple_of(24 + mine * 32, 8), 32), :]
+    piece = gram_ref[pl.ds(pl.multiple_of(mine * 32, 32), 32), :]
     for device in range(out_ref.shape[0]):
         out_ref[device, 0:24] = sums
         out_ref[device, 24:56] = piece
 
 
-def merge(own, other):
-    return pl.pallas_call(
-        merge_kernel,
+def relay(got, gram):
+    return pl.pallas_call(
+        relay_kernel,
         in_specs=[VMEM] * 2,
         out_specs=VMEM,
         out_shape=jax.ShapeDtypeStruct((lax.axis_size(("y", "x")), 56, 128), jnp.float32),
-        scratch_shapes=[pltpu.VMEM((152, 128), jnp.float32)],
-        compiler_params=pltpu.CompilerParams(vmem_limit_bytes=KERNEL_VMEM),
-    )(own, other)
-
-
-def relay_kernel(got_ref, out_ref, gram_ref):
-    sums = jnp.sum(got_ref[:, 0:24], axis=0)
-    for device in range(out_ref.shape[0]):
-        out_ref[device] = sums
+        compiler_params=pltpu.CompilerParams(vmem_limit_bytes=KERNEL_VMEM),
+    )(got, gram)
+
+
+def dot_high(left, right, numbers):
+    return lax.dot_general(
+        left, right, numbers, precision=lax.Precision.HIGHEST, preferred_element_type=jnp.float32
+    )
+
+
+def finish_kernel(
+    scale, got_ref, image_ref, high_ref, low_ref, total_ref, new_ref, block_ref, gram_ref
+):
+    sums = jnp.sum(got_ref[:, 0:24], axis=0) * scale
     for quarter in range(4):
         at = quarter // 2 * 4 + quarter % 2
         gram_ref[quarter * 32 : (quarter + 1) * 32] = (got_ref[at, 24:56] + got_ref[at + 2, 24:56]) + (
             got_ref[at + 8, 24:56] + got_ref[at + 10, 24:56]
         )
-
-
-def relay(got):
-    return pl.pallas_call(
-        relay_kernel,
-        in_specs=[VMEM],
-        out_specs=[VMEM] * 2,
-        out_shape=[
-            jax.ShapeDtypeStruct((lax.axis_size("z"), 24, 128), jnp.float32),
-            jax.ShapeDtypeStruct((128, 128), jnp.float32),
-        ],
-        compiler_params=pltpu.CompilerParams(vmem_limit_bytes=KERNEL_VMEM),
-    )(got)
-
-
-def dot_high(left, right, numbers):
-    return lax.dot_general(
-        left, right, numbers, precision=lax.Precision.HIGHEST, preferred_element_type=jnp.float32
-    )
-
-
-def finish_kernel(
-    scale, got_ref, gram_ref, image_ref, high_ref, low_ref, total_ref, new_ref, block_ref
-):
-    sums = jnp.sum(got_ref[...], axis=0) * scale
     first = sums[:16]
     packed = gram_ref[...] * scale
     row = lax.broadcasted_iota(jnp.int32, (128, 128), 0)
@@ -377,21 +376,22 @@
         total_ref[1, angle] = turned[8:, angle * 16 : (angle + 1) * 16]
 
 
-def finish(scale, got, gram, image, parts):
+def finish(scale, got, image, parts):
     return pl.pallas_call(
         lambda *refs: finish_kernel(scale, *refs),
-        in_specs=[VMEM] * 5,
+        in_specs=[VMEM] * 4,
         out_specs=[VMEM] * 3,
         out_shape=[
             jax.ShapeDtypeStruct((2, 8, 8, 16), jnp.float32),
             jax.ShapeDtypeStruct((2, 8, 4096), jnp.float32),
             jax.ShapeDtypeStruct((2, 8, 8), jnp.float32),
         ],
+        scratch_shapes=[pltpu.VMEM((128, 128), jnp.float32)],
         compiler_params=pltpu.CompilerParams(vmem_limit_bytes=KERNEL_VMEM),
         cost_estimate=pl.CostEstimate(
             flops=6 * 16 * 256 * 4096 * 2, bytes_accessed=6 << 20, transcendentals=0
         ),
-    )(got, gram, image, *[in_vmem(part) for part in parts])
+    )(got, image, *[in_vmem(part) for part in parts])
 
 
 def add_kernel(left_ref, right_ref, before_ref, out_ref):
@@ -437,11 +437,11 @@
                 level, lower, coeffs[1], partner[1], tables, close, leaf_out, parts
             )
     sums = stack(sums, gram, exchange(gram, "z", 2))
-    got = merge(sums, exchange(sums, "core", 0))
-    got, gram = relay(lax.all_to_all(got, ("y", "x"), 0, 0))
-    got = lax.all_to_all(got, "z", 0, 0)
+    got, gram = merge(sums, exchange(sums, "core", 0))
+    got = relay(lax.all_to_all(got, "z", 0, 0), gram)
+    got = lax.all_to_all(got, ("y", "x"), 0, 0)
     scale = 1.0 / (krylov_basis.shape[3] * lax.axis_size(AXES))
-    total, new_block, block_gram = finish(scale, got, gram, image, parts)
+    total, new_block, block_gram = finish(scale, got, image, parts)
     return jnp.transpose(total, (3, 0, 1, 2)), new_block, block_gram
 
 

time: 85.6 us -> 84.3 us (0.985)
  blocking collectives: 29.9 us -> 28.5 us
    all_to_all x2, blocking collectives: 29.9 us -> 28.5 us  [the longest x1 14.9 us: per_device(): got = relay(lax.all_to_all(got, 'z', 0, 0), gram)]
where the time goes in v9:
time: 84.3 us; the launch traced here: 84.1 us
  starting transfers between devices  37.6 us (45%)
  blocking collectives  28.5 us (34%)
  Pallas kernels  12 us (14%)
  waiting for transfers between devices  5.24 us (6%)
    ppermute x16, starting transfers between devices, exchange(): return lax.ppermute(value, axis, pairs)  37.6 us
    all_to_all x1, blocking collectives, per_device(): got = relay(lax.all_to_all(got, 'z', 0, 0), gram)  14.9 us
    all_to_all x1, blocking collectives, per_device(): got = lax.all_to_all(got, ('y', 'x'), 0, 0)  13.6 us
    ppermute x16, waiting for transfers between devices, exchange(): return lax.ppermute(value, axis, pairs)  5.24 us
    pallas_call x9, Pallas kernels, next_level(): pl.pallas_call(lambda *refs: level_kernel(level, *refs), in_specs=[VMEM]...  3.21 us
    pallas_call x1, Pallas kernels, project(): pl.pallas_call(lambda *refs: project_kernel(level, *refs), in_specs=[VMEM...  2.47 us
    pallas_call x1, Pallas kernels, leaves_in(): pl.pallas_call(leaves_in_kernel, in_specs=[pl.BlockSpec(memory_space=pltp...  2.22 us
    pallas_call x1, Pallas kernels, finish(): pl.pallas_call(lambda *refs: finish_kernel(scale, *refs), in_specs=[VMEM]...  1.9 us
  transfers between devices with their start and end apart: 16, of which 7 were waited for; matrix products, arithmetic and copies ran while one was open for 0% of the time, Pallas kernels for 9%

profile of v9, /device:TPU:2, one launch (start us, length us, event | category | flops | bytes accessed | tf_op | source)
XLA Modules:
  0.0 84.1 jit_solution(1889275910616797111)
XLA Ops:
  0.6 2.2 %shard_map.94 = (f32[32,8,128]{2,1,0:T(8,128)S(1)}, f32[32,8,128]{2,1,0:T(8,128)S(1)}, f32[32,16,128]{2,1,0:T(8,128)S(1)}) custom-call(f32[16,2,8,4096]{3,2,1,0:T(8,128)} %basis_ref.3, bf16[2,32,128,128]{3,2,1,0:T(8,128)(2,1)} %leaf_ref.2), custom_call_target="tpu_custom_call" | custom-call | flops 33554432 | bytes 2359296 | tf_op jit(solution)/shard_map/pallas_call | solution.py:102
  2.9 3.3 %collective-permute-start = (f32[32,8,128]{2,1,0:T(8,128)S(1)}, f32[32,8,128]{2,1,0:T(8,128)S(1)}, u32[]{:S(2)}, u32[]{:S(2)}) collective-permute-start(f32[32,8,128]{2,1,0:T(8,128)S(1)} %get-tuple-element.16.before_ref.refs_0_), channel_id=1, source_target_pairs={{0,128},{64,192},{128,0},{192,64},{1,129},{65,193},{129,1},{193,65... | collective-permute-start | bytes 393224 | tf_op jit(solution)/shard_map/ppermute | solution.py:413
  6.2 0.3 collective-permute-start.5
  6.5 1.4 %shard_map.95 = (f32[128,128]{1,0:T(8,128)S(1)}, bf16[256,4096]{1,0:T(8,128)(2,1)S(1)}, bf16[256,4096]{1,0:T(8,128)(2,1)S(1)}) custom-call(f32[16,2,8,4096]{3,2,1,0:T(8,128)S(1)} %copy-done, f32[32,8,128]{2,1,0:T(8,128)S(1)} %get-tuple-element.16.before_ref.refs_0_), custom_call_target="tpu_custom_call" | custom-call | flops 1073741824 | bytes 8388608 | tf_op jit(solution)/shard_map/pallas_call | solution.py:166
  7.9 2.4 %collective-permute-start.6 = (f32[128,128]{1,0:T(8,128)S(1)}, f32[128,128]{1,0:T(8,128)S(1)}, u32[]{:S(2)}, u32[]{:S(2)}) collective-permute-start(f32[128,128]{1,0:T(8,128)S(1)} %get-tuple-element.17.refs_5_.left_ref), channel_id=1, source_target_pairs={{0,8},{8,0},{16,24},{24,16},{1,9},{9,1},{17,25},{25,17},{2,10},{10... | collective-permute-start | bytes 196616 | tf_op jit(solution)/shard_map/ppermute | solution.py:413
  10.3 0.0 collective-permute-done.refs_1_
  10.3 0.4 shard_map.96.refs_0_.refs_5_
  10.7 1.9 %collective-permute-start.1 = (f32[32,8,128]{2,1,0:T(8,128)S(1)}, f32[32,8,128]{2,1,0:T(8,128)S(1)}, u32[]{:S(2)}, u32[]{:S(2)}) collective-permute-start(f32[32,8,128]{2,1,0:T(8,128)S(1)} %shard_map.96.refs_0_.refs_5_), channel_id=1, source_target_pairs={{0,64},{64,0},{128,192},{192,128},{1,65},{65,1},{129,193},{193,129... | collective-permute-start | bytes 393224 | tf_op jit(solution)/shard_map/ppermute | solution.py:413
  12.5 0.0 collective-permute-done.6.refs_6_.right_ref
  12.5 0.1 collective-permute-done.5.refs_1_
  12.6 0.4 shard_map.101.before_ref.refs_0_
  13.0 1.5 %collective-permute-start.7 = (f32[32,8,128]{2,1,0:T(8,128)S(1)}, f32[32,8,128]{2,1,0:T(8,128)S(1)}, u32[]{:S(2)}, u32[]{:S(2)}) collective-permute-start(f32[32,8,128]{2,1,0:T(8,128)S(1)} %shard_map.101.before_ref.refs_0_), channel_id=1, source_target_pairs={{0,64},{64,0},{128,192},{192,128},{1,65},{65,1},{129,193},{193,129... | collective-permute-start | bytes 393224 | tf_op jit(solution)/shard_map/ppermute | solution.py:413
  14.5 2.0 %collective-permute-start.8 = (f32[128,128]{1,0:T(8,128)S(1)}, f32[128,128]{1,0:T(8,128)S(1)}, u32[]{:S(2)}, u32[]{:S(2)}) collective-permute-start(f32[128,128]{1,0:T(8,128)S(1)} %shard_map.102.left_ref), channel_id=1, source_target_pairs={{0,1},{1,0},{2,3},{3,2},{4,5},{5,4},{6,7},{7,6},{8,9},{9,8},{10,11... | collective-permute-start | bytes 196616 | tf_op jit(solution)/shard_map/ppermute | solution.py:413
  16.5 0.3 collective-permute-done.1.refs_1_
  16.8 0.4 shard_map.97.refs_0_.refs_5_
  17.2 2.1 %collective-permute-start.2 = (f32[32,8,128]{2,1,0:T(8,128)S(1)}, f32[32,8,128]{2,1,0:T(8,128)S(1)}, u32[]{:S(2)}, u32[]{:S(2)}) collective-permute-start(f32[32,8,128]{2,1,0:T(8,128)S(1)} %shard_map.97.refs_0_.refs_5_), channel_id=1, source_target_pairs={{0,16},{8,24},{16,0},{24,8},{1,17},{9,25},{17,1},{25,9},{2,18},{10... | collective-permute-start | bytes 393224 | tf_op jit(solution)/shard_map/ppermute | solution.py:413
  19.2 0.0 collective-permute-done.8.refs_6_.right_ref
  19.2 0.0 collective-permute-done.7.refs_1_
  19.2 0.4 shard_map.103.before_ref.refs_0_
  19.6 1.9 %collective-permute-start.9 = (f32[32,8,128]{2,1,0:T(8,128)S(1)}, f32[32,8,128]{2,1,0:T(8,128)S(1)}, u32[]{:S(2)}, u32[]{:S(2)}) collective-permute-start(f32[32,8,128]{2,1,0:T(8,128)S(1)} %shard_map.103.before_ref.refs_0_), channel_id=1, source_target_pairs={{0,16},{8,24},{16,0},{24,8},{1,17},{9,25},{17,1},{25,9},{2,18},{10... | collective-permute-start | bytes 393224 | tf_op jit(solution)/shard_map/ppermute | solution.py:413
  21.5 3.4 %collective-permute-start.10 = (f32[128,128]{1,0:T(8,128)S(1)}, f32[128,128]{1,0:T(8,128)S(1)}, u32[]{:S(2)}, u32[]{:S(2)}) collective-permute-start(f32[128,128]{1,0:T(8,128)S(1)} %shard_map.104.left_ref), channel_id=1, source_target_pairs={{0,2},{1,3},{2,0},{3,1},{4,6},{5,7},{6,4},{7,5},{8,10},{9,11},{10,... | collective-permute-start | bytes 196616 | tf_op jit(solution)/shard_map/ppermute | solution.py:413
  24.8 0.1 collective-permute-done.2.refs_1_
  25.0 0.4 shard_map.98.refs_0_.refs_5_
  25.3 1.5 %collective-permute-start.3 = (f32[32,8,128]{2,1,0:T(8,128)S(1)}, f32[32,8,128]{2,1,0:T(8,128)S(1)}, u32[]{:S(2)}, u32[]{:S(2)}) collective-permute-start(f32[32,8,128]{2,1,0:T(8,128)S(1)} %shard_map.98.refs_0_.refs_5_), channel_id=1, source_target_pairs={{0,8},{8,0},{16,24},{24,16},{1,9},{9,1},{17,25},{25,17},{2,10},{10... | collective-permute-start | bytes 393224 | tf_op jit(solution)/shard_map/ppermute | solution.py:413
  26.8 0.3 collective-permute-done.10.refs_6_.right_ref
  27.1 0.0 collective-permute-done.9.refs_1_
  27.1 0.4 shard_map.105.refs_0_.before_ref
  27.4 1.8 %collective-permute-start.11 = (f32[32,8,128]{2,1,0:T(8,128)S(1)}, f32[32,8,128]{2,1,0:T(8,128)S(1)}, u32[]{:S(2)}, u32[]{:S(2)}) collective-permute-start(f32[32,8,128]{2,1,0:T(8,128)S(1)} %shard_map.105.refs_0_.before_ref), channel_id=1, source_target_pairs={{0,8},{8,0},{16,24},{24,16},{1,9},{9,1},{17,25},{25,17},{2,10},{10... | collective-permute-start | bytes 393224 | tf_op jit(solution)/shard_map/ppermute | solution.py:413
  29.3 1.3 %collective-permute-start.13 = (f32[128,128]{1,0:T(8,128)S(1)}, f32[128,128]{1,0:T(8,128)S(1)}, u32[]{:S(2)}, u32[]{:S(2)}) collective-permute-start(f32[128,128]{1,0:T(8,128)S(1)} %shard_map.107.left_ref), channel_id=1, source_target_pairs={{0,64},{64,0},{128,192},{192,128},{1,65},{65,1},{129,193},{193,129... | collective-permute-start | bytes 196616 | tf_op jit(solution)/shard_map/ppermute | solution.py:413
  30.6 0.1 collective-permute-done.3.refs_1_
  30.7 0.4 shard_map.99.refs_0_.refs_5_
  31.1 0.0 copy-start.2
  31.1 7.9 %collective-permute-start.4 = (f32[32,8,128]{2,1,0:T(8,128)S(1)}, f32[32,8,128]{2,1,0:T(8,128)S(1)}, u32[]{:S(2)}, u32[]{:S(2)}) collective-permute-start(f32[32,8,128]{2,1,0:T(8,128)S(1)} %shard_map.99.refs_0_.refs_5_), channel_id=1, source_target_pairs={{0,4},{1,5},{2,6},{3,7},{4,0},{5,1},{6,2},{7,3},{8,12},{9,13},{10,... | collective-permute-start | bytes 393224 | tf_op jit(solution)/shard_map/ppermute | solution.py:413
  39.0 0.0 collective-permute-done.11.refs_1_
  39.0 0.4 shard_map.106.before_ref.refs_1_
  39.4 1.4 %collective-permute-start.12 = (f32[32,8,128]{2,1,0:T(8,128)S(1)}, f32[32,8,128]{2,1,0:T(8,128)S(1)}, u32[]{:S(2)}, u32[]{:S(2)}) collective-permute-start(f32[32,8,128]{2,1,0:T(8,128)S(1)} %shard_map.106.before_ref.refs_1_), channel_id=1, source_target_pairs={{0,4},{1,5},{2,6},{3,7},{4,0},{5,1},{6,2},{7,3},{8,12},{9,13},{10,... | collective-permute-start | bytes 393224 | tf_op jit(solution)/shard_map/ppermute | solution.py:413
  40.8 0.0 collective-permute-done.13.right_ref
  40.8 4.9 %collective-permute-start.14 = (f32[128,128]{1,0:T(8,128)S(1)}, f32[128,128]{1,0:T(8,128)S(1)}, u32[]{:S(2)}, u32[]{:S(2)}) collective-permute-start(f32[128,128]{1,0:T(8,128)S(1)} %shard_map.108.before_ref.gram_ref), channel_id=1, source_target_pairs={{0,4},{1,5},{2,6},{3,7},{4,0},{5,1},{6,2},{7,3},{8,12},{9,13},{10,... | collective-permute-start | bytes 196616 | tf_op jit(solution)/shard_map/ppermute | solution.py:413
  45.7 0.6 shard_map.109.refs_6_
  46.3 0.4 shard_map.100.refs_0_
  46.7 3.1 %collective-permute-done.12.refs_2_ = f32[32,8,128]{2,1,0:T(8,128)S(1)} collective-permute-done((f32[32,8,128]{2,1,0:T(8,128)S(1)}, f32[32,8,128]{2,1,0:T(8,128)S(1)}, u32[]{:S(2)}, u32[]{:S(2)}) %collective-permute-start.12) | collective-permute-done | bytes 131104 | tf_op jit(solution)/shard_map/ppermute | solution.py:413
  49.8 2.5 %shard_map.110 = (f32[16,4096]{1,0:T(8,128)S(1)}, f32[24,128]{1,0:T(8,128)S(1)}) custom-call(f32[32,8,128]{2,1,0:T(8,128)S(1)} %shard_map.100.refs_0_, f32[32,8,128]{2,1,0:T(8,128)S(1)} %shard_map.106.before_ref.refs_1_, f32[32,8,128]{2,1,0:T(8,128)S(1)} %collective-permute-done.12.refs_2_, f32[5,2,2,128,128]{4,3,2,1,0:T(8,128)S(1)} %copy-done.3, ...), custom_call_target="tpu_custom_call" | custom-call | flops 402653184 | bytes 8388608 | tf_op jit(solution)/shard_map/pallas_call | solution.py:251
  52.3 0.0 collective-permute-done.14.other_ref
  52.3 0.1 collective-permute-start.15
  52.4 1.3 %collective-permute-done.15.other_ref = f32[152,128]{1,0:T(8,128)S(1)} collective-permute-done((f32[152,128]{1,0:T(8,128)S(1)}, f32[152,128]{1,0:T(8,128)S(1)}, u32[]{:S(2)}, u32[]{:S(2)}) %collective-permute-start.15) | collective-permute-done | bytes 77856 | tf_op jit(solution)/shard_map/ppermute | solution.py:413
  53.7 14.9 %all_to_all.10.got_ref = f32[8,24,128]{2,1,0:T(8,128)S(1)} all-to-all(f32[8,24,128]{2,1,0:T(8,128)S(1)} %get-tuple-element.23), channel_id=1, replica_groups=mesh['y'=4,'core'=2,'x'=4,'z'=8] {'z'}, dimensions={0} | all-to-all | bytes 196608 | tf_op jit(solution)/shard_map/all_to_all | solution.py:441
  68.7 13.6 %all_to_all.11.refs_0_ = f32[16,56,128]{2,1,0:T(8,128)S(1)} all-to-all(f32[16,56,128]{2,1,0:T(8,128)S(1)} %shard_map.113), channel_id=1, replica_groups=mesh['y'=4,'core'=2,'x'=4,'z'=8] {'y','x'}, dimensions={0} | all-to-all | bytes 917504 | tf_op jit(solution)/shard_map/all_to_all | solution.py:442
  82.2 1.9 %shard_map.114 = (f32[2,8,8,16]{3,2,1,0:T(8,128)}, f32[2,8,4096]{2,1,0:T(8,128)}, f32[2,8,8]{2,1,0:T(8,128)}) custom-call(f32[16,56,128]{2,1,0:T(8,128)S(1)} %all_to_all.11.refs_0_, f32[16,4096]{1,0:T(8,128)S(1)} %get-tuple-element.25.refs_1_, bf16[256,4096]{1,0:T(8,128)(2,1)S(1)} %get-tuple-element.20.refs_8_.refs_2_, ...), custom_call_target="tpu_custom_call" | custom-call | flops 201326592 | bytes 6291456 | tf_op jit(solution)/shard_map/pallas_call | solution.py:380
  (19 shorter events, 0.2 us)
Async XLA Ops:
  0.6 5.9 %copy-start = (f32[16,2,8,4096]{3,2,1,0:T(8,128)S(1)}, f32[16,2,8,4096]{3,2,1,0:T(8,128)}, u32[]{:S(2)}) copy-start(f32[16,2,8,4096]{3,2,1,0:T(8,128)} %basis_ref.3) | copy-start | bytes 12582916
  2.9 7.4 %collective-permute-start = (f32[32,8,128]{2,1,0:T(8,128)S(1)}, f32[32,8,128]{2,1,0:T(8,128)S(1)}, u32[]{:S(2)}, u32[]{:S(2)}) collective-permute-start(f32[32,8,128]{2,1,0:T(8,128)S(1)} %get-tuple-element.16.before_ref.refs_0_), channel_id=1, source_target_pairs={{0,128},{64,192},{128,0},{192,64},{1,129},{65,193},{129,1},{193,65... | collective-permute-start | bytes 393224 | tf_op jit(solution)/shard_map/ppermute | solution.py:413
  6.1 4.1 %copy-start.3 = (f32[5,2,2,128,128]{4,3,2,1,0:T(8,128)S(1)}, f32[5,2,2,128,128]{4,3,2,1,0:T(8,128)}, u32[]{:S(2)}) copy-start(f32[5,2,2,128,128]{4,3,2,1,0:T(8,128)} %refs_3_.19) | copy-start | bytes 3932164
  6.2 4.1 %copy-start.4 = (s32[5,32]{1,0:T(8,128)S(1)}, s32[5,32]{1,0:T(8,128)}, u32[]{:S(2)}) copy-start(s32[5,32]{1,0:T(8,128)} %refs_4_.19) | copy-start | bytes 1924
  6.2 4.1 %copy-start.5 = (s32[5,1,32]{2,1,0:T(1,128)S(1)}, s32[5,1,32]{2,1,0:T(1,128)}, u32[]{:S(2)}) copy-start(s32[5,1,32]{2,1,0:T(1,128)} %refs_5_.1) | copy-start | bytes 1924
  6.2 6.5 %collective-permute-start.5 = (f32[32,8,128]{2,1,0:T(8,128)S(1)}, f32[32,8,128]{2,1,0:T(8,128)S(1)}, u32[]{:S(2)}, u32[]{:S(2)}) collective-permute-start(f32[32,8,128]{2,1,0:T(8,128)S(1)} %get-tuple-element.18.refs_0_), channel_id=1, source_target_pairs={{0,128},{64,192},{128,0},{192,64},{1,129},{65,193},{129,1},{193,65... | collective-permute-start | bytes 393224 | tf_op jit(solution)/shard_map/ppermute | solution.py:413
  7.9 4.6 %collective-permute-start.6 = (f32[128,128]{1,0:T(8,128)S(1)}, f32[128,128]{1,0:T(8,128)S(1)}, u32[]{:S(2)}, u32[]{:S(2)}) collective-permute-start(f32[128,128]{1,0:T(8,128)S(1)} %get-tuple-element.17.refs_5_.left_ref), channel_id=1, source_target_pairs={{0,8},{8,0},{16,24},{24,16},{1,9},{9,1},{17,25},{25,17},{2,10},{10... | collective-permute-start | bytes 196616 | tf_op jit(solution)/shard_map/ppermute | solution.py:413
  10.7 6.2 %collective-permute-start.1 = (f32[32,8,128]{2,1,0:T(8,128)S(1)}, f32[32,8,128]{2,1,0:T(8,128)S(1)}, u32[]{:S(2)}, u32[]{:S(2)}) collective-permute-start(f32[32,8,128]{2,1,0:T(8,128)S(1)} %shard_map.96.refs_0_.refs_5_), channel_id=1, source_target_pairs={{0,64},{64,0},{128,192},{192,128},{1,65},{65,1},{129,193},{193,129... | collective-permute-start | bytes 393224 | tf_op jit(solution)/shard_map/ppermute | solution.py:413
  13.0 6.3 %collective-permute-start.7 = (f32[32,8,128]{2,1,0:T(8,128)S(1)}, f32[32,8,128]{2,1,0:T(8,128)S(1)}, u32[]{:S(2)}, u32[]{:S(2)}) collective-permute-start(f32[32,8,128]{2,1,0:T(8,128)S(1)} %shard_map.101.before_ref.refs_0_), channel_id=1, source_target_pairs={{0,64},{64,0},{128,192},{192,128},{1,65},{65,1},{129,193},{193,129... | collective-permute-start | bytes 393224 | tf_op jit(solution)/shard_map/ppermute | solution.py:413
  14.5 4.7 %collective-permute-start.8 = (f32[128,128]{1,0:T(8,128)S(1)}, f32[128,128]{1,0:T(8,128)S(1)}, u32[]{:S(2)}, u32[]{:S(2)}) collective-permute-start(f32[128,128]{1,0:T(8,128)S(1)} %shard_map.102.left_ref), channel_id=1, source_target_pairs={{0,1},{1,0},{2,3},{3,2},{4,5},{5,4},{6,7},{7,6},{8,9},{9,8},{10,11... | collective-permute-start | bytes 196616 | tf_op jit(solution)/shard_map/ppermute | solution.py:413
  17.2 7.8 %collective-permute-start.2 = (f32[32,8,128]{2,1,0:T(8,128)S(1)}, f32[32,8,128]{2,1,0:T(8,128)S(1)}, u32[]{:S(2)}, u32[]{:S(2)}) collective-permute-start(f32[32,8,128]{2,1,0:T(8,128)S(1)} %shard_map.97.refs_0_.refs_5_), channel_id=1, source_target_pairs={{0,16},{8,24},{16,0},{24,8},{1,17},{9,25},{17,1},{25,9},{2,18},{10... | collective-permute-start | bytes 393224 | tf_op jit(solution)/shard_map/ppermute | solution.py:413
  19.6 7.5 %collective-permute-start.9 = (f32[32,8,128]{2,1,0:T(8,128)S(1)}, f32[32,8,128]{2,1,0:T(8,128)S(1)}, u32[]{:S(2)}, u32[]{:S(2)}) collective-permute-start(f32[32,8,128]{2,1,0:T(8,128)S(1)} %shard_map.103.before_ref.refs_0_), channel_id=1, source_target_pairs={{0,16},{8,24},{16,0},{24,8},{1,17},{9,25},{17,1},{25,9},{2,18},{10... | collective-permute-start | bytes 393224 | tf_op jit(solution)/shard_map/ppermute | solution.py:413
  21.5 5.6 %collective-permute-start.10 = (f32[128,128]{1,0:T(8,128)S(1)}, f32[128,128]{1,0:T(8,128)S(1)}, u32[]{:S(2)}, u32[]{:S(2)}) collective-permute-start(f32[128,128]{1,0:T(8,128)S(1)} %shard_map.104.left_ref), channel_id=1, source_target_pairs={{0,2},{1,3},{2,0},{3,1},{4,6},{5,7},{6,4},{7,5},{8,10},{9,11},{10,... | collective-permute-start | bytes 196616 | tf_op jit(solution)/shard_map/ppermute | solution.py:413
  25.3 5.4 %collective-permute-start.3 = (f32[32,8,128]{2,1,0:T(8,128)S(1)}, f32[32,8,128]{2,1,0:T(8,128)S(1)}, u32[]{:S(2)}, u32[]{:S(2)}) collective-permute-start(f32[32,8,128]{2,1,0:T(8,128)S(1)} %shard_map.98.refs_0_.refs_5_), channel_id=1, source_target_pairs={{0,8},{8,0},{16,24},{24,16},{1,9},{9,1},{17,25},{25,17},{2,10},{10... | collective-permute-start | bytes 393224 | tf_op jit(solution)/shard_map/ppermute | solution.py:413
  27.4 11.5 %collective-permute-start.11 = (f32[32,8,128]{2,1,0:T(8,128)S(1)}, f32[32,8,128]{2,1,0:T(8,128)S(1)}, u32[]{:S(2)}, u32[]{:S(2)}) collective-permute-start(f32[32,8,128]{2,1,0:T(8,128)S(1)} %shard_map.105.refs_0_.before_ref), channel_id=1, source_target_pairs={{0,8},{8,0},{16,24},{24,16},{1,9},{9,1},{17,25},{25,17},{2,10},{10... | collective-permute-start | bytes 393224 | tf_op jit(solution)/shard_map/ppermute | solution.py:413
  29.3 11.5 %collective-permute-start.13 = (f32[128,128]{1,0:T(8,128)S(1)}, f32[128,128]{1,0:T(8,128)S(1)}, u32[]{:S(2)}, u32[]{:S(2)}) collective-permute-start(f32[128,128]{1,0:T(8,128)S(1)} %shard_map.107.left_ref), channel_id=1, source_target_pairs={{0,64},{64,0},{128,192},{192,128},{1,65},{65,1},{129,193},{193,129... | collective-permute-start | bytes 196616 | tf_op jit(solution)/shard_map/ppermute | solution.py:413
  31.1 14.6 %copy-start.2 = (bf16[2,32,128,128]{3,2,1,0:T(8,128)(2,1)S(1)}, bf16[2,32,128,128]{3,2,1,0:T(8,128)(2,1)}, u32[]{:S(2)}) copy-start(bf16[2,32,128,128]{3,2,1,0:T(8,128)(2,1)} %leaf_ref.3) | copy-start | bytes 6291460
  31.1 15.2 %collective-permute-start.4 = (f32[32,8,128]{2,1,0:T(8,128)S(1)}, f32[32,8,128]{2,1,0:T(8,128)S(1)}, u32[]{:S(2)}, u32[]{:S(2)}) collective-permute-start(f32[32,8,128]{2,1,0:T(8,128)S(1)} %shard_map.99.refs_0_.refs_5_), channel_id=1, source_target_pairs={{0,4},{1,5},{2,6},{3,7},{4,0},{5,1},{6,2},{7,3},{8,12},{9,13},{10,... | collective-permute-start | bytes 393224 | tf_op jit(solution)/shard_map/ppermute | solution.py:413
  39.4 10.4 %collective-permute-start.12 = (f32[32,8,128]{2,1,0:T(8,128)S(1)}, f32[32,8,128]{2,1,0:T(8,128)S(1)}, u32[]{:S(2)}, u32[]{:S(2)}) collective-permute-start(f32[32,8,128]{2,1,0:T(8,128)S(1)} %shard_map.106.before_ref.refs_1_), channel_id=1, source_target_pairs={{0,4},{1,5},{2,6},{3,7},{4,0},{5,1},{6,2},{7,3},{8,12},{9,13},{10,... | collective-permute-start | bytes 393224 | tf_op jit(solution)/shard_map/ppermute | solution.py:413
  40.8 11.5 %collective-permute-start.14 = (f32[128,128]{1,0:T(8,128)S(1)}, f32[128,128]{1,0:T(8,128)S(1)}, u32[]{:S(2)}, u32[]{:S(2)}) collective-permute-start(f32[128,128]{1,0:T(8,128)S(1)} %shard_map.108.before_ref.gram_ref), channel_id=1, source_target_pairs={{0,4},{1,5},{2,6},{3,7},{4,0},{5,1},{6,2},{7,3},{8,12},{9,13},{10,... | collective-permute-start | bytes 196616 | tf_op jit(solution)/shard_map/ppermute | solution.py:413
  46.3 3.5 %copy-start.1 = (bf16[2,32,128,128]{3,2,1,0:T(8,128)(2,1)S(1)}, bf16[2,32,128,128]{3,2,1,0:T(8,128)(2,1)}, u32[]{:S(2)}) copy-start(bf16[2,32,128,128]{3,2,1,0:T(8,128)(2,1)} %refs_7_.1) | copy-start | bytes 6291460
  52.3 1.4 %collective-permute-start.15 = (f32[152,128]{1,0:T(8,128)S(1)}, f32[152,128]{1,0:T(8,128)S(1)}, u32[]{:S(2)}, u32[]{:S(2)}) collective-permute-start(f32[152,128]{1,0:T(8,128)S(1)} %shard_map.111.own_ref), channel_id=1, source_target_pairs={{0,32},{32,0},{1,33},{33,1},{2,34},{34,2},{3,35},{35,3},{4,36},{36... | collective-permute-start | bytes 233480 | tf_op jit(solution)/shard_map/ppermute | solution.py:413

commit v10 on v9

--- a/solution.py
+++ b/solution.py
@@ -370,7 +370,11 @@
         taken = one[:16] + one[16:] + dot_nn(high, low_ref[:, here])
         new_ref[:, :, here] = (image_ref[:, here] - taken).reshape(2, 8, width)
     turn = jnp.where(row == lax.rem(column, 16) * 8 + lax.div(column, 16), 1.0, 0.0)
-    turned = dot_high(total, turn, NN)
+    upper, middle = split2(total)
+    lower = (total - upper.astype(jnp.float32)) - middle.astype(jnp.float32)
+    parts = jnp.concatenate([upper, middle, lower.astype(jnp.bfloat16)], axis=0)
+    parts = dot_nn(parts, turn.astype(jnp.bfloat16))
+    turned = parts[:16] + parts[16:32] + parts[32:]
     for angle in range(8):
         total_ref[0, angle] = turned[:8, angle * 16 : (angle + 1) * 16]
         total_ref[1, angle] = turned[8:, angle * 16 : (angle + 1) * 16]

time: 84.3 us -> 84.3 us (level)
  no operation moved by 1% of the time
where the time goes in v10:
time: 84.3 us; the launch traced here: 84.1 us
  starting transfers between devices  37.6 us (45%)
  blocking collectives  28.5 us (34%)
  Pallas kernels  11.9 us (14%)
  waiting for transfers between devices  5.23 us (6%)
    ppermute x16, starting transfers between devices, exchange(): return lax.ppermute(value, axis, pairs)  37.6 us
    all_to_all x1, blocking collectives, per_device(): got = relay(lax.all_to_all(got, 'z', 0, 0), gram)  14.9 us
    all_to_all x1, blocking collectives, per_device(): got = lax.all_to_all(got, ('y', 'x'), 0, 0)  13.6 us
    ppermute x16, waiting for transfers between devices, exchange(): return lax.ppermute(value, axis, pairs)  5.23 us
    pallas_call x9, Pallas kernels, next_level(): pl.pallas_call(lambda *refs: level_kernel(level, *refs), in_specs=[VMEM]...  3.2 us
    pallas_call x1, Pallas kernels, project(): pl.pallas_call(lambda *refs: project_kernel(level, *refs), in_specs=[VMEM...  2.47 us
    pallas_call x1, Pallas kernels, leaves_in(): pl.pallas_call(leaves_in_kernel, in_specs=[pl.BlockSpec(memory_space=pltp...  2.22 us
    pallas_call x1, Pallas kernels, finish(): pl.pallas_call(lambda *refs: finish_kernel(scale, *refs), in_specs=[VMEM]...  1.83 us
  transfers between devices with their start and end apart: 16, of which 7 were waited for; matrix products, arithmetic and copies ran while one was open for 0% of the time, Pallas kernels for 9%

profile of v10, /device:TPU:2, one launch (start us, length us, event | category | flops | bytes accessed | tf_op | source)
XLA Modules:
  0.0 84.1 jit_solution(2282669407937664771)
XLA Ops:
  0.6 2.2 %shard_map.94 = (f32[32,8,128]{2,1,0:T(8,128)S(1)}, f32[32,8,128]{2,1,0:T(8,128)S(1)}, f32[32,16,128]{2,1,0:T(8,128)S(1)}) custom-call(f32[16,2,8,4096]{3,2,1,0:T(8,128)} %basis_ref.3, bf16[2,32,128,128]{3,2,1,0:T(8,128)(2,1)} %leaf_ref.2), custom_call_target="tpu_custom_call" | custom-call | flops 33554432 | bytes 2359296 | tf_op jit(solution)/shard_map/pallas_call | solution.py:102
  2.9 3.3 %collective-permute-start = (f32[32,8,128]{2,1,0:T(8,128)S(1)}, f32[32,8,128]{2,1,0:T(8,128)S(1)}, u32[]{:S(2)}, u32[]{:S(2)}) collective-permute-start(f32[32,8,128]{2,1,0:T(8,128)S(1)} %get-tuple-element.16.before_ref.refs_0_), channel_id=1, source_target_pairs={{0,128},{64,192},{128,0},{192,64},{1,129},{65,193},{129,1},{193,65... | collective-permute-start | bytes 393224 | tf_op jit(solution)/shard_map/ppermute | solution.py:417
  6.2 0.3 collective-permute-start.5
  6.5 1.4 %shard_map.95 = (f32[128,128]{1,0:T(8,128)S(1)}, bf16[256,4096]{1,0:T(8,128)(2,1)S(1)}, bf16[256,4096]{1,0:T(8,128)(2,1)S(1)}) custom-call(f32[16,2,8,4096]{3,2,1,0:T(8,128)S(1)} %copy-done, f32[32,8,128]{2,1,0:T(8,128)S(1)} %get-tuple-element.16.before_ref.refs_0_), custom_call_target="tpu_custom_call" | custom-call | flops 1073741824 | bytes 8388608 | tf_op jit(solution)/shard_map/pallas_call | solution.py:166
  7.9 2.4 %collective-permute-start.6 = (f32[128,128]{1,0:T(8,128)S(1)}, f32[128,128]{1,0:T(8,128)S(1)}, u32[]{:S(2)}, u32[]{:S(2)}) collective-permute-start(f32[128,128]{1,0:T(8,128)S(1)} %get-tuple-element.17.refs_5_.left_ref), channel_id=1, source_target_pairs={{0,8},{8,0},{16,24},{24,16},{1,9},{9,1},{17,25},{25,17},{2,10},{10... | collective-permute-start | bytes 196616 | tf_op jit(solution)/shard_map/ppermute | solution.py:417
  10.3 0.0 collective-permute-done.refs_1_
  10.3 0.4 shard_map.96.refs_0_.refs_5_
  10.7 1.9 %collective-permute-start.1 = (f32[32,8,128]{2,1,0:T(8,128)S(1)}, f32[32,8,128]{2,1,0:T(8,128)S(1)}, u32[]{:S(2)}, u32[]{:S(2)}) collective-permute-start(f32[32,8,128]{2,1,0:T(8,128)S(1)} %shard_map.96.refs_0_.refs_5_), channel_id=1, source_target_pairs={{0,64},{64,0},{128,192},{192,128},{1,65},{65,1},{129,193},{193,129... | collective-permute-start | bytes 393224 | tf_op jit(solution)/shard_map/ppermute | solution.py:417
  12.5 0.0 collective-permute-done.6.refs_6_.right_ref
  12.5 0.1 collective-permute-done.5.refs_1_
  12.6 0.4 shard_map.101.before_ref.refs_0_
  13.0 1.5 %collective-permute-start.7 = (f32[32,8,128]{2,1,0:T(8,128)S(1)}, f32[32,8,128]{2,1,0:T(8,128)S(1)}, u32[]{:S(2)}, u32[]{:S(2)}) collective-permute-start(f32[32,8,128]{2,1,0:T(8,128)S(1)} %shard_map.101.before_ref.refs_0_), channel_id=1, source_target_pairs={{0,64},{64,0},{128,192},{192,128},{1,65},{65,1},{129,193},{193,129... | collective-permute-start | bytes 393224 | tf_op jit(solution)/shard_map/ppermute | solution.py:417
  14.5 2.0 %collective-permute-start.8 = (f32[128,128]{1,0:T(8,128)S(1)}, f32[128,128]{1,0:T(8,128)S(1)}, u32[]{:S(2)}, u32[]{:S(2)}) collective-permute-start(f32[128,128]{1,0:T(8,128)S(1)} %shard_map.102.left_ref), channel_id=1, source_target_pairs={{0,1},{1,0},{2,3},{3,2},{4,5},{5,4},{6,7},{7,6},{8,9},{9,8},{10,11... | collective-permute-start | bytes 196616 | tf_op jit(solution)/shard_map/ppermute | solution.py:417
  16.5 0.3 collective-permute-done.1.refs_1_
  16.8 0.4 shard_map.97.refs_0_.refs_5_
  17.2 2.1 %collective-permute-start.2 = (f32[32,8,128]{2,1,0:T(8,128)S(1)}, f32[32,8,128]{2,1,0:T(8,128)S(1)}, u32[]{:S(2)}, u32[]{:S(2)}) collective-permute-start(f32[32,8,128]{2,1,0:T(8,128)S(1)} %shard_map.97.refs_0_.refs_5_), channel_id=1, source_target_pairs={{0,16},{8,24},{16,0},{24,8},{1,17},{9,25},{17,1},{25,9},{2,18},{10... | collective-permute-start | bytes 393224 | tf_op jit(solution)/shard_map/ppermute | solution.py:417
  19.2 0.0 collective-permute-done.8.refs_6_.right_ref
  19.3 0.0 collective-permute-done.7.refs_1_
  19.3 0.4 shard_map.103.before_ref.refs_0_
  19.6 1.9 %collective-permute-start.9 = (f32[32,8,128]{2,1,0:T(8,128)S(1)}, f32[32,8,128]{2,1,0:T(8,128)S(1)}, u32[]{:S(2)}, u32[]{:S(2)}) collective-permute-start(f32[32,8,128]{2,1,0:T(8,128)S(1)} %shard_map.103.before_ref.refs_0_), channel_id=1, source_target_pairs={{0,16},{8,24},{16,0},{24,8},{1,17},{9,25},{17,1},{25,9},{2,18},{10... | collective-permute-start | bytes 393224 | tf_op jit(solution)/shard_map/ppermute | solution.py:417
  21.5 3.4 %collective-permute-start.10 = (f32[128,128]{1,0:T(8,128)S(1)}, f32[128,128]{1,0:T(8,128)S(1)}, u32[]{:S(2)}, u32[]{:S(2)}) collective-permute-start(f32[128,128]{1,0:T(8,128)S(1)} %shard_map.104.left_ref), channel_id=1, source_target_pairs={{0,2},{1,3},{2,0},{3,1},{4,6},{5,7},{6,4},{7,5},{8,10},{9,11},{10,... | collective-permute-start | bytes 196616 | tf_op jit(solution)/shard_map/ppermute | solution.py:417
  24.8 0.1 collective-permute-done.2.refs_1_
  24.9 0.4 shard_map.98.refs_0_.refs_5_
  25.3 1.5 %collective-permute-start.3 = (f32[32,8,128]{2,1,0:T(8,128)S(1)}, f32[32,8,128]{2,1,0:T(8,128)S(1)}, u32[]{:S(2)}, u32[]{:S(2)}) collective-permute-start(f32[32,8,128]{2,1,0:T(8,128)S(1)} %shard_map.98.refs_0_.refs_5_), channel_id=1, source_target_pairs={{0,8},{8,0},{16,24},{24,16},{1,9},{9,1},{17,25},{25,17},{2,10},{10... | collective-permute-start | bytes 393224 | tf_op jit(solution)/shard_map/ppermute | solution.py:417
  26.8 0.3 collective-permute-done.10.refs_6_.right_ref
  27.1 0.0 collective-permute-done.9.refs_1_
  27.1 0.4 shard_map.105.refs_0_.before_ref
  27.4 1.8 %collective-permute-start.11 = (f32[32,8,128]{2,1,0:T(8,128)S(1)}, f32[32,8,128]{2,1,0:T(8,128)S(1)}, u32[]{:S(2)}, u32[]{:S(2)}) collective-permute-start(f32[32,8,128]{2,1,0:T(8,128)S(1)} %shard_map.105.refs_0_.before_ref), channel_id=1, source_target_pairs={{0,8},{8,0},{16,24},{24,16},{1,9},{9,1},{17,25},{25,17},{2,10},{10... | collective-permute-start | bytes 393224 | tf_op jit(solution)/shard_map/ppermute | solution.py:417
  29.3 1.3 %collective-permute-start.13 = (f32[128,128]{1,0:T(8,128)S(1)}, f32[128,128]{1,0:T(8,128)S(1)}, u32[]{:S(2)}, u32[]{:S(2)}) collective-permute-start(f32[128,128]{1,0:T(8,128)S(1)} %shard_map.107.left_ref), channel_id=1, source_target_pairs={{0,64},{64,0},{128,192},{192,128},{1,65},{65,1},{129,193},{193,129... | collective-permute-start | bytes 196616 | tf_op jit(solution)/shard_map/ppermute | solution.py:417
  30.6 0.1 collective-permute-done.3.refs_1_
  30.7 0.4 shard_map.99.refs_0_.refs_5_
  31.1 0.0 copy-start.2
  31.1 7.9 %collective-permute-start.4 = (f32[32,8,128]{2,1,0:T(8,128)S(1)}, f32[32,8,128]{2,1,0:T(8,128)S(1)}, u32[]{:S(2)}, u32[]{:S(2)}) collective-permute-start(f32[32,8,128]{2,1,0:T(8,128)S(1)} %shard_map.99.refs_0_.refs_5_), channel_id=1, source_target_pairs={{0,4},{1,5},{2,6},{3,7},{4,0},{5,1},{6,2},{7,3},{8,12},{9,13},{10,... | collective-permute-start | bytes 393224 | tf_op jit(solution)/shard_map/ppermute | solution.py:417
  39.0 0.0 collective-permute-done.11.refs_1_
  39.0 0.4 shard_map.106.before_ref.refs_1_
  39.4 1.4 %collective-permute-start.12 = (f32[32,8,128]{2,1,0:T(8,128)S(1)}, f32[32,8,128]{2,1,0:T(8,128)S(1)}, u32[]{:S(2)}, u32[]{:S(2)}) collective-permute-start(f32[32,8,128]{2,1,0:T(8,128)S(1)} %shard_map.106.before_ref.refs_1_), channel_id=1, source_target_pairs={{0,4},{1,5},{2,6},{3,7},{4,0},{5,1},{6,2},{7,3},{8,12},{9,13},{10,... | collective-permute-start | bytes 393224 | tf_op jit(solution)/shard_map/ppermute | solution.py:417
  40.8 0.0 collective-permute-done.13.right_ref
  40.8 4.9 %collective-permute-start.14 = (f32[128,128]{1,0:T(8,128)S(1)}, f32[128,128]{1,0:T(8,128)S(1)}, u32[]{:S(2)}, u32[]{:S(2)}) collective-permute-start(f32[128,128]{1,0:T(8,128)S(1)} %shard_map.108.before_ref.gram_ref), channel_id=1, source_target_pairs={{0,4},{1,5},{2,6},{3,7},{4,0},{5,1},{6,2},{7,3},{8,12},{9,13},{10,... | collective-permute-start | bytes 196616 | tf_op jit(solution)/shard_map/ppermute | solution.py:417
  45.7 0.6 shard_map.109.refs_6_
  46.3 0.0 collective-permute-done.4.refs_1_
  46.3 0.4 shard_map.100.refs_0_
  46.7 3.1 %collective-permute-done.12.refs_2_ = f32[32,8,128]{2,1,0:T(8,128)S(1)} collective-permute-done((f32[32,8,128]{2,1,0:T(8,128)S(1)}, f32[32,8,128]{2,1,0:T(8,128)S(1)}, u32[]{:S(2)}, u32[]{:S(2)}) %collective-permute-start.12) | collective-permute-done | bytes 131104 | tf_op jit(solution)/shard_map/ppermute | solution.py:417
  49.8 2.5 %shard_map.110 = (f32[16,4096]{1,0:T(8,128)S(1)}, f32[24,128]{1,0:T(8,128)S(1)}) custom-call(f32[32,8,128]{2,1,0:T(8,128)S(1)} %shard_map.100.refs_0_, f32[32,8,128]{2,1,0:T(8,128)S(1)} %shard_map.106.before_ref.refs_1_, f32[32,8,128]{2,1,0:T(8,128)S(1)} %collective-permute-done.12.refs_2_, f32[5,2,2,128,128]{4,3,2,1,0:T(8,128)S(1)} %copy-done.3, ...), custom_call_target="tpu_custom_call" | custom-call | flops 402653184 | bytes 8388608 | tf_op jit(solution)/shard_map/pallas_call | solution.py:251
  52.3 0.1 collective-permute-start.15
  52.4 1.3 %collective-permute-done.15.other_ref = f32[152,128]{1,0:T(8,128)S(1)} collective-permute-done((f32[152,128]{1,0:T(8,128)S(1)}, f32[152,128]{1,0:T(8,128)S(1)}, u32[]{:S(2)}, u32[]{:S(2)}) %collective-permute-start.15) | collective-permute-done | bytes 77856 | tf_op jit(solution)/shard_map/ppermute | solution.py:417
  53.7 14.9 %all_to_all.10.got_ref = f32[8,24,128]{2,1,0:T(8,128)S(1)} all-to-all(f32[8,24,128]{2,1,0:T(8,128)S(1)} %get-tuple-element.23), channel_id=1, replica_groups=mesh['y'=4,'core'=2,'x'=4,'z'=8] {'z'}, dimensions={0} | all-to-all | bytes 196608 | tf_op jit(solution)/shard_map/all_to_all | solution.py:445
  68.7 13.6 %all_to_all.11.refs_0_ = f32[16,56,128]{2,1,0:T(8,128)S(1)} all-to-all(f32[16,56,128]{2,1,0:T(8,128)S(1)} %shard_map.113), channel_id=1, replica_groups=mesh['y'=4,'core'=2,'x'=4,'z'=8] {'y','x'}, dimensions={0} | all-to-all | bytes 917504 | tf_op jit(solution)/shard_map/all_to_all | solution.py:446
  82.3 1.8 %shard_map.114 = (f32[2,8,8,16]{3,2,1,0:T(8,128)}, f32[2,8,4096]{2,1,0:T(8,128)}, f32[2,8,8]{2,1,0:T(8,128)}) custom-call(f32[16,56,128]{2,1,0:T(8,128)S(1)} %all_to_all.11.refs_0_, f32[16,4096]{1,0:T(8,128)S(1)} %get-tuple-element.25.refs_1_, bf16[256,4096]{1,0:T(8,128)(2,1)S(1)} %get-tuple-element.20.refs_8_.refs_2_, ...), custom_call_target="tpu_custom_call" | custom-call | flops 201326592 | bytes 6291456 | tf_op jit(solution)/shard_map/pallas_call | solution.py:384
  (19 shorter events, 0.2 us)
Async XLA Ops:
  0.6 5.9 %copy-start = (f32[16,2,8,4096]{3,2,1,0:T(8,128)S(1)}, f32[16,2,8,4096]{3,2,1,0:T(8,128)}, u32[]{:S(2)}) copy-start(f32[16,2,8,4096]{3,2,1,0:T(8,128)} %basis_ref.3) | copy-start | bytes 12582916
  2.9 7.4 %collective-permute-start = (f32[32,8,128]{2,1,0:T(8,128)S(1)}, f32[32,8,128]{2,1,0:T(8,128)S(1)}, u32[]{:S(2)}, u32[]{:S(2)}) collective-permute-start(f32[32,8,128]{2,1,0:T(8,128)S(1)} %get-tuple-element.16.before_ref.refs_0_), channel_id=1, source_target_pairs={{0,128},{64,192},{128,0},{192,64},{1,129},{65,193},{129,1},{193,65... | collective-permute-start | bytes 393224 | tf_op jit(solution)/shard_map/ppermute | solution.py:417
  6.1 4.1 %copy-start.3 = (f32[5,2,2,128,128]{4,3,2,1,0:T(8,128)S(1)}, f32[5,2,2,128,128]{4,3,2,1,0:T(8,128)}, u32[]{:S(2)}) copy-start(f32[5,2,2,128,128]{4,3,2,1,0:T(8,128)} %refs_3_.19) | copy-start | bytes 3932164
  6.2 4.1 %copy-start.4 = (s32[5,32]{1,0:T(8,128)S(1)}, s32[5,32]{1,0:T(8,128)}, u32[]{:S(2)}) copy-start(s32[5,32]{1,0:T(8,128)} %refs_4_.19) | copy-start | bytes 1924
  6.2 4.1 %copy-start.5 = (s32[5,1,32]{2,1,0:T(1,128)S(1)}, s32[5,1,32]{2,1,0:T(1,128)}, u32[]{:S(2)}) copy-start(s32[5,1,32]{2,1,0:T(1,128)} %refs_5_.1) | copy-start | bytes 1924
  6.2 6.5 %collective-permute-start.5 = (f32[32,8,128]{2,1,0:T(8,128)S(1)}, f32[32,8,128]{2,1,0:T(8,128)S(1)}, u32[]{:S(2)}, u32[]{:S(2)}) collective-permute-start(f32[32,8,128]{2,1,0:T(8,128)S(1)} %get-tuple-element.18.refs_0_), channel_id=1, source_target_pairs={{0,128},{64,192},{128,0},{192,64},{1,129},{65,193},{129,1},{193,65... | collective-permute-start | bytes 393224 | tf_op jit(solution)/shard_map/ppermute | solution.py:417
  7.9 4.6 %collective-permute-start.6 = (f32[128,128]{1,0:T(8,128)S(1)}, f32[128,128]{1,0:T(8,128)S(1)}, u32[]{:S(2)}, u32[]{:S(2)}) collective-permute-start(f32[128,128]{1,0:T(8,128)S(1)} %get-tuple-element.17.refs_5_.left_ref), channel_id=1, source_target_pairs={{0,8},{8,0},{16,24},{24,16},{1,9},{9,1},{17,25},{25,17},{2,10},{10... | collective-permute-start | bytes 196616 | tf_op jit(solution)/shard_map/ppermute | solution.py:417
  10.7 6.2 %collective-permute-start.1 = (f32[32,8,128]{2,1,0:T(8,128)S(1)}, f32[32,8,128]{2,1,0:T(8,128)S(1)}, u32[]{:S(2)}, u32[]{:S(2)}) collective-permute-start(f32[32,8,128]{2,1,0:T(8,128)S(1)} %shard_map.96.refs_0_.refs_5_), channel_id=1, source_target_pairs={{0,64},{64,0},{128,192},{192,128},{1,65},{65,1},{129,193},{193,129... | collective-permute-start | bytes 393224 | tf_op jit(solution)/shard_map/ppermute | solution.py:417
  13.0 6.3 %collective-permute-start.7 = (f32[32,8,128]{2,1,0:T(8,128)S(1)}, f32[32,8,128]{2,1,0:T(8,128)S(1)}, u32[]{:S(2)}, u32[]{:S(2)}) collective-permute-start(f32[32,8,128]{2,1,0:T(8,128)S(1)} %shard_map.101.before_ref.refs_0_), channel_id=1, source_target_pairs={{0,64},{64,0},{128,192},{192,128},{1,65},{65,1},{129,193},{193,129... | collective-permute-start | bytes 393224 | tf_op jit(solution)/shard_map/ppermute | solution.py:417
  14.5 4.7 %collective-permute-start.8 = (f32[128,128]{1,0:T(8,128)S(1)}, f32[128,128]{1,0:T(8,128)S(1)}, u32[]{:S(2)}, u32[]{:S(2)}) collective-permute-start(f32[128,128]{1,0:T(8,128)S(1)} %shard_map.102.left_ref), channel_id=1, source_target_pairs={{0,1},{1,0},{2,3},{3,2},{4,5},{5,4},{6,7},{7,6},{8,9},{9,8},{10,11... | collective-permute-start | bytes 196616 | tf_op jit(solution)/shard_map/ppermute | solution.py:417
  17.2 7.8 %collective-permute-start.2 = (f32[32,8,128]{2,1,0:T(8,128)S(1)}, f32[32,8,128]{2,1,0:T(8,128)S(1)}, u32[]{:S(2)}, u32[]{:S(2)}) collective-permute-start(f32[32,8,128]{2,1,0:T(8,128)S(1)} %shard_map.97.refs_0_.refs_5_), channel_id=1, source_target_pairs={{0,16},{8,24},{16,0},{24,8},{1,17},{9,25},{17,1},{25,9},{2,18},{10... | collective-permute-start | bytes 393224 | tf_op jit(solution)/shard_map/ppermute | solution.py:417
  19.6 7.5 %collective-permute-start.9 = (f32[32,8,128]{2,1,0:T(8,128)S(1)}, f32[32,8,128]{2,1,0:T(8,128)S(1)}, u32[]{:S(2)}, u32[]{:S(2)}) collective-permute-start(f32[32,8,128]{2,1,0:T(8,128)S(1)} %shard_map.103.before_ref.refs_0_), channel_id=1, source_target_pairs={{0,16},{8,24},{16,0},{24,8},{1,17},{9,25},{17,1},{25,9},{2,18},{10... | collective-permute-start | bytes 393224 | tf_op jit(solution)/shard_map/ppermute | solution.py:417
  21.5 5.6 %collective-permute-start.10 = (f32[128,128]{1,0:T(8,128)S(1)}, f32[128,128]{1,0:T(8,128)S(1)}, u32[]{:S(2)}, u32[]{:S(2)}) collective-permute-start(f32[128,128]{1,0:T(8,128)S(1)} %shard_map.104.left_ref), channel_id=1, source_target_pairs={{0,2},{1,3},{2,0},{3,1},{4,6},{5,7},{6,4},{7,5},{8,10},{9,11},{10,... | collective-permute-start | bytes 196616 | tf_op jit(solution)/shard_map/ppermute | solution.py:417
  25.3 5.4 %collective-permute-start.3 = (f32[32,8,128]{2,1,0:T(8,128)S(1)}, f32[32,8,128]{2,1,0:T(8,128)S(1)}, u32[]{:S(2)}, u32[]{:S(2)}) collective-permute-start(f32[32,8,128]{2,1,0:T(8,128)S(1)} %shard_map.98.refs_0_.refs_5_), channel_id=1, source_target_pairs={{0,8},{8,0},{16,24},{24,16},{1,9},{9,1},{17,25},{25,17},{2,10},{10... | collective-permute-start | bytes 393224 | tf_op jit(solution)/shard_map/ppermute | solution.py:417
  27.4 11.6 %collective-permute-start.11 = (f32[32,8,128]{2,1,0:T(8,128)S(1)}, f32[32,8,128]{2,1,0:T(8,128)S(1)}, u32[]{:S(2)}, u32[]{:S(2)}) collective-permute-start(f32[32,8,128]{2,1,0:T(8,128)S(1)} %shard_map.105.refs_0_.before_ref), channel_id=1, source_target_pairs={{0,8},{8,0},{16,24},{24,16},{1,9},{9,1},{17,25},{25,17},{2,10},{10... | collective-permute-start | bytes 393224 | tf_op jit(solution)/shard_map/ppermute | solution.py:417
  29.3 11.5 %collective-permute-start.13 = (f32[128,128]{1,0:T(8,128)S(1)}, f32[128,128]{1,0:T(8,128)S(1)}, u32[]{:S(2)}, u32[]{:S(2)}) collective-permute-start(f32[128,128]{1,0:T(8,128)S(1)} %shard_map.107.left_ref), channel_id=1, source_target_pairs={{0,64},{64,0},{128,192},{192,128},{1,65},{65,1},{129,193},{193,129... | collective-permute-start | bytes 196616 | tf_op jit(solution)/shard_map/ppermute | solution.py:417
  31.1 14.6 %copy-start.2 = (bf16[2,32,128,128]{3,2,1,0:T(8,128)(2,1)S(1)}, bf16[2,32,128,128]{3,2,1,0:T(8,128)(2,1)}, u32[]{:S(2)}) copy-start(bf16[2,32,128,128]{3,2,1,0:T(8,128)(2,1)} %leaf_ref.3) | copy-start | bytes 6291460
  31.1 15.2 %collective-permute-start.4 = (f32[32,8,128]{2,1,0:T(8,128)S(1)}, f32[32,8,128]{2,1,0:T(8,128)S(1)}, u32[]{:S(2)}, u32[]{:S(2)}) collective-permute-start(f32[32,8,128]{2,1,0:T(8,128)S(1)} %shard_map.99.refs_0_.refs_5_), channel_id=1, source_target_pairs={{0,4},{1,5},{2,6},{3,7},{4,0},{5,1},{6,2},{7,3},{8,12},{9,13},{10,... | collective-permute-start | bytes 393224 | tf_op jit(solution)/shard_map/ppermute | solution.py:417
  39.4 10.4 %collective-permute-start.12 = (f32[32,8,128]{2,1,0:T(8,128)S(1)}, f32[32,8,128]{2,1,0:T(8,128)S(1)}, u32[]{:S(2)}, u32[]{:S(2)}) collective-permute-start(f32[32,8,128]{2,1,0:T(8,128)S(1)} %shard_map.106.before_ref.refs_1_), channel_id=1, source_target_pairs={{0,4},{1,5},{2,6},{3,7},{4,0},{5,1},{6,2},{7,3},{8,12},{9,13},{10,... | collective-permute-start | bytes 393224 | tf_op jit(solution)/shard_map/ppermute | solution.py:417
  40.8 11.5 %collective-permute-start.14 = (f32[128,128]{1,0:T(8,128)S(1)}, f32[128,128]{1,0:T(8,128)S(1)}, u32[]{:S(2)}, u32[]{:S(2)}) collective-permute-start(f32[128,128]{1,0:T(8,128)S(1)} %shard_map.108.before_ref.gram_ref), channel_id=1, source_target_pairs={{0,4},{1,5},{2,6},{3,7},{4,0},{5,1},{6,2},{7,3},{8,12},{9,13},{10,... | collective-permute-start | bytes 196616 | tf_op jit(solution)/shard_map/ppermute | solution.py:417
  46.3 3.5 %copy-start.1 = (bf16[2,32,128,128]{3,2,1,0:T(8,128)(2,1)S(1)}, bf16[2,32,128,128]{3,2,1,0:T(8,128)(2,1)}, u32[]{:S(2)}) copy-start(bf16[2,32,128,128]{3,2,1,0:T(8,128)(2,1)} %refs_7_.1) | copy-start | bytes 6291460
  52.3 1.4 %collective-permute-start.15 = (f32[152,128]{1,0:T(8,128)S(1)}, f32[152,128]{1,0:T(8,128)S(1)}, u32[]{:S(2)}, u32[]{:S(2)}) collective-permute-start(f32[152,128]{1,0:T(8,128)S(1)} %shard_map.111.own_ref), channel_id=1, source_target_pairs={{0,32},{32,0},{1,33},{33,1},{2,34},{34,2},{3,35},{35,3},{4,36},{36... | collective-permute-start | bytes 233480 | tf_op jit(solution)/shard_map/ppermute | solution.py:417
